TPU v7x, 32 devices: a whole 2x2x4 slice. The times are simulated.
32 devices in a mesh: ang: 16 (over z, y, core), ax: 2 (over x).
Axes of the slice: x: 2, y: 2, z: 4, core: 2. Of those that a mesh axis runs over, the one named last changes fastest.
Arguments:
- concentration: float32 [3, 512, 32, 512], P(None, 'ang', 'ax'), may hold values from 0.1 to 2
- courant: float32 [512], replicated, may hold values from 0.1 to 0.35
- axial_diffusion: float32 [3], replicated, may hold values from 0.05 to 0.12
- angular_rate: float32 [3, 512], replicated, may hold values from 0.05 to 0.18
- rate_constants: float32 [4], replicated, may hold values from 0.05 to 0.2
- species_map: int32 [4, 3], replicated, may hold values from 0 to 2, each once within a row
- wall_flags: int32 [3, 512], P(None, 'ang'), may hold values 0 or 1
- radial_inverse: bfloat16 [3, 1024, 1024], replicated, may hold values from -1 to 1, as said below
Outputs:
- final_field: float32 [3, 512, 32, 512], P(None, 'ang', 'ax')
Inputs may be any that keep to these rules, and one draw needn't show every extreme that they name: Every matrix is centrosymmetric: radial_inverse[s, i, j] equals radial_inverse[s, 1023 - i, 1023 - j].
All inputs are finite; a program needn't handle non-finite values. No bound on the sum of `wall_flags` on one device may be relied on, other than what follows from the above.
Results may differ from a plain program's by a relative error of at most 0.0029.
Values may be sent and summed in bfloat16 or wider, within the bound.
No kernel may reach another device: no remote copies, remote signals or barrier semaphores. Data moves between devices by JAX's collectives and lax.ppermute only.
A program may use at most 64 MiB of HBM per device.

v0:
```python
import jax
import jax.numpy as jnp
from jax import lax
from jax.sharding import PartitionSpec as P

STEPS = 2


def extended(block, sides, width, periodic):
    for axis, dim in sides:
        count = lax.axis_size(axis)
        forward = [(i, i + 1) for i in range(count - 1)]
        if periodic:
            forward.append((count - 1, 0))
        backward = [(target, source) for source, target in forward]
        low = lax.ppermute(
            lax.slice_in_dim(block, block.shape[dim] - width, None, axis=dim), axis, forward
        )
        high = lax.ppermute(lax.slice_in_dim(block, 0, width, axis=dim), axis, backward)
        block = jnp.concatenate([low, block, high], axis=dim)
    return block


def swapped(value, axis, distance):
    mask = 2**distance
    pairs = [(source, source ^ mask) for source in range(lax.axis_size(axis))]
    return lax.ppermute(value, axis, pairs)


def product(matrix, values):
    return jnp.einsum("sij,sapj->sapi", matrix, values, preferred_element_type=jnp.float32)


def radial(matrices, mine, theirs):
    return product(matrices, jnp.concatenate((mine, theirs), 3))


def transport(field, courant, axial_diffusion, angular_rate, rate_constants, selectors, weights):
    angle_ext = extended(field, (("ang", 1),), 1, True)
    axial_ext = extended(field, (("ax", 2),), 1, False)
    angle_before = angle_ext[:, :-2]
    angle_after = angle_ext[:, 2:]
    axial_before = axial_ext[:, :, :-2]
    axial_after = axial_ext[:, :, 2:]
    reaction = jnp.zeros_like(field)
    for which_reaction in range(selectors.shape[0]):
        first_part = jnp.sum(selectors[which_reaction, 0][:, None, None, None] * field, axis=0)
        second_part = jnp.sum(selectors[which_reaction, 1][:, None, None, None] * field, axis=0)
        rate_term = rate_constants[which_reaction] * first_part * second_part
        reaction = reaction + weights[which_reaction][:, None, None, None] * rate_term[None]
    return (
        field
        - courant * (field - axial_before)
        + axial_diffusion[:, None, None, None] * (axial_after - 2.0 * field + axial_before)
        + angular_rate[:, None, None, :] * (angle_after - 2.0 * field + angle_before)
        + reaction
    )


def per_device(
    concentration,
    courant,
    axial_diffusion,
    angular_rate,
    rate_constants,
    species_map,
    wall_flags,
    radial_inverse,
):
    half_radial = concentration.shape[3]
    species_count = concentration.shape[0]
    angle_count = lax.axis_size("ang")
    pair_bit = angle_count.bit_length() - 2
    species_ids = lax.broadcasted_iota(
        jnp.int32, (species_map.shape[0], species_map.shape[1], species_count), 2
    )
    selectors = (species_map[:, :, None] == species_ids).astype(jnp.float32)
    weights = selectors[:, 2] - selectors[:, 0] - selectors[:, 1]
    own_left = radial_inverse[:, :half_radial, :half_radial]
    own_right = radial_inverse[:, :half_radial, half_radial:][:, :, ::-1]
    own_mats = jnp.concatenate((own_left, own_right), 2)
    wall_mask = lax.broadcasted_iota(jnp.int32, concentration.shape, 3) == 0
    absorbing = wall_flags[:, :, None, None] == 1
    field = concentration
    for step_index in range(STEPS):
        explicit = transport(
            field, courant, axial_diffusion, angular_rate, rate_constants, selectors, weights
        )
        explicit_low = explicit.astype(jnp.bfloat16)
        theirs = swapped(explicit_low, "ang", pair_bit)
        updated = radial(own_mats, explicit_low, theirs)
        wall_value = jnp.where(absorbing, 0.0, updated[:, :, :, 1:2])
        field = jnp.where(wall_mask, wall_value, updated)
    return field


def solution(mesh):
    in_specs = (P(None, "ang", "ax", None), P(), P(), P(), P(), P(), P(None, "ang"), P())
    out_specs = P(None, "ang", "ax", None)
    return jax.shard_map(
        per_device, mesh=mesh, in_specs=in_specs, out_specs=out_specs, check_vma=False
    )
```

profile of v0, /device:TPU:0, one launch (start us, length us, event | category | flops | bytes accessed | tf_op | source)
XLA Modules:
  0.0 205.4 jit_solution(6241528969904623870)
XLA Ops:
  1.0 5.5 %collective-permute-start.2 = (f32[3,1,16,512]{3,2,1,0:T(8,128)S(1)}, f32[3,1,16,512]{3,2,1,0:T(8,128)S(1)}, u32[]{:S(2)}, u32[]{:S(2)}) collective-permute-start(f32[3,1,16,512]{3,2,1,0:T(8,128)S(1)} %get-tuple-element.30), channel_id=1, source_target_pairs={{2,0},{4,2},{6,4},{8,6},{10,8},{12,10},{14,12},{16,14},{18,16},{20... | collective-permute-start | bytes 294920 | tf_op jit(solution)/shard_map/ppermute | solution.py:19
  6.5 2.3 %fusion.40 = (f32[3,32,1,512]{3,2,1,0:T(1,128)S(1)}, f32[3,32,1,512]{3,2,1,0:T(1,128)S(1)}) fusion(f32[3,32,16,512]{3,2,1,0:T(8,128)} %param.8), kind=kLoop, calls=%fused_computation.94 | loop fusion | bytes 786432 | tf_op jit(solution)/shard_map/slice | solution.py:17
  8.7 3.4 %collective-permute-start = (f32[3,32,1,512]{3,2,1,0:T(1,128)S(1)}, f32[3,32,1,512]{3,2,1,0:T(1,128)S(1)}, u32[]{:S(2)}, u32[]{:S(2)}) collective-permute-start(f32[3,32,1,512]{3,2,1,0:T(1,128)S(1)} %get-tuple-element.28), channel_id=1, source_target_pairs={{0,1},{2,3},{4,5},{6,7},{8,9},{10,11},{12,13},{14,15},{16,17},{18,... | collective-permute-start | bytes 589832 | tf_op jit(solution)/shard_map/ppermute | solution.py:16
  12.1 1.3 collective-permute-start.1
  14.2 1.5 fusion.42
  15.7 4.4 %multiply_reduce_fusion.15 = (f32[32,16,512]{2,1,0:T(8,128)S(1)}, f32[32,16,512]{2,1,0:T(8,128)S(1)}, f32[32,16,512]{2,1,0:T(8,128)S(1)}, f32[32,16,512]{2,1,0:T...) fusion(f32[3,32,16,512]{3,2,1,0:T(8,128)} %param.8, ...), kind=kLoop, calls=%fused_computation.58 | loop fusion | flops 10485760 | bytes 11534432 | tf_op jit(solution)/shard_map/reduce_sum | solution.py:47
  20.1 1.7 multiply_multiply_fusion.6
  21.8 2.3 %multiply_multiply_fusion.4 = (f32[32,16,512]{2,1,0:T(8,128)S(1)}, f32[32,16,512]{2,1,0:T(8,128)S(1)}) fusion(f32[32,16,512]{2,1,0:T(8,128)S(1)} %get-tuple-element.19, f32[32,16,512]{2,1,0:T(8,128)S(1)} %get-tuple-element.20, f32[]{:T(128)} %bitcast.13, f32[32,16,512]{2,1,0:T(8,128)S(1)} %get-tuple-element.17, f32[32,16,512]{2,1,0:T(8,128)S(1)} %get-tuple-element.16, ...), kind=kLoop, calls=%fused_computation.65 | loop fusion | flops 1048576 | bytes 6291464 | tf_op jit(solution)/shard_map/mul | solution.py:49
  24.2 3.8 %fusion.17 = bf16[3,32,16,512]{3,2,1,0:T(8,128)(2,1)S(1)} fusion(f32[3,32,16,512]{3,2,1,0:T(8,128)S(1)} %copy-done, f32[3,1,16,512]{3,2,1,0:T(8,128)S(1)} %collective-permute-done.3, f32[3,1,16,512]{3,2,1,0:T(8,128)S(1)} %collective-permute-done.2, f32[3,32,1,512]{3,2,1,0:T(1,128)S(1)} %collective-permute-done.1, ...), kind=kLoop, calls=%fused_computation.22 | loop fusion | flops 19660800 | bytes 9510972 | tf_op jit(solution)/shard_map/convert_element_type | solution.py:89
  28.2 1.6 fusion.37
  29.7 16.9 %rev.3 = bf16[3,512,512]{2,1,0:T(8,128)(2,1)} reverse(bf16[3,512,512]{2,1,0:T(8,128)(2,1)S(1)} %get-tuple-element.23), dimensions={2} | reverse | bytes 3145728 | tf_op jit(solution)/shard_map/rev | solution.py:80
  46.7 49.9 %collective-permute-done.4 = bf16[3,32,16,512]{3,2,1,0:T(8,128)(2,1)} collective-permute-done((bf16[3,32,16,512]{3,2,1,0:T(8,128)(2,1)S(1)}, bf16[3,32,16,512]{3,2,1,0:T(8,128)(2,1)}, u32[]{:S(2)}, u32[]{:S(2)}) %collective-permute-start.4) | collective-permute-done | bytes 1572896 | tf_op jit(solution)/shard_map/ppermute | solution.py:27
  96.6 4.7 %fusion.26 = f32[3,32,16,512]{3,2,1,0:T(8,128)S(1)} fusion(bf16[3,32,16,512]{3,2,1,0:T(8,128)(2,1)} %collective-permute-done.4, bf16[3,32,16,512]{3,2,1,0:T(8,128)(2,1)} %copy-done.1, bf16[3,512,512]{2,1,0:T(8,128)(2,1)} %rev.3, bf16[3,512,512]{2,1,0:T(8,128)(2,1)} %get-tuple-element.22), kind=kOutput, calls=%fused_computation.34 | convolution fusion | flops 1623195648 | bytes 9437184 | tf_op jit(solution)/shard_map/sij,sapj->sapi/dot_general | solution.py:31
  102.5 1.7 copy.14
  104.2 7.1 %multiply_reduce_fusion.7 = (f32[32,16,512]{2,1,0:T(8,128)S(1)}, f32[32,16,512]{2,1,0:T(8,128)S(1)}, f32[32,16,512]{2,1,0:T(8,128)S(1)}, f32[32,16,512]{2,1,0:T(...) fusion(f32[3]{0:T(128)S(1)} %get-tuple-element.37, ...), kind=kLoop, calls=%fused_computation.50 | loop fusion | flops 11272192 | bytes 14686816 | tf_op jit(solution)/shard_map/reduce_sum | solution.py:47
  111.7 4.2 %collective-permute-start.7 = (f32[3,1,16,512]{3,2,1,0:T(8,128)S(1)}, f32[3,1,16,512]{3,2,1,0:T(8,128)S(1)}, u32[]{:S(2)}, u32[]{:S(2)}) collective-permute-start(f32[3,1,16,512]{3,2,1,0:T(8,128)S(1)} %get-tuple-element.26), channel_id=1, source_target_pairs={{2,0},{4,2},{6,4},{8,6},{10,8},{12,10},{14,12},{16,14},{18,16},{20... | collective-permute-start | bytes 294920 | tf_op jit(solution)/shard_map/ppermute | solution.py:19
  115.9 4.6 %collective-permute-start.5 = (f32[3,32,1,512]{3,2,1,0:T(1,128)S(1)}, f32[3,32,1,512]{3,2,1,0:T(1,128)S(1)}, u32[]{:S(2)}, u32[]{:S(2)}) collective-permute-start(f32[3,32,1,512]{3,2,1,0:T(1,128)S(1)} %get-tuple-element.24), channel_id=1, source_target_pairs={{0,1},{2,3},{4,5},{6,7},{8,9},{10,11},{12,13},{14,15},{16,17},{18,... | collective-permute-start | bytes 589832 | tf_op jit(solution)/shard_map/ppermute | solution.py:16
  120.4 1.5 collective-permute-start.6
  125.3 2.7 %collective-permute-done.6 = f32[3,32,1,512]{3,2,1,0:T(1,128)S(1)} collective-permute-done((f32[3,32,1,512]{3,2,1,0:T(1,128)S(1)}, f32[3,32,1,512]{3,2,1,0:T(1,128)S(1)}, u32[]{:S(2)}, u32[]{:S(2)}) %collective-permute-start.6) | collective-permute-done | bytes 196640 | tf_op jit(solution)/shard_map/ppermute | solution.py:19
  128.0 3.8 %fusion.4 = bf16[3,32,16,512]{3,2,1,0:T(8,128)(2,1)S(1)} fusion(f32[3,32,16,512]{3,2,1,0:T(8,128)S(1)} %get-tuple-element.21, f32[3,1,16,512]{3,2,1,0:T(8,128)S(1)} %collective-permute-done.8, f32[3,1,16,512]{3,2,1,0:T(8,128)S(1)} %collective-permute-done.7, f32[3,32,1,512]{3,2,1,0:T(1,128)S(1)} %collective-permute-done.6, ...), kind=kLoop, calls=%fused_computation.5 | loop fusion | flops 19660800 | bytes 9510972 | tf_op jit(solution)/shard_map/convert_element_type | solution.py:89
  131.9 66.7 %collective-permute-done.9 = bf16[3,32,16,512]{3,2,1,0:T(8,128)(2,1)S(1)} collective-permute-done((bf16[3,32,16,512]{3,2,1,0:T(8,128)(2,1)S(1)}, bf16[3,32,16,512]{3,2,1,0:T(8,128)(2,1)S(1)}, u32[]{:S(2)}, u32[]{:S(2)}) %collective-permute-start.9) | collective-permute-done | bytes 1572896 | tf_op jit(solution)/shard_map/ppermute | solution.py:27
  198.6 1.8 fusion.30
  201.7 1.7 copy.15
  203.4 2.0 broadcast_select_fusion
  (47 shorter events, 8.2 us)
Async XLA Ops:
  1.0 23.2 %collective-permute-start.2 = (f32[3,1,16,512]{3,2,1,0:T(8,128)S(1)}, f32[3,1,16,512]{3,2,1,0:T(8,128)S(1)}, u32[]{:S(2)}, u32[]{:S(2)}) collective-permute-start(f32[3,1,16,512]{3,2,1,0:T(8,128)S(1)} %get-tuple-element.30), channel_id=1, source_target_pairs={{2,0},{4,2},{6,4},{8,6},{10,8},{12,10},{14,12},{16,14},{18,16},{20... | collective-permute-start | bytes 294920 | tf_op jit(solution)/shard_map/ppermute | solution.py:19
  6.5 17.7 %collective-permute-start.3 = (f32[3,1,16,512]{3,2,1,0:T(8,128)S(1)}, f32[3,1,16,512]{3,2,1,0:T(8,128)S(1)}, u32[]{:S(2)}, u32[]{:S(2)}) collective-permute-start(f32[3,1,16,512]{3,2,1,0:T(8,128)S(1)} %get-tuple-element.31), channel_id=1, source_target_pairs={{0,2},{2,4},{4,6},{6,8},{8,10},{10,12},{12,14},{14,16},{16,18},{18... | collective-permute-start | bytes 294920 | tf_op jit(solution)/shard_map/ppermute | solution.py:16
  8.7 15.4 %collective-permute-start = (f32[3,32,1,512]{3,2,1,0:T(1,128)S(1)}, f32[3,32,1,512]{3,2,1,0:T(1,128)S(1)}, u32[]{:S(2)}, u32[]{:S(2)}) collective-permute-start(f32[3,32,1,512]{3,2,1,0:T(1,128)S(1)} %get-tuple-element.28), channel_id=1, source_target_pairs={{0,1},{2,3},{4,5},{6,7},{8,9},{10,11},{12,13},{14,15},{16,17},{18,... | collective-permute-start | bytes 589832 | tf_op jit(solution)/shard_map/ppermute | solution.py:16
  12.1 12.0 %collective-permute-start.1 = (f32[3,32,1,512]{3,2,1,0:T(1,128)S(1)}, f32[3,32,1,512]{3,2,1,0:T(1,128)S(1)}, u32[]{:S(2)}, u32[]{:S(2)}) collective-permute-start(f32[3,32,1,512]{3,2,1,0:T(1,128)S(1)} %get-tuple-element.29), channel_id=1, source_target_pairs={{1,0},{3,2},{5,4},{7,6},{9,8},{11,10},{13,12},{15,14},{17,16},{19,... | collective-permute-start | bytes 589832 | tf_op jit(solution)/shard_map/ppermute | solution.py:19
  20.1 4.1 %copy-start.4 = (f32[3,512]{1,0:T(4,128)S(1)}, f32[3,512]{1,0:T(4,128)}, u32[]{:S(2)}) copy-start(f32[3,512]{1,0:T(4,128)} %param.11) | copy-start | bytes 18436
  20.1 4.1 %copy-start.5 = (f32[512]{0:T(512)S(1)}, f32[512]{0:T(512)}, u32[]{:S(2)}) copy-start(f32[512]{0:T(512)} %param.9) | copy-start | bytes 6148
  20.1 4.1 %copy-start.6 = (f32[3]{0:T(128)S(1)}, f32[3]{0:T(128)}, u32[]{:S(2)}) copy-start(f32[3]{0:T(128)} %param.10) | copy-start | bytes 40
  21.8 2.4 %copy-start = (f32[3,32,16,512]{3,2,1,0:T(8,128)S(1)}, f32[3,32,16,512]{3,2,1,0:T(8,128)}, u32[]{:S(2)}) copy-start(f32[3,32,16,512]{3,2,1,0:T(8,128)} %param.8) | copy-start | bytes 9437188
  21.8 6.3 %slice-start = ((s8[6291456]{0:T(1024)(128)(4,1)}), s8[4194304]{0:T(1024)(128)(4,1)S(1)}, s32[]{:S(2)}) async-start(s8[6291456]{0:T(1024)(128)(4,1)} %bitcast.38), calls=%async_computation | async-start | bytes 8388608
  24.2 4.0 %slice-start.1 = ((s8[6291456]{0:T(1024)(128)(4,1)}), s8[2097152]{0:T(1024)(128)(4,1)S(1)}, s32[]{:S(2)}) async-start(s8[6291456]{0:T(1024)(128)(4,1)} %bitcast.38), calls=%async_computation.1 | async-start | bytes 4194304
  28.1 1.7 copy-start.1
  28.1 68.5 %collective-permute-start.4 = (bf16[3,32,16,512]{3,2,1,0:T(8,128)(2,1)S(1)}, bf16[3,32,16,512]{3,2,1,0:T(8,128)(2,1)}, u32[]{:S(2)}, u32[]{:S(2)}) collective-permute-start(bf16[3,32,16,512]{3,2,1,0:T(8,128)(2,1)S(1)} %fusion.17), channel_id=1, source_target_pairs={{0,16},{2,18},{4,20},{6,22},{8,24},{10,26},{12,28},{14,30},{16,0},... | collective-permute-start | bytes 4718600 | tf_op jit(solution)/shard_map/ppermute | solution.py:27
  29.7 16.9 %copy-start.7 = (s32[3,32]{1,0:T(4,128)S(1)}, s32[3,32]{1,0:T(4,128)}, u32[]{:S(2)}) copy-start(s32[3,32]{1,0:T(4,128)} %param.14) | copy-start | bytes 1156
  111.7 13.6 %collective-permute-start.7 = (f32[3,1,16,512]{3,2,1,0:T(8,128)S(1)}, f32[3,1,16,512]{3,2,1,0:T(8,128)S(1)}, u32[]{:S(2)}, u32[]{:S(2)}) collective-permute-start(f32[3,1,16,512]{3,2,1,0:T(8,128)S(1)} %get-tuple-element.26), channel_id=1, source_target_pairs={{2,0},{4,2},{6,4},{8,6},{10,8},{12,10},{14,12},{16,14},{18,16},{20... | collective-permute-start | bytes 294920 | tf_op jit(solution)/shard_map/ppermute | solution.py:19
  115.9 9.4 %collective-permute-start.8 = (f32[3,1,16,512]{3,2,1,0:T(8,128)S(1)}, f32[3,1,16,512]{3,2,1,0:T(8,128)S(1)}, u32[]{:S(2)}, u32[]{:S(2)}) collective-permute-start(f32[3,1,16,512]{3,2,1,0:T(8,128)S(1)} %get-tuple-element.27), channel_id=1, source_target_pairs={{0,2},{2,4},{4,6},{6,8},{8,10},{10,12},{12,14},{14,16},{16,18},{18... | collective-permute-start | bytes 294920 | tf_op jit(solution)/shard_map/ppermute | solution.py:16
  115.9 9.4 %collective-permute-start.5 = (f32[3,32,1,512]{3,2,1,0:T(1,128)S(1)}, f32[3,32,1,512]{3,2,1,0:T(1,128)S(1)}, u32[]{:S(2)}, u32[]{:S(2)}) collective-permute-start(f32[3,32,1,512]{3,2,1,0:T(1,128)S(1)} %get-tuple-element.24), channel_id=1, source_target_pairs={{0,1},{2,3},{4,5},{6,7},{8,9},{10,11},{12,13},{14,15},{16,17},{18,... | collective-permute-start | bytes 589832 | tf_op jit(solution)/shard_map/ppermute | solution.py:16
  120.4 7.6 %collective-permute-start.6 = (f32[3,32,1,512]{3,2,1,0:T(1,128)S(1)}, f32[3,32,1,512]{3,2,1,0:T(1,128)S(1)}, u32[]{:S(2)}, u32[]{:S(2)}) collective-permute-start(f32[3,32,1,512]{3,2,1,0:T(1,128)S(1)} %get-tuple-element.25), channel_id=1, source_target_pairs={{1,0},{3,2},{5,4},{7,6},{9,8},{11,10},{13,12},{15,14},{17,16},{19,... | collective-permute-start | bytes 589832 | tf_op jit(solution)/shard_map/ppermute | solution.py:19
  125.2 73.4 %copy-start.2 = (bf16[3,512,512]{2,1,0:T(8,128)(2,1)S(1)}, bf16[3,512,512]{2,1,0:T(8,128)(2,1)}, u32[]{:S(2)}) copy-start(bf16[3,512,512]{2,1,0:T(8,128)(2,1)} %rev.3) | copy-start | bytes 4718596
  125.3 73.4 %copy-start.3 = (bf16[3,512,512]{2,1,0:T(8,128)(2,1)S(1)}, bf16[3,512,512]{2,1,0:T(8,128)(2,1)}, u32[]{:S(2)}) copy-start(bf16[3,512,512]{2,1,0:T(8,128)(2,1)} %get-tuple-element.22) | copy-start | bytes 4718596
  131.8 66.8 %collective-permute-start.9 = (bf16[3,32,16,512]{3,2,1,0:T(8,128)(2,1)S(1)}, bf16[3,32,16,512]{3,2,1,0:T(8,128)(2,1)S(1)}, u32[]{:S(2)}, u32[]{:S(2)}) collective-permute-start(bf16[3,32,16,512]{3,2,1,0:T(8,128)(2,1)S(1)} %fusion.4), channel_id=1, source_target_pairs={{0,16},{2,18},{4,20},{6,22},{8,24},{10,26},{12,28},{14,30},{16,0},... | collective-permute-start | bytes 4718600 | tf_op jit(solution)/shard_map/ppermute | solution.py:27
where the time goes:
time: 207 us; the launch traced here: 205 us
  waiting for transfers between devices  119 us (57%)
  other arithmetic  31.6 us (15%)
  local copies, waits for them, and re-layouts  27.1 us (13%)
  starting transfers between devices  20.5 us (10%)
  matrix products  6.47 us (3%)
    ppermute x2, waiting for transfers between devices, swapped(): return lax.ppermute(value, axis, pairs)  117 us
    rev x1, local copies, waits for them, and re-layouts, per_device(): own_right = radial_inverse[:, :half_radial, half_radial:][:, :, ::-1]  16.9 us
    ppermute x4, starting transfers between devices, extended(): lax.ppermute(lax.slice_in_dim(block, 0, width, axis=dim), axis, backward)  12.4 us
    reduce_sum x2, other arithmetic, transport(): jnp.sum(selectors[which_reaction, 0][:, None, None, None] * field, axis=0)  11.4 us
    ppermute x4, starting transfers between devices, extended(): lax.ppermute(lax.slice_in_dim(block, block.shape[dim] - width, None, axis...  7.97 us
    convert_element_type x2, other arithmetic, per_device(): explicit_low = explicit.astype(jnp.bfloat16)  7.62 us
    mul x6, other arithmetic, transport(): rate_term = rate_constants[which_reaction] * first_part * second_part  7.28 us
    dot_general x2, matrix products, product(): jnp.einsum('sij,sapj->sapi', matrix, values, preferred_element_type=jnp.f...  6.47 us
  transfers between devices with their start and end apart: 10, of which 3 were waited for; matrix products, arithmetic and copies ran while one was open for 17% of the time, Pallas kernels for 0%

commit v1 on v0

v1 whole, which is shorter than its diff:
```python
import functools

import jax
import jax.numpy as jnp
from jax import lax
from jax.experimental import pallas as pl
from jax.experimental.pallas import tpu as pltpu
from jax.sharding import PartitionSpec as P

STEPS = 2
F32 = jnp.float32
BF16 = jnp.bfloat16
VMEM_LIMIT = 48 * 1024 * 1024

ANY = pl.BlockSpec(memory_space=pl.ANY)
VM = pl.BlockSpec(memory_space=pltpu.VMEM)
SM = pl.BlockSpec(memory_space=pltpu.SMEM)


def call(body, out_shape, in_specs, out_specs, scratch, args, cost, aliases=None):
    return pl.pallas_call(
        body,
        out_shape=out_shape,
        in_specs=in_specs,
        out_specs=out_specs,
        scratch_shapes=scratch,
        input_output_aliases=aliases or {},
        cost_estimate=pl.CostEstimate(flops=cost[0], bytes_accessed=cost[1], transcendentals=0),
        compiler_params=pltpu.CompilerParams(vmem_limit_bytes=VMEM_LIMIT),
    )(*args)


def product_rates(rate_ref, map_ref):
    rates = []
    for species in range(3):
        total = jnp.float32(0.0)
        for k in range(map_ref.shape[0]):
            total = total + jnp.where(map_ref[k, 2] == species, rate_ref[k], 0.0)
        rates.append(total)
    return rates


def transport(now, before, after, around, courant, axial, angular, rates):
    made = (
        rates[0] * (now[1] * now[2]),
        rates[1] * (now[0] * now[2]),
        rates[2] * (now[0] * now[1]),
    )
    spent = made[0] + made[1] + made[2]
    out = []
    for s in range(3):
        own = (1.0 - 2.0 * axial[s]) - courant - 2.0 * angular[s]
        value = now[s] * own + before[s] * (courant + axial[s]) + after[s] * axial[s]
        value = value + around[s] * angular[s]
        out.append(value + (2.0 * made[s] - spent))
    return out


def coefficients(cour_ref, diff_ref, ang_ref, rate_ref, map_ref):
    courant = cour_ref[...]
    axial = [diff_ref[s] for s in range(3)]
    angular = [ang_ref[s : s + 1, :] for s in range(3)]
    return courant, axial, angular, product_rates(rate_ref, map_ref)


def plane_edges(nz, nr, first, last):
    row = lax.broadcasted_iota(jnp.int32, (nz, nr), 0)
    return row == first, row == last


def first_step_angle(read, low, high, coef, nz):
    now = [read(s, 0) for s in range(3)]
    around = [read(s, -1) + read(s, 1) for s in range(3)]
    before = [pltpu.roll(v, 1, 0) for v in now]
    after = [pltpu.roll(v, nz - 1, 0) for v in now]
    if low is not None:
        is_first, is_last = plane_edges(nz, now[0].shape[1], 0, nz - 1)
        before = [jnp.where(is_first, low(s), before[s]) for s in range(3)]
        after = [jnp.where(is_last, high(s), after[s]) for s in range(3)]
    out = transport(now, before, after, around, *coef)
    return [pltpu.roll(v, nz - nz // 4, 0) for v in out]


def head_kernel(sizes, conc, cour, diff, ang, rate, smap, low, high, first, last, mid, field, sems):
    na, nz, lo, hi = sizes
    half = nz // 2
    inner = pl.ds((lo - 1) * nz, (hi - lo + 2) * nz)
    left = pl.ds(0, (lo - 1) * nz)
    right = pl.ds((hi + 1) * nz, (na - hi - 1) * nz)
    copies = [
        pltpu.make_async_copy(conc.at[:, rows], field.at[:, rows], sems.at[k])
        for k, rows in enumerate((inner, left, right))
    ]
    for copy in copies:
        copy.start()
    coef = coefficients(cour, diff, ang, rate, smap)
    copies[0].wait()

    def pair(step, carry):
        tiles = []
        for k in range(2):
            t = lo + step * 2 + k

            def read(s, shift):
                return field[s, pl.ds(pl.multiple_of((t + shift) * nz, nz), nz), :]

            tiles.append(first_step_angle(read, None, None, coef, nz))
        for s in range(3):
            both = jnp.concatenate([tiles[0][s][:half], tiles[1][s][:half]], 0)
            mid[s, pl.ds(pl.multiple_of(step * nz, nz), nz), :] = both.astype(BF16)
        return carry

    lax.fori_loop(0, (hi - lo) // 2, pair, 0)
    copies[1].wait()
    copies[2].wait()
    for s in range(3):
        for t in range(na):
            low[s, t : t + 1, :] = field[s, t * nz : t * nz + 1, :]
            high[s, t : t + 1, :] = field[s, (t + 1) * nz - 1 : (t + 1) * nz, :]
        first[s] = field[s, pl.ds(0, nz), :]
        last[s] = field[s, pl.ds((na - 1) * nz, nz), :]


def inner_kernel(sizes, runs, conc, cour, diff, ang, rate, smap, *rest):
    na, nz = sizes
    half = nz // 2
    outs, field, sem = rest[:-2], rest[-2], rest[-1]
    copy = pltpu.make_async_copy(conc, field, sem)
    copy.start()
    coef = coefficients(cour, diff, ang, rate, smap)
    copy.wait()
    for out, begin, count, at in runs:

        def pair(step, carry):
            tiles = []
            for k in range(2):
                t = begin + step * 2 + k

                def read(s, shift):
                    return field[s, pl.ds(pl.multiple_of((t + shift) * nz, nz), nz), :]

                tiles.append(first_step_angle(read, None, None, coef, nz))
            for s in range(3):
                both = jnp.concatenate([tiles[0][s][:half], tiles[1][s][:half]], 0)
                rows = pl.ds(pl.multiple_of(at * half + step * nz, nz), nz)
                outs[out][s, rows, :] = both.astype(BF16)
            return carry

        lax.fori_loop(0, count // 2, pair, 0)


def frame_kernel(sizes, conc, before, after, low, high, cour, diff, ang, rate, smap, out1, out2, field, sems):
    na, nz, ends = sizes
    half = nz // 2
    copies = [
        pltpu.make_async_copy(conc, field.at[:, pl.ds(nz, na * nz)], sems.at[0]),
        pltpu.make_async_copy(before, field.at[:, pl.ds(0, nz)], sems.at[1]),
        pltpu.make_async_copy(after, field.at[:, pl.ds((na + 1) * nz, nz)], sems.at[2]),
    ]
    for copy in copies:
        copy.start()
    coef = coefficients(cour, diff, ang, rate, smap)
    for copy in copies:
        copy.wait()

    def angle(t):
        def read(s, shift):
            return field[s, pl.ds(pl.multiple_of((t + 1 + shift) * nz, nz), nz), :]

        return first_step_angle(
            read, lambda s: low[s, pl.ds(t, 1), :], lambda s: high[s, pl.ds(t, 1), :], coef, nz
        )

    def pair(t, out, row, ends_row):
        tiles = [angle(t), angle(t + 1)]
        for s in range(3):
            both = jnp.concatenate([tiles[0][s][half:], tiles[1][s][half:]], 0)
            out[s, pl.ds(row, nz), :] = both.astype(BF16)
            if ends_row is not None:
                both = jnp.concatenate([tiles[0][s][:half], tiles[1][s][:half]], 0)
                out2[s, pl.ds(ends_row, nz), :] = both.astype(BF16)

    quarter = na // 4
    tail = na // 2 * half
    pair(0, out1, 0, tail)
    pair(na - 2, out2, (na // 2 - 2) * half, tail + nz)

    def first_part(step, carry):
        pair(step * 2, out1, pl.multiple_of(step * nz, nz), None)
        return carry

    def second_part(step, carry):
        pair(na // 2 + step * 2, out2, pl.multiple_of(step * nz, nz), None)
        return carry

    lax.fori_loop(1, quarter, first_part, 0)
    lax.fori_loop(0, quarter - 1, second_part, 0)


def weights_kernel(matrix, out, left, lower, sems):
    half = out.shape[1]
    copies = []
    for s in range(out.shape[0]):
        copies.append(
            pltpu.make_async_copy(
                matrix.at[s, pl.ds(0, half), pl.ds(0, half)], left.at[s], sems.at[0, s]
            )
        )
        copies.append(
            pltpu.make_async_copy(
                matrix.at[s, pl.ds(half, half), pl.ds(0, half)], lower.at[s], sems.at[1, s]
            )
        )
    for copy in copies:
        copy.start()
    row = lax.broadcasted_iota(jnp.int32, (half, half), 0)
    col = lax.broadcasted_iota(jnp.int32, (half, half), 1)
    row = jnp.maximum(row, 1)
    pick = jnp.where(col == row, 1.0, 0.0).astype(BF16)
    flip = jnp.where(col == half - 1 - row, 1.0, 0.0).astype(BF16)
    for copy in copies:
        copy.wait()
    for s in range(out.shape[0]):
        out[s, :, :half] = jnp.dot(pick, left[s], preferred_element_type=F32).astype(BF16)
        out[s, :, half:] = jnp.dot(flip, lower[s], preferred_element_type=F32).astype(BF16)


def both_sides(mine, theirs, weights):
    rows = jnp.concatenate(
        [jnp.concatenate([mine, theirs], 1), jnp.concatenate([theirs, mine], 1)], 0
    )
    return lax.dot_general(rows, weights, (((1,), (1,)), ((), ())), preferred_element_type=F32)


def absorb(value, flag):
    lane = lax.broadcasted_iota(jnp.int32, value.shape, 1)
    return jnp.where((lane == 0) & (flag == 1), 0.0, value)


def store_absorbed(out, ab, s, at, value, flags, angles, half):
    lanes = 128
    out[ab, s, pl.ds(at, value.shape[0]), :] = value
    for k, t in enumerate(angles):
        part = value[k * half : (k + 1) * half, :lanes]
        out[ab, s, pl.ds(at + k * half, half), :lanes] = absorb(part, flags[s, t])


def radial_kernel(groups, half, weights, flags_own, flags_opp, *refs):
    n = len(groups)
    mines, theirs, outs = refs[:n], refs[n : 2 * n], refs[2 * n :]
    for s in range(3):
        for k, angles in enumerate(groups):
            rows = len(angles) * half
            value = both_sides(mines[k][s], theirs[k][s], weights[s])
            store_absorbed(outs[k], 0, s, 0, value[:rows], flags_own, angles, half)
            store_absorbed(outs[k], 1, s, 0, value[rows:], flags_opp, angles, half)


def edges_kernel(na, nz, outer1, outer2, low, high, first, last):
    half = nz // 2
    part = na // 2
    tail = part * half
    for ab in range(2):
        for s in range(3):
            for k, outer in enumerate((outer1, outer2)):
                for t in range(part):
                    to = pl.ds(k * part + t, 1)
                    at = t * half + half // 2
                    high[ab, s, to, :] = outer[ab, s, at - 1 : at, :]
                    low[ab, s, to, :] = outer[ab, s, at : at + 1, :]
            first[ab, s, pl.ds(0, half), :] = outer2[ab, s, pl.ds(tail, half), :]
            first[ab, s, pl.ds(half, half), :] = outer1[ab, s, pl.ds(0, half), :]
            last[ab, s, pl.ds(0, half), :] = outer2[ab, s, pl.ds(tail + 3 * half, half), :]
            last[ab, s, pl.ds(half, half), :] = outer2[ab, s, pl.ds(tail - half, half), :]


def second_step(read_mid, read_outer, low, high, coef, nz):
    now = [jnp.concatenate([read_mid(s, 0), read_outer(s, 0)], 0) for s in range(3)]
    around = [
        jnp.concatenate(
            [read_mid(s, -1) + read_mid(s, 1), read_outer(s, -1) + read_outer(s, 1)], 0
        )
        for s in range(3)
    ]
    quarter = nz // 4
    is_first, is_last = plane_edges(nz, now[0].shape[1], nz - quarter, nz - quarter - 1)
    before = [jnp.where(is_first, low(s), pltpu.roll(now[s], 1, 0)) for s in range(3)]
    after = [jnp.where(is_last, high(s), pltpu.roll(now[s], nz - 1, 0)) for s in range(3)]
    return transport(now, before, after, around, *coef)


def step_angles(begin, count, mid, outer, low, high, coef, rows, nz):
    half = nz // 2

    def one(step, carry):
        t = begin + step
        for ab in range(2):

            def read(ref, s, shift):
                return ref[ab, s, pl.ds(pl.multiple_of((t + 1 + shift) * half, half), half), :]

            out = second_step(
                lambda s, shift: read(mid, s, shift),
                lambda s, shift: read(outer, s, shift),
                lambda s: low[ab, s, pl.ds(t, 1), :],
                lambda s: high[ab, s, pl.ds(t, 1), :],
                coef,
                nz,
            )
            width = out[0].shape[1]
            for s in range(3):
                at = pl.ds(pl.multiple_of(t * nz, nz), nz)
                rows[s, at, ab * width : (ab + 1) * width] = out[s].astype(BF16)
        return carry

    lax.fori_loop(0, count, one, 0)


def finish_angles(begin, count, s, rows, weights, flags, result, nz):
    lanes = 128
    value = lax.dot_general(
        rows[s, pl.ds(begin * nz, count * nz), :],
        weights[s],
        (((1,), (1,)), ((), ())),
        preferred_element_type=F32,
    )
    for k in range(count):
        part = pltpu.roll(value[k * nz : (k + 1) * nz], nz // 4, 0)
        result[s, begin + k] = part
        result[s, begin + k, :, :lanes] = absorb(part[:, :lanes], flags[s, begin + k])


def early_kernel(
    sizes, weights, flags, swap, outer1, outer2, mid_a, mid_c, before, after, low, high,
    cour, diff, ang, rate, smap, out, mid, outer, rows, result, sems, out_sems,
):
    na, nz, lo, hi, ends = sizes
    half = nz // 2
    part = na // 2
    tail = part * half
    copies = []

    def bring(src, dst):
        copies.append(pltpu.make_async_copy(src, dst, sems.at[len(copies)]))

    def slots(ref, t, count):
        return ref.at[:, :, pl.ds((t + 1) * half, count * half)]

    def cut(ref, at, count):
        return ref.at[:, :, pl.ds(at, count * half)]

    bring(cut(outer1, 0, part), slots(outer, 0, part))
    bring(cut(outer2, 0, part), slots(outer, part, part))
    bring(cut(outer2, tail, 2), slots(mid, 0, 2))
    bring(cut(outer2, tail + 2 * half, 2), slots(mid, na - 2, 2))
    bring(mid_a, slots(mid, lo, hi - lo))
    bring(cut(mid_c, 0, lo - 2), slots(mid, 2, lo - 2))
    bring(cut(mid_c, (lo - 2) * half, lo - 2), slots(mid, na - lo, lo - 2))
    for ab in range(2):
        src = jnp.where(swap[0] == 1, 1 - ab, ab)
        bring(before.at[src, :, pl.ds(0, half)], mid.at[ab, :, pl.ds(0, half)])
        bring(before.at[src, :, pl.ds(half, half)], outer.at[ab, :, pl.ds(0, half)])
        src = jnp.where(swap[1] == 1, 1 - ab, ab)
        end = pl.ds((na + 1) * half, half)
        bring(after.at[src, :, pl.ds(0, half)], mid.at[ab, :, end])
        bring(after.at[src, :, pl.ds(half, half)], outer.at[ab, :, end])
    for copy in copies:
        copy.start()
    coef = coefficients(cour, diff, ang, rate, smap)
    for copy in copies:
        copy.wait()
    runs = ((0, hi - 1), (na - lo + 1, lo - 1))
    for begin, count in runs:
        step_angles(begin, count, mid, outer, low, high, coef, rows, nz)
    leaves = []
    for s in range(3):
        for k, (begin, count) in enumerate(runs):
            finish_angles(begin, count, s, rows, weights, flags, result, nz)
            span = pl.ds(begin, count)
            leave = pltpu.make_async_copy(
                result.at[s, span], out.at[s, span], out_sems.at[k, s]
            )
            leave.start()
            leaves.append(leave)
    for leave in leaves:
        leave.wait()


def late_kernel(
    sizes, given, weights, flags_own, flags_opp, mine, theirs, outer1, outer2, mid_a, mid_c,
    low, high, cour, diff, ang, rate, smap, out, mid, outer, rows, result, sems, out_sems,
):
    na, nz, lo, hi = sizes
    half = nz // 2
    part = na // 2
    copies = []

    def bring(src, dst):
        copies.append(pltpu.make_async_copy(src, dst, sems.at[len(copies)]))

    def slots(ref, t, count):
        return ref.at[:, :, pl.ds((t + 1) * half, count * half)]

    def cut(ref, at, count):
        return ref.at[:, :, pl.ds(at, count * half)]

    bring(cut(outer1, (lo - 2) * half, 2), slots(outer, lo - 2, 2))
    bring(cut(outer2, 0, hi + 2 - part), slots(outer, part, hi + 2 - part))
    bring(cut(mid_a, mid_a.shape[2] - 2 * half, 2), slots(mid, lo - 2, 2))
    bring(cut(mid_c, mid_c.shape[2] // 2, 2), slots(mid, hi, 2))
    for copy in copies:
        copy.start()
    coef = coefficients(cour, diff, ang, rate, smap)
    count = hi - lo
    size = count * half
    for s in range(3):
        value = both_sides(mine[s], theirs[s], weights[s])
        for ab, flags in ((0, flags_own), (1, flags_opp)):
            store_absorbed(
                mid, ab, s, (lo + 1) * half, value[ab * size : (ab + 1) * size],
                flags, range(lo, hi), half,
            )
    for copy in copies:
        copy.wait()
    step_angles(lo - 1, count + 2, mid, outer, low, high, coef, rows, nz)
    leaves = []
    for s in range(3):
        finish_angles(lo - 1, count + 2, s, rows, weights, flags_own, result, nz)
        span = pl.ds(lo - 1, count + 2)
        leave = pltpu.make_async_copy(result.at[s, span], out.at[s, span], out_sems.at[s])
        leave.start()
        leaves.append(leave)
    for leave in leaves:
        leave.wait()


def ring(count, step):
    half = count // 2
    return [(i, i // half * half + (i % half + step) % half) for i in range(count)]


def per_device(
    concentration, courant, axial_diffusion, angular_rate, rate_constants, species_map,
    wall_flags, radial_inverse,
):
    ns, na, nz, nr = concentration.shape
    half = nz // 2
    count = lax.axis_size("ang")
    planes = lax.axis_size("ax")
    quarter = na // 4
    lo, hi = quarter, 2 * quarter
    ends = 2
    opposite = [(i, (i + count // 2) % count) for i in range(count)]
    up = [(i, i + 1) for i in range(planes - 1)]
    down = [(i + 1, i) for i in range(planes - 1)]
    after_ring = [(i, (i - 1) % count) for i in range(count)]
    before_ring = [(i, (i + 1) % count) for i in range(count)]

    def shape(*dims, dtype=F32):
        return jax.ShapeDtypeStruct(dims, dtype)

    conc = concentration.reshape(ns, na * nz, nr)
    cour = courant[None]
    params = (cour, axial_diffusion, angular_rate, rate_constants, species_map)
    param_specs = [VM, SM, VM, SM, SM]
    field = ns * na * nz * nr

    low, high, first, last, mid_a = call(
        functools.partial(head_kernel, (na, nz, lo, hi)),
        [
            shape(ns, na, nr), shape(ns, na, nr), shape(ns, nz, nr), shape(ns, nz, nr),
            shape(ns, quarter * half, nr, dtype=BF16),
        ],
        [ANY] + param_specs,
        [VM] * 5,
        [pltpu.VMEM((ns, na * nz, nr), F32), pltpu.SemaphoreType.DMA((3,))],
        (conc,) + params,
        (field * 10, field * 4),
    )
    plane_before = lax.ppermute(high, "ax", up)
    plane_after = lax.ppermute(low, "ax", down)
    angle_before = lax.ppermute(last, "ang", before_ring)
    angle_after = lax.ppermute(first, "ang", after_ring)
    opp_a = lax.ppermute(mid_a, "ang", opposite)

    inner_count = quarter - ends
    mid_c, mid_d = call(
        functools.partial(
            inner_kernel,
            (na, nz),
            (
                (0, ends, inner_count, 0),
                (0, na - quarter, inner_count, inner_count),
                (1, hi, quarter, 0),
            ),
        ),
        [
            shape(ns, 2 * inner_count * half, nr, dtype=BF16),
            shape(ns, quarter * half, nr, dtype=BF16),
        ],
        [ANY] + param_specs,
        [VM] * 2,
        [pltpu.VMEM((ns, na * nz, nr), F32), pltpu.SemaphoreType.DMA],
        (conc,) + params,
        (field * 10, field * 4),
    )
    out1, out2 = call(
        functools.partial(frame_kernel, (na, nz, ends)),
        [
            shape(ns, na // 2 * half, nr, dtype=BF16),
            shape(ns, (na // 2 + 2 * ends) * half, nr, dtype=BF16),
        ],
        [ANY] * 3 + [VM] * 2 + param_specs,
        [VM] * 2,
        [pltpu.VMEM((ns, (na + 2) * nz, nr), F32), pltpu.SemaphoreType.DMA((3,))],
        (conc, angle_before, angle_after, plane_before, plane_after) + params,
        (field * 20, field * 4),
    )
    opp_1 = lax.ppermute(out1, "ang", opposite)
    opp_2 = lax.ppermute(out2, "ang", opposite)
    mid_c, opp_a = lax.optimization_barrier((mid_c, opp_a))
    opp_c = lax.ppermute(mid_c, "ang", opposite)
    mid_d, opp_1 = lax.optimization_barrier((mid_d, opp_1))
    opp_d = lax.ppermute(mid_d, "ang", opposite)

    weights = call(
        weights_kernel,
        shape(ns, nr, 2 * nr, dtype=BF16),
        [ANY],
        VM,
        [
            pltpu.VMEM((ns, nr, nr), BF16), pltpu.VMEM((ns, nr, nr), BF16),
            pltpu.SemaphoreType.DMA((2, ns)),
        ],
        (radial_inverse,),
        (ns * 4 * nr**3, ns * 8 * nr * nr),
    )
    flags_opp = lax.ppermute(wall_flags, "ang", opposite)

    middle = tuple(range(lo, hi))
    group_1 = tuple(range(na // 2))
    group_2 = tuple(range(na // 2, na)) + (0, 1, na - 2, na - 1)
    group_c = tuple(range(ends, quarter)) + tuple(range(na - quarter, na - ends))

    def radial(groups, mines, theirs):
        rows = sum(len(g) for g in groups) * half
        return call(
            functools.partial(radial_kernel, groups, half),
            [shape(2, ns, len(g) * half, nr) for g in groups],
            [VM, SM, SM] + [VM] * (2 * len(groups)),
            [VM] * len(groups),
            [],
            (weights, wall_flags, flags_opp) + tuple(mines) + tuple(theirs),
            (ns * 2 * rows * 4 * nr * nr, ns * rows * nr * 12),
        )

    new_a, new_1, new_2 = radial((middle, group_1, group_2), (mid_a, out1, out2), (opp_a, opp_1, opp_2))
    (new_c,) = radial((group_c,), (mid_c,), (opp_c,))
    low2, high2, first2, last2 = call(
        functools.partial(edges_kernel, na, nz),
        [shape(2, ns, na, nr), shape(2, ns, na, nr), shape(2, ns, nz, nr), shape(2, ns, nz, nr)],
        [VM] * 2,
        [VM] * 4,
        [],
        (new_1, new_2),
        (0, field * 8),
    )
    plane_before = lax.ppermute(high2, "ax", up)
    plane_after = lax.ppermute(low2, "ax", down)
    angle_before = lax.ppermute(last2, "ang", ring(count, 1))
    angle_after = lax.ppermute(first2, "ang", ring(count, -1))
    place = lax.axis_index("ang") % (count // 2)
    swap = jnp.stack([place == 0, place == count // 2 - 1]).astype(jnp.int32)

    stage = [
        pltpu.VMEM((2, ns, (na + 2) * half, nr), F32),
        pltpu.VMEM((2, ns, (na + 2) * half, nr), F32),
        pltpu.VMEM((ns, na * nz, 2 * nr), BF16),
        pltpu.VMEM((ns, na, nz, nr), F32),
    ]
    partial = call(
        functools.partial(early_kernel, (na, nz, lo, hi, ends)),
        shape(ns, na, nz, nr),
        [VM, SM, SM] + [ANY] * 6 + [VM] * 2 + param_specs,
        ANY,
        stage + [pltpu.SemaphoreType.DMA((15,)), pltpu.SemaphoreType.DMA((2, ns))],
        (weights, wall_flags, swap, new_1, new_2, new_a, new_c, angle_before, angle_after,
         plane_before, plane_after) + params,
        (field * 1024 * 2, field * 16),
    )
    return call(
        functools.partial(late_kernel, (na, nz, hi, hi + quarter)),
        shape(ns, na, nz, nr),
        [ANY, VM, SM, SM] + [VM] * 2 + [ANY] * 4 + [VM] * 2 + param_specs,
        ANY,
        stage + [pltpu.SemaphoreType.DMA((4,)), pltpu.SemaphoreType.DMA((ns,))],
        (partial, weights, wall_flags, flags_opp, mid_d, opp_d, new_1, new_2, new_a, new_c,
         plane_before, plane_after) + params,
        (field * 512 * 2, field * 4),
        {0: 0},
    )


def solution(mesh):
    in_specs = (P(None, "ang", "ax", None), P(), P(), P(), P(), P(), P(None, "ang"), P())
    out_specs = P(None, "ang", "ax", None)
    return jax.shard_map(
        per_device, mesh=mesh, in_specs=in_specs, out_specs=out_specs, check_vma=False
    )
```

time: 207 us -> 129 us (0.62)
  waiting for transfers between devices: 119 us -> 51.8 us
  Pallas kernels: 0 us -> 37.7 us
  other arithmetic: 31.6 us -> 0.07 us
  local copies, waits for them, and re-layouts: 27.1 us -> 13.4 us
  matrix products: 6.47 us -> 0 us
  starting transfers between devices: 20.5 us -> 25.1 us
    ppermute x10 -> x14, waiting for transfers between devices: 119 us -> 51.8 us  [the longest x1 36 us: per_device(): opp_a = lax.ppermute(mid_a, 'ang', opposite)]
    pallas_call x0 -> x9, Pallas kernels: none -> 37.7 us  [call(): pl.pallas_call(body, out_shape=out_shape, in_specs=in_specs, out_specs=ou...]
    rev x1 -> x0, local copies, waits for them, and re-layouts: 16.9 us -> none  [per_device(): own_right = radial_inverse[:, :half_radial, half_radial:][:, :, ::-1]]
    unnamed x20 -> x54, local copies, waits for them, and re-layouts: 0.06 us -> 13.4 us
    reduce_sum x2 -> x0, other arithmetic: 11.4 us -> none  [transport(): jnp.sum(selectors[which_reaction, 0][:, None, None, None] * field, axis=0)]
    convert_element_type x3 -> x1, other arithmetic: 8.37 us -> 0.07 us  [per_device(): swap = jnp.stack([place == 0, place == count // 2 - 1]).astype(jnp.int32)]
    mul x6 -> x0, other arithmetic: 7.28 us -> none  [transport(): rate_term = rate_constants[which_reaction] * first_part * second_part]
    slice x6 -> x0, local copies, waits for them, and re-layouts: 6.62 us -> none  [the longest x2 2.64 us: extended(): lax.slice_in_dim(block, block.shape[dim] - width, None, axis=dim)]
  transfers between devices with their start and end apart: 10 -> 14, of which waited for: 3 -> 4; matrix products, arithmetic and copies ran while one was open for 17% -> 0% of each run, Pallas kernels for 0% -> 14%
where the time goes in v1:
time: 129 us; the launch traced here: 128 us
  waiting for transfers between devices  51.8 us (40%)
  Pallas kernels  37.7 us (29%)
  starting transfers between devices  25.1 us (19%)
  local copies, waits for them, and re-layouts  13.4 us (10%)
    pallas_call x9, Pallas kernels, call(): pl.pallas_call(body, out_shape=out_shape, in_specs=in_specs, out_specs=ou...  37.7 us
    ppermute x1, waiting for transfers between devices, per_device(): opp_a = lax.ppermute(mid_a, 'ang', opposite)  36 us
    unnamed x54, local copies, waits for them, and re-layouts  13.4 us
    ppermute x1, waiting for transfers between devices, per_device(): opp_c = lax.ppermute(mid_c, 'ang', opposite)  13.3 us
    ppermute x1, starting transfers between devices, per_device(): plane_before = lax.ppermute(high, 'ax', up)  4.85 us
    ppermute x1, starting transfers between devices, per_device(): plane_before = lax.ppermute(high2, 'ax', up)  4.51 us
    ppermute x1, starting transfers between devices, per_device(): angle_after = lax.ppermute(first, 'ang', after_ring)  4.43 us
    ppermute x1, starting transfers between devices, per_device(): opp_2 = lax.ppermute(out2, 'ang', opposite)  2.65 us
  transfers between devices with their start and end apart: 14, of which 4 were waited for; matrix products, arithmetic and copies ran while one was open for 0% of the time, Pallas kernels for 14%

profile of v1, /device:TPU:0, one launch (start us, length us, event | category | flops | bytes accessed | tf_op | source)
XLA Modules:
  0.0 128.3 jit_solution(16098070945511401396)
XLA Ops:
  0.0 1.9 %copy-done.2 = f32[3,32,16,512]{3,2,1,0:T(8,128)S(1)} copy-done((f32[3,32,16,512]{3,2,1,0:T(8,128)S(1)}, f32[3,32,16,512]{3,2,1,0:T(8,128)}, u32[]{:S(2)}) %copy-start.2) | copy-done | bytes 3145752
  5.3 1.6 %shard_map.83 = (f32[3,32,512]{2,1,0:T(8,128)S(1)}, f32[3,32,512]{2,1,0:T(8,128)S(1)}, f32[3,16,512]{2,1,0:T(8,128)S(1)}, f32[3,16,512]{2,1,0:T(8,128)S(1)}, bf16[3,64,512]{2,1,0:T(8,128)(2,1)S(1)}) custom-call(f32[3,512,512]{2,1,0:T(8,128)S(1)} %bitcast.4, f32[1,512]{1,0:T(1,128)S(1)} %bitcast.7, f32[3]{0:T(128)S(1)} %copy-done.19, f32[3,512]{1,0:T(4,128)S(1)} %copy-done.8, ...), custom_call_target="tpu_custom_call" | custom-call | flops 7864320 | bytes 3145728 | tf_op jit(solution)/shard_map/pallas_call | solution.py:21
  6.9 4.9 %collective-permute-start.3 = (f32[3,32,512]{2,1,0:T(8,128)S(1)}, f32[3,32,512]{2,1,0:T(8,128)S(1)}, u32[]{:S(2)}, u32[]{:S(2)}) collective-permute-start(f32[3,32,512]{2,1,0:T(8,128)S(1)} %get-tuple-element.28), channel_id=1, source_target_pairs={{0,1},{2,3},{4,5},{6,7},{8,9},{10,11},{12,13},{14,15},{16,17},{18,... | collective-permute-start | bytes 589832 | tf_op jit(solution)/shard_map/ppermute | solution.py:480
  11.7 1.3 %collective-permute-start.4 = (f32[3,32,512]{2,1,0:T(8,128)S(1)}, f32[3,32,512]{2,1,0:T(8,128)S(1)}, u32[]{:S(2)}, u32[]{:S(2)}) collective-permute-start(f32[3,32,512]{2,1,0:T(8,128)S(1)} %get-tuple-element.29), channel_id=1, source_target_pairs={{1,0},{3,2},{5,4},{7,6},{9,8},{11,10},{13,12},{15,14},{17,16},{19,... | collective-permute-start | bytes 589832 | tf_op jit(solution)/shard_map/ppermute | solution.py:481
  13.1 4.4 %collective-permute-start.2 = (f32[3,16,512]{2,1,0:T(8,128)S(1)}, f32[3,16,512]{2,1,0:T(8,128)S(1)}, u32[]{:S(2)}, u32[]{:S(2)}) collective-permute-start(f32[3,16,512]{2,1,0:T(8,128)S(1)} %get-tuple-element.27), channel_id=1, source_target_pairs={{0,30},{2,0},{4,2},{6,4},{8,6},{10,8},{12,10},{14,12},{16,14},{18,... | collective-permute-start | bytes 294920 | tf_op jit(solution)/shard_map/ppermute | solution.py:483
  17.5 2.4 %collective-permute-done.1.before = f32[3,16,512]{2,1,0:T(8,128)S(1)} collective-permute-done((f32[3,16,512]{2,1,0:T(8,128)S(1)}, f32[3,16,512]{2,1,0:T(8,128)S(1)}, u32[]{:S(2)}, u32[]{:S(2)}) %collective-permute-start.1) | collective-permute-done | bytes 98336 | tf_op jit(solution)/shard_map/ppermute | solution.py:482
  20.0 3.2 %shard_map.84 = (bf16[3,128,512]{2,1,0:T(8,128)(2,1)S(1)}, bf16[3,160,512]{2,1,0:T(8,128)(2,1)S(1)}) custom-call(f32[3,512,512]{2,1,0:T(8,128)S(1)} %bitcast.5, f32[3,16,512]{2,1,0:T(8,128)S(1)} %collective-permute-done.1.before, f32[3,16,512]{2,1,0:T(8,128)S(1)} %collective-permute-done.2.after, f32[3,32,512]{2,1,0:T(8,128)S(1)} %collective-permute-done.3.low, ...), custom_call_target="tpu_custom_call" | custom-call | flops 15728640 | bytes 3145728 | tf_op jit(solution)/shard_map/pallas_call | solution.py:21
  23.2 2.7 %collective-permute-start.7 = (bf16[3,160,512]{2,1,0:T(8,128)(2,1)S(1)}, bf16[3,160,512]{2,1,0:T(8,128)(2,1)S(1)}, u32[]{:S(2)}, u32[]{:S(2)}) collective-permute-start(bf16[3,160,512]{2,1,0:T(8,128)(2,1)S(1)} %get-tuple-element.31.refs_2_), channel_id=1, source_target_pairs={{0,16},{2,18},{4,20},{6,22},{8,24},{10,26},{12,28},{14,30},{16,0},... | collective-permute-start | bytes 1474568 | tf_op jit(solution)/shard_map/ppermute | solution.py:520
  26.2 2.6 %collective-permute-start.5 = (bf16[3,64,512]{2,1,0:T(8,128)(2,1)S(1)}, bf16[3,64,512]{2,1,0:T(8,128)(2,1)S(1)}, u32[]{:S(2)}, u32[]{:S(2)}) collective-permute-start(bf16[3,64,512]{2,1,0:T(8,128)(2,1)S(1)} %get-tuple-element.25.refs_0_), channel_id=1, source_target_pairs={{0,16},{2,18},{4,20},{6,22},{8,24},{10,26},{12,28},{14,30},{16,0},... | collective-permute-start | bytes 589832 | tf_op jit(solution)/shard_map/ppermute | solution.py:484
  29.1 2.7 %shard_map.85 = (bf16[3,96,512]{2,1,0:T(8,128)(2,1)}, bf16[3,64,512]{2,1,0:T(8,128)(2,1)S(1)}) custom-call(f32[3,512,512]{2,1,0:T(8,128)S(1)} %bitcast.6, f32[1,512]{1,0:T(1,128)S(1)} %bitcast.9, f32[3]{0:T(128)S(1)} %copy-done.20, f32[3,512]{1,0:T(4,128)S(1)} %copy-done.8, f32[4]{0:T(128)S(1)} %copy-done.22, s32[4,3]{1,0:T(4,128)S(1)} %copy-done.15), custom_call_target="tpu_custom_call" | custom-call | flops 7864320 | bytes 3145728 | tf_op jit(solution)/shard_map/pallas_call | solution.py:21
  31.9 3.8 %shard_map.82.weights = bf16[3,512,1024]{2,1,0:T(8,128)(2,1)S(1)} custom-call(bf16[3,1024,1024]{2,1,0:T(8,128)(2,1)} %matrix.1), custom_call_target="tpu_custom_call" | custom-call | flops 1610612736 | bytes 6291456 | tf_op jit(solution)/shard_map/pallas_call | solution.py:21
  35.7 1.6 %copy-done = bf16[3,512,1024]{2,1,0:T(8,128)(2,1)} copy-done((bf16[3,512,1024]{2,1,0:T(8,128)(2,1)}, bf16[3,512,1024]{2,1,0:T(8,128)(2,1)S(1)}, u32[]{:S(2)}) %copy-start) | copy-done | bytes 3145752
  37.3 36.0 %collective-permute-done.5.refs_3_ = bf16[3,64,512]{2,1,0:T(8,128)(2,1)S(1)} collective-permute-done((bf16[3,64,512]{2,1,0:T(8,128)(2,1)S(1)}, bf16[3,64,512]{2,1,0:T(8,128)(2,1)S(1)}, u32[]{:S(2)}, u32[]{:S(2)}) %collective-permute-start.5) | collective-permute-done | bytes 196640 | tf_op jit(solution)/shard_map/ppermute | solution.py:484
  73.4 6.3 %shard_map.86 = (f32[2,3,64,512]{3,2,1,0:T(8,128)S(1)}, f32[2,3,128,512]{3,2,1,0:T(8,128)S(1)}, f32[2,3,160,512]{3,2,1,0:T(8,128)}) custom-call(bf16[3,512,1024]{2,1,0:T(8,128)(2,1)} %copy-done, s32[3,32]{1,0:T(4,128)S(1)} %copy-done.16, s32[3,32]{1,0:T(4,128)S(1)} %collective-permute-done.flags_opp, bf16[3,64,512]{2,1,0:T(8,128)(2,1)S(1)} %get-tuple-element.25.refs_0_, ...), custom_call_target="tpu_custom_call" | custom-call | flops 2214592512 | bytes 6488064 | tf_op jit(solution)/shard_map/pallas_call | solution.py:21
  79.6 0.9 copy-done.6
  80.5 2.2 %copy-done.3 = f32[2,3,160,512]{3,2,1,0:T(8,128)S(1)} copy-done((f32[2,3,160,512]{3,2,1,0:T(8,128)S(1)}, f32[2,3,160,512]{3,2,1,0:T(8,128)}, u32[]{:S(2)}) %copy-start.3) | copy-done | bytes 1966104
  82.7 1.2 shard_map.88
  83.9 4.5 %collective-permute-start.11 = (f32[2,3,32,512]{3,2,1,0:T(8,128)}, f32[2,3,32,512]{3,2,1,0:T(8,128)S(1)}, u32[]{:S(2)}, u32[]{:S(2)}) collective-permute-start(f32[2,3,32,512]{3,2,1,0:T(8,128)} %get-tuple-element.42), channel_id=1, source_target_pairs={{0,1},{2,3},{4,5},{6,7},{8,9},{10,11},{12,13},{14,15},{16,17},{18,... | collective-permute-start | bytes 1179656 | tf_op jit(solution)/shard_map/ppermute | solution.py:568
  88.4 1.3 %collective-permute-start.12 = (f32[2,3,32,512]{3,2,1,0:T(8,128)}, f32[2,3,32,512]{3,2,1,0:T(8,128)}, u32[]{:S(2)}, u32[]{:S(2)}) collective-permute-start(f32[2,3,32,512]{3,2,1,0:T(8,128)} %get-tuple-element.43), channel_id=1, source_target_pairs={{1,0},{3,2},{5,4},{7,6},{9,8},{11,10},{13,12},{15,14},{17,16},{19,... | collective-permute-start | bytes 1179656 | tf_op jit(solution)/shard_map/ppermute | solution.py:569
  89.9 2.6 %collective-permute-start.10 = (f32[2,3,16,512]{3,2,1,0:T(8,128)}, f32[2,3,16,512]{3,2,1,0:T(8,128)}, u32[]{:S(2)}, u32[]{:S(2)}) collective-permute-start(f32[2,3,16,512]{3,2,1,0:T(8,128)} %get-tuple-element.41), channel_id=1, source_target_pairs={{0,14},{2,0},{4,2},{6,4},{8,6},{10,8},{12,10},{14,12},{16,30},{18,... | collective-permute-start | bytes 589832 | tf_op jit(solution)/shard_map/ppermute | solution.py:571
  92.6 13.3 %collective-permute-done.8.refs_1_ = bf16[3,96,512]{2,1,0:T(8,128)(2,1)} collective-permute-done((bf16[3,96,512]{2,1,0:T(8,128)(2,1)}, bf16[3,96,512]{2,1,0:T(8,128)(2,1)}, u32[]{:S(2)}, u32[]{:S(2)}) %collective-permute-start.8) | collective-permute-done | bytes 294944 | tf_op jit(solution)/shard_map/ppermute | solution.py:522
  107.3 2.2 %shard_map.87.mid_c = f32[2,3,96,512]{3,2,1,0:T(8,128)S(1)} custom-call(bf16[3,512,1024]{2,1,0:T(8,128)(2,1)S(1)} %copy-done.1, s32[3,32]{1,0:T(4,128)S(1)} %copy-done.17, s32[3,32]{1,0:T(4,128)S(1)} %copy-done.25, bf16[3,96,512]{2,1,0:T(8,128)(2,1)} %get-tuple-element.39.refs_0_, bf16[3,96,512]{2,1,0:T(8,128)(2,1)} %collective-permute-done.8.refs_1_), custom_call_target="tpu_custom_call" | custom-call | flops 603979776 | bytes 1769472 | tf_op jit(solution)/shard_map/pallas_call | solution.py:21
  111.6 9.9 %shard_map.89.given = f32[3,32,16,512]{3,2,1,0:T(8,128)} custom-call(bf16[3,512,1024]{2,1,0:T(8,128)(2,1)} %copy-done, s32[3,32]{1,0:T(4,128)S(1)} %copy-done.18, s32[2]{0:T(128)S(1)} %add_convert_fusion.swap, f32[2,3,128,512]{3,2,1,0:T(8,128)S(1)} %copy-done.5, f32[2,3,160,512]{3,2,1,0:T(8,128)} %get-tuple-element.37.outer2, ...), custom_call_target="tpu_custom_call" | custom-call | flops 1610612736 | bytes 12582912 | tf_op jit(solution)/shard_map/pallas_call | solution.py:21
  121.5 6.8 %shard_map.90 = f32[3,32,16,512]{3,2,1,0:T(8,128)} custom-call(f32[3,32,16,512]{3,2,1,0:T(8,128)} %shard_map.89.given, bf16[3,512,1024]{2,1,0:T(8,128)(2,1)} %copy-done, s32[3,32]{1,0:T(4,128)S(1)} %copy-done.18, s32[3,32]{1,0:T(4,128)S(1)} %copy-done.26, bf16[3,64,512]{2,1,0:T(8,128)(2,1)S(1)} %copy-done.11, ...), custom_call_target="tpu_custom_call", output_to_operand_aliasing={{}: (0, {})} | custom-call | flops 805306368 | bytes 3145728 | tf_op jit(solution)/shard_map/pallas_call | solution.py:21
  (68 shorter events, 7.8 us)
Async XLA Ops:
  0.0 20.0 %copy-start.20 = (f32[3]{0:T(128)S(1)}, f32[3]{0:T(128)}, u32[]{:S(2)}) copy-start(f32[3]{0:T(128)} %diff.9) | copy-start | bytes 40
  0.0 20.0 %copy-start.13 = (f32[512]{0:T(512)S(1)}, f32[512]{0:T(512)}, u32[]{:S(2)}) copy-start(f32[512]{0:T(512)} %param.9) | copy-start | bytes 6148
  5.3 14.7 %copy-start.15 = (s32[4,3]{1,0:T(4,128)S(1)}, s32[4,3]{1,0:T(4,128)}, u32[]{:S(2)}) copy-start(s32[4,3]{1,0:T(4,128)} %smap.9) | copy-start | bytes 148
  5.3 23.5 %copy-start.16 = (s32[3,32]{1,0:T(4,128)S(1)}, s32[3,32]{1,0:T(4,128)}, u32[]{:S(2)}) copy-start(s32[3,32]{1,0:T(4,128)} %flags_own.5) | copy-start | bytes 1156
  6.9 13.1 %collective-permute-start.3 = (f32[3,32,512]{2,1,0:T(8,128)S(1)}, f32[3,32,512]{2,1,0:T(8,128)S(1)}, u32[]{:S(2)}, u32[]{:S(2)}) collective-permute-start(f32[3,32,512]{2,1,0:T(8,128)S(1)} %get-tuple-element.28), channel_id=1, source_target_pairs={{0,1},{2,3},{4,5},{6,7},{8,9},{10,11},{12,13},{14,15},{16,17},{18,... | collective-permute-start | bytes 589832 | tf_op jit(solution)/shard_map/ppermute | solution.py:480
  11.7 8.3 %collective-permute-start.4 = (f32[3,32,512]{2,1,0:T(8,128)S(1)}, f32[3,32,512]{2,1,0:T(8,128)S(1)}, u32[]{:S(2)}, u32[]{:S(2)}) collective-permute-start(f32[3,32,512]{2,1,0:T(8,128)S(1)} %get-tuple-element.29), channel_id=1, source_target_pairs={{1,0},{3,2},{5,4},{7,6},{9,8},{11,10},{13,12},{15,14},{17,16},{19,... | collective-permute-start | bytes 589832 | tf_op jit(solution)/shard_map/ppermute | solution.py:481
  13.0 6.9 %collective-permute-start.1 = (f32[3,16,512]{2,1,0:T(8,128)S(1)}, f32[3,16,512]{2,1,0:T(8,128)S(1)}, u32[]{:S(2)}, u32[]{:S(2)}) collective-permute-start(f32[3,16,512]{2,1,0:T(8,128)S(1)} %get-tuple-element.26), channel_id=1, source_target_pairs={{0,2},{2,4},{4,6},{6,8},{8,10},{10,12},{12,14},{14,16},{16,18},{18... | collective-permute-start | bytes 294920 | tf_op jit(solution)/shard_map/ppermute | solution.py:482
  13.1 6.8 %collective-permute-start.2 = (f32[3,16,512]{2,1,0:T(8,128)S(1)}, f32[3,16,512]{2,1,0:T(8,128)S(1)}, u32[]{:S(2)}, u32[]{:S(2)}) collective-permute-start(f32[3,16,512]{2,1,0:T(8,128)S(1)} %get-tuple-element.27), channel_id=1, source_target_pairs={{0,30},{2,0},{4,2},{6,4},{8,6},{10,8},{12,10},{14,12},{16,14},{18,... | collective-permute-start | bytes 294920 | tf_op jit(solution)/shard_map/ppermute | solution.py:483
  23.2 50.1 %collective-permute-start.7 = (bf16[3,160,512]{2,1,0:T(8,128)(2,1)S(1)}, bf16[3,160,512]{2,1,0:T(8,128)(2,1)S(1)}, u32[]{:S(2)}, u32[]{:S(2)}) collective-permute-start(bf16[3,160,512]{2,1,0:T(8,128)(2,1)S(1)} %get-tuple-element.31.refs_2_), channel_id=1, source_target_pairs={{0,16},{2,18},{4,20},{6,22},{8,24},{10,26},{12,28},{14,30},{16,0},... | collective-permute-start | bytes 1474568 | tf_op jit(solution)/shard_map/ppermute | solution.py:520
  25.9 47.5 %collective-permute-start.6 = (bf16[3,128,512]{2,1,0:T(8,128)(2,1)S(1)}, bf16[3,128,512]{2,1,0:T(8,128)(2,1)S(1)}, u32[]{:S(2)}, u32[]{:S(2)}) collective-permute-start(bf16[3,128,512]{2,1,0:T(8,128)(2,1)S(1)} %get-tuple-element.30.refs_1_), channel_id=1, source_target_pairs={{0,16},{2,18},{4,20},{6,22},{8,24},{10,26},{12,28},{14,30},{16,0},... | collective-permute-start | bytes 1179656 | tf_op jit(solution)/shard_map/ppermute | solution.py:519
  26.2 47.1 %collective-permute-start.5 = (bf16[3,64,512]{2,1,0:T(8,128)(2,1)S(1)}, bf16[3,64,512]{2,1,0:T(8,128)(2,1)S(1)}, u32[]{:S(2)}, u32[]{:S(2)}) collective-permute-start(bf16[3,64,512]{2,1,0:T(8,128)(2,1)S(1)} %get-tuple-element.25.refs_0_), channel_id=1, source_target_pairs={{0,16},{2,18},{4,20},{6,22},{8,24},{10,26},{12,28},{14,30},{16,0},... | collective-permute-start | bytes 589832 | tf_op jit(solution)/shard_map/ppermute | solution.py:484
  28.8 44.5 %collective-permute-start = (s32[3,32]{1,0:T(4,128)S(1)}, s32[3,32]{1,0:T(4,128)S(1)}, u32[]{:S(2)}, u32[]{:S(2)}) collective-permute-start(s32[3,32]{1,0:T(4,128)S(1)} %copy-done.16), channel_id=1, source_target_pairs={{0,16},{2,18},{4,20},{6,22},{8,24},{10,26},{12,28},{14,30},{16,0},... | collective-permute-start | bytes 1160 | tf_op jit(solution)/shard_map/ppermute | solution.py:538
  80.5 25.4 %copy-start.1 = (bf16[3,512,1024]{2,1,0:T(8,128)(2,1)S(1)}, bf16[3,512,1024]{2,1,0:T(8,128)(2,1)}, u32[]{:S(2)}) copy-start(bf16[3,512,1024]{2,1,0:T(8,128)(2,1)} %copy-done) | copy-start | bytes 9437188
  83.9 25.6 %copy-start.9 = (f32[3,512]{1,0:T(4,128)S(1)}, f32[3,512]{1,0:T(4,128)}, u32[]{:S(2)}) copy-start(f32[3,512]{1,0:T(4,128)} %ang.9) | copy-start | bytes 18436
  83.9 25.6 %collective-permute-start.11 = (f32[2,3,32,512]{3,2,1,0:T(8,128)}, f32[2,3,32,512]{3,2,1,0:T(8,128)S(1)}, u32[]{:S(2)}, u32[]{:S(2)}) collective-permute-start(f32[2,3,32,512]{3,2,1,0:T(8,128)} %get-tuple-element.42), channel_id=1, source_target_pairs={{0,1},{2,3},{4,5},{6,7},{8,9},{10,11},{12,13},{14,15},{16,17},{18,... | collective-permute-start | bytes 1179656 | tf_op jit(solution)/shard_map/ppermute | solution.py:568
  88.4 21.1 %collective-permute-start.12 = (f32[2,3,32,512]{3,2,1,0:T(8,128)}, f32[2,3,32,512]{3,2,1,0:T(8,128)}, u32[]{:S(2)}, u32[]{:S(2)}) collective-permute-start(f32[2,3,32,512]{3,2,1,0:T(8,128)} %get-tuple-element.43), channel_id=1, source_target_pairs={{1,0},{3,2},{5,4},{7,6},{9,8},{11,10},{13,12},{15,14},{17,16},{19,... | collective-permute-start | bytes 1179656 | tf_op jit(solution)/shard_map/ppermute | solution.py:569
  89.7 16.2 %collective-permute-start.8 = (bf16[3,96,512]{2,1,0:T(8,128)(2,1)}, bf16[3,96,512]{2,1,0:T(8,128)(2,1)}, u32[]{:S(2)}, u32[]{:S(2)}) collective-permute-start(bf16[3,96,512]{2,1,0:T(8,128)(2,1)} %get-tuple-element.39.refs_0_), channel_id=1, source_target_pairs={{0,16},{2,18},{4,20},{6,22},{8,24},{10,26},{12,28},{14,30},{16,0},... | collective-permute-start | bytes 884744 | tf_op jit(solution)/shard_map/ppermute | solution.py:522
  89.8 19.7 %collective-permute-start.9 = (f32[2,3,16,512]{3,2,1,0:T(8,128)}, f32[2,3,16,512]{3,2,1,0:T(8,128)}, u32[]{:S(2)}, u32[]{:S(2)}) collective-permute-start(f32[2,3,16,512]{3,2,1,0:T(8,128)} %get-tuple-element.40), channel_id=1, source_target_pairs={{0,2},{2,4},{4,6},{6,8},{8,10},{10,12},{12,14},{14,0},{16,18},{18,... | collective-permute-start | bytes 589832 | tf_op jit(solution)/shard_map/ppermute | solution.py:570
  89.9 19.6 %collective-permute-start.10 = (f32[2,3,16,512]{3,2,1,0:T(8,128)}, f32[2,3,16,512]{3,2,1,0:T(8,128)}, u32[]{:S(2)}, u32[]{:S(2)}) collective-permute-start(f32[2,3,16,512]{3,2,1,0:T(8,128)} %get-tuple-element.41), channel_id=1, source_target_pairs={{0,14},{2,0},{4,2},{6,4},{8,6},{10,8},{12,10},{14,12},{16,30},{18,... | collective-permute-start | bytes 589832 | tf_op jit(solution)/shard_map/ppermute | solution.py:571
  92.5 17.1 %copy-start.5 = (f32[2,3,128,512]{3,2,1,0:T(8,128)S(1)}, f32[2,3,128,512]{3,2,1,0:T(8,128)}, u32[]{:S(2)}) copy-start(f32[2,3,128,512]{3,2,1,0:T(8,128)} %copy-done.4) | copy-start | bytes 4718596
  92.5 17.1 %copy-start.7 = (f32[2,3,64,512]{3,2,1,0:T(8,128)S(1)}, f32[2,3,64,512]{3,2,1,0:T(8,128)}, u32[]{:S(2)}) copy-start(f32[2,3,64,512]{3,2,1,0:T(8,128)} %copy-done.6) | copy-start | bytes 2359300
  105.9 15.5 %collective-permute-start.13 = (bf16[3,64,512]{2,1,0:T(8,128)(2,1)}, bf16[3,64,512]{2,1,0:T(8,128)(2,1)S(1)}, u32[]{:S(2)}, u32[]{:S(2)}) collective-permute-start(bf16[3,64,512]{2,1,0:T(8,128)(2,1)} %copy-done.10), channel_id=1, source_target_pairs={{0,16},{2,18},{4,20},{6,22},{8,24},{10,26},{12,28},{14,30},{16,0},... | collective-permute-start | bytes 589832 | tf_op jit(solution)/shard_map/ppermute | solution.py:524
  111.6 9.9 %copy-start.11 = (bf16[3,64,512]{2,1,0:T(8,128)(2,1)S(1)}, bf16[3,64,512]{2,1,0:T(8,128)(2,1)}, u32[]{:S(2)}) copy-start(bf16[3,64,512]{2,1,0:T(8,128)(2,1)} %copy-done.10) | copy-start | bytes 589828
  111.6 9.9 %copy-start.26 = (s32[3,32]{1,0:T(4,128)S(1)}, s32[3,32]{1,0:T(4,128)}, u32[]{:S(2)}) copy-start(s32[3,32]{1,0:T(4,128)} %copy-done.24) | copy-start | bytes 1156
  (17 other events, 26.8 us)

commit v2 on v0

v2 whole, which is shorter than its diff:
```python
import functools

import jax
import jax.numpy as jnp
from jax import lax
from jax.experimental import pallas as pl
from jax.experimental.pallas import tpu as pltpu
from jax.sharding import PartitionSpec as P

F32 = jnp.float32
BF16 = jnp.bfloat16
MIB = 1024 * 1024
LANES = 128

ANY = pl.BlockSpec(memory_space=pl.ANY)
HBM = pl.BlockSpec(memory_space=pltpu.HBM)
VM = pl.BlockSpec(memory_space=pltpu.VMEM)
SM = pl.BlockSpec(memory_space=pltpu.SMEM)

OWN, BEFORE, ANGULAR, AXIAL, RATE = 0, 3, 6, 9, 12


def call(body, out_shape, in_specs, out_specs, scratch, args, mib, aliases=None):
    return pl.pallas_call(
        body,
        out_shape=out_shape,
        in_specs=in_specs,
        out_specs=out_specs,
        scratch_shapes=scratch,
        input_output_aliases=aliases or {},
        cost_estimate=pl.CostEstimate(flops=1, bytes_accessed=1, transcendentals=0),
        compiler_params=pltpu.CompilerParams(vmem_limit_bytes=mib * MIB),
    )(*args)


def shape(*dims, dtype=F32):
    return jax.ShapeDtypeStruct(dims, dtype)


def transport(now, before, after, around, coef):
    made = (
        coef[RATE] * (now[1] * now[2]),
        coef[RATE + 1] * (now[0] * now[2]),
        coef[RATE + 2] * (now[0] * now[1]),
    )
    spent = made[0] + made[1] + made[2]
    out = []
    for s in range(3):
        value = now[s] * coef[OWN + s] + before[s] * coef[BEFORE + s]
        value = value + after[s] * coef[AXIAL + s] + around[s] * coef[ANGULAR + s]
        out.append(value + ((made[s] + made[s]) - spent))
    return out


def turned(first, second, rows):
    first, second = pltpu.roll(first, rows // 2, 0), pltpu.roll(second, rows // 2, 0)
    upper = lax.broadcasted_iota(jnp.int32, first.shape, 0) < rows // 2
    return jnp.where(upper, first, second), jnp.where(upper, second, first)


def first_step(read, low, high, coef, half):
    tiles = [[read(s, 0, k) for s in range(3)] for k in range(2)]
    around = [[read(s, -1, k) + read(s, 1, k) for s in range(3)] for k in range(2)]
    row = lax.broadcasted_iota(jnp.int32, tiles[0][0].shape, 0)
    top, bottom = row == 0, row == half - 1
    fall = [[pltpu.roll(v, 1, 0) for v in tile] for tile in tiles]
    rise = [[pltpu.roll(v, half - 1, 0) for v in tile] for tile in tiles]
    out = []
    for k in range(2):
        other = 1 - k
        before = [
            jnp.where(top, low(s) if low is not None and k == 0 else fall[other][s], fall[k][s])
            for s in range(3)
        ]
        after = [
            jnp.where(bottom, high(s) if high is not None and k == 1 else rise[other][s], rise[k][s])
            for s in range(3)
        ]
        out.append(transport(tiles[k], before, after, around[k], coef))
    pairs = [turned(out[0][s], out[1][s], half) for s in range(3)]
    return [p[0] for p in pairs], [p[1] for p in pairs]


def second_step(read, low, high, coef, half):
    tiles = [[read(k, s, 0) for s in range(3)] for k in range(2)]
    around = [[read(k, s, -1) + read(k, s, 1) for s in range(3)] for k in range(2)]
    row = lax.broadcasted_iota(jnp.int32, tiles[0][0].shape, 0)
    top, bottom = row == 0, row == half - 1
    first, last = row == half // 2, row == half // 2 - 1
    fall = [[pltpu.roll(v, 1, 0) for v in tile] for tile in tiles]
    rise = [[pltpu.roll(v, half - 1, 0) for v in tile] for tile in tiles]
    out = []
    for k in range(2):
        before = [jnp.where(top, fall[1 - k][s], fall[k][s]) for s in range(3)]
        after = [jnp.where(bottom, rise[1 - k][s], rise[k][s]) for s in range(3)]
        if k == 1:
            before = [jnp.where(first, low(s), before[s]) for s in range(3)]
            after = [jnp.where(last, high(s), after[s]) for s in range(3)]
        out.append(transport(tiles[k], before, after, around[k], coef))
    return out


def pack(tiles):
    return jnp.concatenate(tiles, 0).astype(BF16)


def at_rows(start, count, step):
    return pl.ds(pl.multiple_of(start, step), count)


def field_reader(field, t, nz):
    half = nz // 2
    return lambda s, shift, k: field[s, at_rows((t + shift) * nz + k * half, half, half), :]


def mid_run(field, out, begin, count, at, coef, nz):
    half = nz // 2

    def pair(step, carry):
        t = begin + step * 2
        tiles = [first_step(field_reader(field, t + k, nz), None, None, coef, half)[0] for k in range(2)]
        for s in range(3):
            out[s, at_rows(at * half + step * nz, nz, nz), :] = pack([tiles[0][s], tiles[1][s]])
        return carry

    lax.fori_loop(0, count // 2, pair, 0)


def head_kernel(sizes, conc, cour, diff, ang, rate, smap, *rest):
    na, nz, lo, hi, planes = sizes
    edges = rest[: 1 if planes == 2 else 2]
    first, last, mid, coef, field, cour_v, ang_v, diff_s, rate_s, map_s, sems = rest[len(edges) :]
    half = nz // 2
    inner = pl.ds((lo - 1) * nz, (hi - lo + 2) * nz)
    left = pl.ds(0, (lo - 1) * nz)
    right = pl.ds((hi + 1) * nz, (na - hi - 1) * nz)
    small = [
        pltpu.make_async_copy(src, dst, sems.at[k + 3])
        for k, (src, dst) in enumerate(
            ((cour, cour_v), (ang, ang_v), (diff, diff_s), (rate, rate_s), (smap, map_s))
        )
    ]
    copies = [
        pltpu.make_async_copy(conc.at[:, rows], field.at[:, rows], sems.at[k])
        for k, rows in enumerate((inner, left, right))
    ]
    for copy in small + copies:
        copy.start()
    for copy in small:
        copy.wait()
    tile = coef.shape[1:]
    for s in range(3):
        courant, angular = cour_v[...], ang_v[s : s + 1, :]
        axial = diff_s[s]
        total = jnp.float32(0.0)
        for k in range(map_s.shape[0]):
            total = total + jnp.where(map_s[k, 2] == s, rate_s[k], 0.0)
        coef[OWN + s] = jnp.broadcast_to((1.0 - 2.0 * axial) - courant - 2.0 * angular, tile)
        coef[BEFORE + s] = jnp.broadcast_to(courant + axial, tile)
        coef[ANGULAR + s] = jnp.broadcast_to(angular, tile)
        coef[AXIAL + s] = jnp.full(tile, axial, F32)
        coef[RATE + s] = jnp.full(tile, total, F32)
    copies[0].wait()
    mid_run(field, mid, lo, hi - lo, 0, coef, nz)
    copies[1].wait()
    copies[2].wait()
    for s in range(3):
        if planes == 2:
            row = jnp.where(lax.axis_index("ax") == 0, nz - 1, 0)
            for t in range(na):
                edges[0][s, t : t + 1, :] = field[s, pl.ds(t * nz + row, 1), :]
        else:
            for t in range(na):
                edges[0][s, t : t + 1, :] = field[s, t * nz : t * nz + 1, :]
                edges[1][s, t : t + 1, :] = field[s, (t + 1) * nz - 1 : (t + 1) * nz, :]
        first[s] = field[s, pl.ds(0, nz), :]
        last[s] = field[s, pl.ds((na - 1) * nz, nz), :]


def inner_kernel(sizes, runs, conc, coef, *rest):
    na, nz = sizes
    outs, field, sem = rest[:-2], rest[-2], rest[-1]
    copy = pltpu.make_async_copy(conc, field, sem)
    copy.start()
    copy.wait()
    for out, parts in runs:
        at = 0
        for begin, count in parts:
            mid_run(field, outs[out], begin, count, at, coef, nz)
            at += count


def edge_weights(planes):
    if planes != 2:
        return 1.0, 1.0
    place = lax.axis_index("ax")
    return jnp.where(place == 1, 1.0, 0.0), jnp.where(place == 0, 1.0, 0.0)


def frame_kernel(sizes, conc, before, after, low, high, coef, out1, out2, field, sems):
    na, nz, ends, planes = sizes
    half = nz // 2
    copies = [
        pltpu.make_async_copy(conc, field.at[:, pl.ds(nz, na * nz)], sems.at[0]),
        pltpu.make_async_copy(before, field.at[:, pl.ds(0, nz)], sems.at[1]),
        pltpu.make_async_copy(after, field.at[:, pl.ds((na + 1) * nz, nz)], sems.at[2]),
    ]
    for copy in copies:
        copy.start()
    low_weight, high_weight = edge_weights(planes)
    for copy in copies:
        copy.wait()

    def angle(t):
        return first_step(
            field_reader(field, t + 1, nz),
            lambda s: low[s, pl.ds(t, 1), :] * low_weight,
            lambda s: high[s, pl.ds(t, 1), :] * high_weight,
            coef,
            half,
        )

    def pair(t, out, row, ends_row):
        tiles = [angle(t), angle(t + 1)]
        for s in range(3):
            out[s, pl.ds(row, nz), :] = pack([tiles[0][1][s], tiles[1][1][s]])
            if ends_row is not None:
                out2[s, pl.ds(ends_row, nz), :] = pack([tiles[0][0][s], tiles[1][0][s]])

    quarter = na // 4
    tail = na // 2 * half
    pair(0, out1, 0, tail)
    pair(na - 2, out2, (na // 2 - 2) * half, tail + nz)

    def first_part(step, carry):
        pair(step * 2, out1, pl.multiple_of(step * nz, nz), None)
        return carry

    def second_part(step, carry):
        pair(na // 2 + step * 2, out2, pl.multiple_of(step * nz, nz), None)
        return carry

    lax.fori_loop(1, quarter, first_part, 0)
    lax.fori_loop(0, quarter - 1, second_part, 0)


def weights_kernel(matrix, flags_own, flags_opp, out, keep, left, lower, sems):
    half = out.shape[1]
    copies = []
    for s in range(out.shape[0]):
        for k, ref in enumerate((left, lower)):
            src = matrix.at[s, pl.ds(k * half, half), pl.ds(0, half)]
            copies.append(pltpu.make_async_copy(src, ref.at[s], sems.at[k, s]))
    for copy in copies:
        copy.start()
    lane = lax.broadcasted_iota(jnp.int32, (1, LANES), 1)
    for ab, flags in enumerate((flags_own, flags_opp)):
        for s in range(out.shape[0]):
            for t in range(keep.shape[2]):
                keep[ab, s, t : t + 1, :] = jnp.where((lane == 0) & (flags[s, t] == 1), 0.0, 1.0)
    row = lax.broadcasted_iota(jnp.int32, (half, half), 0)
    col = lax.broadcasted_iota(jnp.int32, (half, half), 1)
    row = jnp.maximum(row, 1)
    pick = jnp.where(col == row, 1.0, 0.0).astype(BF16)
    flip = jnp.where(col == half - 1 - row, 1.0, 0.0).astype(BF16)
    for copy in copies:
        copy.wait()
    for s in range(out.shape[0]):
        out[s, :, :half] = jnp.dot(pick, left[s], preferred_element_type=F32).astype(BF16)
        out[s, :, half:] = jnp.dot(flip, lower[s], preferred_element_type=F32).astype(BF16)


def rows_product(rows, weights):
    return lax.dot_general(rows, weights, (((1,), (1,)), ((), ())), preferred_element_type=F32)


def both_sides(mine, theirs, weights):
    rows = jnp.concatenate(
        [jnp.concatenate([mine, theirs], 1), jnp.concatenate([theirs, mine], 1)], 0
    )
    return rows_product(rows, weights)


def store_run(state, s, begin, place, count, at, value, keep, half):
    total = value.shape[0] // 2
    for ab in range(2):
        part = value[ab * total + at * half : ab * total + (at + count) * half]
        state[ab, s, pl.ds(place * half, count * half), LANES:] = part[:, LANES:]
        for k in range(count):
            state[ab, s, pl.ds((place + k) * half, half), :LANES] = (
                part[k * half : (k + 1) * half, :LANES] * keep[ab, s, begin + k : begin + k + 1, :]
            )


def radial_kernel(runs, copies, half, weights, keep, mine, theirs, *refs):
    n_in = 1 + max((part for part, *_ in copies), default=-1)
    parts, states = refs[:n_in], refs[n_in:]
    for s in range(3):
        value = both_sides(mine[s], theirs[s], weights[s])
        at = 0
        for which, begin, place, count in runs:
            store_run(states[which], s, begin, place, count, at, value, keep, half)
            at += count
    for part, source, which, place, count in copies:
        to, rows = pl.ds(place * half, count * half), pl.ds(source * half, count * half)
        for ab in range(2):
            for s in range(3):
                states[which][ab, s, to, :] = parts[part][ab, s, rows, :]


def edges_of_state(na, nz, planes, mid, outer, edges, first, last, stage):
    half = nz // 2
    if planes == 2:
        row = jnp.where(lax.axis_index("ax") == 0, half // 2 - 1, half // 2)
    end = pl.ds((na - 1) * half, half)
    ends_end = pl.ds(mid.shape[2] - half, half)
    for ab in range(2):
        for s in range(3):
            for t in range(na):
                to = pl.ds(t, 1)
                at = t * half + half // 2
                if planes == 2:
                    stage[0, to, :] = outer[ab, s, pl.ds(t * half + row, 1), :]
                else:
                    stage[0, to, :] = outer[ab, s, at : at + 1, :]
                    stage[1, to, :] = outer[ab, s, at - 1 : at, :]
            for k, edge in enumerate(edges):
                edge[ab, s] = stage[k].astype(BF16)
            begin = pl.ds(0, half)
            first[ab, s] = pack([mid[ab, s, begin, :], outer[ab, s, begin, :]])
            last[ab, s] = pack([mid[ab, s, ends_end, :], outer[ab, s, end, :]])


def radial_edges_kernel(sizes, runs, copies, half, weights, keep, mine, theirs, *refs):
    na, nz, planes = sizes
    n_edges = 1 if planes == 2 else 2
    *edges, first, last, stage = refs[-3 - n_edges :]
    refs = refs[: -3 - n_edges]
    radial_kernel(runs, copies, half, weights, keep, mine, theirs, *refs)
    edges_of_state(na, nz, planes, refs[-2], refs[-1], edges, first, last, stage)


def explicit_angle(t, reader, low, high, edge_factors, coef, rows, nz):
    half = nz // 2
    for ab in range(2):
        out = second_step(
            functools.partial(reader, ab),
            lambda s: low[ab, s, pl.ds(t, 1), :] * edge_factors[0],
            lambda s: high[ab, s, pl.ds(t, 1), :] * edge_factors[1],
            coef,
            half,
        )
        width = out[0][0].shape[1]
        for s in range(3):
            rows[s, at_rows(t * nz, nz, nz), ab * width : (ab + 1) * width] = pack(
                [out[0][s], out[1][s]]
            )


def explicit_run(begin, count, states, low, high, edge_factors, coef, rows, nz):
    half = nz // 2

    def one(step, carry):
        t = begin + step

        def reader(ab, k, s, shift):
            state, base = states[k]
            return state[ab, s, at_rows((t - base + shift) * half, half, half), :]

        explicit_angle(t, reader, low, high, edge_factors, coef, rows, nz)
        return carry

    lax.fori_loop(0, count, one, 0)


def finish_run(begin, count, s, rows, weights, keep, result, nz):
    half = nz // 2
    value = rows_product(rows[s, pl.ds(begin * nz, count * nz), :], weights[s])
    for k in range(count):
        t = begin + k
        parts = turned(value[k * nz + half : (k + 1) * nz], value[k * nz : k * nz + half], half)
        for p in range(2):
            span = pl.ds(p * half, half)
            result[s, t, span, LANES:] = parts[p][:, LANES:]
            result[s, t, span, :LANES] = parts[p][:, :LANES] * keep[0, s, t : t + 1, :]


def widen(pairs):
    for source, target in pairs:
        target[...] = source[...].astype(F32)


def early_kernel(
    sizes, weights, keep, mid, outer, before_low, after_low, low_low, high_low, coef,
    out, before, after, low, high, rows, result, out_sems
):
    na, nz, runs, half_ring, planes = sizes
    half = nz // 2
    place = lax.rem(lax.axis_index("ang"), half_ring)
    wrap_before = jnp.where(place == 0, 1, 0)
    wrap_after = jnp.where(place == half_ring - 1, 1, 0)
    factors = edge_weights(planes)
    states = (mid, outer)
    widen(((before_low, before), (after_low, after), (low_low, low), (high_low, high)))
    for begin, count in runs:
        end = begin + count
        if begin == 0:

            def reader(ab, k, s, shift):
                if shift == -1:
                    return before[jnp.where(wrap_before == 1, 1 - ab, ab), s, pl.ds(k * half, half), :]
                return states[k][ab, s, pl.ds(shift * half, half), :]

            explicit_angle(0, reader, low, high, factors, coef, rows, nz)
        if end == na:

            def reader(ab, k, s, shift):
                if shift == 1:
                    return after[jnp.where(wrap_after == 1, 1 - ab, ab), s, pl.ds(k * half, half), :]
                return states[k][ab, s, pl.ds((na - 1 + shift) * half, half), :]

            explicit_angle(na - 1, reader, low, high, factors, coef, rows, nz)
        start, stop = max(begin, 1), min(end, na - 1)
        explicit_run(start, stop - start, ((mid, 0), (outer, 0)), low, high, factors, coef, rows, nz)
    leaves = []
    for s in range(3):
        for k, (begin, count) in enumerate(runs):
            finish_run(begin, count, s, rows, weights, keep, result, nz)
            span = pl.ds(begin, count)
            leave = pltpu.make_async_copy(result.at[s, span], out.at[s, span], out_sems.at[k, s])
            leave.start()
            leaves.append(leave)
    for leave in leaves:
        leave.wait()


def late_kernel(
    sizes, given, state, weights, keep, mine, theirs, outer, low_low, high_low, coef,
    out, mid, low, high, rows, result, out_sems,
):
    na, nz, lo, hi, planes = sizes
    half = nz // 2
    factors = edge_weights(planes)
    count = hi - lo
    widen(((low_low, low), (high_low, high)))
    for s in range(3):
        value = both_sides(mine[s], theirs[s], weights[s])
        store_run(mid, s, lo, 2, count, 0, value, keep, half)
        for ab in range(2):
            for k in range(2):
                to = pl.ds((2 + count) * k * half, 2 * half)
                mid[ab, s, to, :] = state[ab, s, pl.ds((lo - 2 + (2 + count) * k) * half, 2 * half), :]
    explicit_run(lo - 1, count + 2, ((mid, lo - 2), (outer, 0)), low, high, factors, coef, rows, nz)
    leaves = []
    for s in range(3):
        finish_run(lo - 1, count + 2, s, rows, weights, keep, result, nz)
        span = pl.ds(lo - 1, count + 2)
        leave = pltpu.make_async_copy(result.at[s, span], out.at[s, span], out_sems.at[s])
        leave.start()
        leaves.append(leave)
    for leave in leaves:
        leave.wait()


def ring(count, step):
    half = count // 2
    return [(i, i // half * half + (i % half + step) % half) for i in range(count)]


def plane_halos(edges, planes):
    if planes == 2:
        got = lax.ppermute(edges[0], "ax", [(0, 1), (1, 0)])
        return got, got
    up = [(i, i + 1) for i in range(planes - 1)]
    down = [(i + 1, i) for i in range(planes - 1)]
    return lax.ppermute(edges[1], "ax", up), lax.ppermute(edges[0], "ax", down)


def after(value, done):
    return lax.optimization_barrier((value, done))


def per_device(
    concentration, courant, axial_diffusion, angular_rate, rate_constants, species_map,
    wall_flags, radial_inverse,
):
    ns, na, nz, nr = concentration.shape
    half = nz // 2
    count = lax.axis_size("ang")
    planes = lax.axis_size("ax")
    n_edges = 1 if planes == 2 else 2
    quarter = na // 4
    ends = 2
    first_lo, first_hi = quarter, 2 * quarter
    last_lo, last_hi = first_hi, 3 * quarter + ends
    inner = ((ends, first_lo - ends), (last_hi, na - ends - last_hi))
    inner_count = sum(n for _, n in inner)
    opposite = [(i, (i + count // 2) % count) for i in range(count)]

    def dma(*dims):
        return pltpu.SemaphoreType.DMA(dims)

    def message(angles):
        return shape(ns, angles * half, nr, dtype=BF16)

    conc = concentration.reshape(ns, na * nz, nr)
    field = pltpu.VMEM((ns, na * nz, nr), F32)
    *edges, first, last, mid_a, coef = call(
        functools.partial(head_kernel, (na, nz, first_lo, first_hi, planes)),
        [shape(ns, na, nr)] * n_edges
        + [shape(ns, nz, nr)] * 2
        + [message(first_hi - first_lo), shape(RATE + 3, half, nr)],
        [HBM] * 6,
        [VM] * (n_edges + 4),
        [
            field, pltpu.VMEM((1, nr), F32), pltpu.VMEM(angular_rate.shape, F32),
            pltpu.SMEM(axial_diffusion.shape, F32), pltpu.SMEM(rate_constants.shape, F32),
            pltpu.SMEM(species_map.shape, jnp.int32), dma(8),
        ],
        (conc, courant[None], axial_diffusion, angular_rate, rate_constants, species_map),
        58,
    )
    opp_a = lax.ppermute(mid_a, "ang", opposite)
    low, high = plane_halos(edges, planes)
    angle_before = lax.ppermute(last, "ang", [(i, (i + 1) % count) for i in range(count)])
    angle_after = lax.ppermute(first, "ang", [(i, (i - 1) % count) for i in range(count)])
    flags_opp = lax.ppermute(wall_flags, "ang", opposite)

    mid_c, mid_d = call(
        functools.partial(
            inner_kernel,
            (na, nz),
            ((0, inner), (1, ((last_lo, last_hi - last_lo),))),
        ),
        [message(inner_count), message(last_hi - last_lo)],
        [ANY, VM],
        [VM] * 2,
        [field, pltpu.SemaphoreType.DMA],
        (conc, coef),
        8,
    )
    out1, out2 = call(
        functools.partial(frame_kernel, (na, nz, ends, planes)),
        [message(na // 2), message(na // 2 + 2 * ends)],
        [ANY] * 3 + [VM] * 3,
        [VM] * 2,
        [pltpu.VMEM((ns, (na + 2) * nz, nr), F32), dma(3)],
        (conc, angle_before, angle_after, low, high, coef),
        8,
    )
    (out1, out2), opp_a = after((out1, out2), opp_a)
    opp_1 = lax.ppermute(out1, "ang", opposite)
    opp_2 = lax.ppermute(out2, "ang", opposite)
    weights, keep = call(
        weights_kernel,
        [shape(ns, nr, 2 * nr, dtype=BF16), shape(2, ns, na, LANES)],
        [ANY, SM, SM],
        [VM] * 2,
        [pltpu.VMEM((ns, nr, nr), BF16), pltpu.VMEM((ns, nr, nr), BF16), dma(2, ns)],
        (radial_inverse, wall_flags, flags_opp),
        12,
    )

    def state(angles):
        return shape(2, ns, angles * half, nr)

    count_a, side = first_hi - first_lo, na // 2
    (mid_first,) = call(
        functools.partial(radial_kernel, ((0, first_lo, 0, count_a),), (), half),
        [state(count_a)],
        [VM] * 4,
        [VM],
        [],
        (weights, keep, mid_a, opp_a),
        8,
    )
    opp_1, mid_first = after(opp_1, mid_first)
    (outer_first,) = call(
        functools.partial(radial_kernel, ((0, 0, 0, side),), (), half),
        [state(side)],
        [VM] * 4,
        [VM],
        [],
        (weights, keep, out1, opp_1),
        8,
    )
    mid_c, outer_first = after(mid_c, outer_first)
    opp_c = lax.ppermute(mid_c, "ang", opposite)
    mid_d, opp_2 = after(mid_d, opp_2)
    opp_d = lax.ppermute(mid_d, "ang", opposite)
    runs = ((1, side, side, side), (0, 0, 0, ends), (0, na - ends, ends, ends))
    mid_ends, outer_state, *rest = call(
        functools.partial(
            radial_edges_kernel, (na, nz, planes), runs, ((0, 0, 1, 0, side),), half
        ),
        [state(2 * ends), state(na)]
        + [shape(2, ns, na, nr, dtype=BF16)] * n_edges
        + [shape(2, ns, nz, nr, dtype=BF16)] * 2,
        [VM] * 5,
        [VM] * (4 + n_edges),
        [pltpu.VMEM((n_edges, na, nr), F32)],
        (weights, keep, out2, opp_2, outer_first),
        8,
    )
    *edges, first, last = rest
    low, high = plane_halos(edges, planes)
    angle_before = lax.ppermute(last, "ang", ring(count, 1))
    angle_after = lax.ppermute(first, "ang", ring(count, -1))
    (mid_state,) = call(
        functools.partial(
            radial_kernel,
            tuple((0, begin, begin, n) for begin, n in inner),
            ((0, 0, 0, first_lo, count_a), (1, 0, 0, 0, ends), (1, ends, 0, na - ends, ends)),
            half,
        ),
        [state(na)],
        [VM] * 6,
        [VM],
        [],
        (weights, keep, mid_c, opp_c, mid_first, mid_ends),
        8,
    )

    stage = [pltpu.VMEM((ns, na * nz, 2 * nr), BF16), pltpu.VMEM((ns, na, nz, nr), F32)]
    edge_scratch = [pltpu.VMEM((2, ns, na, nr), F32)] * 2
    early = ((0, last_lo - 1), (last_hi + 1, na - last_hi - 1))
    partial = call(
        functools.partial(early_kernel, (na, nz, early, count // 2, planes)),
        shape(ns, na, nz, nr),
        [VM] * 9,
        ANY,
        [pltpu.VMEM((2, ns, nz, nr), F32)] * 2 + edge_scratch + stage + [dma(2, ns)],
        (weights, keep, mid_state, outer_state, angle_before, angle_after, low, high, coef),
        12,
    )
    wide = last_hi - last_lo + 4
    return call(
        functools.partial(late_kernel, (na, nz, last_lo, last_hi, planes)),
        shape(ns, na, nz, nr),
        [ANY] + [VM] * 9,
        ANY,
        [pltpu.VMEM((2, ns, wide * half, nr), F32)] + edge_scratch + stage + [dma(ns)],
        (partial, mid_state, weights, keep, mid_d, opp_d, outer_state, low, high, coef),
        12,
        {0: 0},
    )


def solution(mesh):
    in_specs = (P(None, "ang", "ax", None), P(), P(), P(), P(), P(), P(None, "ang"), P())
    out_specs = P(None, "ang", "ax", None)
    return jax.shard_map(
        per_device, mesh=mesh, in_specs=in_specs, out_specs=out_specs, check_vma=False
    )
```

time: 207 us -> 95.5 us (0.46)
  waiting for transfers between devices: 119 us -> 43.4 us
  other arithmetic: 31.6 us -> 0 us
  local copies, waits for them, and re-layouts: 27.1 us -> 0.96 us
  Pallas kernels: 0 us -> 25.9 us
  matrix products: 6.47 us -> 0 us
  starting transfers between devices: 20.5 us -> 24.9 us
    ppermute x10 -> x12, waiting for transfers between devices: 119 us -> 43.4 us  [the longest x1 29.5 us: per_device(): flags_opp = lax.ppermute(wall_flags, 'ang', opposite)]
    pallas_call x0 -> x10, Pallas kernels: none -> 25.9 us  [call(): pl.pallas_call(body, out_shape=out_shape, in_specs=in_specs, out_specs=ou...]
    rev x1 -> x0, local copies, waits for them, and re-layouts: 16.9 us -> none  [per_device(): own_right = radial_inverse[:, :half_radial, half_radial:][:, :, ::-1]]
    reduce_sum x2 -> x0, other arithmetic: 11.4 us -> none  [transport(): jnp.sum(selectors[which_reaction, 0][:, None, None, None] * field, axis=0)]
    convert_element_type x3 -> x0, other arithmetic: 8.37 us -> none  [the longest x2 7.62 us: per_device(): explicit_low = explicit.astype(jnp.bfloat16)]
    mul x6 -> x0, other arithmetic: 7.28 us -> none  [transport(): rate_term = rate_constants[which_reaction] * first_part * second_part]
    slice x6 -> x0, local copies, waits for them, and re-layouts: 6.62 us -> none  [the longest x2 2.64 us: extended(): lax.slice_in_dim(block, block.shape[dim] - width, None, axis=dim)]
    dot_general x2 -> x0, matrix products: 6.47 us -> none  [product(): jnp.einsum('sij,sapj->sapi', matrix, values, preferred_element_type=jnp.f...]
  transfers between devices with their start and end apart: 10 -> 12, of which waited for: 3 -> 3; matrix products, arithmetic and copies ran while one was open for 17% -> 0% of each run, Pallas kernels for 0% -> 19%
where the time goes in v2:
time: 95.5 us; the launch traced here: 95.3 us
  waiting for transfers between devices  43.4 us (45%)
  Pallas kernels  25.9 us (27%)
  starting transfers between devices  24.9 us (26%)
  local copies, waits for them, and re-layouts  0.96 us (1%)
    ppermute x1, waiting for transfers between devices, per_device(): flags_opp = lax.ppermute(wall_flags, 'ang', opposite)  29.5 us
    pallas_call x10, Pallas kernels, call(): pl.pallas_call(body, out_shape=out_shape, in_specs=in_specs, out_specs=ou...  25.9 us
    ppermute x1, waiting for transfers between devices, per_device(): opp_c = lax.ppermute(mid_c, 'ang', opposite)  10.3 us
    ppermute x1, starting transfers between devices, per_device(): opp_2 = lax.ppermute(out2, 'ang', opposite)  5.75 us
    ppermute x1, starting transfers between devices, per_device(): lax.ppermute(first, 'ang', [(i, (i - 1) % count) for i in range(count)])  4.44 us
    ppermute x2, starting transfers between devices, plane_halos(): got = lax.ppermute(edges[0], 'ax', [(0, 1), (1, 0)])  3.6 us
    ppermute x1, waiting for transfers between devices, per_device(): lax.ppermute(last, 'ang', [(i, (i + 1) % count) for i in range(count)])  3.56 us
    ppermute x1, starting transfers between devices, per_device(): opp_d = lax.ppermute(mid_d, 'ang', opposite)  2.9 us
  transfers between devices with their start and end apart: 12, of which 3 were waited for; matrix products, arithmetic and copies ran while one was open for 0% of the time, Pallas kernels for 19%

profile of v2, /device:TPU:0, one launch (start us, length us, event | category | flops | bytes accessed | tf_op | source)
XLA Modules:
  0.0 95.3 jit_solution(8042004014292969118)
XLA Ops:
  0.0 3.0 %shard_map.83 = (f32[3,32,512]{2,1,0:T(8,128)}, f32[3,16,512]{2,1,0:T(8,128)}, f32[3,16,512]{2,1,0:T(8,128)}, bf16[3,64,512]{2,1,0:T(8,128)(2,1)}, f32[15,8,512]{2,1,0:T(8,128)}) custom-call(f32[3,512,512]{2,1,0:T(8,128)} %bitcast.2, f32[1,512]{1,0:T(1,128)} %bitcast.5, f32[3]{0:T(128)} %diff.1, f32[3,512]{1,0:T(4,128)} %ang.1, f32[4]{0:T(128)} %rate.1, ...), custom_call_target="tpu_custom_call" | custom-call | flops 1 | bytes 1 | tf_op jit(solution)/shard_map/pallas_call | solution.py:24
  3.0 3.0 %collective-permute-start.3 = (f32[3,32,512]{2,1,0:T(8,128)}, f32[3,32,512]{2,1,0:T(8,128)S(1)}, u32[]{:S(2)}, u32[]{:S(2)}) collective-permute-start(f32[3,32,512]{2,1,0:T(8,128)} %get-tuple-element.36), channel_id=1, source_target_pairs={{0,1},{1,0},{2,3},{3,2},{4,5},{5,4},{6,7},{7,6},{8,9},{9,8},{10,11... | collective-permute-start | bytes 589832 | tf_op jit(solution)/shard_map/ppermute | solution.py:472
  6.0 2.6 %collective-permute-start.4 = (bf16[3,64,512]{2,1,0:T(8,128)(2,1)}, bf16[3,64,512]{2,1,0:T(8,128)(2,1)S(1)}, u32[]{:S(2)}, u32[]{:S(2)}) collective-permute-start(bf16[3,64,512]{2,1,0:T(8,128)(2,1)} %get-tuple-element.39.mine), channel_id=1, source_target_pairs={{0,16},{2,18},{4,20},{6,22},{8,24},{10,26},{12,28},{14,30},{16,0},... | collective-permute-start | bytes 589832 | tf_op jit(solution)/shard_map/ppermute | solution.py:523
  8.6 4.4 %collective-permute-start.2 = (f32[3,16,512]{2,1,0:T(8,128)}, f32[3,16,512]{2,1,0:T(8,128)S(1)}, u32[]{:S(2)}, u32[]{:S(2)}) collective-permute-start(f32[3,16,512]{2,1,0:T(8,128)} %get-tuple-element.35), channel_id=1, source_target_pairs={{0,30},{2,0},{4,2},{6,4},{8,6},{10,8},{12,10},{14,12},{16,14},{18,... | collective-permute-start | bytes 294920 | tf_op jit(solution)/shard_map/ppermute | solution.py:526
  13.1 3.6 %collective-permute-done.1.before = f32[3,16,512]{2,1,0:T(8,128)S(1)} collective-permute-done((f32[3,16,512]{2,1,0:T(8,128)}, f32[3,16,512]{2,1,0:T(8,128)S(1)}, u32[]{:S(2)}, u32[]{:S(2)}) %collective-permute-start.1) | collective-permute-done | bytes 98336 | tf_op jit(solution)/shard_map/ppermute | solution.py:525
  16.7 0.9 copy-done.2
  17.6 2.7 %shard_map.85 = (bf16[3,128,512]{2,1,0:T(8,128)(2,1)S(1)}, bf16[3,160,512]{2,1,0:T(8,128)(2,1)S(1)}) custom-call(f32[3,512,512]{2,1,0:T(8,128)S(1)} %bitcast.3, f32[3,16,512]{2,1,0:T(8,128)S(1)} %collective-permute-done.1.before, f32[3,16,512]{2,1,0:T(8,128)S(1)} %collective-permute-done.2.after, f32[3,32,512]{2,1,0:T(8,128)S(1)} %collective-permute-done.3.low.high, ...), custom_call_target="tpu_custom_call" | custom-call | flops 1 | bytes 1 | tf_op jit(solution)/shard_map/pallas_call | solution.py:24
  20.3 5.8 %collective-permute-start.7 = (bf16[3,160,512]{2,1,0:T(8,128)(2,1)S(1)}, bf16[3,160,512]{2,1,0:T(8,128)(2,1)S(1)}, u32[]{:S(2)}, u32[]{:S(2)}) collective-permute-start(bf16[3,160,512]{2,1,0:T(8,128)(2,1)S(1)} %get-tuple-element.45.mine), channel_id=1, source_target_pairs={{0,16},{2,18},{4,20},{6,22},{8,24},{10,26},{12,28},{14,30},{16,0},... | collective-permute-start | bytes 1474568 | tf_op jit(solution)/shard_map/ppermute | solution.py:553
  26.0 0.1 collective-permute-start.5
  26.1 2.8 %collective-permute-start = (s32[3,32]{1,0:T(4,128)S(1)}, s32[3,32]{1,0:T(4,128)S(1)}, u32[]{:S(2)}, u32[]{:S(2)}) collective-permute-start(s32[3,32]{1,0:T(4,128)S(1)} %copy-done.5), channel_id=1, source_target_pairs={{0,16},{2,18},{4,20},{6,22},{8,24},{10,26},{12,28},{14,30},{16,0},... | collective-permute-start | bytes 1160 | tf_op jit(solution)/shard_map/ppermute | solution.py:527
  29.0 1.6 %shard_map.84 = (bf16[3,80,512]{2,1,0:T(8,128)(2,1)S(1)}, bf16[3,80,512]{2,1,0:T(8,128)(2,1)S(1)}) custom-call(f32[3,512,512]{2,1,0:T(8,128)S(1)} %bitcast.4, f32[15,8,512]{2,1,0:T(8,128)S(1)} %copy-done.2), custom_call_target="tpu_custom_call" | custom-call | flops 1 | bytes 1 | tf_op jit(solution)/shard_map/pallas_call | solution.py:24
  30.5 29.5 %collective-permute-done.flags_opp = s32[3,32]{1,0:T(4,128)S(1)} collective-permute-done((s32[3,32]{1,0:T(4,128)S(1)}, s32[3,32]{1,0:T(4,128)S(1)}, u32[]{:S(2)}, u32[]{:S(2)}) %collective-permute-start) | collective-permute-done | bytes 416 | tf_op jit(solution)/shard_map/ppermute | solution.py:527
  60.1 3.1 %shard_map.82 = (bf16[3,512,1024]{2,1,0:T(8,128)(2,1)S(1)}, f32[2,3,32,128]{3,2,1,0:T(8,128)S(1)}) custom-call(bf16[3,1024,1024]{2,1,0:T(8,128)(2,1)S(1)} %copy-done.1, s32[3,32]{1,0:T(4,128)S(1)} %copy-done.5, s32[3,32]{1,0:T(4,128)S(1)} %collective-permute-done.flags_opp), custom_call_target="tpu_custom_call" | custom-call | flops 1 | bytes 1 | tf_op jit(solution)/shard_map/pallas_call | solution.py:24
  63.2 1.2 %shard_map.86.refs_0_ = f32[2,3,64,512]{3,2,1,0:T(8,128)S(1)} custom-call(bf16[3,512,1024]{2,1,0:T(8,128)(2,1)S(1)} %get-tuple-element.30.weights, f32[2,3,32,128]{3,2,1,0:T(8,128)S(1)} %get-tuple-element.31.keep, bf16[3,64,512]{2,1,0:T(8,128)(2,1)S(1)} %copy-done.4, bf16[3,64,512]{2,1,0:T(8,128)(2,1)S(1)} %collective-permute-done.4.theirs), custom_call_target="tpu_custom_call" | custom-call | flops 1 | bytes 1 | tf_op jit(solution)/shard_map/pallas_call | solution.py:24
  64.4 1.0 %shard_map.87.refs_0_ = f32[2,3,128,512]{3,2,1,0:T(8,128)S(1)} custom-call(bf16[3,512,1024]{2,1,0:T(8,128)(2,1)S(1)} %get-tuple-element.30.weights, f32[2,3,32,128]{3,2,1,0:T(8,128)S(1)} %get-tuple-element.31.keep, bf16[3,128,512]{2,1,0:T(8,128)(2,1)S(1)} %get-tuple-element.40.mine, bf16[3,128,512]{2,1,0:T(8,128)(2,1)S(1)} %collective-permute-done.5.theirs), custom_call_target="tpu_custom_call" | custom-call | flops 1 | bytes 1 | tf_op jit(solution)/shard_map/pallas_call | solution.py:24
  65.4 0.1 collective-permute-start.6
  65.5 2.9 %collective-permute-start.11 = (bf16[3,80,512]{2,1,0:T(8,128)(2,1)S(1)}, bf16[3,80,512]{2,1,0:T(8,128)(2,1)S(1)}, u32[]{:S(2)}, u32[]{:S(2)}) collective-permute-start(bf16[3,80,512]{2,1,0:T(8,128)(2,1)S(1)} %get-tuple-element.54.mine), channel_id=1, source_target_pairs={{0,16},{2,18},{4,20},{6,22},{8,24},{10,26},{12,28},{14,30},{16,0},... | collective-permute-start | bytes 737288 | tf_op jit(solution)/shard_map/ppermute | solution.py:590
  68.4 1.5 %shard_map.88 = (f32[2,3,32,512]{3,2,1,0:T(8,128)S(1)}, f32[2,3,256,512]{3,2,1,0:T(8,128)S(1)}, bf16[2,3,32,512]{3,2,1,0:T(8,128)(2,1)S(1)}, bf16[2,3,16,512]{3,...) custom-call(bf16[3,512,1024]{2,1,0:T(8,128)(2,1)S(1)} %get-tuple-element.30.weights, ...), custom_call_target="tpu_custom_call" | custom-call | flops 1 | bytes 1 | tf_op jit(solution)/shard_map/pallas_call | solution.py:24
  69.9 0.6 collective-permute-start.10
  70.5 2.6 %collective-permute-start.9 = (bf16[2,3,16,512]{3,2,1,0:T(8,128)(2,1)S(1)}, bf16[2,3,16,512]{3,2,1,0:T(8,128)(2,1)S(1)}, u32[]{:S(2)}, u32[]{:S(2)}) collective-permute-start(bf16[2,3,16,512]{3,2,1,0:T(8,128)(2,1)S(1)} %get-tuple-element.52), channel_id=1, source_target_pairs={{0,14},{2,0},{4,2},{6,4},{8,6},{10,8},{12,10},{14,12},{16,30},{18,... | collective-permute-start | bytes 294920 | tf_op jit(solution)/shard_map/ppermute | solution.py:608
  73.1 10.3 %collective-permute-done.6.theirs = bf16[3,80,512]{2,1,0:T(8,128)(2,1)S(1)} collective-permute-done((bf16[3,80,512]{2,1,0:T(8,128)(2,1)S(1)}, bf16[3,80,512]{2,1,0:T(8,128)(2,1)S(1)}, u32[]{:S(2)}, u32[]{:S(2)}) %collective-permute-start.6) | collective-permute-done | bytes 245792 | tf_op jit(solution)/shard_map/ppermute | solution.py:588
  83.4 1.2 %shard_map.89.mid.state = f32[2,3,256,512]{3,2,1,0:T(8,128)S(1)} custom-call(bf16[3,512,1024]{2,1,0:T(8,128)(2,1)S(1)} %get-tuple-element.30.weights, f32[2,3,32,128]{3,2,1,0:T(8,128)S(1)} %get-tuple-element.31.keep, bf16[3,80,512]{2,1,0:T(8,128)(2,1)S(1)} %get-tuple-element.43.mine, bf16[3,80,512]{2,1,0:T(8,128)(2,1)S(1)} %collective-permute-done.6.theirs, ...), custom_call_target="tpu_custom_call" | custom-call | flops 1 | bytes 1 | tf_op jit(solution)/shard_map/pallas_call | solution.py:24
  84.7 5.7 %shard_map.90.given = f32[3,32,16,512]{3,2,1,0:T(8,128)} custom-call(bf16[3,512,1024]{2,1,0:T(8,128)(2,1)S(1)} %get-tuple-element.30.weights, f32[2,3,32,128]{3,2,1,0:T(8,128)S(1)} %get-tuple-element.31.keep, f32[2,3,256,512]{3,2,1,0:T(8,128)S(1)} %shard_map.89.mid.state, f32[2,3,256,512]{3,2,1,0:T(8,128)S(1)} %get-tuple-element.50.outer, ...), custom_call_target="tpu_custom_call" | custom-call | flops 1 | bytes 1 | tf_op jit(solution)/shard_map/pallas_call | solution.py:24
  90.4 5.0 %shard_map.91 = f32[3,32,16,512]{3,2,1,0:T(8,128)} custom-call(f32[3,32,16,512]{3,2,1,0:T(8,128)} %shard_map.90.given, f32[2,3,256,512]{3,2,1,0:T(8,128)S(1)} %shard_map.89.mid.state, bf16[3,512,1024]{2,1,0:T(8,128)(2,1)S(1)} %get-tuple-element.30.weights, f32[2,3,32,128]{3,2,1,0:T(8,128)S(1)} %get-tuple-element.31.keep, ...), custom_call_target="tpu_custom_call", output_to_operand_aliasing={{}: (0, {})} | custom-call | flops 1 | bytes 1 | tf_op jit(solution)/shard_map/pallas_call | solution.py:24
  (22 shorter events, 0.1 us)
Async XLA Ops:
  0.0 16.6 %copy-start = (f32[3,32,16,512]{3,2,1,0:T(8,128)S(1)}, f32[3,32,16,512]{3,2,1,0:T(8,128)}, u32[]{:S(2)}) copy-start(f32[3,32,16,512]{3,2,1,0:T(8,128)} %param.8) | copy-start | bytes 9437188
  0.0 26.1 %copy-start.5 = (s32[3,32]{1,0:T(4,128)S(1)}, s32[3,32]{1,0:T(4,128)}, u32[]{:S(2)}) copy-start(s32[3,32]{1,0:T(4,128)} %flags_own.1) | copy-start | bytes 1156
  3.0 13.6 %collective-permute-start.3 = (f32[3,32,512]{2,1,0:T(8,128)}, f32[3,32,512]{2,1,0:T(8,128)S(1)}, u32[]{:S(2)}, u32[]{:S(2)}) collective-permute-start(f32[3,32,512]{2,1,0:T(8,128)} %get-tuple-element.36), channel_id=1, source_target_pairs={{0,1},{1,0},{2,3},{3,2},{4,5},{5,4},{6,7},{7,6},{8,9},{9,8},{10,11... | collective-permute-start | bytes 589832 | tf_op jit(solution)/shard_map/ppermute | solution.py:472
  6.0 14.2 %collective-permute-start.4 = (bf16[3,64,512]{2,1,0:T(8,128)(2,1)}, bf16[3,64,512]{2,1,0:T(8,128)(2,1)S(1)}, u32[]{:S(2)}, u32[]{:S(2)}) collective-permute-start(bf16[3,64,512]{2,1,0:T(8,128)(2,1)} %get-tuple-element.39.mine), channel_id=1, source_target_pairs={{0,16},{2,18},{4,20},{6,22},{8,24},{10,26},{12,28},{14,30},{16,0},... | collective-permute-start | bytes 589832 | tf_op jit(solution)/shard_map/ppermute | solution.py:523
  8.6 8.0 %collective-permute-start.1 = (f32[3,16,512]{2,1,0:T(8,128)}, f32[3,16,512]{2,1,0:T(8,128)S(1)}, u32[]{:S(2)}, u32[]{:S(2)}) collective-permute-start(f32[3,16,512]{2,1,0:T(8,128)} %get-tuple-element.34), channel_id=1, source_target_pairs={{0,2},{2,4},{4,6},{6,8},{8,10},{10,12},{12,14},{14,16},{16,18},{18... | collective-permute-start | bytes 294920 | tf_op jit(solution)/shard_map/ppermute | solution.py:525
  8.6 8.0 %collective-permute-start.2 = (f32[3,16,512]{2,1,0:T(8,128)}, f32[3,16,512]{2,1,0:T(8,128)S(1)}, u32[]{:S(2)}, u32[]{:S(2)}) collective-permute-start(f32[3,16,512]{2,1,0:T(8,128)} %get-tuple-element.35), channel_id=1, source_target_pairs={{0,30},{2,0},{4,2},{6,4},{8,6},{10,8},{12,10},{14,12},{16,14},{18,... | collective-permute-start | bytes 294920 | tf_op jit(solution)/shard_map/ppermute | solution.py:526
  16.6 0.9 copy-start.2
  17.6 42.5 %copy-start.1 = (bf16[3,1024,1024]{2,1,0:T(8,128)(2,1)S(1)}, bf16[3,1024,1024]{2,1,0:T(8,128)(2,1)}, u32[]{:S(2)}) copy-start(bf16[3,1024,1024]{2,1,0:T(8,128)(2,1)} %matrix.1) | copy-start | bytes 18874372
  20.3 45.2 %collective-permute-start.7 = (bf16[3,160,512]{2,1,0:T(8,128)(2,1)S(1)}, bf16[3,160,512]{2,1,0:T(8,128)(2,1)S(1)}, u32[]{:S(2)}, u32[]{:S(2)}) collective-permute-start(bf16[3,160,512]{2,1,0:T(8,128)(2,1)S(1)} %get-tuple-element.45.mine), channel_id=1, source_target_pairs={{0,16},{2,18},{4,20},{6,22},{8,24},{10,26},{12,28},{14,30},{16,0},... | collective-permute-start | bytes 1474568 | tf_op jit(solution)/shard_map/ppermute | solution.py:553
  26.0 38.3 %collective-permute-start.5 = (bf16[3,128,512]{2,1,0:T(8,128)(2,1)S(1)}, bf16[3,128,512]{2,1,0:T(8,128)(2,1)S(1)}, u32[]{:S(2)}, u32[]{:S(2)}) collective-permute-start(bf16[3,128,512]{2,1,0:T(8,128)(2,1)S(1)} %get-tuple-element.40.mine), channel_id=1, source_target_pairs={{0,16},{2,18},{4,20},{6,22},{8,24},{10,26},{12,28},{14,30},{16,0},... | collective-permute-start | bytes 1179656 | tf_op jit(solution)/shard_map/ppermute | solution.py:552
  26.1 33.9 %collective-permute-start = (s32[3,32]{1,0:T(4,128)S(1)}, s32[3,32]{1,0:T(4,128)S(1)}, u32[]{:S(2)}, u32[]{:S(2)}) collective-permute-start(s32[3,32]{1,0:T(4,128)S(1)} %copy-done.5), channel_id=1, source_target_pairs={{0,16},{2,18},{4,20},{6,22},{8,24},{10,26},{12,28},{14,30},{16,0},... | collective-permute-start | bytes 1160 | tf_op jit(solution)/shard_map/ppermute | solution.py:527
  30.5 32.7 %copy-start.4 = (bf16[3,64,512]{2,1,0:T(8,128)(2,1)S(1)}, bf16[3,64,512]{2,1,0:T(8,128)(2,1)}, u32[]{:S(2)}) copy-start(bf16[3,64,512]{2,1,0:T(8,128)(2,1)} %get-tuple-element.39.mine) | copy-start | bytes 589828
  65.4 18.0 %collective-permute-start.6 = (bf16[3,80,512]{2,1,0:T(8,128)(2,1)S(1)}, bf16[3,80,512]{2,1,0:T(8,128)(2,1)S(1)}, u32[]{:S(2)}, u32[]{:S(2)}) collective-permute-start(bf16[3,80,512]{2,1,0:T(8,128)(2,1)S(1)} %get-tuple-element.43.mine), channel_id=1, source_target_pairs={{0,16},{2,18},{4,20},{6,22},{8,24},{10,26},{12,28},{14,30},{16,0},... | collective-permute-start | bytes 737288 | tf_op jit(solution)/shard_map/ppermute | solution.py:588
  65.5 24.9 %collective-permute-start.11 = (bf16[3,80,512]{2,1,0:T(8,128)(2,1)S(1)}, bf16[3,80,512]{2,1,0:T(8,128)(2,1)S(1)}, u32[]{:S(2)}, u32[]{:S(2)}) collective-permute-start(bf16[3,80,512]{2,1,0:T(8,128)(2,1)S(1)} %get-tuple-element.54.mine), channel_id=1, source_target_pairs={{0,16},{2,18},{4,20},{6,22},{8,24},{10,26},{12,28},{14,30},{16,0},... | collective-permute-start | bytes 737288 | tf_op jit(solution)/shard_map/ppermute | solution.py:590
  69.9 14.8 %collective-permute-start.10 = (bf16[2,3,32,512]{3,2,1,0:T(8,128)(2,1)S(1)}, bf16[2,3,32,512]{3,2,1,0:T(8,128)(2,1)S(1)}, u32[]{:S(2)}, u32[]{:S(2)}) collective-permute-start(bf16[2,3,32,512]{3,2,1,0:T(8,128)(2,1)S(1)} %get-tuple-element.53), channel_id=1, source_target_pairs={{0,1},{1,0},{2,3},{3,2},{4,5},{5,4},{6,7},{7,6},{8,9},{9,8},{10,11... | collective-permute-start | bytes 589832 | tf_op jit(solution)/shard_map/ppermute | solution.py:472
  70.5 14.1 %collective-permute-start.8 = (bf16[2,3,16,512]{3,2,1,0:T(8,128)(2,1)S(1)}, bf16[2,3,16,512]{3,2,1,0:T(8,128)(2,1)S(1)}, u32[]{:S(2)}, u32[]{:S(2)}) collective-permute-start(bf16[2,3,16,512]{3,2,1,0:T(8,128)(2,1)S(1)} %get-tuple-element.51), channel_id=1, source_target_pairs={{0,2},{2,4},{4,6},{6,8},{8,10},{10,12},{12,14},{14,0},{16,18},{18,... | collective-permute-start | bytes 294920 | tf_op jit(solution)/shard_map/ppermute | solution.py:607
  70.5 14.1 %collective-permute-start.9 = (bf16[2,3,16,512]{3,2,1,0:T(8,128)(2,1)S(1)}, bf16[2,3,16,512]{3,2,1,0:T(8,128)(2,1)S(1)}, u32[]{:S(2)}, u32[]{:S(2)}) collective-permute-start(bf16[2,3,16,512]{3,2,1,0:T(8,128)(2,1)S(1)} %get-tuple-element.52), channel_id=1, source_target_pairs={{0,14},{2,0},{4,2},{6,4},{8,6},{10,8},{12,10},{14,12},{16,30},{18,... | collective-permute-start | bytes 294920 | tf_op jit(solution)/shard_map/ppermute | solution.py:608
  83.4 1.2 %copy-start.3 = (f32[15,8,512]{2,1,0:T(8,128)S(1)}, f32[15,8,512]{2,1,0:T(8,128)}, u32[]{:S(2)}) copy-start(f32[15,8,512]{2,1,0:T(8,128)} %get-tuple-element.32.coef) | copy-start | bytes 737284

commit v3 on v2

--- a/solution.py
+++ b/solution.py
@@ -113,23 +113,25 @@
     return lambda s, shift, k: field[s, at_rows((t + shift) * nz + k * half, half, half), :]
 
 
-def mid_run(field, out, begin, count, at, coef, nz):
+def mid_run(field, out_of, begin, count, at, coef, nz):
     half = nz // 2
 
     def pair(step, carry):
         t = begin + step * 2
         tiles = [first_step(field_reader(field, t + k, nz), None, None, coef, half)[0] for k in range(2)]
         for s in range(3):
-            out[s, at_rows(at * half + step * nz, nz, nz), :] = pack([tiles[0][s], tiles[1][s]])
+            out_of(s)[at_rows(at * half + step * nz, nz, nz), :] = pack([tiles[0][s], tiles[1][s]])
         return carry
 
     lax.fori_loop(0, count // 2, pair, 0)
 
 
-def head_kernel(sizes, conc, cour, diff, ang, rate, smap, *rest):
+def head_kernel(sizes, conc, cour, diff, ang, rate, smap, flags, *rest):
     na, nz, lo, hi, planes = sizes
     edges = rest[: 1 if planes == 2 else 2]
-    first, last, mid, coef, field, cour_v, ang_v, diff_s, rate_s, map_s, sems = rest[len(edges) :]
+    first, last, mid, coef, field, flag_v, cour_v, ang_v, diff_s, rate_s, map_s, flags_s, sems = rest[
+        len(edges) :
+    ]
     half = nz // 2
     inner = pl.ds((lo - 1) * nz, (hi - lo + 2) * nz)
     left = pl.ds(0, (lo - 1) * nz)
@@ -137,7 +139,7 @@
     small = [
         pltpu.make_async_copy(src, dst, sems.at[k + 3])
         for k, (src, dst) in enumerate(
-            ((cour, cour_v), (ang, ang_v), (diff, diff_s), (rate, rate_s), (smap, map_s))
+            ((cour, cour_v), (ang, ang_v), (diff, diff_s), (rate, rate_s), (smap, map_s), (flags, flags_s))
         )
     ]
     copies = [
@@ -160,8 +162,18 @@
         coef[ANGULAR + s] = jnp.broadcast_to(angular, tile)
         coef[AXIAL + s] = jnp.full(tile, axial, F32)
         coef[RATE + s] = jnp.full(tile, total, F32)
+    lane = lax.broadcasted_iota(jnp.int32, (1, LANES), 1)
+    for t in range(na):
+        row = jnp.zeros((1, LANES), jnp.int32)
+        for s in range(3):
+            row = jnp.where(lane == s, flags_s[s, t], row)
+        flag_v[t : t + 1, :] = row.astype(F32)
+    rows = (hi - lo) * half
+    span = pl.ds(3 * rows, na)
+    mid[span, :] = jnp.zeros((na, mid.shape[1]), BF16)
+    mid[span, :LANES] = flag_v[...].astype(BF16)
     copies[0].wait()
-    mid_run(field, mid, lo, hi - lo, 0, coef, nz)
+    mid_run(field, lambda s: mid.at[pl.ds(s * rows, rows)], lo, hi - lo, 0, coef, nz)
     copies[1].wait()
     copies[2].wait()
     for s in range(3):
@@ -186,7 +198,7 @@
     for out, parts in runs:
         at = 0
         for begin, count in parts:
-            mid_run(field, outs[out], begin, count, at, coef, nz)
+            mid_run(field, outs[out].at.__getitem__, begin, count, at, coef, nz)
             at += count
 
 
@@ -197,13 +209,16 @@
     return jnp.where(place == 1, 1.0, 0.0), jnp.where(place == 0, 1.0, 0.0)
 
 
-def frame_kernel(sizes, conc, before, after, low, high, coef, out1, out2, field, sems):
+def frame_kernel(
+    sizes, conc, before, after, low, high, coef_in, out1, out2, field, coef, sems
+):
     na, nz, ends, planes = sizes
     half = nz // 2
     copies = [
         pltpu.make_async_copy(conc, field.at[:, pl.ds(nz, na * nz)], sems.at[0]),
         pltpu.make_async_copy(before, field.at[:, pl.ds(0, nz)], sems.at[1]),
         pltpu.make_async_copy(after, field.at[:, pl.ds((na + 1) * nz, nz)], sems.at[2]),
+        pltpu.make_async_copy(coef_in, coef, sems.at[3]),
     ]
     for copy in copies:
         copy.start()
@@ -244,7 +259,7 @@
     lax.fori_loop(0, quarter - 1, second_part, 0)
 
 
-def weights_kernel(matrix, flags_own, flags_opp, out, keep, left, lower, sems):
+def weights_kernel(matrix, mine, theirs, out, keep, left, lower, sems):
     half = out.shape[1]
     copies = []
     for s in range(out.shape[0]):
@@ -253,11 +268,13 @@
             copies.append(pltpu.make_async_copy(src, ref.at[s], sems.at[k, s]))
     for copy in copies:
         copy.start()
-    lane = lax.broadcasted_iota(jnp.int32, (1, LANES), 1)
-    for ab, flags in enumerate((flags_own, flags_opp)):
+    na = keep.shape[2]
+    lane = lax.broadcasted_iota(jnp.int32, (na, LANES), 1)
+    for ab, ref in enumerate((mine, theirs)):
+        flags = ref[pl.ds(ref.shape[0] - na, na), :LANES].astype(F32)
         for s in range(out.shape[0]):
-            for t in range(keep.shape[2]):
-                keep[ab, s, t : t + 1, :] = jnp.where((lane == 0) & (flags[s, t] == 1), 0.0, 1.0)
+            moved = pltpu.roll(flags, LANES - s, 1) if s else flags
+            keep[ab, s] = jnp.where(lane == 0, 1.0 - moved, 1.0)
     row = lax.broadcasted_iota(jnp.int32, (half, half), 0)
     col = lax.broadcasted_iota(jnp.int32, (half, half), 1)
     row = jnp.maximum(row, 1)
@@ -292,11 +309,18 @@
             )
 
 
+def species_rows(ref, s, runs, half):
+    if len(ref.shape) == 3:
+        return ref[s]
+    rows = sum(run[3] for run in runs) * half
+    return ref[pl.ds(s * rows, rows), :]
+
+
 def radial_kernel(runs, copies, half, weights, keep, mine, theirs, *refs):
     n_in = 1 + max((part for part, *_ in copies), default=-1)
     parts, states = refs[:n_in], refs[n_in:]
     for s in range(3):
-        value = both_sides(mine[s], theirs[s], weights[s])
+        value = both_sides(species_rows(mine, s, runs, half), species_rows(theirs, s, runs, half), weights[s])
         at = 0
         for which, begin, place, count in runs:
             store_run(states[which], s, begin, place, count, at, value, keep, half)
@@ -308,12 +332,12 @@
                 states[which][ab, s, to, :] = parts[part][ab, s, rows, :]
 
 
-def edges_of_state(na, nz, planes, mid, outer, edges, first, last, stage):
+def edges_of_state(na, nz, planes, mid, mid_end, outer, edges, first, last, stage):
     half = nz // 2
     if planes == 2:
         row = jnp.where(lax.axis_index("ax") == 0, half // 2 - 1, half // 2)
     end = pl.ds((na - 1) * half, half)
-    ends_end = pl.ds(mid.shape[2] - half, half)
+    ends_end = pl.ds(mid_end.shape[2] - half, half)
     for ab in range(2):
         for s in range(3):
             for t in range(na):
@@ -328,7 +352,7 @@
                 edge[ab, s] = stage[k].astype(BF16)
             begin = pl.ds(0, half)
             first[ab, s] = pack([mid[ab, s, begin, :], outer[ab, s, begin, :]])
-            last[ab, s] = pack([mid[ab, s, ends_end, :], outer[ab, s, end, :]])
+            last[ab, s] = pack([mid_end[ab, s, ends_end, :], outer[ab, s, end, :]])
 
 
 def radial_edges_kernel(sizes, runs, copies, half, weights, keep, mine, theirs, *refs):
@@ -337,7 +361,7 @@
     *edges, first, last, stage = refs[-3 - n_edges :]
     refs = refs[: -3 - n_edges]
     radial_kernel(runs, copies, half, weights, keep, mine, theirs, *refs)
-    edges_of_state(na, nz, planes, refs[-2], refs[-1], edges, first, last, stage)
+    edges_of_state(na, nz, planes, refs[-3], refs[-2], refs[-1], edges, first, last, stage)
 
 
 def explicit_angle(t, reader, low, high, edge_factors, coef, rows, nz):
@@ -390,38 +414,44 @@
         target[...] = source[...].astype(F32)
 
 
-def early_kernel(
-    sizes, weights, keep, mid, outer, before_low, after_low, low_low, high_low, coef,
-    out, before, after, low, high, rows, result, out_sems
-):
-    na, nz, runs, half_ring, planes = sizes
+def early_kernel(sizes, *refs):
+    na, nz, runs, base, half_ring, planes = sizes
+    if len(refs) == 18:
+        refs = refs[1:]
+    (weights, keep, mid, outer, before_low, after_low, low_low, high_low, coef, out,
+     before, after, low, high, rows, result, out_sems) = refs
     half = nz // 2
     place = lax.rem(lax.axis_index("ang"), half_ring)
     wrap_before = jnp.where(place == 0, 1, 0)
     wrap_after = jnp.where(place == half_ring - 1, 1, 0)
     factors = edge_weights(planes)
-    states = (mid, outer)
-    widen(((before_low, before), (after_low, after), (low_low, low), (high_low, high)))
+    states = ((mid, base), (outer, 0))
+    widen(((low_low, low), (high_low, high)))
     for begin, count in runs:
         end = begin + count
         if begin == 0:
+            widen(((before_low, before),))
 
             def reader(ab, k, s, shift):
                 if shift == -1:
-                    return before[jnp.where(wrap_before == 1, 1 - ab, ab), s, pl.ds(k * half, half), :]
-                return states[k][ab, s, pl.ds(shift * half, half), :]
+                    source = jnp.where(wrap_before == 1, 1 - ab, ab)
+                    return before[source, s, pl.ds(k * half, half), :]
+                return states[k][0][ab, s, pl.ds((shift - states[k][1]) * half, half), :]
 
             explicit_angle(0, reader, low, high, factors, coef, rows, nz)
         if end == na:
+            widen(((after_low, after),))
 
             def reader(ab, k, s, shift):
                 if shift == 1:
-                    return after[jnp.where(wrap_after == 1, 1 - ab, ab), s, pl.ds(k * half, half), :]
-                return states[k][ab, s, pl.ds((na - 1 + shift) * half, half), :]
+                    source = jnp.where(wrap_after == 1, 1 - ab, ab)
+                    return after[source, s, pl.ds(k * half, half), :]
+                return states[k][0][ab, s, pl.ds((na - 1 + shift - states[k][1]) * half, half), :]
 
             explicit_angle(na - 1, reader, low, high, factors, coef, rows, nz)
         start, stop = max(begin, 1), min(end, na - 1)
-        explicit_run(start, stop - start, ((mid, 0), (outer, 0)), low, high, factors, coef, rows, nz)
+        if stop > start:
+            explicit_run(start, stop - start, states, low, high, factors, coef, rows, nz)
     leaves = []
     for s in range(3):
         for k, (begin, count) in enumerate(runs):
@@ -438,7 +468,7 @@
     sizes, given, state, weights, keep, mine, theirs, outer, low_low, high_low, coef,
     out, mid, low, high, rows, result, out_sems,
 ):
-    na, nz, lo, hi, planes = sizes
+    na, nz, lo, hi, base, planes = sizes
     half = nz // 2
     factors = edge_weights(planes)
     count = hi - lo
@@ -449,7 +479,9 @@
         for ab in range(2):
             for k in range(2):
                 to = pl.ds((2 + count) * k * half, 2 * half)
-                mid[ab, s, to, :] = state[ab, s, pl.ds((lo - 2 + (2 + count) * k) * half, 2 * half), :]
+                mid[ab, s, to, :] = state[
+                    ab, s, pl.ds((lo - 2 - base + (2 + count) * k) * half, 2 * half), :
+                ]
     explicit_run(lo - 1, count + 2, ((mid, lo - 2), (outer, 0)), low, high, factors, coef, rows, nz)
     leaves = []
     for s in range(3):
@@ -491,10 +523,9 @@
     n_edges = 1 if planes == 2 else 2
     quarter = na // 4
     ends = 2
-    first_lo, first_hi = quarter, 2 * quarter
-    last_lo, last_hi = first_hi, 3 * quarter + ends
-    inner = ((ends, first_lo - ends), (last_hi, na - ends - last_hi))
-    inner_count = sum(n for _, n in inner)
+    side = na // 2
+    first_lo, first_hi = ends, side
+    last_lo, last_hi = na - 3 * ends, na - ends
     opposite = [(i, (i + count // 2) % count) for i in range(count)]
 
     def dma(*dims):
@@ -509,30 +540,31 @@
         functools.partial(head_kernel, (na, nz, first_lo, first_hi, planes)),
         [shape(ns, na, nr)] * n_edges
         + [shape(ns, nz, nr)] * 2
-        + [message(first_hi - first_lo), shape(RATE + 3, half, nr)],
-        [HBM] * 6,
+        + [
+            shape(ns * (first_hi - first_lo) * half + na, nr, dtype=BF16),
+            shape(RATE + 3, half, nr),
+        ],
+        [HBM] * 7,
         [VM] * (n_edges + 4),
         [
-            field, pltpu.VMEM((1, nr), F32), pltpu.VMEM(angular_rate.shape, F32),
+            field, pltpu.VMEM((na, LANES), F32), pltpu.VMEM((1, nr), F32), pltpu.VMEM(angular_rate.shape, F32),
             pltpu.SMEM(axial_diffusion.shape, F32), pltpu.SMEM(rate_constants.shape, F32),
-            pltpu.SMEM(species_map.shape, jnp.int32), dma(8),
+            pltpu.SMEM(species_map.shape, jnp.int32), pltpu.SMEM(wall_flags.shape, jnp.int32), dma(9),
         ],
-        (conc, courant[None], axial_diffusion, angular_rate, rate_constants, species_map),
+        (conc, courant[None], axial_diffusion, angular_rate, rate_constants, species_map, wall_flags),
         58,
     )
     opp_a = lax.ppermute(mid_a, "ang", opposite)
     low, high = plane_halos(edges, planes)
     angle_before = lax.ppermute(last, "ang", [(i, (i + 1) % count) for i in range(count)])
     angle_after = lax.ppermute(first, "ang", [(i, (i - 1) % count) for i in range(count)])
-    flags_opp = lax.ppermute(wall_flags, "ang", opposite)
-
-    mid_c, mid_d = call(
+    mid_x, mid_l = call(
         functools.partial(
             inner_kernel,
             (na, nz),
-            ((0, inner), (1, ((last_lo, last_hi - last_lo),))),
+            ((0, ((first_hi, last_lo - first_hi),)), (1, ((last_lo, last_hi - last_lo),))),
         ),
-        [message(inner_count), message(last_hi - last_lo)],
+        [message(last_lo - first_hi), message(last_hi - last_lo)],
         [ANY, VM],
         [VM] * 2,
         [field, pltpu.SemaphoreType.DMA],
@@ -542,9 +574,9 @@
     out1, out2 = call(
         functools.partial(frame_kernel, (na, nz, ends, planes)),
         [message(na // 2), message(na // 2 + 2 * ends)],
-        [ANY] * 3 + [VM] * 3,
+        [ANY] * 3 + [VM] * 2 + [ANY],
         [VM] * 2,
-        [pltpu.VMEM((ns, (na + 2) * nz, nr), F32), dma(3)],
+        [pltpu.VMEM((ns, (na + 2) * nz, nr), F32), pltpu.VMEM((RATE + 3, half, nr), F32), dma(4)],
         (conc, angle_before, angle_after, low, high, coef),
         8,
     )
@@ -554,17 +586,17 @@
     weights, keep = call(
         weights_kernel,
         [shape(ns, nr, 2 * nr, dtype=BF16), shape(2, ns, na, LANES)],
-        [ANY, SM, SM],
+        [ANY, VM, VM],
         [VM] * 2,
         [pltpu.VMEM((ns, nr, nr), BF16), pltpu.VMEM((ns, nr, nr), BF16), dma(2, ns)],
-        (radial_inverse, wall_flags, flags_opp),
+        (radial_inverse, mid_a, opp_a),
         12,
     )
 
     def state(angles):
         return shape(2, ns, angles * half, nr)
 
-    count_a, side = first_hi - first_lo, na // 2
+    count_a = first_hi - first_lo
     (mid_first,) = call(
         functools.partial(radial_kernel, ((0, first_lo, 0, count_a),), (), half),
         [state(count_a)],
@@ -575,6 +607,8 @@
         8,
     )
     opp_1, mid_first = after(opp_1, mid_first)
+    mid_x, opp_1 = after(mid_x, opp_1)
+    opp_x = lax.ppermute(mid_x, "ang", opposite)
     (outer_first,) = call(
         functools.partial(radial_kernel, ((0, 0, 0, side),), (), half),
         [state(side)],
@@ -584,63 +618,73 @@
         (weights, keep, out1, opp_1),
         8,
     )
-    mid_c, outer_first = after(mid_c, outer_first)
-    opp_c = lax.ppermute(mid_c, "ang", opposite)
-    mid_d, opp_2 = after(mid_d, opp_2)
-    opp_d = lax.ppermute(mid_d, "ang", opposite)
-    runs = ((1, side, side, side), (0, 0, 0, ends), (0, na - ends, ends, ends))
-    mid_ends, outer_state, *rest = call(
+    mid_l, opp_2 = after(mid_l, opp_2)
+    opp_l = lax.ppermute(mid_l, "ang", opposite)
+    runs = ((2, side, side, side), (0, 0, 0, ends), (1, na - ends, 0, ends))
+    mid_left, ends_right, outer_state, *rest = call(
         functools.partial(
-            radial_edges_kernel, (na, nz, planes), runs, ((0, 0, 1, 0, side),), half
+            radial_edges_kernel,
+            (na, nz, planes),
+            runs,
+            ((0, 0, 0, first_lo, count_a), (1, 0, 2, 0, side)),
+            half,
         ),
-        [state(2 * ends), state(na)]
+        [state(side), state(ends), state(na)]
         + [shape(2, ns, na, nr, dtype=BF16)] * n_edges
         + [shape(2, ns, nz, nr, dtype=BF16)] * 2,
-        [VM] * 5,
-        [VM] * (4 + n_edges),
+        [VM] * 6,
+        [VM] * (5 + n_edges),
         [pltpu.VMEM((n_edges, na, nr), F32)],
-        (weights, keep, out2, opp_2, outer_first),
+        (weights, keep, out2, opp_2, mid_first, outer_first),
         8,
     )
     *edges, first, last = rest
     low, high = plane_halos(edges, planes)
     angle_before = lax.ppermute(last, "ang", ring(count, 1))
     angle_after = lax.ppermute(first, "ang", ring(count, -1))
-    (mid_state,) = call(
+    stage = [pltpu.VMEM((ns, na * nz, 2 * nr), BF16), pltpu.VMEM((ns, na, nz, nr), F32)]
+    edge_scratch = [pltpu.VMEM((2, ns, na, nr), F32)] * 2
+    def early(runs, base, mid, given):
+        return call(
+            functools.partial(early_kernel, (na, nz, runs, base, count // 2, planes)),
+            shape(ns, na, nz, nr),
+            [ANY] * len(given) + [VM] * 9,
+            ANY,
+            [pltpu.VMEM((2, ns, nz, nr), F32)] * 2 + edge_scratch + stage + [dma(len(runs), ns)],
+            (*given, weights, keep, mid, outer_state, angle_before, angle_after, low, high, coef),
+            12,
+            {0: 0} if given else None,
+        )
+
+    partial = early(((0, first_hi - 1),), 0, mid_left, ())
+    opp_x, partial = after(opp_x, partial)
+    base = first_hi - 2
+    (mid_right,) = call(
         functools.partial(
             radial_kernel,
-            tuple((0, begin, begin, n) for begin, n in inner),
-            ((0, 0, 0, first_lo, count_a), (1, 0, 0, 0, ends), (1, ends, 0, na - ends, ends)),
+            ((0, first_hi, 2, last_lo - first_hi),),
+            ((0, base, 0, 0, 2), (1, 0, 0, na - ends - base, ends)),
             half,
         ),
-        [state(na)],
+        [state(na - base)],
         [VM] * 6,
         [VM],
         [],
-        (weights, keep, mid_c, opp_c, mid_first, mid_ends),
+        (weights, keep, mid_x, opp_x, mid_left, ends_right),
         8,
     )
 
-    stage = [pltpu.VMEM((ns, na * nz, 2 * nr), BF16), pltpu.VMEM((ns, na, nz, nr), F32)]
-    edge_scratch = [pltpu.VMEM((2, ns, na, nr), F32)] * 2
-    early = ((0, last_lo - 1), (last_hi + 1, na - last_hi - 1))
-    partial = call(
-        functools.partial(early_kernel, (na, nz, early, count // 2, planes)),
-        shape(ns, na, nz, nr),
-        [VM] * 9,
-        ANY,
-        [pltpu.VMEM((2, ns, nz, nr), F32)] * 2 + edge_scratch + stage + [dma(2, ns)],
-        (weights, keep, mid_state, outer_state, angle_before, angle_after, low, high, coef),
-        12,
+    partial = early(
+        ((first_hi - 1, last_lo - first_hi), (na - 1, 1)), base, mid_right, (partial,)
     )
     wide = last_hi - last_lo + 4
     return call(
-        functools.partial(late_kernel, (na, nz, last_lo, last_hi, planes)),
+        functools.partial(late_kernel, (na, nz, last_lo, last_hi, base, planes)),
         shape(ns, na, nz, nr),
         [ANY] + [VM] * 9,
         ANY,
         [pltpu.VMEM((2, ns, wide * half, nr), F32)] + edge_scratch + stage + [dma(ns)],
-        (partial, mid_state, weights, keep, mid_d, opp_d, outer_state, low, high, coef),
+        (partial, mid_right, weights, keep, mid_l, opp_l, outer_state, low, high, coef),
         12,
         {0: 0},
     )

time: 95.5 us -> 93.9 us (0.983)
  waiting for transfers between devices: 43.4 us -> 39.8 us
  Pallas kernels: 25.9 us -> 27.1 us
    ppermute x3 -> x2, waiting for transfers between devices: 39.8 us -> 0.01 us  [the longest x1 0.01 us: per_device(): opp_l = lax.ppermute(mid_l, 'ang', opposite)]
    ppermute x1, waiting for transfers between devices: 0.01 us -> 29.8 us  [per_device(): opp_1 = lax.ppermute(out1, 'ang', opposite)]
    ppermute x1, starting transfers between devices: 5.75 us -> 8.68 us  [per_device(): opp_2 = lax.ppermute(out2, 'ang', opposite)]
    ppermute x3 -> x2, starting transfers between devices: 5.82 us -> 2.92 us  [the longest x1 2.92 us: per_device(): opp_l = lax.ppermute(mid_l, 'ang', opposite)]
    ppermute x1, waiting for transfers between devices: 0.01 us -> 2.74 us  [per_device(): angle_before = lax.ppermute(last, 'ang', ring(count, 1))]
    ppermute x1, waiting for transfers between devices: 3.56 us -> 6.16 us  [per_device(): lax.ppermute(last, 'ang', [(i, (i + 1) % count) for i in range(count)])]
    ppermute x1, starting transfers between devices: 2.59 us -> 4.1 us  [per_device(): opp_a = lax.ppermute(mid_a, 'ang', opposite)]
    pallas_call x10 -> x11, Pallas kernels: 25.9 us -> 27.1 us  [call(): pl.pallas_call(body, out_shape=out_shape, in_specs=in_specs, out_specs=ou...]
  transfers between devices with their start and end apart: 12 -> 11, of which waited for: 3 -> 4; matrix products, arithmetic and copies ran while one was open for 0% -> 0% of each run, Pallas kernels for 19% -> 21%
where the time goes in v3:
time: 93.9 us; the launch traced here: 93.6 us
  waiting for transfers between devices  39.8 us (42%)
  Pallas kernels  27.1 us (29%)
  starting transfers between devices  25.7 us (27%)
  local copies, waits for them, and re-layouts  0.95 us (1%)
    ppermute x1, waiting for transfers between devices, per_device(): opp_1 = lax.ppermute(out1, 'ang', opposite)  29.8 us
    pallas_call x11, Pallas kernels, call(): pl.pallas_call(body, out_shape=out_shape, in_specs=in_specs, out_specs=ou...  27.1 us
    ppermute x1, starting transfers between devices, per_device(): opp_2 = lax.ppermute(out2, 'ang', opposite)  8.68 us
    ppermute x1, waiting for transfers between devices, per_device(): lax.ppermute(last, 'ang', [(i, (i + 1) % count) for i in range(count)])  6.16 us
    ppermute x1, starting transfers between devices, per_device(): lax.ppermute(first, 'ang', [(i, (i - 1) % count) for i in range(count)])  4.44 us
    ppermute x1, starting transfers between devices, per_device(): opp_a = lax.ppermute(mid_a, 'ang', opposite)  4.1 us
    ppermute x1, starting transfers between devices, per_device(): opp_l = lax.ppermute(mid_l, 'ang', opposite)  2.92 us
    ppermute x2, starting transfers between devices, plane_halos(): got = lax.ppermute(edges[0], 'ax', [(0, 1), (1, 0)])  2.8 us
  transfers between devices with their start and end apart: 11, of which 4 were waited for; matrix products, arithmetic and copies ran while one was open for 0% of the time, Pallas kernels for 21%

profile of v3, /device:TPU:0, one launch (start us, length us, event | category | flops | bytes accessed | tf_op | source)
XLA Modules:
  0.0 93.6 jit_solution(6897449076469000745)
XLA Ops:
  0.0 3.5 %shard_map.82 = (f32[3,32,512]{2,1,0:T(8,128)}, f32[3,16,512]{2,1,0:T(8,128)}, f32[3,16,512]{2,1,0:T(8,128)}, bf16[368,512]{1,0:T(8,128)(2,1)}, f32[15,8,512]{2,1,0:T(8,128)}) custom-call(f32[3,512,512]{2,1,0:T(8,128)} %bitcast.2, f32[1,512]{1,0:T(1,128)} %bitcast.5, f32[3]{0:T(128)} %diff.1, f32[3,512]{1,0:T(4,128)} %ang.1, f32[4]{0:T(128)} %rate.1, ...), custom_call_target="tpu_custom_call" | custom-call | flops 1 | bytes 1 | tf_op jit(solution)/shard_map/pallas_call | solution.py:24
  3.6 4.1 %collective-permute-start.3 = (bf16[368,512]{1,0:T(8,128)(2,1)}, bf16[368,512]{1,0:T(8,128)(2,1)S(1)}, u32[]{:S(2)}, u32[]{:S(2)}) collective-permute-start(bf16[368,512]{1,0:T(8,128)(2,1)} %get-tuple-element.40.mine), channel_id=1, source_target_pairs={{0,16},{2,18},{4,20},{6,22},{8,24},{10,26},{12,28},{14,30},{16,0},... | collective-permute-start | bytes 1130504 | tf_op jit(solution)/shard_map/ppermute | solution.py:557
  7.7 1.5 %collective-permute-start.2 = (f32[3,32,512]{2,1,0:T(8,128)}, f32[3,32,512]{2,1,0:T(8,128)S(1)}, u32[]{:S(2)}, u32[]{:S(2)}) collective-permute-start(f32[3,32,512]{2,1,0:T(8,128)} %get-tuple-element.37), channel_id=1, source_target_pairs={{0,1},{1,0},{2,3},{3,2},{4,5},{5,4},{6,7},{7,6},{8,9},{9,8},{10,11... | collective-permute-start | bytes 589832 | tf_op jit(solution)/shard_map/ppermute | solution.py:504
  9.2 4.4 %collective-permute-start.1 = (f32[3,16,512]{2,1,0:T(8,128)}, f32[3,16,512]{2,1,0:T(8,128)S(1)}, u32[]{:S(2)}, u32[]{:S(2)}) collective-permute-start(f32[3,16,512]{2,1,0:T(8,128)} %get-tuple-element.36), channel_id=1, source_target_pairs={{0,30},{2,0},{4,2},{6,4},{8,6},{10,8},{12,10},{14,12},{16,14},{18,... | collective-permute-start | bytes 294920 | tf_op jit(solution)/shard_map/ppermute | solution.py:560
  13.6 6.2 %collective-permute-done.before = f32[3,16,512]{2,1,0:T(8,128)S(1)} collective-permute-done((f32[3,16,512]{2,1,0:T(8,128)}, f32[3,16,512]{2,1,0:T(8,128)S(1)}, u32[]{:S(2)}, u32[]{:S(2)}) %collective-permute-start) | collective-permute-done | bytes 98336 | tf_op jit(solution)/shard_map/ppermute | solution.py:559
  19.8 0.9 copy-done.2
  20.7 3.0 %shard_map.84 = (bf16[3,128,512]{2,1,0:T(8,128)(2,1)S(1)}, bf16[3,160,512]{2,1,0:T(8,128)(2,1)S(1)}) custom-call(f32[3,512,512]{2,1,0:T(8,128)S(1)} %bitcast.3, f32[3,16,512]{2,1,0:T(8,128)S(1)} %collective-permute-done.before, f32[3,16,512]{2,1,0:T(8,128)S(1)} %collective-permute-done.1.after, f32[3,32,512]{2,1,0:T(8,128)S(1)} %collective-permute-done.2.low.high, ...), custom_call_target="tpu_custom_call" | custom-call | flops 1 | bytes 1 | tf_op jit(solution)/shard_map/pallas_call | solution.py:24
  23.7 1.0 %collective-permute-done.3.theirs = bf16[368,512]{1,0:T(8,128)(2,1)S(1)} collective-permute-done((bf16[368,512]{1,0:T(8,128)(2,1)}, bf16[368,512]{1,0:T(8,128)(2,1)S(1)}, u32[]{:S(2)}, u32[]{:S(2)}) %collective-permute-start.3) | collective-permute-done | bytes 376864 | tf_op jit(solution)/shard_map/ppermute | solution.py:557
  24.7 8.7 %collective-permute-start.6 = (bf16[3,160,512]{2,1,0:T(8,128)(2,1)S(1)}, bf16[3,160,512]{2,1,0:T(8,128)(2,1)S(1)}, u32[]{:S(2)}, u32[]{:S(2)}) collective-permute-start(bf16[3,160,512]{2,1,0:T(8,128)(2,1)S(1)} %get-tuple-element.47.mine), channel_id=1, source_target_pairs={{0,16},{2,18},{4,20},{6,22},{8,24},{10,26},{12,28},{14,30},{16,0},... | collective-permute-start | bytes 1474568 | tf_op jit(solution)/shard_map/ppermute | solution.py:585
  33.4 0.1 collective-permute-start.4
  33.5 1.2 %shard_map.83 = (bf16[3,80,512]{2,1,0:T(8,128)(2,1)S(1)}, bf16[3,32,512]{2,1,0:T(8,128)(2,1)S(1)}) custom-call(f32[3,512,512]{2,1,0:T(8,128)S(1)} %bitcast.4, f32[15,8,512]{2,1,0:T(8,128)S(1)} %copy-done.2), custom_call_target="tpu_custom_call" | custom-call | flops 1 | bytes 1 | tf_op jit(solution)/shard_map/pallas_call | solution.py:24
  34.6 2.4 %shard_map.85 = (bf16[3,512,1024]{2,1,0:T(8,128)(2,1)S(1)}, f32[2,3,32,128]{3,2,1,0:T(8,128)S(1)}) custom-call(bf16[3,1024,1024]{2,1,0:T(8,128)(2,1)S(1)} %copy-done.1, bf16[368,512]{1,0:T(8,128)(2,1)S(1)} %copy-done.4, bf16[368,512]{1,0:T(8,128)(2,1)S(1)} %collective-permute-done.3.theirs), custom_call_target="tpu_custom_call" | custom-call | flops 1 | bytes 1 | tf_op jit(solution)/shard_map/pallas_call | solution.py:24
  37.1 1.1 %shard_map.86.refs_0_ = f32[2,3,112,512]{3,2,1,0:T(8,128)S(1)} custom-call(bf16[3,512,1024]{2,1,0:T(8,128)(2,1)S(1)} %get-tuple-element.43.weights.refs_0_.refs_1_, f32[2,3,32,128]{3,2,1,0:T(8,128)S(1)} %get-tuple-element.44.keep.refs_1_.refs_2_, bf16[368,512]{1,0:T(8,128)(2,1)S(1)} %copy-done.4, bf16[368,512]{1,0:T(8,128)(2,1)S(1)} %collective-permute-done.3.theirs), custom_call_target="tpu_custom_call" | custom-call | flops 1 | bytes 1 | tf_op jit(solution)/shard_map/pallas_call | solution.py:24
  38.2 29.8 %collective-permute-done.4.theirs = bf16[3,128,512]{2,1,0:T(8,128)(2,1)S(1)} collective-permute-done((bf16[3,128,512]{2,1,0:T(8,128)(2,1)S(1)}, bf16[3,128,512]{2,1,0:T(8,128)(2,1)S(1)}, u32[]{:S(2)}, u32[]{:S(2)}) %collective-permute-start.4) | collective-permute-done | bytes 393248 | tf_op jit(solution)/shard_map/ppermute | solution.py:584
  68.0 1.0 %shard_map.87.refs_1_ = f32[2,3,128,512]{3,2,1,0:T(8,128)S(1)} custom-call(bf16[3,512,1024]{2,1,0:T(8,128)(2,1)S(1)} %get-tuple-element.43.weights.refs_0_.refs_1_, f32[2,3,32,128]{3,2,1,0:T(8,128)S(1)} %get-tuple-element.44.keep.refs_1_.refs_2_, bf16[3,128,512]{2,1,0:T(8,128)(2,1)S(1)} %get-tuple-element.41.mine, ...), custom_call_target="tpu_custom_call" | custom-call | flops 1 | bytes 1 | tf_op jit(solution)/shard_map/pallas_call | solution.py:24
  69.1 1.6 %shard_map.88 = (f32[2,3,128,512]{3,2,1,0:T(8,128)S(1)}, f32[2,3,16,512]{3,2,1,0:T(8,128)S(1)}, f32[2,3,256,512]{3,2,1,0:T(8,128)S(1)}, bf16[2,3,32,512]{3,2,1,0...) custom-call(bf16[3,512,1024]{2,1,0:T(8,128)(2,1)S(1)} %get-tuple-element.43.weights.refs_0_.ref, ...), custom_call_target="tpu_custom_call" | custom-call | flops 1 | bytes 1 | tf_op jit(solution)/shard_map/pallas_call | solution.py:24
  70.6 1.3 %collective-permute-start.9 = (bf16[2,3,32,512]{3,2,1,0:T(8,128)(2,1)S(1)}, bf16[2,3,32,512]{3,2,1,0:T(8,128)(2,1)S(1)}, u32[]{:S(2)}, u32[]{:S(2)}) collective-permute-start(bf16[2,3,32,512]{3,2,1,0:T(8,128)(2,1)S(1)} %get-tuple-element.56), channel_id=1, source_target_pairs={{0,1},{1,0},{2,3},{3,2},{4,5},{5,4},{6,7},{7,6},{8,9},{9,8},{10,11... | collective-permute-start | bytes 589832 | tf_op jit(solution)/shard_map/ppermute | solution.py:504
  71.9 2.6 %collective-permute-start.8 = (bf16[2,3,16,512]{3,2,1,0:T(8,128)(2,1)S(1)}, bf16[2,3,16,512]{3,2,1,0:T(8,128)(2,1)S(1)}, u32[]{:S(2)}, u32[]{:S(2)}) collective-permute-start(bf16[2,3,16,512]{3,2,1,0:T(8,128)(2,1)S(1)} %get-tuple-element.55), channel_id=1, source_target_pairs={{0,14},{2,0},{4,2},{6,4},{8,6},{10,8},{12,10},{14,12},{16,30},{18,... | collective-permute-start | bytes 294920 | tf_op jit(solution)/shard_map/ppermute | solution.py:644
  74.6 2.9 %collective-permute-start.10 = (bf16[3,32,512]{2,1,0:T(8,128)(2,1)S(1)}, bf16[3,32,512]{2,1,0:T(8,128)(2,1)S(1)}, u32[]{:S(2)}, u32[]{:S(2)}) collective-permute-start(bf16[3,32,512]{2,1,0:T(8,128)(2,1)S(1)} %get-tuple-element.60.mine), channel_id=1, source_target_pairs={{0,16},{2,18},{4,20},{6,22},{8,24},{10,26},{12,28},{14,30},{16,0},... | collective-permute-start | bytes 294920 | tf_op jit(solution)/shard_map/ppermute | solution.py:622
  77.5 2.7 %collective-permute-done.7.refs_4_.refs_5_ = bf16[2,3,16,512]{3,2,1,0:T(8,128)(2,1)S(1)} collective-permute-done((bf16[2,3,16,512]{3,2,1,0:T(8,128)(2,1)S(1)}, bf16[2,3,16,512]{3,2,1,0:T(8,128)(2,1)S(1)}, u32[]{:S(2)}, u32[]{:S(2)}) %collective-permute-start.7) | collective-permute-done | bytes 98336 | tf_op jit(solution)/shard_map/ppermute | solution.py:643
  80.3 4.1 %shard_map.89.refs_0_ = f32[3,32,16,512]{3,2,1,0:T(8,128)} custom-call(bf16[3,512,1024]{2,1,0:T(8,128)(2,1)S(1)} %get-tuple-element.43.weights.refs_0_.refs_1_, f32[2,3,32,128]{3,2,1,0:T(8,128)S(1)} %get-tuple-element.44.keep.refs_1_.refs_2_, f32[2,3,128,512]{3,2,1,0:T(8,128)S(1)} %get-tuple-element.52.refs_2_.refs_0_, ...), custom_call_target="tpu_custom_call" | custom-call | flops 1 | bytes 1 | tf_op jit(solution)/shard_map/pallas_call | solution.py:24
  84.4 1.2 %shard_map.90.refs_3_.state = f32[2,3,144,512]{3,2,1,0:T(8,128)S(1)} custom-call(bf16[3,512,1024]{2,1,0:T(8,128)(2,1)S(1)} %get-tuple-element.43.weights.refs_0_.refs_1_, f32[2,3,32,128]{3,2,1,0:T(8,128)S(1)} %get-tuple-element.44.keep.refs_1_.refs_2_, bf16[3,80,512]{2,1,0:T(8,128)(2,1)S(1)} %get-tuple-element.46.mine, ...), custom_call_target="tpu_custom_call" | custom-call | flops 1 | bytes 1 | tf_op jit(solution)/shard_map/pallas_call | solution.py:24
  85.6 4.2 %shard_map.91.given = f32[3,32,16,512]{3,2,1,0:T(8,128)} custom-call(f32[3,32,16,512]{3,2,1,0:T(8,128)} %shard_map.89.refs_0_, bf16[3,512,1024]{2,1,0:T(8,128)(2,1)S(1)} %get-tuple-element.43.weights.refs_0_.refs_1_, f32[2,3,32,128]{3,2,1,0:T(8,128)S(1)} %get-tuple-element.44.keep.refs_1_.refs_2_, ...), custom_call_target="tpu_custom_call", output_to_operand_aliasing={{}: (0, {})} | custom-call | flops 1 | bytes 1 | tf_op jit(solution)/shard_map/pallas_call | solution.py:24
  89.8 3.8 %shard_map.92 = f32[3,32,16,512]{3,2,1,0:T(8,128)} custom-call(f32[3,32,16,512]{3,2,1,0:T(8,128)} %shard_map.91.given, f32[2,3,144,512]{3,2,1,0:T(8,128)S(1)} %shard_map.90.refs_3_.state, bf16[3,512,1024]{2,1,0:T(8,128)(2,1)S(1)} %get-tuple-element.43.weights.refs_0_.refs_1_, ...), custom_call_target="tpu_custom_call", output_to_operand_aliasing={{}: (0, {})} | custom-call | flops 1 | bytes 1 | tf_op jit(solution)/shard_map/pallas_call | solution.py:24
  (19 shorter events, 0.0 us)
Async XLA Ops:
  0.0 19.8 %copy-start = (f32[3,32,16,512]{3,2,1,0:T(8,128)S(1)}, f32[3,32,16,512]{3,2,1,0:T(8,128)}, u32[]{:S(2)}) copy-start(f32[3,32,16,512]{3,2,1,0:T(8,128)} %param.8) | copy-start | bytes 9437188
  3.6 21.2 %collective-permute-start.3 = (bf16[368,512]{1,0:T(8,128)(2,1)}, bf16[368,512]{1,0:T(8,128)(2,1)S(1)}, u32[]{:S(2)}, u32[]{:S(2)}) collective-permute-start(bf16[368,512]{1,0:T(8,128)(2,1)} %get-tuple-element.40.mine), channel_id=1, source_target_pairs={{0,16},{2,18},{4,20},{6,22},{8,24},{10,26},{12,28},{14,30},{16,0},... | collective-permute-start | bytes 1130504 | tf_op jit(solution)/shard_map/ppermute | solution.py:557
  7.7 12.1 %collective-permute-start.2 = (f32[3,32,512]{2,1,0:T(8,128)}, f32[3,32,512]{2,1,0:T(8,128)S(1)}, u32[]{:S(2)}, u32[]{:S(2)}) collective-permute-start(f32[3,32,512]{2,1,0:T(8,128)} %get-tuple-element.37), channel_id=1, source_target_pairs={{0,1},{1,0},{2,3},{3,2},{4,5},{5,4},{6,7},{7,6},{8,9},{9,8},{10,11... | collective-permute-start | bytes 589832 | tf_op jit(solution)/shard_map/ppermute | solution.py:504
  9.1 10.6 %collective-permute-start = (f32[3,16,512]{2,1,0:T(8,128)}, f32[3,16,512]{2,1,0:T(8,128)S(1)}, u32[]{:S(2)}, u32[]{:S(2)}) collective-permute-start(f32[3,16,512]{2,1,0:T(8,128)} %get-tuple-element.35), channel_id=1, source_target_pairs={{0,2},{2,4},{4,6},{6,8},{8,10},{10,12},{12,14},{14,16},{16,18},{18... | collective-permute-start | bytes 294920 | tf_op jit(solution)/shard_map/ppermute | solution.py:559
  9.2 10.6 %collective-permute-start.1 = (f32[3,16,512]{2,1,0:T(8,128)}, f32[3,16,512]{2,1,0:T(8,128)S(1)}, u32[]{:S(2)}, u32[]{:S(2)}) collective-permute-start(f32[3,16,512]{2,1,0:T(8,128)} %get-tuple-element.36), channel_id=1, source_target_pairs={{0,30},{2,0},{4,2},{6,4},{8,6},{10,8},{12,10},{14,12},{16,14},{18,... | collective-permute-start | bytes 294920 | tf_op jit(solution)/shard_map/ppermute | solution.py:560
  19.8 0.9 %copy-start.2 = (f32[15,8,512]{2,1,0:T(8,128)S(1)}, f32[15,8,512]{2,1,0:T(8,128)}, u32[]{:S(2)}) copy-start(f32[15,8,512]{2,1,0:T(8,128)} %get-tuple-element.33.coef.coef_in.refs_8_.refs_9_) | copy-start | bytes 737284
  20.7 13.9 %copy-start.1 = (bf16[3,1024,1024]{2,1,0:T(8,128)(2,1)S(1)}, bf16[3,1024,1024]{2,1,0:T(8,128)(2,1)}, u32[]{:S(2)}) copy-start(bf16[3,1024,1024]{2,1,0:T(8,128)(2,1)} %matrix.1) | copy-start | bytes 18874372
  20.7 13.9 %copy-start.4 = (bf16[368,512]{1,0:T(8,128)(2,1)S(1)}, bf16[368,512]{1,0:T(8,128)(2,1)}, u32[]{:S(2)}) copy-start(bf16[368,512]{1,0:T(8,128)(2,1)} %get-tuple-element.40.mine) | copy-start | bytes 1130500
  24.7 44.3 %collective-permute-start.6 = (bf16[3,160,512]{2,1,0:T(8,128)(2,1)S(1)}, bf16[3,160,512]{2,1,0:T(8,128)(2,1)S(1)}, u32[]{:S(2)}, u32[]{:S(2)}) collective-permute-start(bf16[3,160,512]{2,1,0:T(8,128)(2,1)S(1)} %get-tuple-element.47.mine), channel_id=1, source_target_pairs={{0,16},{2,18},{4,20},{6,22},{8,24},{10,26},{12,28},{14,30},{16,0},... | collective-permute-start | bytes 1474568 | tf_op jit(solution)/shard_map/ppermute | solution.py:585
  33.4 34.6 %collective-permute-start.4 = (bf16[3,128,512]{2,1,0:T(8,128)(2,1)S(1)}, bf16[3,128,512]{2,1,0:T(8,128)(2,1)S(1)}, u32[]{:S(2)}, u32[]{:S(2)}) collective-permute-start(bf16[3,128,512]{2,1,0:T(8,128)(2,1)S(1)} %get-tuple-element.41.mine), channel_id=1, source_target_pairs={{0,16},{2,18},{4,20},{6,22},{8,24},{10,26},{12,28},{14,30},{16,0},... | collective-permute-start | bytes 1179656 | tf_op jit(solution)/shard_map/ppermute | solution.py:584
  68.0 16.4 %collective-permute-start.5 = (bf16[3,80,512]{2,1,0:T(8,128)(2,1)S(1)}, bf16[3,80,512]{2,1,0:T(8,128)(2,1)S(1)}, u32[]{:S(2)}, u32[]{:S(2)}) collective-permute-start(bf16[3,80,512]{2,1,0:T(8,128)(2,1)S(1)} %get-tuple-element.46.mine), channel_id=1, source_target_pairs={{0,16},{2,18},{4,20},{6,22},{8,24},{10,26},{12,28},{14,30},{16,0},... | collective-permute-start | bytes 737288 | tf_op jit(solution)/shard_map/ppermute | solution.py:611
  69.1 11.2 %copy-start.3 = (f32[15,8,512]{2,1,0:T(8,128)S(1)}, f32[15,8,512]{2,1,0:T(8,128)}, u32[]{:S(2)}) copy-start(f32[15,8,512]{2,1,0:T(8,128)} %get-tuple-element.33.coef.coef_in.refs_8_.refs_9_) | copy-start | bytes 737284
  70.6 9.6 %collective-permute-start.9 = (bf16[2,3,32,512]{3,2,1,0:T(8,128)(2,1)S(1)}, bf16[2,3,32,512]{3,2,1,0:T(8,128)(2,1)S(1)}, u32[]{:S(2)}, u32[]{:S(2)}) collective-permute-start(bf16[2,3,32,512]{3,2,1,0:T(8,128)(2,1)S(1)} %get-tuple-element.56), channel_id=1, source_target_pairs={{0,1},{1,0},{2,3},{3,2},{4,5},{5,4},{6,7},{7,6},{8,9},{9,8},{10,11... | collective-permute-start | bytes 589832 | tf_op jit(solution)/shard_map/ppermute | solution.py:504
  71.9 8.3 %collective-permute-start.7 = (bf16[2,3,16,512]{3,2,1,0:T(8,128)(2,1)S(1)}, bf16[2,3,16,512]{3,2,1,0:T(8,128)(2,1)S(1)}, u32[]{:S(2)}, u32[]{:S(2)}) collective-permute-start(bf16[2,3,16,512]{3,2,1,0:T(8,128)(2,1)S(1)} %get-tuple-element.54), channel_id=1, source_target_pairs={{0,2},{2,4},{4,6},{6,8},{8,10},{10,12},{12,14},{14,0},{16,18},{18,... | collective-permute-start | bytes 294920 | tf_op jit(solution)/shard_map/ppermute | solution.py:643
  71.9 8.3 %collective-permute-start.8 = (bf16[2,3,16,512]{3,2,1,0:T(8,128)(2,1)S(1)}, bf16[2,3,16,512]{3,2,1,0:T(8,128)(2,1)S(1)}, u32[]{:S(2)}, u32[]{:S(2)}) collective-permute-start(bf16[2,3,16,512]{3,2,1,0:T(8,128)(2,1)S(1)} %get-tuple-element.55), channel_id=1, source_target_pairs={{0,14},{2,0},{4,2},{6,4},{8,6},{10,8},{12,10},{14,12},{16,30},{18,... | collective-permute-start | bytes 294920 | tf_op jit(solution)/shard_map/ppermute | solution.py:644
  74.6 15.2 %collective-permute-start.10 = (bf16[3,32,512]{2,1,0:T(8,128)(2,1)S(1)}, bf16[3,32,512]{2,1,0:T(8,128)(2,1)S(1)}, u32[]{:S(2)}, u32[]{:S(2)}) collective-permute-start(bf16[3,32,512]{2,1,0:T(8,128)(2,1)S(1)} %get-tuple-element.60.mine), channel_id=1, source_target_pairs={{0,16},{2,18},{4,20},{6,22},{8,24},{10,26},{12,28},{14,30},{16,0},... | collective-permute-start | bytes 294920 | tf_op jit(solution)/shard_map/ppermute | solution.py:622

commit v4 on v3

--- a/solution.py
+++ b/solution.py
@@ -209,16 +209,12 @@
     return jnp.where(place == 1, 1.0, 0.0), jnp.where(place == 0, 1.0, 0.0)
 
 
-def frame_kernel(
-    sizes, conc, before, after, low, high, coef_in, out1, out2, field, coef, sems
-):
+def frame_kernel(sizes, conc, low, high, coef_in, out1, out2, field, coef, sems):
     na, nz, ends, planes = sizes
     half = nz // 2
     copies = [
-        pltpu.make_async_copy(conc, field.at[:, pl.ds(nz, na * nz)], sems.at[0]),
-        pltpu.make_async_copy(before, field.at[:, pl.ds(0, nz)], sems.at[1]),
-        pltpu.make_async_copy(after, field.at[:, pl.ds((na + 1) * nz, nz)], sems.at[2]),
-        pltpu.make_async_copy(coef_in, coef, sems.at[3]),
+        pltpu.make_async_copy(conc, field, sems.at[0]),
+        pltpu.make_async_copy(coef_in, coef, sems.at[1]),
     ]
     for copy in copies:
         copy.start()
@@ -226,37 +222,65 @@
     for copy in copies:
         copy.wait()
 
-    def angle(t):
-        return first_step(
-            field_reader(field, t + 1, nz),
-            lambda s: low[s, pl.ds(t, 1), :] * low_weight,
-            lambda s: high[s, pl.ds(t, 1), :] * high_weight,
-            coef,
-            half,
+    def part(begin, out):
+        def pair(step, carry):
+            tiles = []
+            for k in range(2):
+                t = begin + step * 2 + k
+                tiles.append(
+                    first_step(
+                        field_reader(field, t, nz),
+                        lambda s: low[s, pl.ds(t, 1), :] * low_weight,
+                        lambda s: high[s, pl.ds(t, 1), :] * high_weight,
+                        coef,
+                        half,
+                    )[1]
+                )
+            for s in range(3):
+                out[s, at_rows(step * nz, nz, nz), :] = pack([tiles[0][s], tiles[1][s]])
+            return carry
+
+        lax.fori_loop(0, out.shape[1] // nz, pair, 0)
+
+    part(ends, out1)
+    part(ends + out1.shape[1] // half, out2)
+
+
+def ends_kernel(sizes, conc, before, after, low, high, coef, out, field, sems):
+    na, nz, planes = sizes
+    half = nz // 2
+    copies = [
+        pltpu.make_async_copy(src, field.at[:, pl.ds(at * nz, count * nz)], sems.at[k])
+        for k, (src, at, count) in enumerate(
+            (
+                (before, 0, 1),
+                (conc.at[:, pl.ds(0, 3 * nz)], 1, 3),
+                (conc.at[:, pl.ds((na - 3) * nz, 3 * nz)], 4, 3),
+                (after, 7, 1),
+            )
         )
-
-    def pair(t, out, row, ends_row):
-        tiles = [angle(t), angle(t + 1)]
+    ]
+    for copy in copies:
+        copy.start()
+    low_weight, high_weight = edge_weights(planes)
+    for copy in copies:
+        copy.wait()
+    for k, (slot, first) in enumerate(((1, 0), (5, na - 2))):
+        tiles = []
+        for j in range(2):
+            t = first + j
+            tiles.append(
+                first_step(
+                    field_reader(field, slot + j, nz),
+                    lambda s: low[s, t : t + 1, :] * low_weight,
+                    lambda s: high[s, t : t + 1, :] * high_weight,
+                    coef,
+                    half,
+                )
+            )
         for s in range(3):
-            out[s, pl.ds(row, nz), :] = pack([tiles[0][1][s], tiles[1][1][s]])
-            if ends_row is not None:
-                out2[s, pl.ds(ends_row, nz), :] = pack([tiles[0][0][s], tiles[1][0][s]])
-
-    quarter = na // 4
-    tail = na // 2 * half
-    pair(0, out1, 0, tail)
-    pair(na - 2, out2, (na // 2 - 2) * half, tail + nz)
-
-    def first_part(step, carry):
-        pair(step * 2, out1, pl.multiple_of(step * nz, nz), None)
-        return carry
-
-    def second_part(step, carry):
-        pair(na // 2 + step * 2, out2, pl.multiple_of(step * nz, nz), None)
-        return carry
-
-    lax.fori_loop(1, quarter, first_part, 0)
-    lax.fori_loop(0, quarter - 1, second_part, 0)
+            out[s, pl.ds(k * nz, nz), :] = pack([tiles[0][1][s], tiles[1][1][s]])
+            out[s, pl.ds((k + 2) * nz, nz), :] = pack([tiles[0][0][s], tiles[1][0][s]])
 
 
 def weights_kernel(matrix, mine, theirs, out, keep, left, lower, sems):
@@ -316,15 +340,22 @@
     return ref[pl.ds(s * rows, rows), :]
 
 
-def radial_kernel(runs, copies, half, weights, keep, mine, theirs, *refs):
+def radial_kernel(plan, copies, half, weights, keep, *refs):
+    n = len(plan)
+    mines, theirs, refs = refs[:n], refs[n : 2 * n], refs[2 * n :]
     n_in = 1 + max((part for part, *_ in copies), default=-1)
     parts, states = refs[:n_in], refs[n_in:]
     for s in range(3):
-        value = both_sides(species_rows(mine, s, runs, half), species_rows(theirs, s, runs, half), weights[s])
-        at = 0
-        for which, begin, place, count in runs:
-            store_run(states[which], s, begin, place, count, at, value, keep, half)
-            at += count
+        for k, runs in enumerate(plan):
+            value = both_sides(
+                species_rows(mines[k], s, runs, half),
+                species_rows(theirs[k], s, runs, half),
+                weights[s],
+            )
+            at = 0
+            for which, begin, place, count in runs:
+                store_run(states[which], s, begin, place, count, at, value, keep, half)
+                at += count
     for part, source, which, place, count in copies:
         to, rows = pl.ds(place * half, count * half), pl.ds(source * half, count * half)
         for ab in range(2):
@@ -355,12 +386,12 @@
             last[ab, s] = pack([mid_end[ab, s, ends_end, :], outer[ab, s, end, :]])
 
 
-def radial_edges_kernel(sizes, runs, copies, half, weights, keep, mine, theirs, *refs):
+def radial_edges_kernel(sizes, plan, copies, half, weights, keep, *refs):
     na, nz, planes = sizes
     n_edges = 1 if planes == 2 else 2
     *edges, first, last, stage = refs[-3 - n_edges :]
     refs = refs[: -3 - n_edges]
-    radial_kernel(runs, copies, half, weights, keep, mine, theirs, *refs)
+    radial_kernel(plan, copies, half, weights, keep, *refs)
     edges_of_state(na, nz, planes, refs[-3], refs[-2], refs[-1], edges, first, last, stage)
 
 
@@ -524,7 +555,8 @@
     quarter = na // 4
     ends = 2
     side = na // 2
-    first_lo, first_hi = ends, side
+    cut = 7 * na // 16
+    first_lo, first_cut, first_hi = ends, ends + na // 4, side
     last_lo, last_hi = na - 3 * ends, na - ends
     opposite = [(i, (i + count // 2) % count) for i in range(count)]
 
@@ -537,11 +569,11 @@
     conc = concentration.reshape(ns, na * nz, nr)
     field = pltpu.VMEM((ns, na * nz, nr), F32)
     *edges, first, last, mid_a, coef = call(
-        functools.partial(head_kernel, (na, nz, first_lo, first_hi, planes)),
+        functools.partial(head_kernel, (na, nz, first_lo, first_cut, planes)),
         [shape(ns, na, nr)] * n_edges
         + [shape(ns, nz, nr)] * 2
         + [
-            shape(ns * (first_hi - first_lo) * half + na, nr, dtype=BF16),
+            shape(ns * (first_cut - first_lo) * half + na, nr, dtype=BF16),
             shape(RATE + 3, half, nr),
         ],
         [HBM] * 7,
@@ -558,31 +590,48 @@
     low, high = plane_halos(edges, planes)
     angle_before = lax.ppermute(last, "ang", [(i, (i + 1) % count) for i in range(count)])
     angle_after = lax.ppermute(first, "ang", [(i, (i - 1) % count) for i in range(count)])
-    mid_x, mid_l = call(
+    mid_b, mid_x, mid_l = call(
         functools.partial(
             inner_kernel,
             (na, nz),
-            ((0, ((first_hi, last_lo - first_hi),)), (1, ((last_lo, last_hi - last_lo),))),
+            (
+                (0, ((first_cut, first_hi - first_cut),)),
+                (1, ((first_hi, last_lo - first_hi),)),
+                (2, ((last_lo, last_hi - last_lo),)),
+            ),
         ),
-        [message(last_lo - first_hi), message(last_hi - last_lo)],
+        [message(first_hi - first_cut), message(last_lo - first_hi), message(last_hi - last_lo)],
         [ANY, VM],
-        [VM] * 2,
+        [VM] * 3,
         [field, pltpu.SemaphoreType.DMA],
         (conc, coef),
         8,
     )
+    opp_b = lax.ppermute(mid_b, "ang", opposite)
     out1, out2 = call(
         functools.partial(frame_kernel, (na, nz, ends, planes)),
-        [message(na // 2), message(na // 2 + 2 * ends)],
-        [ANY] * 3 + [VM] * 2 + [ANY],
+        [message(cut - ends), message(na - ends - cut)],
+        [ANY] + [VM] * 2 + [ANY],
         [VM] * 2,
-        [pltpu.VMEM((ns, (na + 2) * nz, nr), F32), pltpu.VMEM((RATE + 3, half, nr), F32), dma(4)],
+        [field, pltpu.VMEM((RATE + 3, half, nr), F32), dma(2)],
+        (conc, low, high, coef),
+        8,
+    )
+    out2, opp_a = after(out2, opp_a)
+    opp_2 = lax.ppermute(out2, "ang", opposite)
+    out1, (opp_b, angle_before, angle_after) = after(out1, (opp_b, angle_before, angle_after))
+    opp_1 = lax.ppermute(out1, "ang", opposite)
+    out_e = call(
+        functools.partial(ends_kernel, (na, nz, planes)),
+        message(4 * ends),
+        [ANY] * 3 + [VM] * 3,
+        VM,
+        [pltpu.VMEM((ns, 8 * nz, nr), F32), dma(4)],
         (conc, angle_before, angle_after, low, high, coef),
         8,
     )
-    (out1, out2), opp_a = after((out1, out2), opp_a)
-    opp_1 = lax.ppermute(out1, "ang", opposite)
-    opp_2 = lax.ppermute(out2, "ang", opposite)
+    opp_e = lax.ppermute(out_e, "ang", opposite)
+
     weights, keep = call(
         weights_kernel,
         [shape(ns, nr, 2 * nr, dtype=BF16), shape(2, ns, na, LANES)],
@@ -596,37 +645,48 @@
     def state(angles):
         return shape(2, ns, angles * half, nr)
 
-    count_a = first_hi - first_lo
+    count_a, count_b = first_cut - first_lo, first_hi - first_cut
     (mid_first,) = call(
-        functools.partial(radial_kernel, ((0, first_lo, 0, count_a),), (), half),
-        [state(count_a)],
-        [VM] * 4,
+        functools.partial(
+            radial_kernel,
+            (((0, first_lo, 0, count_a),), ((0, first_cut, count_a, count_b),)),
+            (),
+            half,
+        ),
+        [state(count_a + count_b)],
+        [VM] * 6,
         [VM],
         [],
-        (weights, keep, mid_a, opp_a),
+        (weights, keep, mid_a, mid_b, opp_a, opp_b),
         8,
     )
     opp_1, mid_first = after(opp_1, mid_first)
     mid_x, opp_1 = after(mid_x, opp_1)
     opp_x = lax.ppermute(mid_x, "ang", opposite)
+    span = na - 2 * ends
     (outer_first,) = call(
-        functools.partial(radial_kernel, ((0, 0, 0, side),), (), half),
-        [state(side)],
-        [VM] * 4,
+        functools.partial(radial_kernel, (((0, ends, 0, cut - ends),), ((0, cut, cut - ends, na - ends - cut),)), (), half),
+        [state(span)],
+        [VM] * 6,
         [VM],
         [],
-        (weights, keep, out1, opp_1),
+        (weights, keep, out1, out2, opp_1, opp_2),
         8,
     )
-    mid_l, opp_2 = after(mid_l, opp_2)
+    mid_l, opp_e = after(mid_l, opp_e)
     opp_l = lax.ppermute(mid_l, "ang", opposite)
-    runs = ((2, side, side, side), (0, 0, 0, ends), (1, na - ends, 0, ends))
+    plan = (
+        (
+            (2, 0, 0, ends), (2, na - ends, na - ends, ends),
+            (0, 0, 0, ends), (1, na - ends, 0, ends),
+        ),
+    )
     mid_left, ends_right, outer_state, *rest = call(
         functools.partial(
             radial_edges_kernel,
             (na, nz, planes),
-            runs,
-            ((0, 0, 0, first_lo, count_a), (1, 0, 2, 0, side)),
+            plan,
+            ((0, 0, 0, first_lo, count_a + count_b), (1, 0, 2, ends, span)),
             half,
         ),
         [state(side), state(ends), state(na)]
@@ -635,7 +695,7 @@
         [VM] * 6,
         [VM] * (5 + n_edges),
         [pltpu.VMEM((n_edges, na, nr), F32)],
-        (weights, keep, out2, opp_2, mid_first, outer_first),
+        (weights, keep, out_e, opp_e, mid_first, outer_first),
         8,
     )
     *edges, first, last = rest
@@ -662,7 +722,7 @@
     (mid_right,) = call(
         functools.partial(
             radial_kernel,
-            ((0, first_hi, 2, last_lo - first_hi),),
+            (((0, first_hi, 2, last_lo - first_hi),),),
             ((0, base, 0, 0, 2), (1, 0, 0, na - ends - base, ends)),
             half,
         ),

time: 93.9 us -> 96 us (1.022)
  starting transfers between devices: 25.7 us -> 37.8 us
  waiting for transfers between devices: 39.8 us -> 27.9 us
  Pallas kernels: 27.1 us -> 28.9 us
    ppermute x1, starting transfers between devices: 0.08 us -> 24.2 us  [per_device(): opp_1 = lax.ppermute(out1, 'ang', opposite)]
    ppermute x1, waiting for transfers between devices: 29.8 us -> 11 us  [per_device(): opp_1 = lax.ppermute(out1, 'ang', opposite)]
    ppermute x0 -> x2, waiting for transfers between devices: none -> 10 us  [the longest x1 7.37 us: per_device(): opp_e = lax.ppermute(out_e, 'ang', opposite)]
    ppermute x1, starting transfers between devices: 8.68 us -> 0.01 us  [per_device(): opp_2 = lax.ppermute(out2, 'ang', opposite)]
    ppermute x1, waiting for transfers between devices: 6.16 us -> 0.01 us  [per_device(): lax.ppermute(last, 'ang', [(i, (i + 1) % count) for i in range(count)])]
    ppermute x1, starting transfers between devices: 2.64 us -> 0.01 us  [per_device(): angle_after = lax.ppermute(first, 'ang', ring(count, -1))]
    ppermute x1, waiting for transfers between devices: 1 us -> 3.44 us  [per_device(): opp_a = lax.ppermute(mid_a, 'ang', opposite)]
    ppermute x1, starting transfers between devices: 2.92 us -> 1.07 us  [per_device(): opp_l = lax.ppermute(mid_l, 'ang', opposite)]
  transfers between devices with their start and end apart: 11 -> 13, of which waited for: 4 -> 6; matrix products, arithmetic and copies ran while one was open for 0% -> 0% of each run, Pallas kernels for 21% -> 23%
where the time goes in v4:
time: 96 us; the launch traced here: 95.8 us
  starting transfers between devices  37.8 us (39%)
  Pallas kernels  28.9 us (30%)
  waiting for transfers between devices  27.9 us (29%)
  local copies, waits for them, and re-layouts  0.97 us (1%)
    pallas_call x12, Pallas kernels, call(): pl.pallas_call(body, out_shape=out_shape, in_specs=in_specs, out_specs=ou...  28.9 us
    ppermute x1, starting transfers between devices, per_device(): opp_1 = lax.ppermute(out1, 'ang', opposite)  24.2 us
    ppermute x1, waiting for transfers between devices, per_device(): opp_1 = lax.ppermute(out1, 'ang', opposite)  11 us
    ppermute x1, waiting for transfers between devices, per_device(): opp_e = lax.ppermute(out_e, 'ang', opposite)  7.37 us
    ppermute x1, starting transfers between devices, per_device(): lax.ppermute(first, 'ang', [(i, (i - 1) % count) for i in range(count)])  4.44 us
    ppermute x1, starting transfers between devices, per_device(): opp_a = lax.ppermute(mid_a, 'ang', opposite)  4.1 us
    ppermute x1, waiting for transfers between devices, per_device(): opp_a = lax.ppermute(mid_a, 'ang', opposite)  3.44 us
    ppermute x2, starting transfers between devices, plane_halos(): got = lax.ppermute(edges[0], 'ax', [(0, 1), (1, 0)])  3.05 us
  transfers between devices with their start and end apart: 13, of which 6 were waited for; matrix products, arithmetic and copies ran while one was open for 0% of the time, Pallas kernels for 23%

profile of v4, /device:TPU:0, one launch (start us, length us, event | category | flops | bytes accessed | tf_op | source)
XLA Modules:
  0.0 95.8 jit_solution(2796725658387481772)
XLA Ops:
  0.0 3.1 %shard_map.82 = (f32[3,32,512]{2,1,0:T(8,128)}, f32[3,16,512]{2,1,0:T(8,128)}, f32[3,16,512]{2,1,0:T(8,128)}, bf16[224,512]{1,0:T(8,128)(2,1)}, f32[15,8,512]{2,1,0:T(8,128)}) custom-call(f32[3,512,512]{2,1,0:T(8,128)} %bitcast.2, f32[1,512]{1,0:T(1,128)} %bitcast.8, f32[3]{0:T(128)} %diff.1, f32[3,512]{1,0:T(4,128)} %ang.1, f32[4]{0:T(128)} %rate.1, ...), custom_call_target="tpu_custom_call" | custom-call | flops 1 | bytes 1 | tf_op jit(solution)/shard_map/pallas_call | solution.py:24
  3.1 4.1 %collective-permute-start.5 = (bf16[224,512]{1,0:T(8,128)(2,1)}, bf16[224,512]{1,0:T(8,128)(2,1)S(1)}, u32[]{:S(2)}, u32[]{:S(2)}) collective-permute-start(bf16[224,512]{1,0:T(8,128)(2,1)} %get-tuple-element.45.mine.refs_0_), channel_id=1, source_target_pairs={{0,16},{2,18},{4,20},{6,22},{8,24},{10,26},{12,28},{14,30},{16,0},... | collective-permute-start | bytes 688136 | tf_op jit(solution)/shard_map/ppermute | solution.py:589
  7.2 1.5 %collective-permute-start = (f32[3,32,512]{2,1,0:T(8,128)}, f32[3,32,512]{2,1,0:T(8,128)S(1)}, u32[]{:S(2)}, u32[]{:S(2)}) collective-permute-start(f32[3,32,512]{2,1,0:T(8,128)} %get-tuple-element.39), channel_id=1, source_target_pairs={{0,1},{1,0},{2,3},{3,2},{4,5},{5,4},{6,7},{7,6},{8,9},{9,8},{10,11... | collective-permute-start | bytes 589832 | tf_op jit(solution)/shard_map/ppermute | solution.py:535
  8.7 0.9 copy-done.1
  9.6 1.6 %shard_map.83 = (bf16[3,48,512]{2,1,0:T(8,128)(2,1)S(1)}, bf16[3,80,512]{2,1,0:T(8,128)(2,1)S(1)}, bf16[3,32,512]{2,1,0:T(8,128)(2,1)S(1)}) custom-call(f32[3,512,512]{2,1,0:T(8,128)S(1)} %bitcast.3, f32[15,8,512]{2,1,0:T(8,128)S(1)} %copy-done.1), custom_call_target="tpu_custom_call" | custom-call | flops 1 | bytes 1 | tf_op jit(solution)/shard_map/pallas_call | solution.py:24
  11.6 4.4 %collective-permute-start.3 = (f32[3,16,512]{2,1,0:T(8,128)}, f32[3,16,512]{2,1,0:T(8,128)S(1)}, u32[]{:S(2)}, u32[]{:S(2)}) collective-permute-start(f32[3,16,512]{2,1,0:T(8,128)} %get-tuple-element.43), channel_id=1, source_target_pairs={{0,30},{2,0},{4,2},{6,4},{8,6},{10,8},{12,10},{14,12},{16,14},{18,... | collective-permute-start | bytes 294920 | tf_op jit(solution)/shard_map/ppermute | solution.py:592
  16.0 2.5 %shard_map.84 = (bf16[3,96,512]{2,1,0:T(8,128)(2,1)S(1)}, bf16[3,128,512]{2,1,0:T(8,128)(2,1)S(1)}) custom-call(f32[3,512,512]{2,1,0:T(8,128)S(1)} %bitcast.4, f32[3,32,512]{2,1,0:T(8,128)S(1)} %collective-permute-done.low.high, f32[3,32,512]{2,1,0:T(8,128)S(1)} %collective-permute-done.low.high, f32[15,8,512]{2,1,0:T(8,128)S(1)} %copy-done.1), custom_call_target="tpu_custom_call" | custom-call | flops 1 | bytes 1 | tf_op jit(solution)/shard_map/pallas_call | solution.py:24
  18.6 3.4 %collective-permute-done.5.theirs.refs_2_ = bf16[224,512]{1,0:T(8,128)(2,1)S(1)} collective-permute-done((bf16[224,512]{1,0:T(8,128)(2,1)}, bf16[224,512]{1,0:T(8,128)(2,1)S(1)}, u32[]{:S(2)}, u32[]{:S(2)}) %collective-permute-start.5) | collective-permute-done | bytes 229408 | tf_op jit(solution)/shard_map/ppermute | solution.py:589
  22.0 2.6 %collective-permute-done.1.refs_3_ = bf16[3,48,512]{2,1,0:T(8,128)(2,1)S(1)} collective-permute-done((bf16[3,48,512]{2,1,0:T(8,128)(2,1)S(1)}, bf16[3,48,512]{2,1,0:T(8,128)(2,1)S(1)}, u32[]{:S(2)}, u32[]{:S(2)}) %collective-permute-start.1) | collective-permute-done | bytes 147488 | tf_op jit(solution)/shard_map/ppermute | solution.py:610
  24.6 24.2 %collective-permute-start.4 = (bf16[3,96,512]{2,1,0:T(8,128)(2,1)S(1)}, bf16[3,96,512]{2,1,0:T(8,128)(2,1)S(1)}, u32[]{:S(2)}, u32[]{:S(2)}) collective-permute-start(bf16[3,96,512]{2,1,0:T(8,128)(2,1)S(1)} %get-tuple-element.44.refs_0_), channel_id=1, source_target_pairs={{0,16},{2,18},{4,20},{6,22},{8,24},{10,26},{12,28},{14,30},{16,0},... | collective-permute-start | bytes 884744 | tf_op jit(solution)/shard_map/ppermute | solution.py:623
  49.4 2.4 %shard_map.85 = (bf16[3,512,1024]{2,1,0:T(8,128)(2,1)S(1)}, f32[2,3,32,128]{3,2,1,0:T(8,128)S(1)}) custom-call(bf16[3,1024,1024]{2,1,0:T(8,128)(2,1)S(1)} %bitcast.7, bf16[224,512]{1,0:T(8,128)(2,1)S(1)} %copy-done.3, bf16[224,512]{1,0:T(8,128)(2,1)S(1)} %collective-permute-done.5.theirs.refs_2_), custom_call_target="tpu_custom_call" | custom-call | flops 1 | bytes 1 | tf_op jit(solution)/shard_map/pallas_call | solution.py:24
  51.8 2.1 %shard_map.86.refs_2_ = f32[2,3,112,512]{3,2,1,0:T(8,128)S(1)} custom-call(bf16[3,512,1024]{2,1,0:T(8,128)(2,1)S(1)} %get-tuple-element.48.weights.refs_0_.refs_1_, f32[2,3,32,128]{3,2,1,0:T(8,128)S(1)} %get-tuple-element.49.keep.refs_1_.refs_2_, bf16[224,512]{1,0:T(8,128)(2,1)S(1)} %copy-done.3, bf16[3,48,512]{2,1,0:T(8,128)(2,1)S(1)} %get-tuple-element.41.refs_1_, ...), custom_call_target="tpu_custom_call" | custom-call | flops 1 | bytes 1 | tf_op jit(solution)/shard_map/pallas_call | solution.py:24
  53.9 11.0 %collective-permute-done.4.refs_2_ = bf16[3,96,512]{2,1,0:T(8,128)(2,1)S(1)} collective-permute-done((bf16[3,96,512]{2,1,0:T(8,128)(2,1)S(1)}, bf16[3,96,512]{2,1,0:T(8,128)(2,1)S(1)}, u32[]{:S(2)}, u32[]{:S(2)}) %collective-permute-start.4) | collective-permute-done | bytes 294944 | tf_op jit(solution)/shard_map/ppermute | solution.py:623
  65.0 7.4 %collective-permute-done.7.refs_1_ = bf16[3,64,512]{2,1,0:T(8,128)(2,1)S(1)} collective-permute-done((bf16[3,64,512]{2,1,0:T(8,128)(2,1)S(1)}, bf16[3,64,512]{2,1,0:T(8,128)(2,1)S(1)}, u32[]{:S(2)}, u32[]{:S(2)}) %collective-permute-start.7) | collective-permute-done | bytes 196640 | tf_op jit(solution)/shard_map/ppermute | solution.py:633
  72.3 2.0 %shard_map.88.refs_3_ = f32[2,3,224,512]{3,2,1,0:T(8,128)S(1)} custom-call(bf16[3,512,1024]{2,1,0:T(8,128)(2,1)S(1)} %get-tuple-element.48.weights.refs_0_.refs_1_, f32[2,3,32,128]{3,2,1,0:T(8,128)S(1)} %get-tuple-element.49.keep.refs_1_.refs_2_, bf16[3,96,512]{2,1,0:T(8,128)(2,1)S(1)} %get-tuple-element.44.refs_0_, ...), custom_call_target="tpu_custom_call" | custom-call | flops 1 | bytes 1 | tf_op jit(solution)/shard_map/pallas_call | solution.py:24
  74.4 1.4 %shard_map.89 = (f32[2,3,128,512]{3,2,1,0:T(8,128)S(1)}, f32[2,3,16,512]{3,2,1,0:T(8,128)S(1)}, f32[2,3,256,512]{3,2,1,0:T(8,128)S(1)}, bf16[2,3,32,512]{3,2,1,0...) custom-call(bf16[3,512,1024]{2,1,0:T(8,128)(2,1)S(1)} %get-tuple-element.48.weights.refs_0_.ref, ...), custom_call_target="tpu_custom_call" | custom-call | flops 1 | bytes 1 | tf_op jit(solution)/shard_map/pallas_call | solution.py:24
  75.8 1.6 %collective-permute-start.11 = (bf16[2,3,32,512]{3,2,1,0:T(8,128)(2,1)S(1)}, bf16[2,3,32,512]{3,2,1,0:T(8,128)(2,1)S(1)}, u32[]{:S(2)}, u32[]{:S(2)}) collective-permute-start(bf16[2,3,32,512]{3,2,1,0:T(8,128)(2,1)S(1)} %get-tuple-element.64), channel_id=1, source_target_pairs={{0,1},{1,0},{2,3},{3,2},{4,5},{5,4},{6,7},{7,6},{8,9},{9,8},{10,11... | collective-permute-start | bytes 589832 | tf_op jit(solution)/shard_map/ppermute | solution.py:535
  77.9 1.1 %collective-permute-start.12 = (bf16[3,32,512]{2,1,0:T(8,128)(2,1)S(1)}, bf16[3,32,512]{2,1,0:T(8,128)(2,1)S(1)}, u32[]{:S(2)}, u32[]{:S(2)}) collective-permute-start(bf16[3,32,512]{2,1,0:T(8,128)(2,1)S(1)} %get-tuple-element.68.mine), channel_id=1, source_target_pairs={{0,16},{2,18},{4,20},{6,22},{8,24},{10,26},{12,28},{14,30},{16,0},... | collective-permute-start | bytes 294920 | tf_op jit(solution)/shard_map/ppermute | solution.py:677
  79.0 1.4 %collective-permute-done.10.refs_5_.refs_6_ = bf16[2,3,16,512]{3,2,1,0:T(8,128)(2,1)S(1)} collective-permute-done((bf16[2,3,16,512]{3,2,1,0:T(8,128)(2,1)S(1)}, bf16[2,3,16,512]{3,2,1,0:T(8,128)(2,1)S(1)}, u32[]{:S(2)}, u32[]{:S(2)}) %collective-permute-start.10) | collective-permute-done | bytes 98336 | tf_op jit(solution)/shard_map/ppermute | solution.py:704
  80.4 1.9 %collective-permute-done.9.refs_4_.refs_5_ = bf16[2,3,16,512]{3,2,1,0:T(8,128)(2,1)S(1)} collective-permute-done((bf16[2,3,16,512]{3,2,1,0:T(8,128)(2,1)S(1)}, bf16[2,3,16,512]{3,2,1,0:T(8,128)(2,1)S(1)}, u32[]{:S(2)}, u32[]{:S(2)}) %collective-permute-start.9) | collective-permute-done | bytes 98336 | tf_op jit(solution)/shard_map/ppermute | solution.py:703
  82.3 4.1 %shard_map.90.refs_0_ = f32[3,32,16,512]{3,2,1,0:T(8,128)} custom-call(bf16[3,512,1024]{2,1,0:T(8,128)(2,1)S(1)} %get-tuple-element.48.weights.refs_0_.refs_1_, f32[2,3,32,128]{3,2,1,0:T(8,128)S(1)} %get-tuple-element.49.keep.refs_1_.refs_2_, f32[2,3,128,512]{3,2,1,0:T(8,128)S(1)} %get-tuple-element.60.refs_2_, ...), custom_call_target="tpu_custom_call" | custom-call | flops 1 | bytes 1 | tf_op jit(solution)/shard_map/pallas_call | solution.py:24
  86.5 1.2 %shard_map.91.refs_3_.state = f32[2,3,144,512]{3,2,1,0:T(8,128)S(1)} custom-call(bf16[3,512,1024]{2,1,0:T(8,128)(2,1)S(1)} %get-tuple-element.48.weights.refs_0_.refs_1_, f32[2,3,32,128]{3,2,1,0:T(8,128)S(1)} %get-tuple-element.49.keep.refs_1_.refs_2_, bf16[3,80,512]{2,1,0:T(8,128)(2,1)S(1)} %get-tuple-element.52.refs_0_, ...), custom_call_target="tpu_custom_call" | custom-call | flops 1 | bytes 1 | tf_op jit(solution)/shard_map/pallas_call | solution.py:24
  87.7 4.2 %shard_map.92.given = f32[3,32,16,512]{3,2,1,0:T(8,128)} custom-call(f32[3,32,16,512]{3,2,1,0:T(8,128)} %shard_map.90.refs_0_, bf16[3,512,1024]{2,1,0:T(8,128)(2,1)S(1)} %get-tuple-element.48.weights.refs_0_.refs_1_, f32[2,3,32,128]{3,2,1,0:T(8,128)S(1)} %get-tuple-element.49.keep.refs_1_.refs_2_, ...), custom_call_target="tpu_custom_call", output_to_operand_aliasing={{}: (0, {})} | custom-call | flops 1 | bytes 1 | tf_op jit(solution)/shard_map/pallas_call | solution.py:24
  91.9 3.8 %shard_map.93 = f32[3,32,16,512]{3,2,1,0:T(8,128)} custom-call(f32[3,32,16,512]{3,2,1,0:T(8,128)} %shard_map.92.given, f32[2,3,144,512]{3,2,1,0:T(8,128)S(1)} %shard_map.91.refs_3_.state, bf16[3,512,1024]{2,1,0:T(8,128)(2,1)S(1)} %get-tuple-element.48.weights.refs_0_.refs_1_, ...), custom_call_target="tpu_custom_call", output_to_operand_aliasing={{}: (0, {})} | custom-call | flops 1 | bytes 1 | tf_op jit(solution)/shard_map/pallas_call | solution.py:24
  (27 shorter events, 1.5 us)
Async XLA Ops:
  0.0 8.7 %copy-start = (f32[3,32,16,512]{3,2,1,0:T(8,128)S(1)}, f32[3,32,16,512]{3,2,1,0:T(8,128)}, u32[]{:S(2)}) copy-start(f32[3,32,16,512]{3,2,1,0:T(8,128)} %param.8) | copy-start | bytes 9437188
  3.1 18.9 %collective-permute-start.5 = (bf16[224,512]{1,0:T(8,128)(2,1)}, bf16[224,512]{1,0:T(8,128)(2,1)S(1)}, u32[]{:S(2)}, u32[]{:S(2)}) collective-permute-start(bf16[224,512]{1,0:T(8,128)(2,1)} %get-tuple-element.45.mine.refs_0_), channel_id=1, source_target_pairs={{0,16},{2,18},{4,20},{6,22},{8,24},{10,26},{12,28},{14,30},{16,0},... | collective-permute-start | bytes 688136 | tf_op jit(solution)/shard_map/ppermute | solution.py:589
  7.2 8.9 %collective-permute-start = (f32[3,32,512]{2,1,0:T(8,128)}, f32[3,32,512]{2,1,0:T(8,128)S(1)}, u32[]{:S(2)}, u32[]{:S(2)}) collective-permute-start(f32[3,32,512]{2,1,0:T(8,128)} %get-tuple-element.39), channel_id=1, source_target_pairs={{0,1},{1,0},{2,3},{3,2},{4,5},{5,4},{6,7},{7,6},{8,9},{9,8},{10,11... | collective-permute-start | bytes 589832 | tf_op jit(solution)/shard_map/ppermute | solution.py:535
  8.7 0.9 copy-start.1
  9.6 39.7 %slice-start = ((s8[6291456]{0:T(1024)(128)(4,1)}), s8[4194304]{0:T(1024)(128)(4,1)S(1)}, s32[]{:S(2)}) async-start(s8[6291456]{0:T(1024)(128)(4,1)} %bitcast.6), calls=%async_computation | async-start | bytes 8388608
  11.2 13.5 %collective-permute-start.1 = (bf16[3,48,512]{2,1,0:T(8,128)(2,1)S(1)}, bf16[3,48,512]{2,1,0:T(8,128)(2,1)S(1)}, u32[]{:S(2)}, u32[]{:S(2)}) collective-permute-start(bf16[3,48,512]{2,1,0:T(8,128)(2,1)S(1)} %get-tuple-element.41.refs_1_), channel_id=1, source_target_pairs={{0,16},{2,18},{4,20},{6,22},{8,24},{10,26},{12,28},{14,30},{16,0},... | collective-permute-start | bytes 442376 | tf_op jit(solution)/shard_map/ppermute | solution.py:610
  11.6 10.4 %collective-permute-start.2 = (f32[3,16,512]{2,1,0:T(8,128)}, f32[3,16,512]{2,1,0:T(8,128)S(1)}, u32[]{:S(2)}, u32[]{:S(2)}) collective-permute-start(f32[3,16,512]{2,1,0:T(8,128)} %get-tuple-element.42), channel_id=1, source_target_pairs={{0,2},{2,4},{4,6},{6,8},{8,10},{10,12},{12,14},{14,16},{16,18},{18... | collective-permute-start | bytes 294920 | tf_op jit(solution)/shard_map/ppermute | solution.py:591
  11.6 37.8 %slice-start.1 = ((s8[6291456]{0:T(1024)(128)(4,1)}), s8[2097152]{0:T(1024)(128)(4,1)S(1)}, s32[]{:S(2)}) async-start(s8[6291456]{0:T(1024)(128)(4,1)} %bitcast.6), calls=%async_computation.1 | async-start | bytes 4194304
  11.6 37.8 %copy-start.3 = (bf16[224,512]{1,0:T(8,128)(2,1)S(1)}, bf16[224,512]{1,0:T(8,128)(2,1)}, u32[]{:S(2)}) copy-start(bf16[224,512]{1,0:T(8,128)(2,1)} %get-tuple-element.45.mine.refs_0_) | copy-start | bytes 688132
  11.6 10.4 %collective-permute-start.3 = (f32[3,16,512]{2,1,0:T(8,128)}, f32[3,16,512]{2,1,0:T(8,128)S(1)}, u32[]{:S(2)}, u32[]{:S(2)}) collective-permute-start(f32[3,16,512]{2,1,0:T(8,128)} %get-tuple-element.43), channel_id=1, source_target_pairs={{0,30},{2,0},{4,2},{6,4},{8,6},{10,8},{12,10},{14,12},{16,14},{18,... | collective-permute-start | bytes 294920 | tf_op jit(solution)/shard_map/ppermute | solution.py:592
  22.0 50.4 %collective-permute-start.8 = (bf16[3,128,512]{2,1,0:T(8,128)(2,1)S(1)}, bf16[3,128,512]{2,1,0:T(8,128)(2,1)S(1)}, u32[]{:S(2)}, u32[]{:S(2)}) collective-permute-start(bf16[3,128,512]{2,1,0:T(8,128)(2,1)S(1)} %get-tuple-element.58.refs_1_), channel_id=1, source_target_pairs={{0,16},{2,18},{4,20},{6,22},{8,24},{10,26},{12,28},{14,30},{16,0},... | collective-permute-start | bytes 1179656 | tf_op jit(solution)/shard_map/ppermute | solution.py:621
  24.6 40.3 %collective-permute-start.4 = (bf16[3,96,512]{2,1,0:T(8,128)(2,1)S(1)}, bf16[3,96,512]{2,1,0:T(8,128)(2,1)S(1)}, u32[]{:S(2)}, u32[]{:S(2)}) collective-permute-start(bf16[3,96,512]{2,1,0:T(8,128)(2,1)S(1)} %get-tuple-element.44.refs_0_), channel_id=1, source_target_pairs={{0,16},{2,18},{4,20},{6,22},{8,24},{10,26},{12,28},{14,30},{16,0},... | collective-permute-start | bytes 884744 | tf_op jit(solution)/shard_map/ppermute | solution.py:623
  49.3 23.1 %collective-permute-start.7 = (bf16[3,64,512]{2,1,0:T(8,128)(2,1)S(1)}, bf16[3,64,512]{2,1,0:T(8,128)(2,1)S(1)}, u32[]{:S(2)}, u32[]{:S(2)}) collective-permute-start(bf16[3,64,512]{2,1,0:T(8,128)(2,1)S(1)} %shard_map.87.refs_0_), channel_id=1, source_target_pairs={{0,16},{2,18},{4,20},{6,22},{8,24},{10,26},{12,28},{14,30},{16,0},... | collective-permute-start | bytes 589832 | tf_op jit(solution)/shard_map/ppermute | solution.py:633
  65.0 21.5 %collective-permute-start.6 = (bf16[3,80,512]{2,1,0:T(8,128)(2,1)S(1)}, bf16[3,80,512]{2,1,0:T(8,128)(2,1)S(1)}, u32[]{:S(2)}, u32[]{:S(2)}) collective-permute-start(bf16[3,80,512]{2,1,0:T(8,128)(2,1)S(1)} %get-tuple-element.52.refs_0_), channel_id=1, source_target_pairs={{0,16},{2,18},{4,20},{6,22},{8,24},{10,26},{12,28},{14,30},{16,0},... | collective-permute-start | bytes 737288 | tf_op jit(solution)/shard_map/ppermute | solution.py:665
  74.4 7.9 %copy-start.2 = (f32[15,8,512]{2,1,0:T(8,128)S(1)}, f32[15,8,512]{2,1,0:T(8,128)}, u32[]{:S(2)}) copy-start(f32[15,8,512]{2,1,0:T(8,128)} %get-tuple-element.37.coef.coef_in.refs_8_.refs_9_) | copy-start | bytes 737284
  75.8 6.5 %collective-permute-start.11 = (bf16[2,3,32,512]{3,2,1,0:T(8,128)(2,1)S(1)}, bf16[2,3,32,512]{3,2,1,0:T(8,128)(2,1)S(1)}, u32[]{:S(2)}, u32[]{:S(2)}) collective-permute-start(bf16[2,3,32,512]{3,2,1,0:T(8,128)(2,1)S(1)} %get-tuple-element.64), channel_id=1, source_target_pairs={{0,1},{1,0},{2,3},{3,2},{4,5},{5,4},{6,7},{7,6},{8,9},{9,8},{10,11... | collective-permute-start | bytes 589832 | tf_op jit(solution)/shard_map/ppermute | solution.py:535
  77.4 3.0 %collective-permute-start.10 = (bf16[2,3,16,512]{3,2,1,0:T(8,128)(2,1)S(1)}, bf16[2,3,16,512]{3,2,1,0:T(8,128)(2,1)S(1)}, u32[]{:S(2)}, u32[]{:S(2)}) collective-permute-start(bf16[2,3,16,512]{3,2,1,0:T(8,128)(2,1)S(1)} %get-tuple-element.63), channel_id=1, source_target_pairs={{0,14},{2,0},{4,2},{6,4},{8,6},{10,8},{12,10},{14,12},{16,30},{18,... | collective-permute-start | bytes 294920 | tf_op jit(solution)/shard_map/ppermute | solution.py:704
  77.4 4.9 %collective-permute-start.9 = (bf16[2,3,16,512]{3,2,1,0:T(8,128)(2,1)S(1)}, bf16[2,3,16,512]{3,2,1,0:T(8,128)(2,1)S(1)}, u32[]{:S(2)}, u32[]{:S(2)}) collective-permute-start(bf16[2,3,16,512]{3,2,1,0:T(8,128)(2,1)S(1)} %get-tuple-element.62), channel_id=1, source_target_pairs={{0,2},{2,4},{4,6},{6,8},{8,10},{10,12},{12,14},{14,0},{16,18},{18,... | collective-permute-start | bytes 294920 | tf_op jit(solution)/shard_map/ppermute | solution.py:703
  77.9 14.0 %collective-permute-start.12 = (bf16[3,32,512]{2,1,0:T(8,128)(2,1)S(1)}, bf16[3,32,512]{2,1,0:T(8,128)(2,1)S(1)}, u32[]{:S(2)}, u32[]{:S(2)}) collective-permute-start(bf16[3,32,512]{2,1,0:T(8,128)(2,1)S(1)} %get-tuple-element.68.mine), channel_id=1, source_target_pairs={{0,16},{2,18},{4,20},{6,22},{8,24},{10,26},{12,28},{14,30},{16,0},... | collective-permute-start | bytes 294920 | tf_op jit(solution)/shard_map/ppermute | solution.py:677

commit v5 on v3

--- a/solution.py
+++ b/solution.py
@@ -126,26 +126,17 @@
     lax.fori_loop(0, count // 2, pair, 0)
 
 
-def head_kernel(sizes, conc, cour, diff, ang, rate, smap, flags, *rest):
-    na, nz, lo, hi, planes = sizes
+def head_kernel(sizes, conc, cour, diff, ang, rate, smap, *rest):
+    na, nz, planes = sizes
     edges = rest[: 1 if planes == 2 else 2]
-    first, last, mid, coef, field, flag_v, cour_v, ang_v, diff_s, rate_s, map_s, flags_s, sems = rest[
-        len(edges) :
-    ]
-    half = nz // 2
-    inner = pl.ds((lo - 1) * nz, (hi - lo + 2) * nz)
-    left = pl.ds(0, (lo - 1) * nz)
-    right = pl.ds((hi + 1) * nz, (na - hi - 1) * nz)
+    first, last, coef, field, cour_v, ang_v, diff_s, rate_s, map_s, sems = rest[len(edges) :]
     small = [
-        pltpu.make_async_copy(src, dst, sems.at[k + 3])
+        pltpu.make_async_copy(src, dst, sems.at[k + 1])
         for k, (src, dst) in enumerate(
-            ((cour, cour_v), (ang, ang_v), (diff, diff_s), (rate, rate_s), (smap, map_s), (flags, flags_s))
+            ((cour, cour_v), (ang, ang_v), (diff, diff_s), (rate, rate_s), (smap, map_s))
         )
     ]
-    copies = [
-        pltpu.make_async_copy(conc.at[:, rows], field.at[:, rows], sems.at[k])
-        for k, rows in enumerate((inner, left, right))
-    ]
+    copies = [pltpu.make_async_copy(conc, field, sems.at[0])]
     for copy in small + copies:
         copy.start()
     for copy in small:
@@ -162,44 +153,42 @@
         coef[ANGULAR + s] = jnp.broadcast_to(angular, tile)
         coef[AXIAL + s] = jnp.full(tile, axial, F32)
         coef[RATE + s] = jnp.full(tile, total, F32)
+    copies[0].wait()
+    if planes == 2:
+        row = jnp.where(lax.axis_index("ax") == 0, nz - 1, 0)
+    for s in range(3):
+        first[s] = field[s, pl.ds(0, nz), :]
+        last[s] = field[s, pl.ds((na - 1) * nz, nz), :]
+        for t in range(na):
+            if planes == 2:
+                edges[0][s, t : t + 1, :] = field[s, pl.ds(t * nz + row, 1), :]
+            else:
+                edges[0][s, t : t + 1, :] = field[s, t * nz : t * nz + 1, :]
+                edges[1][s, t : t + 1, :] = field[s, (t + 1) * nz - 1 : (t + 1) * nz, :]
+
+
+def inner_kernel(sizes, runs, conc, coef, flags, *rest):
+    na, nz = sizes
+    outs, field, flag_v, sem = rest[:-3], rest[-3], rest[-2], rest[-1]
+    copy = pltpu.make_async_copy(conc, field, sem)
+    copy.start()
     lane = lax.broadcasted_iota(jnp.int32, (1, LANES), 1)
     for t in range(na):
         row = jnp.zeros((1, LANES), jnp.int32)
         for s in range(3):
-            row = jnp.where(lane == s, flags_s[s, t], row)
+            row = jnp.where(lane == s, flags[s, t], row)
         flag_v[t : t + 1, :] = row.astype(F32)
-    rows = (hi - lo) * half
+    rows = runs[0][1] * nz // 2
     span = pl.ds(3 * rows, na)
-    mid[span, :] = jnp.zeros((na, mid.shape[1]), BF16)
-    mid[span, :LANES] = flag_v[...].astype(BF16)
-    copies[0].wait()
-    mid_run(field, lambda s: mid.at[pl.ds(s * rows, rows)], lo, hi - lo, 0, coef, nz)
-    copies[1].wait()
-    copies[2].wait()
-    for s in range(3):
-        if planes == 2:
-            row = jnp.where(lax.axis_index("ax") == 0, nz - 1, 0)
-            for t in range(na):
-                edges[0][s, t : t + 1, :] = field[s, pl.ds(t * nz + row, 1), :]
+    outs[0][span, :] = jnp.zeros((na, outs[0].shape[1]), BF16)
+    outs[0][span, :LANES] = flag_v[...].astype(BF16)
+    copy.wait()
+    for k, (begin, count) in enumerate(runs):
+        out = outs[k]
+        if k == 0:
+            mid_run(field, lambda s: out.at[pl.ds(s * rows, rows)], begin, count, 0, coef, nz)
         else:
-            for t in range(na):
-                edges[0][s, t : t + 1, :] = field[s, t * nz : t * nz + 1, :]
-                edges[1][s, t : t + 1, :] = field[s, (t + 1) * nz - 1 : (t + 1) * nz, :]
-        first[s] = field[s, pl.ds(0, nz), :]
-        last[s] = field[s, pl.ds((na - 1) * nz, nz), :]
-
-
-def inner_kernel(sizes, runs, conc, coef, *rest):
-    na, nz = sizes
-    outs, field, sem = rest[:-2], rest[-2], rest[-1]
-    copy = pltpu.make_async_copy(conc, field, sem)
-    copy.start()
-    copy.wait()
-    for out, parts in runs:
-        at = 0
-        for begin, count in parts:
-            mid_run(field, outs[out].at.__getitem__, begin, count, at, coef, nz)
-            at += count
+            mid_run(field, out.at.__getitem__, begin, count, 0, coef, nz)
 
 
 def edge_weights(planes):
@@ -316,15 +305,22 @@
     return ref[pl.ds(s * rows, rows), :]
 
 
-def radial_kernel(runs, copies, half, weights, keep, mine, theirs, *refs):
+def radial_kernel(plan, copies, half, weights, keep, *refs):
+    n = len(plan)
+    mines, theirs, refs = refs[:n], refs[n : 2 * n], refs[2 * n :]
     n_in = 1 + max((part for part, *_ in copies), default=-1)
     parts, states = refs[:n_in], refs[n_in:]
     for s in range(3):
-        value = both_sides(species_rows(mine, s, runs, half), species_rows(theirs, s, runs, half), weights[s])
-        at = 0
-        for which, begin, place, count in runs:
-            store_run(states[which], s, begin, place, count, at, value, keep, half)
-            at += count
+        for k, runs in enumerate(plan):
+            value = both_sides(
+                species_rows(mines[k], s, runs, half),
+                species_rows(theirs[k], s, runs, half),
+                weights[s],
+            )
+            at = 0
+            for which, begin, place, count in runs:
+                store_run(states[which], s, begin, place, count, at, value, keep, half)
+                at += count
     for part, source, which, place, count in copies:
         to, rows = pl.ds(place * half, count * half), pl.ds(source * half, count * half)
         for ab in range(2):
@@ -355,12 +351,12 @@
             last[ab, s] = pack([mid_end[ab, s, ends_end, :], outer[ab, s, end, :]])
 
 
-def radial_edges_kernel(sizes, runs, copies, half, weights, keep, mine, theirs, *refs):
+def radial_edges_kernel(sizes, plan, copies, half, weights, keep, *refs):
     na, nz, planes = sizes
     n_edges = 1 if planes == 2 else 2
     *edges, first, last, stage = refs[-3 - n_edges :]
     refs = refs[: -3 - n_edges]
-    radial_kernel(runs, copies, half, weights, keep, mine, theirs, *refs)
+    radial_kernel(plan, copies, half, weights, keep, *refs)
     edges_of_state(na, nz, planes, refs[-3], refs[-2], refs[-1], edges, first, last, stage)
 
 
@@ -524,7 +520,7 @@
     quarter = na // 4
     ends = 2
     side = na // 2
-    first_lo, first_hi = ends, side
+    first_lo, first_cut, first_hi = ends, ends + na // 4, side
     last_lo, last_hi = na - 3 * ends, na - ends
     opposite = [(i, (i + count // 2) % count) for i in range(count)]
 
@@ -536,41 +532,47 @@
 
     conc = concentration.reshape(ns, na * nz, nr)
     field = pltpu.VMEM((ns, na * nz, nr), F32)
-    *edges, first, last, mid_a, coef = call(
-        functools.partial(head_kernel, (na, nz, first_lo, first_hi, planes)),
-        [shape(ns, na, nr)] * n_edges
-        + [shape(ns, nz, nr)] * 2
-        + [
-            shape(ns * (first_hi - first_lo) * half + na, nr, dtype=BF16),
-            shape(RATE + 3, half, nr),
+    *edges, first, last, coef = call(
+        functools.partial(head_kernel, (na, nz, planes)),
+        [shape(ns, na, nr)] * n_edges + [shape(ns, nz, nr)] * 2 + [shape(RATE + 3, half, nr)],
+        [HBM] * 6,
+        [VM] * (n_edges + 3),
+        [
+            field, pltpu.VMEM((1, nr), F32), pltpu.VMEM(angular_rate.shape, F32),
+            pltpu.SMEM(axial_diffusion.shape, F32), pltpu.SMEM(rate_constants.shape, F32),
+            pltpu.SMEM(species_map.shape, jnp.int32), dma(6),
         ],
-        [HBM] * 7,
-        [VM] * (n_edges + 4),
-        [
-            field, pltpu.VMEM((na, LANES), F32), pltpu.VMEM((1, nr), F32), pltpu.VMEM(angular_rate.shape, F32),
-            pltpu.SMEM(axial_diffusion.shape, F32), pltpu.SMEM(rate_constants.shape, F32),
-            pltpu.SMEM(species_map.shape, jnp.int32), pltpu.SMEM(wall_flags.shape, jnp.int32), dma(9),
-        ],
-        (conc, courant[None], axial_diffusion, angular_rate, rate_constants, species_map, wall_flags),
+        (conc, courant[None], axial_diffusion, angular_rate, rate_constants, species_map),
         58,
     )
-    opp_a = lax.ppermute(mid_a, "ang", opposite)
     low, high = plane_halos(edges, planes)
     angle_before = lax.ppermute(last, "ang", [(i, (i + 1) % count) for i in range(count)])
     angle_after = lax.ppermute(first, "ang", [(i, (i - 1) % count) for i in range(count)])
-    mid_x, mid_l = call(
+
+    mid_a, mid_b, mid_x, mid_l = call(
         functools.partial(
             inner_kernel,
             (na, nz),
-            ((0, ((first_hi, last_lo - first_hi),)), (1, ((last_lo, last_hi - last_lo),))),
+            (
+                (first_lo, first_cut - first_lo),
+                (first_cut, first_hi - first_cut),
+                (first_hi, last_lo - first_hi),
+                (last_lo, last_hi - last_lo),
+            ),
         ),
-        [message(last_lo - first_hi), message(last_hi - last_lo)],
-        [ANY, VM],
-        [VM] * 2,
-        [field, pltpu.SemaphoreType.DMA],
-        (conc, coef),
+        [
+            shape(ns * (first_cut - first_lo) * half + na, nr, dtype=BF16),
+            message(first_hi - first_cut), message(last_lo - first_hi), message(last_hi - last_lo),
+        ],
+        [ANY, VM, SM],
+        [VM] * 4,
+        [field, pltpu.VMEM((na, LANES), F32), pltpu.SemaphoreType.DMA],
+        (conc, coef, wall_flags),
         8,
     )
+    (mid_a, mid_b), (angle_before, angle_after) = after((mid_a, mid_b), (angle_before, angle_after))
+    opp_a = lax.ppermute(mid_a, "ang", opposite)
+    opp_b = lax.ppermute(mid_b, "ang", opposite)
     out1, out2 = call(
         functools.partial(frame_kernel, (na, nz, ends, planes)),
         [message(na // 2), message(na // 2 + 2 * ends)],
@@ -580,9 +582,11 @@
         (conc, angle_before, angle_after, low, high, coef),
         8,
     )
-    (out1, out2), opp_a = after((out1, out2), opp_a)
+    out2, opp_a = after(out2, opp_a)
+    opp_2 = lax.ppermute(out2, "ang", opposite)
+    out1, opp_b = after(out1, opp_b)
     opp_1 = lax.ppermute(out1, "ang", opposite)
-    opp_2 = lax.ppermute(out2, "ang", opposite)
+
     weights, keep = call(
         weights_kernel,
         [shape(ns, nr, 2 * nr, dtype=BF16), shape(2, ns, na, LANES)],
@@ -596,21 +600,26 @@
     def state(angles):
         return shape(2, ns, angles * half, nr)
 
-    count_a = first_hi - first_lo
+    count_a, count_b = first_cut - first_lo, first_hi - first_cut
     (mid_first,) = call(
-        functools.partial(radial_kernel, ((0, first_lo, 0, count_a),), (), half),
-        [state(count_a)],
-        [VM] * 4,
+        functools.partial(
+            radial_kernel,
+            (((0, first_lo, 0, count_a),), ((0, first_cut, count_a, count_b),)),
+            (),
+            half,
+        ),
+        [state(count_a + count_b)],
+        [VM] * 6,
         [VM],
         [],
-        (weights, keep, mid_a, opp_a),
+        (weights, keep, mid_a, mid_b, opp_a, opp_b),
         8,
     )
     opp_1, mid_first = after(opp_1, mid_first)
     mid_x, opp_1 = after(mid_x, opp_1)
     opp_x = lax.ppermute(mid_x, "ang", opposite)
     (outer_first,) = call(
-        functools.partial(radial_kernel, ((0, 0, 0, side),), (), half),
+        functools.partial(radial_kernel, (((0, 0, 0, side),),), (), half),
         [state(side)],
         [VM] * 4,
         [VM],
@@ -620,13 +629,13 @@
     )
     mid_l, opp_2 = after(mid_l, opp_2)
     opp_l = lax.ppermute(mid_l, "ang", opposite)
-    runs = ((2, side, side, side), (0, 0, 0, ends), (1, na - ends, 0, ends))
+    plan = (((2, side, side, side), (0, 0, 0, ends), (1, na - ends, 0, ends)),)
     mid_left, ends_right, outer_state, *rest = call(
         functools.partial(
             radial_edges_kernel,
             (na, nz, planes),
-            runs,
-            ((0, 0, 0, first_lo, count_a), (1, 0, 2, 0, side)),
+            plan,
+            ((0, 0, 0, first_lo, count_a + count_b), (1, 0, 2, 0, side)),
             half,
         ),
         [state(side), state(ends), state(na)]
@@ -662,7 +671,7 @@
     (mid_right,) = call(
         functools.partial(
             radial_kernel,
-            ((0, first_hi, 2, last_lo - first_hi),),
+            (((0, first_hi, 2, last_lo - first_hi),),),
             ((0, base, 0, 0, 2), (1, 0, 0, na - ends - base, ends)),
             half,
         ),

time: 93.9 us -> 94.8 us (level)
  starting transfers between devices: 25.7 us -> 17.6 us
  waiting for transfers between devices: 39.8 us -> 46.6 us
  Pallas kernels: 27.1 us -> 29 us
    ppermute x1, starting transfers between devices: 8.68 us -> 0.01 us  [per_device(): opp_2 = lax.ppermute(out2, 'ang', opposite)]
    ppermute x1, waiting for transfers between devices: 6.16 us -> 0.01 us  [per_device(): lax.ppermute(last, 'ang', [(i, (i + 1) % count) for i in range(count)])]
    ppermute x1, waiting for transfers between devices: 1 us -> 5.27 us  [per_device(): opp_a = lax.ppermute(mid_a, 'ang', opposite)]
    ppermute x1, waiting for transfers between devices: 29.8 us -> 33.6 us  [per_device(): opp_1 = lax.ppermute(out1, 'ang', opposite)]
    ppermute x0 -> x1, waiting for transfers between devices: none -> 2.96 us  [per_device(): opp_b = lax.ppermute(mid_b, 'ang', opposite)]
    ppermute x1, starting transfers between devices: 4.1 us -> 1.24 us  [per_device(): opp_a = lax.ppermute(mid_a, 'ang', opposite)]
    ppermute x2, waiting for transfers between devices: 0.01 us -> 2.75 us  [plane_halos(): got = lax.ppermute(edges[0], 'ax', [(0, 1), (1, 0)])]
    ppermute x1, waiting for transfers between devices: 2.74 us -> 0.15 us  [per_device(): angle_before = lax.ppermute(last, 'ang', ring(count, 1))]
  transfers between devices with their start and end apart: 11 -> 12, of which waited for: 4 -> 7; matrix products, arithmetic and copies ran while one was open for 0% -> 0% of each run, Pallas kernels for 21% -> 24%
where the time goes in v5:
time: 94.8 us; the launch traced here: 94.5 us
  waiting for transfers between devices  46.6 us (49%)
  Pallas kernels  29 us (31%)
  starting transfers between devices  17.6 us (19%)
  local copies, waits for them, and re-layouts  0.96 us (1%)
    ppermute x1, waiting for transfers between devices, per_device(): opp_1 = lax.ppermute(out1, 'ang', opposite)  33.6 us
    pallas_call x11, Pallas kernels, call(): pl.pallas_call(body, out_shape=out_shape, in_specs=in_specs, out_specs=ou...  29 us
    ppermute x1, waiting for transfers between devices, per_device(): opp_a = lax.ppermute(mid_a, 'ang', opposite)  5.27 us
    ppermute x1, starting transfers between devices, per_device(): lax.ppermute(first, 'ang', [(i, (i - 1) % count) for i in range(count)])  5.06 us
    ppermute x1, starting transfers between devices, per_device(): angle_after = lax.ppermute(first, 'ang', ring(count, -1))  3.34 us
    ppermute x2, starting transfers between devices, plane_halos(): got = lax.ppermute(edges[0], 'ax', [(0, 1), (1, 0)])  3.07 us
    ppermute x1, waiting for transfers between devices, per_device(): opp_b = lax.ppermute(mid_b, 'ang', opposite)  2.96 us
    ppermute x2, waiting for transfers between devices, plane_halos(): got = lax.ppermute(edges[0], 'ax', [(0, 1), (1, 0)])  2.75 us
  transfers between devices with their start and end apart: 12, of which 7 were waited for; matrix products, arithmetic and copies ran while one was open for 0% of the time, Pallas kernels for 24%

profile of v5, /device:TPU:0, one launch (start us, length us, event | category | flops | bytes accessed | tf_op | source)
XLA Modules:
  0.0 94.5 jit_solution(10460031554057350740)
XLA Ops:
  0.0 2.9 %shard_map.82 = (f32[3,32,512]{2,1,0:T(8,128)}, f32[3,16,512]{2,1,0:T(8,128)}, f32[3,16,512]{2,1,0:T(8,128)}, f32[15,8,512]{2,1,0:T(8,128)}) custom-call(f32[3,512,512]{2,1,0:T(8,128)} %bitcast.2, f32[1,512]{1,0:T(1,128)} %bitcast.5, f32[3]{0:T(128)} %diff.1, f32[3,512]{1,0:T(4,128)} %ang.1, f32[4]{0:T(128)} %rate.1, s32[4,3]{1,0:T(4,128)} %smap.1), custom_call_target="tpu_custom_call" | custom-call | flops 1 | bytes 1 | tf_op jit(solution)/shard_map/pallas_call | solution.py:24
  3.5 5.1 %collective-permute-start.1 = (f32[3,16,512]{2,1,0:T(8,128)}, f32[3,16,512]{2,1,0:T(8,128)S(1)}, u32[]{:S(2)}, u32[]{:S(2)}) collective-permute-start(f32[3,16,512]{2,1,0:T(8,128)} %get-tuple-element.44), channel_id=1, source_target_pairs={{0,30},{2,0},{4,2},{6,4},{8,6},{10,8},{12,10},{14,12},{16,14},{18,... | collective-permute-start | bytes 294920 | tf_op jit(solution)/shard_map/ppermute | solution.py:550
  8.5 0.9 copy-done.2
  9.5 2.7 %shard_map.83 = (bf16[224,512]{1,0:T(8,128)(2,1)S(1)}, bf16[3,48,512]{2,1,0:T(8,128)(2,1)S(1)}, bf16[3,80,512]{2,1,0:T(8,128)(2,1)S(1)}, bf16[3,32,512]{2,1,0:T(8,128)(2,1)S(1)}) custom-call(f32[3,512,512]{2,1,0:T(8,128)S(1)} %bitcast.3, f32[15,8,512]{2,1,0:T(8,128)S(1)} %copy-done.2, s32[3,32]{1,0:T(4,128)S(1)} %copy-done.4), custom_call_target="tpu_custom_call" | custom-call | flops 1 | bytes 1 | tf_op jit(solution)/shard_map/pallas_call | solution.py:24
  12.2 1.2 %collective-permute-start.5 = (bf16[224,512]{1,0:T(8,128)(2,1)S(1)}, bf16[224,512]{1,0:T(8,128)(2,1)S(1)}, u32[]{:S(2)}, u32[]{:S(2)}) collective-permute-start(bf16[224,512]{1,0:T(8,128)(2,1)S(1)} %get-tuple-element.51.mine.refs_0_), channel_id=1, source_target_pairs={{0,16},{2,18},{4,20},{6,22},{8,24},{10,26},{12,28},{14,30},{16,0},... | collective-permute-start | bytes 688136 | tf_op jit(solution)/shard_map/ppermute | solution.py:574
  13.4 1.5 %collective-permute-start.2 = (f32[3,32,512]{2,1,0:T(8,128)}, f32[3,32,512]{2,1,0:T(8,128)S(1)}, u32[]{:S(2)}, u32[]{:S(2)}) collective-permute-start(f32[3,32,512]{2,1,0:T(8,128)} %get-tuple-element.47), channel_id=1, source_target_pairs={{0,1},{1,0},{2,3},{3,2},{4,5},{5,4},{6,7},{7,6},{8,9},{9,8},{10,11... | collective-permute-start | bytes 589832 | tf_op jit(solution)/shard_map/ppermute | solution.py:500
  14.9 2.1 %collective-permute-start.3 = (bf16[3,48,512]{2,1,0:T(8,128)(2,1)S(1)}, bf16[3,48,512]{2,1,0:T(8,128)(2,1)S(1)}, u32[]{:S(2)}, u32[]{:S(2)}) collective-permute-start(bf16[3,48,512]{2,1,0:T(8,128)(2,1)S(1)} %get-tuple-element.49.refs_1_), channel_id=1, source_target_pairs={{0,16},{2,18},{4,20},{6,22},{8,24},{10,26},{12,28},{14,30},{16,0},... | collective-permute-start | bytes 442376 | tf_op jit(solution)/shard_map/ppermute | solution.py:575
  17.1 2.7 %collective-permute-done.2.low.high = f32[3,32,512]{2,1,0:T(8,128)S(1)} collective-permute-done((f32[3,32,512]{2,1,0:T(8,128)}, f32[3,32,512]{2,1,0:T(8,128)S(1)}, u32[]{:S(2)}, u32[]{:S(2)}) %collective-permute-start.2) | collective-permute-done | bytes 196640 | tf_op jit(solution)/shard_map/ppermute | solution.py:500
  19.8 3.0 %shard_map.84 = (bf16[3,128,512]{2,1,0:T(8,128)(2,1)S(1)}, bf16[3,160,512]{2,1,0:T(8,128)(2,1)S(1)}) custom-call(f32[3,512,512]{2,1,0:T(8,128)S(1)} %bitcast.4, f32[3,16,512]{2,1,0:T(8,128)S(1)} %collective-permute-done.before, f32[3,16,512]{2,1,0:T(8,128)S(1)} %collective-permute-done.1.after, f32[3,32,512]{2,1,0:T(8,128)S(1)} %collective-permute-done.2.low.high, ...), custom_call_target="tpu_custom_call" | custom-call | flops 1 | bytes 1 | tf_op jit(solution)/shard_map/pallas_call | solution.py:24
  22.8 5.3 %collective-permute-done.5.theirs.refs_2_ = bf16[224,512]{1,0:T(8,128)(2,1)S(1)} collective-permute-done((bf16[224,512]{1,0:T(8,128)(2,1)S(1)}, bf16[224,512]{1,0:T(8,128)(2,1)S(1)}, u32[]{:S(2)}, u32[]{:S(2)}) %collective-permute-start.5) | collective-permute-done | bytes 229408 | tf_op jit(solution)/shard_map/ppermute | solution.py:574
  28.1 3.0 %collective-permute-done.3.refs_3_ = bf16[3,48,512]{2,1,0:T(8,128)(2,1)S(1)} collective-permute-done((bf16[3,48,512]{2,1,0:T(8,128)(2,1)S(1)}, bf16[3,48,512]{2,1,0:T(8,128)(2,1)S(1)}, u32[]{:S(2)}, u32[]{:S(2)}) %collective-permute-start.3) | collective-permute-done | bytes 147488 | tf_op jit(solution)/shard_map/ppermute | solution.py:575
  31.0 2.4 %shard_map.85 = (bf16[3,512,1024]{2,1,0:T(8,128)(2,1)S(1)}, f32[2,3,32,128]{3,2,1,0:T(8,128)S(1)}) custom-call(bf16[3,1024,1024]{2,1,0:T(8,128)(2,1)S(1)} %copy-done.1, bf16[224,512]{1,0:T(8,128)(2,1)S(1)} %get-tuple-element.51.mine.refs_0_, bf16[224,512]{1,0:T(8,128)(2,1)S(1)} %collective-permute-done.5.theirs.refs_2_), custom_call_target="tpu_custom_call" | custom-call | flops 1 | bytes 1 | tf_op jit(solution)/shard_map/pallas_call | solution.py:24
  33.5 2.1 %shard_map.86.refs_2_ = f32[2,3,112,512]{3,2,1,0:T(8,128)S(1)} custom-call(bf16[3,512,1024]{2,1,0:T(8,128)(2,1)S(1)} %get-tuple-element.54.weights.refs_0_.refs_1_, f32[2,3,32,128]{3,2,1,0:T(8,128)S(1)} %get-tuple-element.55.keep.refs_1_.refs_2_, bf16[224,512]{1,0:T(8,128)(2,1)S(1)} %get-tuple-element.51.mine.refs_0_, ...), custom_call_target="tpu_custom_call" | custom-call | flops 1 | bytes 1 | tf_op jit(solution)/shard_map/pallas_call | solution.py:24
  35.6 33.6 %collective-permute-done.4.refs_1_ = bf16[3,128,512]{2,1,0:T(8,128)(2,1)S(1)} collective-permute-done((bf16[3,128,512]{2,1,0:T(8,128)(2,1)S(1)}, bf16[3,128,512]{2,1,0:T(8,128)(2,1)S(1)}, u32[]{:S(2)}, u32[]{:S(2)}) %collective-permute-start.4) | collective-permute-done | bytes 393248 | tf_op jit(solution)/shard_map/ppermute | solution.py:588
  69.2 1.0 %shard_map.87.refs_3_ = f32[2,3,128,512]{3,2,1,0:T(8,128)S(1)} custom-call(bf16[3,512,1024]{2,1,0:T(8,128)(2,1)S(1)} %get-tuple-element.54.weights.refs_0_.refs_1_, f32[2,3,32,128]{3,2,1,0:T(8,128)S(1)} %get-tuple-element.55.keep.refs_1_.refs_2_, bf16[3,128,512]{2,1,0:T(8,128)(2,1)S(1)} %get-tuple-element.50.refs_0_, ...), custom_call_target="tpu_custom_call" | custom-call | flops 1 | bytes 1 | tf_op jit(solution)/shard_map/pallas_call | solution.py:24
  70.2 1.6 %shard_map.88 = (f32[2,3,128,512]{3,2,1,0:T(8,128)S(1)}, f32[2,3,16,512]{3,2,1,0:T(8,128)S(1)}, f32[2,3,256,512]{3,2,1,0:T(8,128)S(1)}, bf16[2,3,32,512]{3,2,1,0...) custom-call(bf16[3,512,1024]{2,1,0:T(8,128)(2,1)S(1)} %get-tuple-element.54.weights.refs_0_.ref, ...), custom_call_target="tpu_custom_call" | custom-call | flops 1 | bytes 1 | tf_op jit(solution)/shard_map/pallas_call | solution.py:24
  71.8 1.6 %collective-permute-start.10 = (bf16[2,3,32,512]{3,2,1,0:T(8,128)(2,1)S(1)}, bf16[2,3,32,512]{3,2,1,0:T(8,128)(2,1)S(1)}, u32[]{:S(2)}, u32[]{:S(2)}) collective-permute-start(bf16[2,3,32,512]{3,2,1,0:T(8,128)(2,1)S(1)} %get-tuple-element.68), channel_id=1, source_target_pairs={{0,1},{1,0},{2,3},{3,2},{4,5},{5,4},{6,7},{7,6},{8,9},{9,8},{10,11... | collective-permute-start | bytes 589832 | tf_op jit(solution)/shard_map/ppermute | solution.py:500
  73.4 3.3 %collective-permute-start.9 = (bf16[2,3,16,512]{3,2,1,0:T(8,128)(2,1)S(1)}, bf16[2,3,16,512]{3,2,1,0:T(8,128)(2,1)S(1)}, u32[]{:S(2)}, u32[]{:S(2)}) collective-permute-start(bf16[2,3,16,512]{3,2,1,0:T(8,128)(2,1)S(1)} %get-tuple-element.67), channel_id=1, source_target_pairs={{0,14},{2,0},{4,2},{6,4},{8,6},{10,8},{12,10},{14,12},{16,30},{18,... | collective-permute-start | bytes 294920 | tf_op jit(solution)/shard_map/ppermute | solution.py:653
  76.7 2.2 %collective-permute-start.11 = (bf16[3,32,512]{2,1,0:T(8,128)(2,1)S(1)}, bf16[3,32,512]{2,1,0:T(8,128)(2,1)S(1)}, u32[]{:S(2)}, u32[]{:S(2)}) collective-permute-start(bf16[3,32,512]{2,1,0:T(8,128)(2,1)S(1)} %get-tuple-element.72.mine), channel_id=1, source_target_pairs={{0,16},{2,18},{4,20},{6,22},{8,24},{10,26},{12,28},{14,30},{16,0},... | collective-permute-start | bytes 294920 | tf_op jit(solution)/shard_map/ppermute | solution.py:631
  79.6 4.1 %shard_map.89.refs_0_ = f32[3,32,16,512]{3,2,1,0:T(8,128)} custom-call(bf16[3,512,1024]{2,1,0:T(8,128)(2,1)S(1)} %get-tuple-element.54.weights.refs_0_.refs_1_, f32[2,3,32,128]{3,2,1,0:T(8,128)S(1)} %get-tuple-element.55.keep.refs_1_.refs_2_, f32[2,3,128,512]{3,2,1,0:T(8,128)S(1)} %get-tuple-element.64.refs_2_, ...), custom_call_target="tpu_custom_call" | custom-call | flops 1 | bytes 1 | tf_op jit(solution)/shard_map/pallas_call | solution.py:24
  83.8 1.3 %collective-permute-done.6.refs_1_ = bf16[3,80,512]{2,1,0:T(8,128)(2,1)S(1)} collective-permute-done((bf16[3,80,512]{2,1,0:T(8,128)(2,1)S(1)}, bf16[3,80,512]{2,1,0:T(8,128)(2,1)S(1)}, u32[]{:S(2)}, u32[]{:S(2)}) %collective-permute-start.6) | collective-permute-done | bytes 245792 | tf_op jit(solution)/shard_map/ppermute | solution.py:620
  85.1 1.2 %shard_map.90.refs_3_.state = f32[2,3,144,512]{3,2,1,0:T(8,128)S(1)} custom-call(bf16[3,512,1024]{2,1,0:T(8,128)(2,1)S(1)} %get-tuple-element.54.weights.refs_0_.refs_1_, f32[2,3,32,128]{3,2,1,0:T(8,128)S(1)} %get-tuple-element.55.keep.refs_1_.refs_2_, bf16[3,80,512]{2,1,0:T(8,128)(2,1)S(1)} %get-tuple-element.58.refs_0_, ...), custom_call_target="tpu_custom_call" | custom-call | flops 1 | bytes 1 | tf_op jit(solution)/shard_map/pallas_call | solution.py:24
  86.3 4.2 %shard_map.91.given = f32[3,32,16,512]{3,2,1,0:T(8,128)} custom-call(f32[3,32,16,512]{3,2,1,0:T(8,128)} %shard_map.89.refs_0_, bf16[3,512,1024]{2,1,0:T(8,128)(2,1)S(1)} %get-tuple-element.54.weights.refs_0_.refs_1_, f32[2,3,32,128]{3,2,1,0:T(8,128)S(1)} %get-tuple-element.55.keep.refs_1_.refs_2_, ...), custom_call_target="tpu_custom_call", output_to_operand_aliasing={{}: (0, {})} | custom-call | flops 1 | bytes 1 | tf_op jit(solution)/shard_map/pallas_call | solution.py:24
  90.5 3.8 %shard_map.92 = f32[3,32,16,512]{3,2,1,0:T(8,128)} custom-call(f32[3,32,16,512]{3,2,1,0:T(8,128)} %shard_map.91.given, f32[2,3,144,512]{3,2,1,0:T(8,128)S(1)} %shard_map.90.refs_3_.state, bf16[3,512,1024]{2,1,0:T(8,128)(2,1)S(1)} %get-tuple-element.54.weights.refs_0_.refs_1_, ...), custom_call_target="tpu_custom_call", output_to_operand_aliasing={{}: (0, {})} | custom-call | flops 1 | bytes 1 | tf_op jit(solution)/shard_map/pallas_call | solution.py:24
  (21 shorter events, 1.2 us)
Async XLA Ops:
  0.0 8.5 %copy-start = (f32[3,32,16,512]{3,2,1,0:T(8,128)S(1)}, f32[3,32,16,512]{3,2,1,0:T(8,128)}, u32[]{:S(2)}) copy-start(f32[3,32,16,512]{3,2,1,0:T(8,128)} %param.8) | copy-start | bytes 9437188
  0.0 8.5 %copy-start.4 = (s32[3,32]{1,0:T(4,128)S(1)}, s32[3,32]{1,0:T(4,128)}, u32[]{:S(2)}) copy-start(s32[3,32]{1,0:T(4,128)} %flags.1) | copy-start | bytes 1156
  2.9 9.2 %collective-permute-start = (f32[3,16,512]{2,1,0:T(8,128)}, f32[3,16,512]{2,1,0:T(8,128)S(1)}, u32[]{:S(2)}, u32[]{:S(2)}) collective-permute-start(f32[3,16,512]{2,1,0:T(8,128)} %get-tuple-element.43), channel_id=1, source_target_pairs={{0,2},{2,4},{4,6},{6,8},{8,10},{10,12},{12,14},{14,16},{16,18},{18... | collective-permute-start | bytes 294920 | tf_op jit(solution)/shard_map/ppermute | solution.py:549
  3.5 8.7 %collective-permute-start.1 = (f32[3,16,512]{2,1,0:T(8,128)}, f32[3,16,512]{2,1,0:T(8,128)S(1)}, u32[]{:S(2)}, u32[]{:S(2)}) collective-permute-start(f32[3,16,512]{2,1,0:T(8,128)} %get-tuple-element.44), channel_id=1, source_target_pairs={{0,30},{2,0},{4,2},{6,4},{8,6},{10,8},{12,10},{14,12},{16,14},{18,... | collective-permute-start | bytes 294920 | tf_op jit(solution)/shard_map/ppermute | solution.py:550
  8.5 0.9 %copy-start.2 = (f32[15,8,512]{2,1,0:T(8,128)S(1)}, f32[15,8,512]{2,1,0:T(8,128)}, u32[]{:S(2)}) copy-start(f32[15,8,512]{2,1,0:T(8,128)} %get-tuple-element.39.coef.coef_in.refs_8_.refs_9_) | copy-start | bytes 737284
  9.5 21.6 %copy-start.1 = (bf16[3,1024,1024]{2,1,0:T(8,128)(2,1)S(1)}, bf16[3,1024,1024]{2,1,0:T(8,128)(2,1)}, u32[]{:S(2)}) copy-start(bf16[3,1024,1024]{2,1,0:T(8,128)(2,1)} %matrix.1) | copy-start | bytes 18874372
  12.2 15.9 %collective-permute-start.5 = (bf16[224,512]{1,0:T(8,128)(2,1)S(1)}, bf16[224,512]{1,0:T(8,128)(2,1)S(1)}, u32[]{:S(2)}, u32[]{:S(2)}) collective-permute-start(bf16[224,512]{1,0:T(8,128)(2,1)S(1)} %get-tuple-element.51.mine.refs_0_), channel_id=1, source_target_pairs={{0,16},{2,18},{4,20},{6,22},{8,24},{10,26},{12,28},{14,30},{16,0},... | collective-permute-start | bytes 688136 | tf_op jit(solution)/shard_map/ppermute | solution.py:574
  13.4 6.4 %collective-permute-start.2 = (f32[3,32,512]{2,1,0:T(8,128)}, f32[3,32,512]{2,1,0:T(8,128)S(1)}, u32[]{:S(2)}, u32[]{:S(2)}) collective-permute-start(f32[3,32,512]{2,1,0:T(8,128)} %get-tuple-element.47), channel_id=1, source_target_pairs={{0,1},{1,0},{2,3},{3,2},{4,5},{5,4},{6,7},{7,6},{8,9},{9,8},{10,11... | collective-permute-start | bytes 589832 | tf_op jit(solution)/shard_map/ppermute | solution.py:500
  14.9 16.1 %collective-permute-start.3 = (bf16[3,48,512]{2,1,0:T(8,128)(2,1)S(1)}, bf16[3,48,512]{2,1,0:T(8,128)(2,1)S(1)}, u32[]{:S(2)}, u32[]{:S(2)}) collective-permute-start(bf16[3,48,512]{2,1,0:T(8,128)(2,1)S(1)} %get-tuple-element.49.refs_1_), channel_id=1, source_target_pairs={{0,16},{2,18},{4,20},{6,22},{8,24},{10,26},{12,28},{14,30},{16,0},... | collective-permute-start | bytes 442376 | tf_op jit(solution)/shard_map/ppermute | solution.py:575
  28.1 42.2 %collective-permute-start.7 = (bf16[3,160,512]{2,1,0:T(8,128)(2,1)S(1)}, bf16[3,160,512]{2,1,0:T(8,128)(2,1)S(1)}, u32[]{:S(2)}, u32[]{:S(2)}) collective-permute-start(bf16[3,160,512]{2,1,0:T(8,128)(2,1)S(1)} %get-tuple-element.59.refs_0_), channel_id=1, source_target_pairs={{0,16},{2,18},{4,20},{6,22},{8,24},{10,26},{12,28},{14,30},{16,0},... | collective-permute-start | bytes 1474568 | tf_op jit(solution)/shard_map/ppermute | solution.py:586
  31.0 38.2 %collective-permute-start.4 = (bf16[3,128,512]{2,1,0:T(8,128)(2,1)S(1)}, bf16[3,128,512]{2,1,0:T(8,128)(2,1)S(1)}, u32[]{:S(2)}, u32[]{:S(2)}) collective-permute-start(bf16[3,128,512]{2,1,0:T(8,128)(2,1)S(1)} %get-tuple-element.50.refs_0_), channel_id=1, source_target_pairs={{0,16},{2,18},{4,20},{6,22},{8,24},{10,26},{12,28},{14,30},{16,0},... | collective-permute-start | bytes 1179656 | tf_op jit(solution)/shard_map/ppermute | solution.py:588
  69.2 15.9 %collective-permute-start.6 = (bf16[3,80,512]{2,1,0:T(8,128)(2,1)S(1)}, bf16[3,80,512]{2,1,0:T(8,128)(2,1)S(1)}, u32[]{:S(2)}, u32[]{:S(2)}) collective-permute-start(bf16[3,80,512]{2,1,0:T(8,128)(2,1)S(1)} %get-tuple-element.58.refs_0_), channel_id=1, source_target_pairs={{0,16},{2,18},{4,20},{6,22},{8,24},{10,26},{12,28},{14,30},{16,0},... | collective-permute-start | bytes 737288 | tf_op jit(solution)/shard_map/ppermute | solution.py:620
  70.2 9.4 %copy-start.3 = (f32[15,8,512]{2,1,0:T(8,128)S(1)}, f32[15,8,512]{2,1,0:T(8,128)}, u32[]{:S(2)}) copy-start(f32[15,8,512]{2,1,0:T(8,128)} %get-tuple-element.39.coef.coef_in.refs_8_.refs_9_) | copy-start | bytes 737284
  71.8 7.8 %collective-permute-start.10 = (bf16[2,3,32,512]{3,2,1,0:T(8,128)(2,1)S(1)}, bf16[2,3,32,512]{3,2,1,0:T(8,128)(2,1)S(1)}, u32[]{:S(2)}, u32[]{:S(2)}) collective-permute-start(bf16[2,3,32,512]{3,2,1,0:T(8,128)(2,1)S(1)} %get-tuple-element.68), channel_id=1, source_target_pairs={{0,1},{1,0},{2,3},{3,2},{4,5},{5,4},{6,7},{7,6},{8,9},{9,8},{10,11... | collective-permute-start | bytes 589832 | tf_op jit(solution)/shard_map/ppermute | solution.py:500
  73.4 5.7 %collective-permute-start.8 = (bf16[2,3,16,512]{3,2,1,0:T(8,128)(2,1)S(1)}, bf16[2,3,16,512]{3,2,1,0:T(8,128)(2,1)S(1)}, u32[]{:S(2)}, u32[]{:S(2)}) collective-permute-start(bf16[2,3,16,512]{3,2,1,0:T(8,128)(2,1)S(1)} %get-tuple-element.66), channel_id=1, source_target_pairs={{0,2},{2,4},{4,6},{6,8},{8,10},{10,12},{12,14},{14,0},{16,18},{18,... | collective-permute-start | bytes 294920 | tf_op jit(solution)/shard_map/ppermute | solution.py:652
  73.4 6.3 %collective-permute-start.9 = (bf16[2,3,16,512]{3,2,1,0:T(8,128)(2,1)S(1)}, bf16[2,3,16,512]{3,2,1,0:T(8,128)(2,1)S(1)}, u32[]{:S(2)}, u32[]{:S(2)}) collective-permute-start(bf16[2,3,16,512]{3,2,1,0:T(8,128)(2,1)S(1)} %get-tuple-element.67), channel_id=1, source_target_pairs={{0,14},{2,0},{4,2},{6,4},{8,6},{10,8},{12,10},{14,12},{16,30},{18,... | collective-permute-start | bytes 294920 | tf_op jit(solution)/shard_map/ppermute | solution.py:653
  76.7 13.8 %collective-permute-start.11 = (bf16[3,32,512]{2,1,0:T(8,128)(2,1)S(1)}, bf16[3,32,512]{2,1,0:T(8,128)(2,1)S(1)}, u32[]{:S(2)}, u32[]{:S(2)}) collective-permute-start(bf16[3,32,512]{2,1,0:T(8,128)(2,1)S(1)} %get-tuple-element.72.mine), channel_id=1, source_target_pairs={{0,16},{2,18},{4,20},{6,22},{8,24},{10,26},{12,28},{14,30},{16,0},... | collective-permute-start | bytes 294920 | tf_op jit(solution)/shard_map/ppermute | solution.py:631

commit v6 on v3

--- a/solution.py
+++ b/solution.py
@@ -129,7 +129,7 @@
 def head_kernel(sizes, conc, cour, diff, ang, rate, smap, flags, *rest):
     na, nz, lo, hi, planes = sizes
     edges = rest[: 1 if planes == 2 else 2]
-    first, last, mid, coef, field, flag_v, cour_v, ang_v, diff_s, rate_s, map_s, flags_s, sems = rest[
+    mid, coef, field, flag_v, cour_v, ang_v, diff_s, rate_s, map_s, flags_s, sems = rest[
         len(edges) :
     ]
     half = nz // 2
@@ -185,8 +185,6 @@
             for t in range(na):
                 edges[0][s, t : t + 1, :] = field[s, t * nz : t * nz + 1, :]
                 edges[1][s, t : t + 1, :] = field[s, (t + 1) * nz - 1 : (t + 1) * nz, :]
-        first[s] = field[s, pl.ds(0, nz), :]
-        last[s] = field[s, pl.ds((na - 1) * nz, nz), :]
 
 
 def inner_kernel(sizes, runs, conc, coef, *rest):
@@ -316,15 +314,22 @@
     return ref[pl.ds(s * rows, rows), :]
 
 
-def radial_kernel(runs, copies, half, weights, keep, mine, theirs, *refs):
+def radial_kernel(plan, copies, half, weights, keep, *refs):
+    n = len(plan)
+    mines, theirs, refs = refs[:n], refs[n : 2 * n], refs[2 * n :]
     n_in = 1 + max((part for part, *_ in copies), default=-1)
     parts, states = refs[:n_in], refs[n_in:]
     for s in range(3):
-        value = both_sides(species_rows(mine, s, runs, half), species_rows(theirs, s, runs, half), weights[s])
-        at = 0
-        for which, begin, place, count in runs:
-            store_run(states[which], s, begin, place, count, at, value, keep, half)
-            at += count
+        for k, runs in enumerate(plan):
+            value = both_sides(
+                species_rows(mines[k], s, runs, half),
+                species_rows(theirs[k], s, runs, half),
+                weights[s],
+            )
+            at = 0
+            for which, begin, place, count in runs:
+                store_run(states[which], s, begin, place, count, at, value, keep, half)
+                at += count
     for part, source, which, place, count in copies:
         to, rows = pl.ds(place * half, count * half), pl.ds(source * half, count * half)
         for ab in range(2):
@@ -355,12 +360,12 @@
             last[ab, s] = pack([mid_end[ab, s, ends_end, :], outer[ab, s, end, :]])
 
 
-def radial_edges_kernel(sizes, runs, copies, half, weights, keep, mine, theirs, *refs):
+def radial_edges_kernel(sizes, plan, copies, half, weights, keep, *refs):
     na, nz, planes = sizes
     n_edges = 1 if planes == 2 else 2
     *edges, first, last, stage = refs[-3 - n_edges :]
     refs = refs[: -3 - n_edges]
-    radial_kernel(runs, copies, half, weights, keep, mine, theirs, *refs)
+    radial_kernel(plan, copies, half, weights, keep, *refs)
     edges_of_state(na, nz, planes, refs[-3], refs[-2], refs[-1], edges, first, last, stage)
 
 
@@ -524,8 +529,8 @@
     quarter = na // 4
     ends = 2
     side = na // 2
-    first_lo, first_hi = ends, side
-    last_lo, last_hi = na - 3 * ends, na - ends
+    a_lo, a_cut, a_hi = ends, na // 4, 3 * na // 8
+    x_hi, y_hi, l_hi = 22 * na // 32, 26 * na // 32, na - ends
     opposite = [(i, (i + count // 2) % count) for i in range(count)]
 
     def dma(*dims):
@@ -534,43 +539,50 @@
     def message(angles):
         return shape(ns, angles * half, nr, dtype=BF16)
 
+    angle_before = lax.ppermute(
+        concentration[:, na - 1], "ang", [(i, (i + 1) % count) for i in range(count)]
+    )
+    angle_after = lax.ppermute(
+        concentration[:, 0], "ang", [(i, (i - 1) % count) for i in range(count)]
+    )
     conc = concentration.reshape(ns, na * nz, nr)
     field = pltpu.VMEM((ns, na * nz, nr), F32)
-    *edges, first, last, mid_a, coef = call(
-        functools.partial(head_kernel, (na, nz, first_lo, first_hi, planes)),
+    *edges, mid_a, coef = call(
+        functools.partial(head_kernel, (na, nz, a_lo, a_cut, planes)),
         [shape(ns, na, nr)] * n_edges
-        + [shape(ns, nz, nr)] * 2
         + [
-            shape(ns * (first_hi - first_lo) * half + na, nr, dtype=BF16),
+            shape(ns * (a_cut - a_lo) * half + na, nr, dtype=BF16),
             shape(RATE + 3, half, nr),
         ],
         [HBM] * 7,
-        [VM] * (n_edges + 4),
+        [VM] * (n_edges + 2),
         [
-            field, pltpu.VMEM((na, LANES), F32), pltpu.VMEM((1, nr), F32), pltpu.VMEM(angular_rate.shape, F32),
-            pltpu.SMEM(axial_diffusion.shape, F32), pltpu.SMEM(rate_constants.shape, F32),
-            pltpu.SMEM(species_map.shape, jnp.int32), pltpu.SMEM(wall_flags.shape, jnp.int32), dma(9),
+            field, pltpu.VMEM((na, LANES), F32), pltpu.VMEM((1, nr), F32),
+            pltpu.VMEM(angular_rate.shape, F32), pltpu.SMEM(axial_diffusion.shape, F32),
+            pltpu.SMEM(rate_constants.shape, F32), pltpu.SMEM(species_map.shape, jnp.int32),
+            pltpu.SMEM(wall_flags.shape, jnp.int32), dma(9),
         ],
         (conc, courant[None], axial_diffusion, angular_rate, rate_constants, species_map, wall_flags),
         58,
     )
+    mid_a, (angle_before, angle_after) = after(mid_a, (angle_before, angle_after))
     opp_a = lax.ppermute(mid_a, "ang", opposite)
     low, high = plane_halos(edges, planes)
-    angle_before = lax.ppermute(last, "ang", [(i, (i + 1) % count) for i in range(count)])
-    angle_after = lax.ppermute(first, "ang", [(i, (i - 1) % count) for i in range(count)])
-    mid_x, mid_l = call(
+    bounds = (a_cut, a_hi, x_hi, y_hi, l_hi)
+    mid_b, mid_x, mid_y, mid_l = call(
         functools.partial(
             inner_kernel,
             (na, nz),
-            ((0, ((first_hi, last_lo - first_hi),)), (1, ((last_lo, last_hi - last_lo),))),
+            tuple((k, ((bounds[k], bounds[k + 1] - bounds[k]),)) for k in range(4)),
         ),
-        [message(last_lo - first_hi), message(last_hi - last_lo)],
+        [message(bounds[k + 1] - bounds[k]) for k in range(4)],
         [ANY, VM],
-        [VM] * 2,
+        [VM] * 4,
         [field, pltpu.SemaphoreType.DMA],
         (conc, coef),
         8,
     )
+    opp_b = lax.ppermute(mid_b, "ang", opposite)
     out1, out2 = call(
         functools.partial(frame_kernel, (na, nz, ends, planes)),
         [message(na // 2), message(na // 2 + 2 * ends)],
@@ -580,9 +592,11 @@
         (conc, angle_before, angle_after, low, high, coef),
         8,
     )
-    (out1, out2), opp_a = after((out1, out2), opp_a)
+    out2, opp_a = after(out2, opp_a)
+    opp_2 = lax.ppermute(out2, "ang", opposite)
+    out1, opp_b = after(out1, opp_b)
     opp_1 = lax.ppermute(out1, "ang", opposite)
-    opp_2 = lax.ppermute(out2, "ang", opposite)
+
     weights, keep = call(
         weights_kernel,
         [shape(ns, nr, 2 * nr, dtype=BF16), shape(2, ns, na, LANES)],
@@ -596,21 +610,26 @@
     def state(angles):
         return shape(2, ns, angles * half, nr)
 
-    count_a = first_hi - first_lo
+    count_a, count_b = a_cut - a_lo, a_hi - a_cut
     (mid_first,) = call(
-        functools.partial(radial_kernel, ((0, first_lo, 0, count_a),), (), half),
-        [state(count_a)],
-        [VM] * 4,
+        functools.partial(
+            radial_kernel,
+            (((0, a_lo, 0, count_a),), ((0, a_cut, count_a, count_b),)),
+            (),
+            half,
+        ),
+        [state(count_a + count_b)],
+        [VM] * 6,
         [VM],
         [],
-        (weights, keep, mid_a, opp_a),
+        (weights, keep, mid_a, mid_b, opp_a, opp_b),
         8,
     )
     opp_1, mid_first = after(opp_1, mid_first)
     mid_x, opp_1 = after(mid_x, opp_1)
     opp_x = lax.ppermute(mid_x, "ang", opposite)
     (outer_first,) = call(
-        functools.partial(radial_kernel, ((0, 0, 0, side),), (), half),
+        functools.partial(radial_kernel, (((0, 0, 0, side),),), (), half),
         [state(side)],
         [VM] * 4,
         [VM],
@@ -618,18 +637,18 @@
         (weights, keep, out1, opp_1),
         8,
     )
-    mid_l, opp_2 = after(mid_l, opp_2)
-    opp_l = lax.ppermute(mid_l, "ang", opposite)
-    runs = ((2, side, side, side), (0, 0, 0, ends), (1, na - ends, 0, ends))
+    mid_y, opp_2 = after(mid_y, opp_2)
+    opp_y = lax.ppermute(mid_y, "ang", opposite)
+    plan = (((2, side, side, side), (0, 0, 0, ends), (1, na - ends, 0, ends)),)
     mid_left, ends_right, outer_state, *rest = call(
         functools.partial(
             radial_edges_kernel,
             (na, nz, planes),
-            runs,
-            ((0, 0, 0, first_lo, count_a), (1, 0, 2, 0, side)),
+            plan,
+            ((0, 0, 0, ends, count_a + count_b), (1, 0, 2, 0, side)),
             half,
         ),
-        [state(side), state(ends), state(na)]
+        [state(a_hi), state(ends), state(na)]
         + [shape(2, ns, na, nr, dtype=BF16)] * n_edges
         + [shape(2, ns, nz, nr, dtype=BF16)] * 2,
         [VM] * 6,
@@ -656,30 +675,39 @@
             {0: 0} if given else None,
         )
 
-    partial = early(((0, first_hi - 1),), 0, mid_left, ())
+    def next_state(mine, theirs, begin, end, copies, parts, base, stop):
+        return call(
+            functools.partial(
+                radial_kernel, (((0, begin, begin - base, end - begin),),), copies, half
+            ),
+            [state(stop - base)],
+            [VM] * (4 + len(parts)),
+            [VM],
+            [],
+            (weights, keep, mine, theirs, *parts),
+            8,
+        )[0]
+
+    partial = early(((0, a_hi - 1),), 0, mid_left, ())
     opp_x, partial = after(opp_x, partial)
-    base = first_hi - 2
-    (mid_right,) = call(
-        functools.partial(
-            radial_kernel,
-            ((0, first_hi, 2, last_lo - first_hi),),
-            ((0, base, 0, 0, 2), (1, 0, 0, na - ends - base, ends)),
-            half,
-        ),
-        [state(na - base)],
-        [VM] * 6,
-        [VM],
-        [],
-        (weights, keep, mid_x, opp_x, mid_left, ends_right),
-        8,
-    )
-
-    partial = early(
-        ((first_hi - 1, last_lo - first_hi), (na - 1, 1)), base, mid_right, (partial,)
-    )
-    wide = last_hi - last_lo + 4
+    mid_l, opp_x = after(mid_l, opp_x)
+    opp_l = lax.ppermute(mid_l, "ang", opposite)
+    base_x = a_hi - 2
+    mid_x_state = next_state(
+        mid_x, opp_x, a_hi, x_hi, ((0, base_x, 0, 0, 2),), (mid_left,), base_x, x_hi
+    )
+    partial = early(((a_hi - 1, x_hi - a_hi),), base_x, mid_x_state, (partial,))
+    opp_y, partial = after(opp_y, partial)
+    base = x_hi - 2
+    mid_right = next_state(
+        mid_y, opp_y, x_hi, y_hi,
+        ((0, base - base_x, 0, 0, 2), (1, 0, 0, na - ends - base, ends)),
+        (mid_x_state, ends_right), base, na,
+    )
+    partial = early(((x_hi - 1, y_hi - x_hi), (na - 1, 1)), base, mid_right, (partial,))
+    wide = l_hi - y_hi + 4
     return call(
-        functools.partial(late_kernel, (na, nz, last_lo, last_hi, base, planes)),
+        functools.partial(late_kernel, (na, nz, y_hi, l_hi, base, planes)),
         shape(ns, na, nz, nr),
         [ANY] + [VM] * 9,
         ANY,

time: 93.9 us -> 93.8 us (level)
  starting transfers between devices: 25.7 us -> 17.1 us
  Pallas kernels: 27.1 us -> 30.9 us
  waiting for transfers between devices: 39.8 us -> 43.3 us
  local copies, waits for them, and re-layouts: 0.95 us -> 2.07 us
    ppermute x1, starting transfers between devices: 8.68 us -> 0.01 us  [per_device(): opp_2 = lax.ppermute(out2, 'ang', opposite)]
    ppermute x2 -> x4, starting transfers between devices: 4.44 us -> 9.01 us  [the longest x1 5.06 us: per_device(): lax.ppermute(concentration[:, 0], 'ang', [(i, (i - 1) % count) for i in r...]
    ppermute x2 -> x4, waiting for transfers between devices: 6.16 us -> 1.68 us  [the longest x1 1.67 us: per_device(): opp_b = lax.ppermute(mid_b, 'ang', opposite)]
    pallas_call x11 -> x13, Pallas kernels: 27.1 us -> 30.9 us  [call(): pl.pallas_call(body, out_shape=out_shape, in_specs=in_specs, out_specs=ou...]
    ppermute x1, waiting for transfers between devices: 29.8 us -> 33.3 us  [per_device(): opp_1 = lax.ppermute(out1, 'ang', opposite)]
    ppermute x1, starting transfers between devices: 4.1 us -> 0.79 us  [per_device(): opp_a = lax.ppermute(mid_a, 'ang', opposite)]
    ppermute x1, starting transfers between devices: 2.92 us -> 0.07 us  [per_device(): opp_l = lax.ppermute(mid_l, 'ang', opposite)]
    ppermute x1, waiting for transfers between devices: 1 us -> 3.21 us  [per_device(): opp_a = lax.ppermute(mid_a, 'ang', opposite)]
  transfers between devices with their start and end apart: 11 -> 13, of which waited for: 4 -> 5; matrix products, arithmetic and copies ran while one was open for 0% -> 0% of each run, Pallas kernels for 21% -> 29%
where the time goes in v6:
time: 93.8 us; the launch traced here: 93.7 us
  waiting for transfers between devices  43.3 us (46%)
  Pallas kernels  30.9 us (33%)
  starting transfers between devices  17.1 us (18%)
  local copies, waits for them, and re-layouts  2.07 us (2%)
    ppermute x1, waiting for transfers between devices, per_device(): opp_1 = lax.ppermute(out1, 'ang', opposite)  33.3 us
    pallas_call x13, Pallas kernels, call(): pl.pallas_call(body, out_shape=out_shape, in_specs=in_specs, out_specs=ou...  30.9 us
    ppermute x1, starting transfers between devices, per_device(): lax.ppermute(concentration[:, 0], 'ang', [(i, (i - 1) % count) for i in r...  5.06 us
    ppermute x1, waiting for transfers between devices, per_device(): angle_before = lax.ppermute(last, 'ang', ring(count, 1))  4.19 us
    ppermute x2, starting transfers between devices, plane_halos(): got = lax.ppermute(edges[0], 'ax', [(0, 1), (1, 0)])  3.77 us
    ppermute x1, waiting for transfers between devices, per_device(): opp_a = lax.ppermute(mid_a, 'ang', opposite)  3.21 us
    ppermute x1, starting transfers between devices, per_device(): opp_b = lax.ppermute(mid_b, 'ang', opposite)  2.2 us
    ppermute x1, starting transfers between devices, per_device(): angle_after = lax.ppermute(first, 'ang', ring(count, -1))  2.18 us
  transfers between devices with their start and end apart: 13, of which 5 were waited for; matrix products, arithmetic and copies ran while one was open for 0% of the time, Pallas kernels for 29%

profile of v6, /device:TPU:0, one launch (start us, length us, event | category | flops | bytes accessed | tf_op | source)
XLA Modules:
  0.0 93.7 jit_solution(16357482910605658172)
XLA Ops:
  0.0 1.1 %slice_bitcast_fusion = (f32[3,16,512]{2,1,0:T(8,128)S(1)}, f32[3,16,512]{2,1,0:T(8,128)S(1)}) fusion(f32[3,32,16,512]{3,2,1,0:T(8,128)} %param.8), kind=kLoop, calls=%fused_computation | loop fusion | bytes 393216 | tf_op jit(solution)/shard_map/squeeze | solution.py:546
  1.6 5.1 %collective-permute-start.1 = (f32[3,16,512]{2,1,0:T(8,128)S(1)}, f32[3,16,512]{2,1,0:T(8,128)S(1)}, u32[]{:S(2)}, u32[]{:S(2)}) collective-permute-start(f32[3,16,512]{2,1,0:T(8,128)S(1)} %get-tuple-element.77), channel_id=1, source_target_pairs={{0,30},{2,0},{4,2},{6,4},{8,6},{10,8},{12,10},{14,12},{16,14},{18,... | collective-permute-start | bytes 294920 | tf_op jit(solution)/shard_map/ppermute | solution.py:545
  6.7 2.8 %shard_map.82 = (f32[3,32,512]{2,1,0:T(8,128)}, bf16[176,512]{1,0:T(8,128)(2,1)}, f32[15,8,512]{2,1,0:T(8,128)}) custom-call(f32[3,512,512]{2,1,0:T(8,128)} %bitcast.10, f32[1,512]{1,0:T(1,128)} %bitcast.13, f32[3]{0:T(128)} %diff.1, f32[3,512]{1,0:T(4,128)} %ang.1, f32[4]{0:T(128)} %rate.1, s32[4,3]{1,0:T(4,128)} %smap.1, s32[3,32]{1,0:T(4,128)} %flags.1), custom_call_target="tpu_custom_call" | custom-call | flops 1 | bytes 1 | tf_op jit(solution)/shard_map/pallas_call | solution.py:24
  9.5 1.9 %collective-permute-start.2 = (f32[3,32,512]{2,1,0:T(8,128)}, f32[3,32,512]{2,1,0:T(8,128)S(1)}, u32[]{:S(2)}, u32[]{:S(2)}) collective-permute-start(f32[3,32,512]{2,1,0:T(8,128)} %get-tuple-element.46), channel_id=1, source_target_pairs={{0,1},{1,0},{2,3},{3,2},{4,5},{5,4},{6,7},{7,6},{8,9},{9,8},{10,11... | collective-permute-start | bytes 589832 | tf_op jit(solution)/shard_map/ppermute | solution.py:509
  13.2 1.7 %shard_map.83 = (bf16[3,32,512]{2,1,0:T(8,128)(2,1)S(1)}, bf16[3,80,512]{2,1,0:T(8,128)(2,1)S(1)}, bf16[3,32,512]{2,1,0:T(8,128)(2,1)S(1)}, bf16[3,32,512]{2,1,0:T(8,128)(2,1)S(1)}) custom-call(f32[3,512,512]{2,1,0:T(8,128)S(1)} %bitcast.11, f32[15,8,512]{2,1,0:T(8,128)S(1)} %copy-done.1), custom_call_target="tpu_custom_call" | custom-call | flops 1 | bytes 1 | tf_op jit(solution)/shard_map/pallas_call | solution.py:24
  14.9 2.2 %collective-permute-start.6 = (bf16[3,32,512]{2,1,0:T(8,128)(2,1)S(1)}, bf16[3,32,512]{2,1,0:T(8,128)(2,1)S(1)}, u32[]{:S(2)}, u32[]{:S(2)}) collective-permute-start(bf16[3,32,512]{2,1,0:T(8,128)(2,1)S(1)} %get-tuple-element.53.refs_1_), channel_id=1, source_target_pairs={{0,16},{2,18},{4,20},{6,22},{8,24},{10,26},{12,28},{14,30},{16,0},... | collective-permute-start | bytes 294920 | tf_op jit(solution)/shard_map/ppermute | solution.py:585
  17.1 3.0 %shard_map.84 = (bf16[3,128,512]{2,1,0:T(8,128)(2,1)S(1)}, bf16[3,160,512]{2,1,0:T(8,128)(2,1)S(1)}) custom-call(f32[3,512,512]{2,1,0:T(8,128)S(1)} %bitcast.12, f32[3,16,512]{2,1,0:T(8,128)S(1)} %collective-permute-done.before, f32[3,16,512]{2,1,0:T(8,128)S(1)} %collective-permute-done.1.after, f32[3,32,512]{2,1,0:T(8,128)S(1)} %collective-permute-done.2.low.high, ...), custom_call_target="tpu_custom_call" | custom-call | flops 1 | bytes 1 | tf_op jit(solution)/shard_map/pallas_call | solution.py:24
  20.1 3.2 %collective-permute-done.3.theirs.refs_2_ = bf16[176,512]{1,0:T(8,128)(2,1)S(1)} collective-permute-done((bf16[176,512]{1,0:T(8,128)(2,1)}, bf16[176,512]{1,0:T(8,128)(2,1)S(1)}, u32[]{:S(2)}, u32[]{:S(2)}) %collective-permute-start.3) | collective-permute-done | bytes 180256 | tf_op jit(solution)/shard_map/ppermute | solution.py:569
  23.3 1.7 %collective-permute-done.6.refs_3_ = bf16[3,32,512]{2,1,0:T(8,128)(2,1)S(1)} collective-permute-done((bf16[3,32,512]{2,1,0:T(8,128)(2,1)S(1)}, bf16[3,32,512]{2,1,0:T(8,128)(2,1)S(1)}, u32[]{:S(2)}, u32[]{:S(2)}) %collective-permute-start.6) | collective-permute-done | bytes 98336 | tf_op jit(solution)/shard_map/ppermute | solution.py:585
  25.0 1.3 %collective-permute-start.7 = (bf16[3,128,512]{2,1,0:T(8,128)(2,1)S(1)}, bf16[3,128,512]{2,1,0:T(8,128)(2,1)S(1)}, u32[]{:S(2)}, u32[]{:S(2)}) collective-permute-start(bf16[3,128,512]{2,1,0:T(8,128)(2,1)S(1)} %get-tuple-element.54.refs_0_), channel_id=1, source_target_pairs={{0,16},{2,18},{4,20},{6,22},{8,24},{10,26},{12,28},{14,30},{16,0},... | collective-permute-start | bytes 1179656 | tf_op jit(solution)/shard_map/ppermute | solution.py:598
  26.2 2.4 %shard_map.85 = (bf16[3,512,1024]{2,1,0:T(8,128)(2,1)S(1)}, f32[2,3,32,128]{3,2,1,0:T(8,128)S(1)}) custom-call(bf16[3,1024,1024]{2,1,0:T(8,128)(2,1)S(1)} %copy-done.3, bf16[176,512]{1,0:T(8,128)(2,1)S(1)} %copy-done.4, bf16[176,512]{1,0:T(8,128)(2,1)S(1)} %collective-permute-done.3.theirs.refs_2_), custom_call_target="tpu_custom_call" | custom-call | flops 1 | bytes 1 | tf_op jit(solution)/shard_map/pallas_call | solution.py:24
  28.7 2.0 %shard_map.86.refs_2_ = f32[2,3,80,512]{3,2,1,0:T(8,128)S(1)} custom-call(bf16[3,512,1024]{2,1,0:T(8,128)(2,1)S(1)} %get-tuple-element.56.weights.refs_0_.refs_1_, f32[2,3,32,128]{3,2,1,0:T(8,128)S(1)} %get-tuple-element.57.keep.refs_1_.refs_2_, bf16[176,512]{1,0:T(8,128)(2,1)S(1)} %copy-done.4, bf16[3,32,512]{2,1,0:T(8,128)(2,1)S(1)} %get-tuple-element.53.refs_1_, ...), custom_call_target="tpu_custom_call" | custom-call | flops 1 | bytes 1 | tf_op jit(solution)/shard_map/pallas_call | solution.py:24
  30.7 33.3 %collective-permute-done.7.refs_1_ = bf16[3,128,512]{2,1,0:T(8,128)(2,1)S(1)} collective-permute-done((bf16[3,128,512]{2,1,0:T(8,128)(2,1)S(1)}, bf16[3,128,512]{2,1,0:T(8,128)(2,1)S(1)}, u32[]{:S(2)}, u32[]{:S(2)}) %collective-permute-start.7) | collective-permute-done | bytes 393248 | tf_op jit(solution)/shard_map/ppermute | solution.py:598
  65.0 1.5 %shard_map.88 = (f32[2,3,96,512]{3,2,1,0:T(8,128)S(1)}, f32[2,3,16,512]{3,2,1,0:T(8,128)S(1)}, f32[2,3,256,512]{3,2,1,0:T(8,128)S(1)}, bf16[2,3,32,512]{3,2,1,0:...) custom-call(bf16[3,512,1024]{2,1,0:T(8,128)(2,1)S(1)} %get-tuple-element.56.weights.refs_0_.refs, ...), custom_call_target="tpu_custom_call" | custom-call | flops 1 | bytes 1 | tf_op jit(solution)/shard_map/pallas_call | solution.py:24
  66.5 1.8 %collective-permute-start.11 = (bf16[2,3,32,512]{3,2,1,0:T(8,128)(2,1)S(1)}, bf16[2,3,32,512]{3,2,1,0:T(8,128)(2,1)S(1)}, u32[]{:S(2)}, u32[]{:S(2)}) collective-permute-start(bf16[2,3,32,512]{3,2,1,0:T(8,128)(2,1)S(1)} %get-tuple-element.68), channel_id=1, source_target_pairs={{0,1},{1,0},{2,3},{3,2},{4,5},{5,4},{6,7},{7,6},{8,9},{9,8},{10,11... | collective-permute-start | bytes 589832 | tf_op jit(solution)/shard_map/ppermute | solution.py:509
  68.4 2.2 %collective-permute-start.10 = (bf16[2,3,16,512]{3,2,1,0:T(8,128)(2,1)S(1)}, bf16[2,3,16,512]{3,2,1,0:T(8,128)(2,1)S(1)}, u32[]{:S(2)}, u32[]{:S(2)}) collective-permute-start(bf16[2,3,16,512]{3,2,1,0:T(8,128)(2,1)S(1)} %get-tuple-element.67), channel_id=1, source_target_pairs={{0,14},{2,0},{4,2},{6,4},{8,6},{10,8},{12,10},{14,12},{16,30},{18,... | collective-permute-start | bytes 294920 | tf_op jit(solution)/shard_map/ppermute | solution.py:663
  70.6 1.2 %collective-permute-start.5 = (bf16[3,32,512]{2,1,0:T(8,128)(2,1)S(1)}, bf16[3,32,512]{2,1,0:T(8,128)(2,1)S(1)}, u32[]{:S(2)}, u32[]{:S(2)}) collective-permute-start(bf16[3,32,512]{2,1,0:T(8,128)(2,1)S(1)} %get-tuple-element.50.refs_0_), channel_id=1, source_target_pairs={{0,16},{2,18},{4,20},{6,22},{8,24},{10,26},{12,28},{14,30},{16,0},... | collective-permute-start | bytes 294920 | tf_op jit(solution)/shard_map/ppermute | solution.py:641
  72.8 4.2 %collective-permute-done.9.refs_4_.refs_5_ = bf16[2,3,16,512]{3,2,1,0:T(8,128)(2,1)S(1)} collective-permute-done((bf16[2,3,16,512]{3,2,1,0:T(8,128)(2,1)S(1)}, bf16[2,3,16,512]{3,2,1,0:T(8,128)(2,1)S(1)}, u32[]{:S(2)}, u32[]{:S(2)}) %collective-permute-start.9) | collective-permute-done | bytes 98336 | tf_op jit(solution)/shard_map/ppermute | solution.py:662
  77.0 3.7 %shard_map.89.refs_0_ = f32[3,32,16,512]{3,2,1,0:T(8,128)} custom-call(bf16[3,512,1024]{2,1,0:T(8,128)(2,1)S(1)} %get-tuple-element.56.weights.refs_0_.refs_1_, f32[2,3,32,128]{3,2,1,0:T(8,128)S(1)} %get-tuple-element.57.keep.refs_1_.refs_2_, f32[2,3,96,512]{3,2,1,0:T(8,128)S(1)} %get-tuple-element.64.refs_2_, ...), custom_call_target="tpu_custom_call" | custom-call | flops 1 | bytes 1 | tf_op jit(solution)/shard_map/pallas_call | solution.py:24
  80.7 1.2 %shard_map.90.refs_3_.refs_2_ = f32[2,3,96,512]{3,2,1,0:T(8,128)S(1)} custom-call(bf16[3,512,1024]{2,1,0:T(8,128)(2,1)S(1)} %get-tuple-element.56.weights.refs_0_.refs_1_, f32[2,3,32,128]{3,2,1,0:T(8,128)S(1)} %get-tuple-element.57.keep.refs_1_.refs_2_, bf16[3,80,512]{2,1,0:T(8,128)(2,1)S(1)} %get-tuple-element.60.refs_0_, ...), custom_call_target="tpu_custom_call" | custom-call | flops 1 | bytes 1 | tf_op jit(solution)/shard_map/pallas_call | solution.py:24
  81.9 3.5 %shard_map.91.refs_0_ = f32[3,32,16,512]{3,2,1,0:T(8,128)} custom-call(f32[3,32,16,512]{3,2,1,0:T(8,128)} %shard_map.89.refs_0_, bf16[3,512,1024]{2,1,0:T(8,128)(2,1)S(1)} %get-tuple-element.56.weights.refs_0_.refs_1_, f32[2,3,32,128]{3,2,1,0:T(8,128)S(1)} %get-tuple-element.57.keep.refs_1_.refs_2_, ...), custom_call_target="tpu_custom_call", output_to_operand_aliasing={{}: (0, {})} | custom-call | flops 1 | bytes 1 | tf_op jit(solution)/shard_map/pallas_call | solution.py:24
  85.4 1.1 %shard_map.92.refs_3_.state = f32[2,3,96,512]{3,2,1,0:T(8,128)S(1)} custom-call(bf16[3,512,1024]{2,1,0:T(8,128)(2,1)S(1)} %get-tuple-element.56.weights.refs_0_.refs_1_, f32[2,3,32,128]{3,2,1,0:T(8,128)S(1)} %get-tuple-element.57.keep.refs_1_.refs_2_, bf16[3,32,512]{2,1,0:T(8,128)(2,1)S(1)} %get-tuple-element.50.refs_0_, ...), custom_call_target="tpu_custom_call" | custom-call | flops 1 | bytes 1 | tf_op jit(solution)/shard_map/pallas_call | solution.py:24
  86.5 3.2 %shard_map.93.given = f32[3,32,16,512]{3,2,1,0:T(8,128)} custom-call(f32[3,32,16,512]{3,2,1,0:T(8,128)} %shard_map.91.refs_0_, bf16[3,512,1024]{2,1,0:T(8,128)(2,1)S(1)} %get-tuple-element.56.weights.refs_0_.refs_1_, f32[2,3,32,128]{3,2,1,0:T(8,128)S(1)} %get-tuple-element.57.keep.refs_1_.refs_2_, ...), custom_call_target="tpu_custom_call", output_to_operand_aliasing={{}: (0, {})} | custom-call | flops 1 | bytes 1 | tf_op jit(solution)/shard_map/pallas_call | solution.py:24
  89.7 3.8 %shard_map.94 = f32[3,32,16,512]{3,2,1,0:T(8,128)} custom-call(f32[3,32,16,512]{3,2,1,0:T(8,128)} %shard_map.93.given, f32[2,3,96,512]{3,2,1,0:T(8,128)S(1)} %shard_map.92.refs_3_.state, bf16[3,512,1024]{2,1,0:T(8,128)(2,1)S(1)} %get-tuple-element.56.weights.refs_0_.refs_1_, ...), custom_call_target="tpu_custom_call", output_to_operand_aliasing={{}: (0, {})} | custom-call | flops 1 | bytes 1 | tf_op jit(solution)/shard_map/pallas_call | solution.py:24
  (26 shorter events, 4.3 us)
Async XLA Ops:
  0.0 12.3 %copy-start = (f32[3,32,16,512]{3,2,1,0:T(8,128)S(1)}, f32[3,32,16,512]{3,2,1,0:T(8,128)}, u32[]{:S(2)}) copy-start(f32[3,32,16,512]{3,2,1,0:T(8,128)} %param.8) | copy-start | bytes 9437188
  1.1 10.3 %collective-permute-start = (f32[3,16,512]{2,1,0:T(8,128)S(1)}, f32[3,16,512]{2,1,0:T(8,128)S(1)}, u32[]{:S(2)}, u32[]{:S(2)}) collective-permute-start(f32[3,16,512]{2,1,0:T(8,128)S(1)} %get-tuple-element.78), channel_id=1, source_target_pairs={{0,2},{2,4},{4,6},{6,8},{8,10},{10,12},{12,14},{14,16},{16,18},{18... | collective-permute-start | bytes 294920 | tf_op jit(solution)/shard_map/ppermute | solution.py:542
  1.6 9.8 %collective-permute-start.1 = (f32[3,16,512]{2,1,0:T(8,128)S(1)}, f32[3,16,512]{2,1,0:T(8,128)S(1)}, u32[]{:S(2)}, u32[]{:S(2)}) collective-permute-start(f32[3,16,512]{2,1,0:T(8,128)S(1)} %get-tuple-element.77), channel_id=1, source_target_pairs={{0,30},{2,0},{4,2},{6,4},{8,6},{10,8},{12,10},{14,12},{16,14},{18,... | collective-permute-start | bytes 294920 | tf_op jit(solution)/shard_map/ppermute | solution.py:545
  9.5 7.6 %collective-permute-start.2 = (f32[3,32,512]{2,1,0:T(8,128)}, f32[3,32,512]{2,1,0:T(8,128)S(1)}, u32[]{:S(2)}, u32[]{:S(2)}) collective-permute-start(f32[3,32,512]{2,1,0:T(8,128)} %get-tuple-element.46), channel_id=1, source_target_pairs={{0,1},{1,0},{2,3},{3,2},{4,5},{5,4},{6,7},{7,6},{8,9},{9,8},{10,11... | collective-permute-start | bytes 589832 | tf_op jit(solution)/shard_map/ppermute | solution.py:509
  11.5 11.9 %collective-permute-start.3 = (bf16[176,512]{1,0:T(8,128)(2,1)}, bf16[176,512]{1,0:T(8,128)(2,1)S(1)}, u32[]{:S(2)}, u32[]{:S(2)}) collective-permute-start(bf16[176,512]{1,0:T(8,128)(2,1)} %get-tuple-element.48.mine.refs_0_), channel_id=1, source_target_pairs={{0,16},{2,18},{4,20},{6,22},{8,24},{10,26},{12,28},{14,30},{16,0},... | collective-permute-start | bytes 540680 | tf_op jit(solution)/shard_map/ppermute | solution.py:569
  12.3 0.9 %copy-start.1 = (f32[15,8,512]{2,1,0:T(8,128)S(1)}, f32[15,8,512]{2,1,0:T(8,128)}, u32[]{:S(2)}) copy-start(f32[15,8,512]{2,1,0:T(8,128)} %get-tuple-element.41.coef.coef_in.refs_8_.refs_9_) | copy-start | bytes 737284
  13.2 13.0 %copy-start.3 = (bf16[3,1024,1024]{2,1,0:T(8,128)(2,1)S(1)}, bf16[3,1024,1024]{2,1,0:T(8,128)(2,1)}, u32[]{:S(2)}) copy-start(bf16[3,1024,1024]{2,1,0:T(8,128)(2,1)} %matrix.1) | copy-start | bytes 18874372
  13.2 13.0 %copy-start.4 = (bf16[176,512]{1,0:T(8,128)(2,1)S(1)}, bf16[176,512]{1,0:T(8,128)(2,1)}, u32[]{:S(2)}) copy-start(bf16[176,512]{1,0:T(8,128)(2,1)} %get-tuple-element.48.mine.refs_0_) | copy-start | bytes 540676
  14.9 10.1 %collective-permute-start.6 = (bf16[3,32,512]{2,1,0:T(8,128)(2,1)S(1)}, bf16[3,32,512]{2,1,0:T(8,128)(2,1)S(1)}, u32[]{:S(2)}, u32[]{:S(2)}) collective-permute-start(bf16[3,32,512]{2,1,0:T(8,128)(2,1)S(1)} %get-tuple-element.53.refs_1_), channel_id=1, source_target_pairs={{0,16},{2,18},{4,20},{6,22},{8,24},{10,26},{12,28},{14,30},{16,0},... | collective-permute-start | bytes 294920 | tf_op jit(solution)/shard_map/ppermute | solution.py:585
  23.3 41.7 %collective-permute-start.4 = (bf16[3,160,512]{2,1,0:T(8,128)(2,1)S(1)}, bf16[3,160,512]{2,1,0:T(8,128)(2,1)S(1)}, u32[]{:S(2)}, u32[]{:S(2)}) collective-permute-start(bf16[3,160,512]{2,1,0:T(8,128)(2,1)S(1)} %get-tuple-element.49.refs_0_), channel_id=1, source_target_pairs={{0,16},{2,18},{4,20},{6,22},{8,24},{10,26},{12,28},{14,30},{16,0},... | collective-permute-start | bytes 1474568 | tf_op jit(solution)/shard_map/ppermute | solution.py:596
  25.0 39.0 %collective-permute-start.7 = (bf16[3,128,512]{2,1,0:T(8,128)(2,1)S(1)}, bf16[3,128,512]{2,1,0:T(8,128)(2,1)S(1)}, u32[]{:S(2)}, u32[]{:S(2)}) collective-permute-start(bf16[3,128,512]{2,1,0:T(8,128)(2,1)S(1)} %get-tuple-element.54.refs_0_), channel_id=1, source_target_pairs={{0,16},{2,18},{4,20},{6,22},{8,24},{10,26},{12,28},{14,30},{16,0},... | collective-permute-start | bytes 1179656 | tf_op jit(solution)/shard_map/ppermute | solution.py:598
  64.0 16.7 %collective-permute-start.8 = (bf16[3,80,512]{2,1,0:T(8,128)(2,1)S(1)}, bf16[3,80,512]{2,1,0:T(8,128)(2,1)S(1)}, u32[]{:S(2)}, u32[]{:S(2)}) collective-permute-start(bf16[3,80,512]{2,1,0:T(8,128)(2,1)S(1)} %get-tuple-element.60.refs_0_), channel_id=1, source_target_pairs={{0,16},{2,18},{4,20},{6,22},{8,24},{10,26},{12,28},{14,30},{16,0},... | collective-permute-start | bytes 737288 | tf_op jit(solution)/shard_map/ppermute | solution.py:630
  65.0 12.0 %copy-start.2 = (f32[15,8,512]{2,1,0:T(8,128)S(1)}, f32[15,8,512]{2,1,0:T(8,128)}, u32[]{:S(2)}) copy-start(f32[15,8,512]{2,1,0:T(8,128)} %get-tuple-element.41.coef.coef_in.refs_8_.refs_9_) | copy-start | bytes 737284
  66.5 10.4 %collective-permute-start.11 = (bf16[2,3,32,512]{3,2,1,0:T(8,128)(2,1)S(1)}, bf16[2,3,32,512]{3,2,1,0:T(8,128)(2,1)S(1)}, u32[]{:S(2)}, u32[]{:S(2)}) collective-permute-start(bf16[2,3,32,512]{3,2,1,0:T(8,128)(2,1)S(1)} %get-tuple-element.68), channel_id=1, source_target_pairs={{0,1},{1,0},{2,3},{3,2},{4,5},{5,4},{6,7},{7,6},{8,9},{9,8},{10,11... | collective-permute-start | bytes 589832 | tf_op jit(solution)/shard_map/ppermute | solution.py:509
  68.4 4.4 %collective-permute-start.10 = (bf16[2,3,16,512]{3,2,1,0:T(8,128)(2,1)S(1)}, bf16[2,3,16,512]{3,2,1,0:T(8,128)(2,1)S(1)}, u32[]{:S(2)}, u32[]{:S(2)}) collective-permute-start(bf16[2,3,16,512]{3,2,1,0:T(8,128)(2,1)S(1)} %get-tuple-element.67), channel_id=1, source_target_pairs={{0,14},{2,0},{4,2},{6,4},{8,6},{10,8},{12,10},{14,12},{16,30},{18,... | collective-permute-start | bytes 294920 | tf_op jit(solution)/shard_map/ppermute | solution.py:663
  70.6 6.4 %collective-permute-start.9 = (bf16[2,3,16,512]{3,2,1,0:T(8,128)(2,1)S(1)}, bf16[2,3,16,512]{3,2,1,0:T(8,128)(2,1)S(1)}, u32[]{:S(2)}, u32[]{:S(2)}) collective-permute-start(bf16[2,3,16,512]{3,2,1,0:T(8,128)(2,1)S(1)} %get-tuple-element.66), channel_id=1, source_target_pairs={{0,2},{2,4},{4,6},{6,8},{8,10},{10,12},{12,14},{14,0},{16,18},{18,... | collective-permute-start | bytes 294920 | tf_op jit(solution)/shard_map/ppermute | solution.py:662
  70.6 14.9 %collective-permute-start.5 = (bf16[3,32,512]{2,1,0:T(8,128)(2,1)S(1)}, bf16[3,32,512]{2,1,0:T(8,128)(2,1)S(1)}, u32[]{:S(2)}, u32[]{:S(2)}) collective-permute-start(bf16[3,32,512]{2,1,0:T(8,128)(2,1)S(1)} %get-tuple-element.50.refs_0_), channel_id=1, source_target_pairs={{0,16},{2,18},{4,20},{6,22},{8,24},{10,26},{12,28},{14,30},{16,0},... | collective-permute-start | bytes 294920 | tf_op jit(solution)/shard_map/ppermute | solution.py:641
  80.7 9.0 %collective-permute-start.12 = (bf16[3,32,512]{2,1,0:T(8,128)(2,1)S(1)}, bf16[3,32,512]{2,1,0:T(8,128)(2,1)S(1)}, u32[]{:S(2)}, u32[]{:S(2)}) collective-permute-start(bf16[3,32,512]{2,1,0:T(8,128)(2,1)S(1)} %get-tuple-element.76.mine), channel_id=1, source_target_pairs={{0,16},{2,18},{4,20},{6,22},{8,24},{10,26},{12,28},{14,30},{16,0},... | collective-permute-start | bytes 294920 | tf_op jit(solution)/shard_map/ppermute | solution.py:694

commit v7 on v6

--- a/solution.py
+++ b/solution.py
@@ -529,8 +529,8 @@
     quarter = na // 4
     ends = 2
     side = na // 2
-    a_lo, a_cut, a_hi = ends, na // 4, 3 * na // 8
-    x_hi, y_hi, l_hi = 22 * na // 32, 26 * na // 32, na - ends
+    a_lo, a_hi = ends, na // 4
+    x_hi, y_hi, l_hi = 18 * na // 32, 26 * na // 32, na - ends
     opposite = [(i, (i + count // 2) % count) for i in range(count)]
 
     def dma(*dims):
@@ -548,10 +548,10 @@
     conc = concentration.reshape(ns, na * nz, nr)
     field = pltpu.VMEM((ns, na * nz, nr), F32)
     *edges, mid_a, coef = call(
-        functools.partial(head_kernel, (na, nz, a_lo, a_cut, planes)),
+        functools.partial(head_kernel, (na, nz, a_lo, a_hi, planes)),
         [shape(ns, na, nr)] * n_edges
         + [
-            shape(ns * (a_cut - a_lo) * half + na, nr, dtype=BF16),
+            shape(ns * (a_hi - a_lo) * half + na, nr, dtype=BF16),
             shape(RATE + 3, half, nr),
         ],
         [HBM] * 7,
@@ -568,21 +568,20 @@
     mid_a, (angle_before, angle_after) = after(mid_a, (angle_before, angle_after))
     opp_a = lax.ppermute(mid_a, "ang", opposite)
     low, high = plane_halos(edges, planes)
-    bounds = (a_cut, a_hi, x_hi, y_hi, l_hi)
-    mid_b, mid_x, mid_y, mid_l = call(
+    bounds = (a_hi, x_hi, y_hi, l_hi)
+    mid_x, mid_y, mid_l = call(
         functools.partial(
             inner_kernel,
             (na, nz),
-            tuple((k, ((bounds[k], bounds[k + 1] - bounds[k]),)) for k in range(4)),
+            tuple((k, ((bounds[k], bounds[k + 1] - bounds[k]),)) for k in range(3)),
         ),
-        [message(bounds[k + 1] - bounds[k]) for k in range(4)],
+        [message(bounds[k + 1] - bounds[k]) for k in range(3)],
         [ANY, VM],
-        [VM] * 4,
+        [VM] * 3,
         [field, pltpu.SemaphoreType.DMA],
         (conc, coef),
         8,
     )
-    opp_b = lax.ppermute(mid_b, "ang", opposite)
     out1, out2 = call(
         functools.partial(frame_kernel, (na, nz, ends, planes)),
         [message(na // 2), message(na // 2 + 2 * ends)],
@@ -592,9 +591,8 @@
         (conc, angle_before, angle_after, low, high, coef),
         8,
     )
-    out2, opp_a = after(out2, opp_a)
+    (out1, out2), opp_a = after((out1, out2), opp_a)
     opp_2 = lax.ppermute(out2, "ang", opposite)
-    out1, opp_b = after(out1, opp_b)
     opp_1 = lax.ppermute(out1, "ang", opposite)
 
     weights, keep = call(
@@ -610,19 +608,14 @@
     def state(angles):
         return shape(2, ns, angles * half, nr)
 
-    count_a, count_b = a_cut - a_lo, a_hi - a_cut
+    count_a = a_hi - a_lo
     (mid_first,) = call(
-        functools.partial(
-            radial_kernel,
-            (((0, a_lo, 0, count_a),), ((0, a_cut, count_a, count_b),)),
-            (),
-            half,
-        ),
-        [state(count_a + count_b)],
-        [VM] * 6,
+        functools.partial(radial_kernel, (((0, a_lo, 0, count_a),),), (), half),
+        [state(count_a)],
+        [VM] * 4,
         [VM],
         [],
-        (weights, keep, mid_a, mid_b, opp_a, opp_b),
+        (weights, keep, mid_a, opp_a),
         8,
     )
     opp_1, mid_first = after(opp_1, mid_first)
@@ -645,7 +638,7 @@
             radial_edges_kernel,
             (na, nz, planes),
             plan,
-            ((0, 0, 0, ends, count_a + count_b), (1, 0, 2, 0, side)),
+            ((0, 0, 0, ends, count_a), (1, 0, 2, 0, side)),
             half,
         ),
         [state(a_hi), state(ends), state(na)]
@@ -688,20 +681,17 @@
             8,
         )[0]
 
-    partial = early(((0, a_hi - 1),), 0, mid_left, ())
-    opp_x, partial = after(opp_x, partial)
     mid_l, opp_x = after(mid_l, opp_x)
     opp_l = lax.ppermute(mid_l, "ang", opposite)
-    base_x = a_hi - 2
     mid_x_state = next_state(
-        mid_x, opp_x, a_hi, x_hi, ((0, base_x, 0, 0, 2),), (mid_left,), base_x, x_hi
-    )
-    partial = early(((a_hi - 1, x_hi - a_hi),), base_x, mid_x_state, (partial,))
+        mid_x, opp_x, a_hi, x_hi, ((0, 0, 0, 0, a_hi),), (mid_left,), 0, x_hi
+    )
+    partial = early(((0, x_hi - 1),), 0, mid_x_state, ())
     opp_y, partial = after(opp_y, partial)
     base = x_hi - 2
     mid_right = next_state(
         mid_y, opp_y, x_hi, y_hi,
-        ((0, base - base_x, 0, 0, 2), (1, 0, 0, na - ends - base, ends)),
+        ((0, base, 0, 0, 2), (1, 0, 0, na - ends - base, ends)),
         (mid_x_state, ends_right), base, na,
     )
     partial = early(((x_hi - 1, y_hi - x_hi), (na - 1, 1)), base, mid_right, (partial,))

time: 93.8 us -> 92.9 us (level)
  Pallas kernels: 30.9 us -> 28.1 us
  starting transfers between devices: 17.1 us -> 18.5 us
    ppermute x1, waiting for transfers between devices: 0.01 us -> 14.8 us  [per_device(): opp_2 = lax.ppermute(out2, 'ang', opposite)]
    ppermute x1, waiting for transfers between devices: 33.3 us -> 22.6 us  [per_device(): opp_1 = lax.ppermute(out1, 'ang', opposite)]
    ppermute x1, waiting for transfers between devices: 4.19 us -> 0.01 us  [per_device(): angle_before = lax.ppermute(last, 'ang', ring(count, 1))]
    ppermute x2, waiting for transfers between devices: 0.01 us -> 3.21 us  [plane_halos(): got = lax.ppermute(edges[0], 'ax', [(0, 1), (1, 0)])]
    ppermute x1, starting transfers between devices: 0.01 us -> 2.9 us  [per_device(): opp_2 = lax.ppermute(out2, 'ang', opposite)]
    ppermute x1, starting transfers between devices: 0.07 us -> 2.92 us  [per_device(): opp_l = lax.ppermute(mid_l, 'ang', opposite)]
    pallas_call x13 -> x12, Pallas kernels: 30.9 us -> 28.1 us  [call(): pl.pallas_call(body, out_shape=out_shape, in_specs=in_specs, out_specs=ou...]
    ppermute x1 -> x0, starting transfers between devices: 2.2 us -> none  [per_device(): opp_b = lax.ppermute(mid_b, 'ang', opposite)]
  transfers between devices with their start and end apart: 13 -> 12, of which waited for: 5 -> 5; matrix products, arithmetic and copies ran while one was open for 0% -> 0% of each run, Pallas kernels for 29% -> 26%
where the time goes in v7:
time: 92.9 us; the launch traced here: 92.1 us
  waiting for transfers between devices  43.1 us (46%)
  Pallas kernels  28.1 us (30%)
  starting transfers between devices  18.5 us (20%)
  local copies, waits for them, and re-layouts  2.06 us (2%)
    pallas_call x12, Pallas kernels, call(): pl.pallas_call(body, out_shape=out_shape, in_specs=in_specs, out_specs=ou...  28.1 us
    ppermute x1, waiting for transfers between devices, per_device(): opp_1 = lax.ppermute(out1, 'ang', opposite)  22.6 us
    ppermute x1, waiting for transfers between devices, per_device(): opp_2 = lax.ppermute(out2, 'ang', opposite)  14.8 us
    ppermute x1, starting transfers between devices, per_device(): lax.ppermute(concentration[:, 0], 'ang', [(i, (i - 1) % count) for i in r...  5.06 us
    ppermute x2, starting transfers between devices, plane_halos(): got = lax.ppermute(edges[0], 'ax', [(0, 1), (1, 0)])  3.66 us
    ppermute x2, waiting for transfers between devices, plane_halos(): got = lax.ppermute(edges[0], 'ax', [(0, 1), (1, 0)])  3.21 us
    ppermute x1, starting transfers between devices, per_device(): opp_l = lax.ppermute(mid_l, 'ang', opposite)  2.92 us
    ppermute x1, starting transfers between devices, per_device(): opp_2 = lax.ppermute(out2, 'ang', opposite)  2.9 us
  transfers between devices with their start and end apart: 12, of which 5 were waited for; matrix products, arithmetic and copies ran while one was open for 0% of the time, Pallas kernels for 26%

profile of v7, /device:TPU:0, one launch (start us, length us, event | category | flops | bytes accessed | tf_op | source)
XLA Modules:
  0.0 92.1 jit_solution(7601166422488000686)
XLA Ops:
  0.0 1.1 %slice_bitcast_fusion = (f32[3,16,512]{2,1,0:T(8,128)S(1)}, f32[3,16,512]{2,1,0:T(8,128)S(1)}) fusion(f32[3,32,16,512]{3,2,1,0:T(8,128)} %param.8), kind=kLoop, calls=%fused_computation | loop fusion | bytes 393216 | tf_op jit(solution)/shard_map/squeeze | solution.py:546
  1.6 5.1 %collective-permute-start.1 = (f32[3,16,512]{2,1,0:T(8,128)S(1)}, f32[3,16,512]{2,1,0:T(8,128)S(1)}, u32[]{:S(2)}, u32[]{:S(2)}) collective-permute-start(f32[3,16,512]{2,1,0:T(8,128)S(1)} %get-tuple-element.69), channel_id=1, source_target_pairs={{0,30},{2,0},{4,2},{6,4},{8,6},{10,8},{12,10},{14,12},{16,14},{18,... | collective-permute-start | bytes 294920 | tf_op jit(solution)/shard_map/ppermute | solution.py:545
  6.7 2.8 %shard_map.82 = (f32[3,32,512]{2,1,0:T(8,128)}, bf16[176,512]{1,0:T(8,128)(2,1)}, f32[15,8,512]{2,1,0:T(8,128)}) custom-call(f32[3,512,512]{2,1,0:T(8,128)} %bitcast.10, f32[1,512]{1,0:T(1,128)} %bitcast.13, f32[3]{0:T(128)} %diff.1, f32[3,512]{1,0:T(4,128)} %ang.1, f32[4]{0:T(128)} %rate.1, s32[4,3]{1,0:T(4,128)} %smap.1, s32[3,32]{1,0:T(4,128)} %flags.1), custom_call_target="tpu_custom_call" | custom-call | flops 1 | bytes 1 | tf_op jit(solution)/shard_map/pallas_call | solution.py:24
  9.5 1.9 %collective-permute-start.2 = (f32[3,32,512]{2,1,0:T(8,128)}, f32[3,32,512]{2,1,0:T(8,128)S(1)}, u32[]{:S(2)}, u32[]{:S(2)}) collective-permute-start(f32[3,32,512]{2,1,0:T(8,128)} %get-tuple-element.42), channel_id=1, source_target_pairs={{0,1},{1,0},{2,3},{3,2},{4,5},{5,4},{6,7},{7,6},{8,9},{9,8},{10,11... | collective-permute-start | bytes 589832 | tf_op jit(solution)/shard_map/ppermute | solution.py:509
  12.3 3.2 %collective-permute-done.2.low.high = f32[3,32,512]{2,1,0:T(8,128)S(1)} collective-permute-done((f32[3,32,512]{2,1,0:T(8,128)}, f32[3,32,512]{2,1,0:T(8,128)S(1)}, u32[]{:S(2)}, u32[]{:S(2)}) %collective-permute-start.2) | collective-permute-done | bytes 196640 | tf_op jit(solution)/shard_map/ppermute | solution.py:509
  16.4 3.0 %shard_map.84 = (bf16[3,128,512]{2,1,0:T(8,128)(2,1)S(1)}, bf16[3,160,512]{2,1,0:T(8,128)(2,1)S(1)}) custom-call(f32[3,512,512]{2,1,0:T(8,128)S(1)} %bitcast.11, f32[3,16,512]{2,1,0:T(8,128)S(1)} %collective-permute-done.before, f32[3,16,512]{2,1,0:T(8,128)S(1)} %collective-permute-done.1.after, f32[3,32,512]{2,1,0:T(8,128)S(1)} %collective-permute-done.2.low.high, ...), custom_call_target="tpu_custom_call" | custom-call | flops 1 | bytes 1 | tf_op jit(solution)/shard_map/pallas_call | solution.py:24
  19.4 1.4 %collective-permute-done.3.theirs.refs_1_ = bf16[176,512]{1,0:T(8,128)(2,1)S(1)} collective-permute-done((bf16[176,512]{1,0:T(8,128)(2,1)}, bf16[176,512]{1,0:T(8,128)(2,1)S(1)}, u32[]{:S(2)}, u32[]{:S(2)}) %collective-permute-start.3) | collective-permute-done | bytes 180256 | tf_op jit(solution)/shard_map/ppermute | solution.py:569
  20.8 2.9 %collective-permute-start.4 = (bf16[3,160,512]{2,1,0:T(8,128)(2,1)S(1)}, bf16[3,160,512]{2,1,0:T(8,128)(2,1)S(1)}, u32[]{:S(2)}, u32[]{:S(2)}) collective-permute-start(bf16[3,160,512]{2,1,0:T(8,128)(2,1)S(1)} %get-tuple-element.46.refs_0_), channel_id=1, source_target_pairs={{0,16},{2,18},{4,20},{6,22},{8,24},{10,26},{12,28},{14,30},{16,0},... | collective-permute-start | bytes 1474568 | tf_op jit(solution)/shard_map/ppermute | solution.py:595
  23.7 1.7 %shard_map.83 = (bf16[3,80,512]{2,1,0:T(8,128)(2,1)S(1)}, bf16[3,64,512]{2,1,0:T(8,128)(2,1)S(1)}, bf16[3,32,512]{2,1,0:T(8,128)(2,1)S(1)}) custom-call(f32[3,512,512]{2,1,0:T(8,128)S(1)} %bitcast.12, f32[15,8,512]{2,1,0:T(8,128)S(1)} %copy-done.2), custom_call_target="tpu_custom_call" | custom-call | flops 1 | bytes 1 | tf_op jit(solution)/shard_map/pallas_call | solution.py:24
  25.4 2.4 %shard_map.85 = (bf16[3,512,1024]{2,1,0:T(8,128)(2,1)S(1)}, f32[2,3,32,128]{3,2,1,0:T(8,128)S(1)}) custom-call(bf16[3,1024,1024]{2,1,0:T(8,128)(2,1)S(1)} %copy-done.1, bf16[176,512]{1,0:T(8,128)(2,1)S(1)} %copy-done.4, bf16[176,512]{1,0:T(8,128)(2,1)S(1)} %collective-permute-done.3.theirs.refs_1_), custom_call_target="tpu_custom_call" | custom-call | flops 1 | bytes 1 | tf_op jit(solution)/shard_map/pallas_call | solution.py:24
  27.9 1.1 %shard_map.86.refs_2_ = f32[2,3,48,512]{3,2,1,0:T(8,128)S(1)} custom-call(bf16[3,512,1024]{2,1,0:T(8,128)(2,1)S(1)} %get-tuple-element.49.weights.refs_0_.refs_1_, f32[2,3,32,128]{3,2,1,0:T(8,128)S(1)} %get-tuple-element.50.keep.refs_1_.refs_2_, bf16[176,512]{1,0:T(8,128)(2,1)S(1)} %copy-done.4, bf16[176,512]{1,0:T(8,128)(2,1)S(1)} %collective-permute-done.3.theirs.refs_1_), custom_call_target="tpu_custom_call" | custom-call | flops 1 | bytes 1 | tf_op jit(solution)/shard_map/pallas_call | solution.py:24
  29.0 22.6 %collective-permute-done.6.refs_1_ = bf16[3,128,512]{2,1,0:T(8,128)(2,1)S(1)} collective-permute-done((bf16[3,128,512]{2,1,0:T(8,128)(2,1)S(1)}, bf16[3,128,512]{2,1,0:T(8,128)(2,1)S(1)}, u32[]{:S(2)}, u32[]{:S(2)}) %collective-permute-start.6) | collective-permute-done | bytes 393248 | tf_op jit(solution)/shard_map/ppermute | solution.py:596
  51.5 1.0 %shard_map.87.refs_3_ = f32[2,3,128,512]{3,2,1,0:T(8,128)S(1)} custom-call(bf16[3,512,1024]{2,1,0:T(8,128)(2,1)S(1)} %get-tuple-element.49.weights.refs_0_.refs_1_, f32[2,3,32,128]{3,2,1,0:T(8,128)S(1)} %get-tuple-element.50.keep.refs_1_.refs_2_, bf16[3,128,512]{2,1,0:T(8,128)(2,1)S(1)} %get-tuple-element.52.refs_0_, ...), custom_call_target="tpu_custom_call" | custom-call | flops 1 | bytes 1 | tf_op jit(solution)/shard_map/pallas_call | solution.py:24
  52.5 14.8 %collective-permute-done.4.refs_1_ = bf16[3,160,512]{2,1,0:T(8,128)(2,1)S(1)} collective-permute-done((bf16[3,160,512]{2,1,0:T(8,128)(2,1)S(1)}, bf16[3,160,512]{2,1,0:T(8,128)(2,1)S(1)}, u32[]{:S(2)}, u32[]{:S(2)}) %collective-permute-start.4) | collective-permute-done | bytes 491552 | tf_op jit(solution)/shard_map/ppermute | solution.py:595
  67.3 1.5 %shard_map.88 = (f32[2,3,64,512]{3,2,1,0:T(8,128)S(1)}, f32[2,3,16,512]{3,2,1,0:T(8,128)S(1)}, f32[2,3,256,512]{3,2,1,0:T(8,128)S(1)}, bf16[2,3,32,512]{3,2,1,0:...) custom-call(bf16[3,512,1024]{2,1,0:T(8,128)(2,1)S(1)} %get-tuple-element.49.weights.refs_0_.refs, ...), custom_call_target="tpu_custom_call" | custom-call | flops 1 | bytes 1 | tf_op jit(solution)/shard_map/pallas_call | solution.py:24
  68.8 1.7 %collective-permute-start.10 = (bf16[2,3,32,512]{3,2,1,0:T(8,128)(2,1)S(1)}, bf16[2,3,32,512]{3,2,1,0:T(8,128)(2,1)S(1)}, u32[]{:S(2)}, u32[]{:S(2)}) collective-permute-start(bf16[2,3,32,512]{3,2,1,0:T(8,128)(2,1)S(1)} %get-tuple-element.64), channel_id=1, source_target_pairs={{0,1},{1,0},{2,3},{3,2},{4,5},{5,4},{6,7},{7,6},{8,9},{9,8},{10,11... | collective-permute-start | bytes 589832 | tf_op jit(solution)/shard_map/ppermute | solution.py:509
  70.6 2.6 %collective-permute-start.9 = (bf16[2,3,16,512]{3,2,1,0:T(8,128)(2,1)S(1)}, bf16[2,3,16,512]{3,2,1,0:T(8,128)(2,1)S(1)}, u32[]{:S(2)}, u32[]{:S(2)}) collective-permute-start(bf16[2,3,16,512]{3,2,1,0:T(8,128)(2,1)S(1)} %get-tuple-element.63), channel_id=1, source_target_pairs={{0,14},{2,0},{4,2},{6,4},{8,6},{10,8},{12,10},{14,12},{16,30},{18,... | collective-permute-start | bytes 294920 | tf_op jit(solution)/shard_map/ppermute | solution.py:656
  73.2 2.9 %collective-permute-start.11 = (bf16[3,32,512]{2,1,0:T(8,128)(2,1)S(1)}, bf16[3,32,512]{2,1,0:T(8,128)(2,1)S(1)}, u32[]{:S(2)}, u32[]{:S(2)}) collective-permute-start(bf16[3,32,512]{2,1,0:T(8,128)(2,1)S(1)} %get-tuple-element.68.mine), channel_id=1, source_target_pairs={{0,16},{2,18},{4,20},{6,22},{8,24},{10,26},{12,28},{14,30},{16,0},... | collective-permute-start | bytes 294920 | tf_op jit(solution)/shard_map/ppermute | solution.py:685
  76.1 1.2 %shard_map.89.refs_2_ = f32[2,3,144,512]{3,2,1,0:T(8,128)S(1)} custom-call(bf16[3,512,1024]{2,1,0:T(8,128)(2,1)S(1)} %get-tuple-element.49.weights.refs_0_.refs_1_, f32[2,3,32,128]{3,2,1,0:T(8,128)S(1)} %get-tuple-element.50.keep.refs_1_.refs_2_, bf16[3,80,512]{2,1,0:T(8,128)(2,1)S(1)} %get-tuple-element.54.refs_0_, ...), custom_call_target="tpu_custom_call" | custom-call | flops 1 | bytes 1 | tf_op jit(solution)/shard_map/pallas_call | solution.py:24
  77.4 4.5 %shard_map.90.refs_0_ = f32[3,32,16,512]{3,2,1,0:T(8,128)} custom-call(bf16[3,512,1024]{2,1,0:T(8,128)(2,1)S(1)} %get-tuple-element.49.weights.refs_0_.refs_1_, f32[2,3,32,128]{3,2,1,0:T(8,128)S(1)} %get-tuple-element.50.keep.refs_1_.refs_2_, f32[2,3,144,512]{3,2,1,0:T(8,128)S(1)} %shard_map.89.refs_2_, ...), custom_call_target="tpu_custom_call" | custom-call | flops 1 | bytes 1 | tf_op jit(solution)/shard_map/pallas_call | solution.py:24
  81.9 1.2 %collective-permute-done.5.refs_1_ = bf16[3,64,512]{2,1,0:T(8,128)(2,1)S(1)} collective-permute-done((bf16[3,64,512]{2,1,0:T(8,128)(2,1)S(1)}, bf16[3,64,512]{2,1,0:T(8,128)(2,1)S(1)}, u32[]{:S(2)}, u32[]{:S(2)}) %collective-permute-start.5) | collective-permute-done | bytes 196640 | tf_op jit(solution)/shard_map/ppermute | solution.py:634
  83.0 1.2 %shard_map.91.refs_3_.state = f32[2,3,128,512]{3,2,1,0:T(8,128)S(1)} custom-call(bf16[3,512,1024]{2,1,0:T(8,128)(2,1)S(1)} %get-tuple-element.49.weights.refs_0_.refs_1_, f32[2,3,32,128]{3,2,1,0:T(8,128)S(1)} %get-tuple-element.50.keep.refs_1_.refs_2_, bf16[3,64,512]{2,1,0:T(8,128)(2,1)S(1)} %get-tuple-element.47.refs_0_, ...), custom_call_target="tpu_custom_call" | custom-call | flops 1 | bytes 1 | tf_op jit(solution)/shard_map/pallas_call | solution.py:24
  84.2 3.9 %shard_map.92.given = f32[3,32,16,512]{3,2,1,0:T(8,128)} custom-call(f32[3,32,16,512]{3,2,1,0:T(8,128)} %shard_map.90.refs_0_, bf16[3,512,1024]{2,1,0:T(8,128)(2,1)S(1)} %get-tuple-element.49.weights.refs_0_.refs_1_, f32[2,3,32,128]{3,2,1,0:T(8,128)S(1)} %get-tuple-element.50.keep.refs_1_.refs_2_, ...), custom_call_target="tpu_custom_call", output_to_operand_aliasing={{}: (0, {})} | custom-call | flops 1 | bytes 1 | tf_op jit(solution)/shard_map/pallas_call | solution.py:24
  88.1 3.8 %shard_map.93 = f32[3,32,16,512]{3,2,1,0:T(8,128)} custom-call(f32[3,32,16,512]{3,2,1,0:T(8,128)} %shard_map.92.given, f32[2,3,128,512]{3,2,1,0:T(8,128)S(1)} %shard_map.91.refs_3_.state, bf16[3,512,1024]{2,1,0:T(8,128)(2,1)S(1)} %get-tuple-element.49.weights.refs_0_.refs_1_, ...), custom_call_target="tpu_custom_call", output_to_operand_aliasing={{}: (0, {})} | custom-call | flops 1 | bytes 1 | tf_op jit(solution)/shard_map/pallas_call | solution.py:24
  (23 shorter events, 2.3 us)
Async XLA Ops:
  0.0 15.5 %copy-start = (f32[3,32,16,512]{3,2,1,0:T(8,128)S(1)}, f32[3,32,16,512]{3,2,1,0:T(8,128)}, u32[]{:S(2)}) copy-start(f32[3,32,16,512]{3,2,1,0:T(8,128)} %param.8) | copy-start | bytes 9437188
  1.1 10.3 %collective-permute-start = (f32[3,16,512]{2,1,0:T(8,128)S(1)}, f32[3,16,512]{2,1,0:T(8,128)S(1)}, u32[]{:S(2)}, u32[]{:S(2)}) collective-permute-start(f32[3,16,512]{2,1,0:T(8,128)S(1)} %get-tuple-element.70), channel_id=1, source_target_pairs={{0,2},{2,4},{4,6},{6,8},{8,10},{10,12},{12,14},{14,16},{16,18},{18... | collective-permute-start | bytes 294920 | tf_op jit(solution)/shard_map/ppermute | solution.py:542
  1.6 9.8 %collective-permute-start.1 = (f32[3,16,512]{2,1,0:T(8,128)S(1)}, f32[3,16,512]{2,1,0:T(8,128)S(1)}, u32[]{:S(2)}, u32[]{:S(2)}) collective-permute-start(f32[3,16,512]{2,1,0:T(8,128)S(1)} %get-tuple-element.69), channel_id=1, source_target_pairs={{0,30},{2,0},{4,2},{6,4},{8,6},{10,8},{12,10},{14,12},{16,14},{18,... | collective-permute-start | bytes 294920 | tf_op jit(solution)/shard_map/ppermute | solution.py:545
  9.5 5.9 %collective-permute-start.2 = (f32[3,32,512]{2,1,0:T(8,128)}, f32[3,32,512]{2,1,0:T(8,128)S(1)}, u32[]{:S(2)}, u32[]{:S(2)}) collective-permute-start(f32[3,32,512]{2,1,0:T(8,128)} %get-tuple-element.42), channel_id=1, source_target_pairs={{0,1},{1,0},{2,3},{3,2},{4,5},{5,4},{6,7},{7,6},{8,9},{9,8},{10,11... | collective-permute-start | bytes 589832 | tf_op jit(solution)/shard_map/ppermute | solution.py:509
  11.5 9.3 %collective-permute-start.3 = (bf16[176,512]{1,0:T(8,128)(2,1)}, bf16[176,512]{1,0:T(8,128)(2,1)S(1)}, u32[]{:S(2)}, u32[]{:S(2)}) collective-permute-start(bf16[176,512]{1,0:T(8,128)(2,1)} %get-tuple-element.45.mine.refs_0_), channel_id=1, source_target_pairs={{0,16},{2,18},{4,20},{6,22},{8,24},{10,26},{12,28},{14,30},{16,0},... | collective-permute-start | bytes 540680 | tf_op jit(solution)/shard_map/ppermute | solution.py:569
  15.5 0.9 %copy-start.2 = (f32[15,8,512]{2,1,0:T(8,128)S(1)}, f32[15,8,512]{2,1,0:T(8,128)}, u32[]{:S(2)}) copy-start(f32[15,8,512]{2,1,0:T(8,128)} %get-tuple-element.37.coef.coef_in.refs_8_.refs_9_) | copy-start | bytes 737284
  16.4 9.0 %copy-start.1 = (bf16[3,1024,1024]{2,1,0:T(8,128)(2,1)S(1)}, bf16[3,1024,1024]{2,1,0:T(8,128)(2,1)}, u32[]{:S(2)}) copy-start(bf16[3,1024,1024]{2,1,0:T(8,128)(2,1)} %matrix.1) | copy-start | bytes 18874372
  16.4 9.0 %copy-start.4 = (bf16[176,512]{1,0:T(8,128)(2,1)S(1)}, bf16[176,512]{1,0:T(8,128)(2,1)}, u32[]{:S(2)}) copy-start(bf16[176,512]{1,0:T(8,128)(2,1)} %get-tuple-element.45.mine.refs_0_) | copy-start | bytes 540676
  20.8 30.7 %collective-permute-start.6 = (bf16[3,128,512]{2,1,0:T(8,128)(2,1)S(1)}, bf16[3,128,512]{2,1,0:T(8,128)(2,1)S(1)}, u32[]{:S(2)}, u32[]{:S(2)}) collective-permute-start(bf16[3,128,512]{2,1,0:T(8,128)(2,1)S(1)} %get-tuple-element.52.refs_0_), channel_id=1, source_target_pairs={{0,16},{2,18},{4,20},{6,22},{8,24},{10,26},{12,28},{14,30},{16,0},... | collective-permute-start | bytes 1179656 | tf_op jit(solution)/shard_map/ppermute | solution.py:596
  20.8 46.5 %collective-permute-start.4 = (bf16[3,160,512]{2,1,0:T(8,128)(2,1)S(1)}, bf16[3,160,512]{2,1,0:T(8,128)(2,1)S(1)}, u32[]{:S(2)}, u32[]{:S(2)}) collective-permute-start(bf16[3,160,512]{2,1,0:T(8,128)(2,1)S(1)} %get-tuple-element.46.refs_0_), channel_id=1, source_target_pairs={{0,16},{2,18},{4,20},{6,22},{8,24},{10,26},{12,28},{14,30},{16,0},... | collective-permute-start | bytes 1474568 | tf_op jit(solution)/shard_map/ppermute | solution.py:595
  51.5 21.7 %collective-permute-start.7 = (bf16[3,80,512]{2,1,0:T(8,128)(2,1)S(1)}, bf16[3,80,512]{2,1,0:T(8,128)(2,1)S(1)}, u32[]{:S(2)}, u32[]{:S(2)}) collective-permute-start(bf16[3,80,512]{2,1,0:T(8,128)(2,1)S(1)} %get-tuple-element.54.refs_0_), channel_id=1, source_target_pairs={{0,16},{2,18},{4,20},{6,22},{8,24},{10,26},{12,28},{14,30},{16,0},... | collective-permute-start | bytes 737288 | tf_op jit(solution)/shard_map/ppermute | solution.py:623
  68.8 8.5 %collective-permute-start.10 = (bf16[2,3,32,512]{3,2,1,0:T(8,128)(2,1)S(1)}, bf16[2,3,32,512]{3,2,1,0:T(8,128)(2,1)S(1)}, u32[]{:S(2)}, u32[]{:S(2)}) collective-permute-start(bf16[2,3,32,512]{3,2,1,0:T(8,128)(2,1)S(1)} %get-tuple-element.64), channel_id=1, source_target_pairs={{0,1},{1,0},{2,3},{3,2},{4,5},{5,4},{6,7},{7,6},{8,9},{9,8},{10,11... | collective-permute-start | bytes 589832 | tf_op jit(solution)/shard_map/ppermute | solution.py:509
  70.6 12.5 %collective-permute-start.5 = (bf16[3,64,512]{2,1,0:T(8,128)(2,1)S(1)}, bf16[3,64,512]{2,1,0:T(8,128)(2,1)S(1)}, u32[]{:S(2)}, u32[]{:S(2)}) collective-permute-start(bf16[3,64,512]{2,1,0:T(8,128)(2,1)S(1)} %get-tuple-element.47.refs_0_), channel_id=1, source_target_pairs={{0,16},{2,18},{4,20},{6,22},{8,24},{10,26},{12,28},{14,30},{16,0},... | collective-permute-start | bytes 589832 | tf_op jit(solution)/shard_map/ppermute | solution.py:634
  70.6 6.8 %collective-permute-start.8 = (bf16[2,3,16,512]{3,2,1,0:T(8,128)(2,1)S(1)}, bf16[2,3,16,512]{3,2,1,0:T(8,128)(2,1)S(1)}, u32[]{:S(2)}, u32[]{:S(2)}) collective-permute-start(bf16[2,3,16,512]{3,2,1,0:T(8,128)(2,1)S(1)} %get-tuple-element.62), channel_id=1, source_target_pairs={{0,2},{2,4},{4,6},{6,8},{8,10},{10,12},{12,14},{14,0},{16,18},{18,... | collective-permute-start | bytes 294920 | tf_op jit(solution)/shard_map/ppermute | solution.py:655
  70.6 6.8 %collective-permute-start.9 = (bf16[2,3,16,512]{3,2,1,0:T(8,128)(2,1)S(1)}, bf16[2,3,16,512]{3,2,1,0:T(8,128)(2,1)S(1)}, u32[]{:S(2)}, u32[]{:S(2)}) collective-permute-start(bf16[2,3,16,512]{3,2,1,0:T(8,128)(2,1)S(1)} %get-tuple-element.63), channel_id=1, source_target_pairs={{0,14},{2,0},{4,2},{6,4},{8,6},{10,8},{12,10},{14,12},{16,30},{18,... | collective-permute-start | bytes 294920 | tf_op jit(solution)/shard_map/ppermute | solution.py:656
  73.2 14.9 %collective-permute-start.11 = (bf16[3,32,512]{2,1,0:T(8,128)(2,1)S(1)}, bf16[3,32,512]{2,1,0:T(8,128)(2,1)S(1)}, u32[]{:S(2)}, u32[]{:S(2)}) collective-permute-start(bf16[3,32,512]{2,1,0:T(8,128)(2,1)S(1)} %get-tuple-element.68.mine), channel_id=1, source_target_pairs={{0,16},{2,18},{4,20},{6,22},{8,24},{10,26},{12,28},{14,30},{16,0},... | collective-permute-start | bytes 294920 | tf_op jit(solution)/shard_map/ppermute | solution.py:685
  76.1 1.2 %copy-start.3 = (f32[15,8,512]{2,1,0:T(8,128)S(1)}, f32[15,8,512]{2,1,0:T(8,128)}, u32[]{:S(2)}) copy-start(f32[15,8,512]{2,1,0:T(8,128)} %get-tuple-element.37.coef.coef_in.refs_8_.refs_9_) | copy-start | bytes 737284

commit v8 on v6

--- a/solution.py
+++ b/solution.py
@@ -366,7 +366,7 @@
     *edges, first, last, stage = refs[-3 - n_edges :]
     refs = refs[: -3 - n_edges]
     radial_kernel(plan, copies, half, weights, keep, *refs)
-    edges_of_state(na, nz, planes, refs[-3], refs[-2], refs[-1], edges, first, last, stage)
+    edges_of_state(na, nz, planes, refs[-2], refs[-2], refs[-1], edges, first, last, stage)
 
 
 def explicit_angle(t, reader, low, high, edge_factors, coef, rows, nz):
@@ -420,9 +420,7 @@
 
 
 def early_kernel(sizes, *refs):
-    na, nz, runs, base, half_ring, planes = sizes
-    if len(refs) == 18:
-        refs = refs[1:]
+    na, nz, runs, half_ring, planes = sizes
     (weights, keep, mid, outer, before_low, after_low, low_low, high_low, coef, out,
      before, after, low, high, rows, result, out_sems) = refs
     half = nz // 2
@@ -430,10 +428,10 @@
     wrap_before = jnp.where(place == 0, 1, 0)
     wrap_after = jnp.where(place == half_ring - 1, 1, 0)
     factors = edge_weights(planes)
-    states = ((mid, base), (outer, 0))
     widen(((low_low, low), (high_low, high)))
-    for begin, count in runs:
+    for begin, count, base in runs:
         end = begin + count
+        states = ((mid, base), (outer, 0))
         if begin == 0:
             widen(((before_low, before),))
 
@@ -459,7 +457,7 @@
             explicit_run(start, stop - start, states, low, high, factors, coef, rows, nz)
     leaves = []
     for s in range(3):
-        for k, (begin, count) in enumerate(runs):
+        for k, (begin, count, _) in enumerate(runs):
             finish_run(begin, count, s, rows, weights, keep, result, nz)
             span = pl.ds(begin, count)
             leave = pltpu.make_async_copy(result.at[s, span], out.at[s, span], out_sems.at[k, s])
@@ -473,7 +471,7 @@
     sizes, given, state, weights, keep, mine, theirs, outer, low_low, high_low, coef,
     out, mid, low, high, rows, result, out_sems,
 ):
-    na, nz, lo, hi, base, planes = sizes
+    na, nz, lo, hi, planes = sizes
     half = nz // 2
     factors = edge_weights(planes)
     count = hi - lo
@@ -484,9 +482,7 @@
         for ab in range(2):
             for k in range(2):
                 to = pl.ds((2 + count) * k * half, 2 * half)
-                mid[ab, s, to, :] = state[
-                    ab, s, pl.ds((lo - 2 - base + (2 + count) * k) * half, 2 * half), :
-                ]
+                mid[ab, s, to, :] = state[ab, s, pl.ds((lo - 2 + 2 * k) * half, 2 * half), :]
     explicit_run(lo - 1, count + 2, ((mid, lo - 2), (outer, 0)), low, high, factors, coef, rows, nz)
     leaves = []
     for s in range(3):
@@ -529,8 +525,7 @@
     quarter = na // 4
     ends = 2
     side = na // 2
-    a_lo, a_cut, a_hi = ends, na // 4, 3 * na // 8
-    x_hi, y_hi, l_hi = 22 * na // 32, 26 * na // 32, na - ends
+    a_lo, a_cut, a_hi, x_hi = ends, ends + na // 4, side, na - ends
     opposite = [(i, (i + count // 2) % count) for i in range(count)]
 
     def dma(*dims):
@@ -568,16 +563,16 @@
     mid_a, (angle_before, angle_after) = after(mid_a, (angle_before, angle_after))
     opp_a = lax.ppermute(mid_a, "ang", opposite)
     low, high = plane_halos(edges, planes)
-    bounds = (a_cut, a_hi, x_hi, y_hi, l_hi)
-    mid_b, mid_x, mid_y, mid_l = call(
+    bounds = (a_cut, a_hi, x_hi)
+    mid_b, mid_x = call(
         functools.partial(
             inner_kernel,
             (na, nz),
-            tuple((k, ((bounds[k], bounds[k + 1] - bounds[k]),)) for k in range(4)),
+            tuple((k, ((bounds[k], bounds[k + 1] - bounds[k]),)) for k in range(2)),
         ),
-        [message(bounds[k + 1] - bounds[k]) for k in range(4)],
+        [message(bounds[k + 1] - bounds[k]) for k in range(2)],
         [ANY, VM],
-        [VM] * 4,
+        [VM] * 2,
         [field, pltpu.SemaphoreType.DMA],
         (conc, coef),
         8,
@@ -637,22 +632,20 @@
         (weights, keep, out1, opp_1),
         8,
     )
-    mid_y, opp_2 = after(mid_y, opp_2)
-    opp_y = lax.ppermute(mid_y, "ang", opposite)
-    plan = (((2, side, side, side), (0, 0, 0, ends), (1, na - ends, 0, ends)),)
-    mid_left, ends_right, outer_state, *rest = call(
+    plan = (((1, side, side, side), (0, 0, 0, ends), (0, na - ends, a_hi, ends)),)
+    mid_left, outer_state, *rest = call(
         functools.partial(
             radial_edges_kernel,
             (na, nz, planes),
             plan,
-            ((0, 0, 0, ends, count_a + count_b), (1, 0, 2, 0, side)),
+            ((0, 0, 0, ends, count_a + count_b), (1, 0, 1, 0, side)),
             half,
         ),
-        [state(a_hi), state(ends), state(na)]
+        [state(a_hi + ends), state(na)]
         + [shape(2, ns, na, nr, dtype=BF16)] * n_edges
         + [shape(2, ns, nz, nr, dtype=BF16)] * 2,
         [VM] * 6,
-        [VM] * (5 + n_edges),
+        [VM] * (4 + n_edges),
         [pltpu.VMEM((n_edges, na, nr), F32)],
         (weights, keep, out2, opp_2, mid_first, outer_first),
         8,
@@ -663,56 +656,24 @@
     angle_after = lax.ppermute(first, "ang", ring(count, -1))
     stage = [pltpu.VMEM((ns, na * nz, 2 * nr), BF16), pltpu.VMEM((ns, na, nz, nr), F32)]
     edge_scratch = [pltpu.VMEM((2, ns, na, nr), F32)] * 2
-    def early(runs, base, mid, given):
-        return call(
-            functools.partial(early_kernel, (na, nz, runs, base, count // 2, planes)),
-            shape(ns, na, nz, nr),
-            [ANY] * len(given) + [VM] * 9,
-            ANY,
-            [pltpu.VMEM((2, ns, nz, nr), F32)] * 2 + edge_scratch + stage + [dma(len(runs), ns)],
-            (*given, weights, keep, mid, outer_state, angle_before, angle_after, low, high, coef),
-            12,
-            {0: 0} if given else None,
-        )
-
-    def next_state(mine, theirs, begin, end, copies, parts, base, stop):
-        return call(
-            functools.partial(
-                radial_kernel, (((0, begin, begin - base, end - begin),),), copies, half
-            ),
-            [state(stop - base)],
-            [VM] * (4 + len(parts)),
-            [VM],
-            [],
-            (weights, keep, mine, theirs, *parts),
-            8,
-        )[0]
-
-    partial = early(((0, a_hi - 1),), 0, mid_left, ())
-    opp_x, partial = after(opp_x, partial)
-    mid_l, opp_x = after(mid_l, opp_x)
-    opp_l = lax.ppermute(mid_l, "ang", opposite)
-    base_x = a_hi - 2
-    mid_x_state = next_state(
-        mid_x, opp_x, a_hi, x_hi, ((0, base_x, 0, 0, 2),), (mid_left,), base_x, x_hi
-    )
-    partial = early(((a_hi - 1, x_hi - a_hi),), base_x, mid_x_state, (partial,))
-    opp_y, partial = after(opp_y, partial)
-    base = x_hi - 2
-    mid_right = next_state(
-        mid_y, opp_y, x_hi, y_hi,
-        ((0, base - base_x, 0, 0, 2), (1, 0, 0, na - ends - base, ends)),
-        (mid_x_state, ends_right), base, na,
-    )
-    partial = early(((x_hi - 1, y_hi - x_hi), (na - 1, 1)), base, mid_right, (partial,))
-    wide = l_hi - y_hi + 4
+    runs = ((0, a_hi - 1, 0), (na - 1, 1, na - ends - a_hi))
+    partial = call(
+        functools.partial(early_kernel, (na, nz, runs, count // 2, planes)),
+        shape(ns, na, nz, nr),
+        [VM] * 9,
+        ANY,
+        [pltpu.VMEM((2, ns, nz, nr), F32)] * 2 + edge_scratch + stage + [dma(len(runs), ns)],
+        (weights, keep, mid_left, outer_state, angle_before, angle_after, low, high, coef),
+        12,
+    )
+    wide = x_hi - a_hi + 4
     return call(
-        functools.partial(late_kernel, (na, nz, y_hi, l_hi, base, planes)),
+        functools.partial(late_kernel, (na, nz, a_hi, x_hi, planes)),
         shape(ns, na, nz, nr),
         [ANY] + [VM] * 9,
         ANY,
         [pltpu.VMEM((2, ns, wide * half, nr), F32)] + edge_scratch + stage + [dma(ns)],
-        (partial, mid_right, weights, keep, mid_l, opp_l, outer_state, low, high, coef),
+        (partial, mid_left, weights, keep, mid_x, opp_x, outer_state, low, high, coef),
         12,
         {0: 0},
     )

time: 93.8 us -> 97.1 us (1.035)
  waiting for transfers between devices: 43.3 us -> 53.8 us
  Pallas kernels: 30.9 us -> 24.7 us
    ppermute x1, waiting for transfers between devices: 0.01 us -> 16.9 us  [per_device(): opp_2 = lax.ppermute(out2, 'ang', opposite)]
    ppermute x1, waiting for transfers between devices: 33.3 us -> 24.4 us  [per_device(): opp_1 = lax.ppermute(out1, 'ang', opposite)]
    pallas_call x13 -> x9, Pallas kernels: 30.9 us -> 24.7 us  [call(): pl.pallas_call(body, out_shape=out_shape, in_specs=in_specs, out_specs=ou...]
    ppermute x1, waiting for transfers between devices: 1.67 us -> 6.46 us  [per_device(): opp_b = lax.ppermute(mid_b, 'ang', opposite)]
    ppermute x1, waiting for transfers between devices: 3.21 us -> 0.01 us  [per_device(): opp_a = lax.ppermute(mid_a, 'ang', opposite)]
    ppermute x1, starting transfers between devices: 0.01 us -> 2.92 us  [per_device(): opp_2 = lax.ppermute(out2, 'ang', opposite)]
    ppermute x1, waiting for transfers between devices: 0.01 us -> 2.31 us  [per_device(): lax.ppermute(concentration[:, na - 1], 'ang', [(i, (i + 1) % count) for i...]
    ppermute x2, starting transfers between devices: 3.77 us -> 2.16 us  [plane_halos(): got = lax.ppermute(edges[0], 'ax', [(0, 1), (1, 0)])]
  transfers between devices with their start and end apart: 13 -> 11, of which waited for: 5 -> 5; matrix products, arithmetic and copies ran while one was open for 0% -> 0% of each run, Pallas kernels for 29% -> 20%
where the time goes in v8:
time: 97.1 us; the launch traced here: 96.9 us
  waiting for transfers between devices  53.8 us (55%)
  Pallas kernels  24.7 us (25%)
  starting transfers between devices  16.2 us (17%)
  local copies, waits for them, and re-layouts  2.06 us (2%)
    pallas_call x9, Pallas kernels, call(): pl.pallas_call(body, out_shape=out_shape, in_specs=in_specs, out_specs=ou...  24.7 us
    ppermute x1, waiting for transfers between devices, per_device(): opp_1 = lax.ppermute(out1, 'ang', opposite)  24.4 us
    ppermute x1, waiting for transfers between devices, per_device(): opp_2 = lax.ppermute(out2, 'ang', opposite)  16.9 us
    ppermute x1, waiting for transfers between devices, per_device(): opp_b = lax.ppermute(mid_b, 'ang', opposite)  6.46 us
    ppermute x1, starting transfers between devices, per_device(): lax.ppermute(concentration[:, 0], 'ang', [(i, (i - 1) % count) for i in r...  5.5 us
    ppermute x1, waiting for transfers between devices, per_device(): angle_before = lax.ppermute(last, 'ang', ring(count, 1))  3.77 us
    ppermute x1, starting transfers between devices, per_device(): opp_b = lax.ppermute(mid_b, 'ang', opposite)  2.99 us
    ppermute x1, starting transfers between devices, per_device(): opp_2 = lax.ppermute(out2, 'ang', opposite)  2.92 us
  transfers between devices with their start and end apart: 11, of which 5 were waited for; matrix products, arithmetic and copies ran while one was open for 0% of the time, Pallas kernels for 20%

profile of v8, /device:TPU:0, one launch (start us, length us, event | category | flops | bytes accessed | tf_op | source)
XLA Modules:
  0.0 96.9 jit_solution(1884378517575667599)
XLA Ops:
  0.0 1.1 %slice_bitcast_fusion = (f32[3,16,512]{2,1,0:T(8,128)S(1)}, f32[3,16,512]{2,1,0:T(8,128)S(1)}) fusion(f32[3,32,16,512]{3,2,1,0:T(8,128)} %param.8), kind=kLoop, calls=%fused_computation | loop fusion | bytes 393216 | tf_op jit(solution)/shard_map/squeeze | solution.py:541
  1.1 5.5 %collective-permute-start.1 = (f32[3,16,512]{2,1,0:T(8,128)S(1)}, f32[3,16,512]{2,1,0:T(8,128)S(1)}, u32[]{:S(2)}, u32[]{:S(2)}) collective-permute-start(f32[3,16,512]{2,1,0:T(8,128)S(1)} %get-tuple-element.55), channel_id=1, source_target_pairs={{0,30},{2,0},{4,2},{6,4},{8,6},{10,8},{12,10},{14,12},{16,14},{18,... | collective-permute-start | bytes 294920 | tf_op jit(solution)/shard_map/ppermute | solution.py:540
  6.6 0.0 collective-permute-start
  6.6 2.9 %shard_map.82 = (f32[3,32,512]{2,1,0:T(8,128)}, bf16[224,512]{1,0:T(8,128)(2,1)}, f32[15,8,512]{2,1,0:T(8,128)}) custom-call(f32[3,512,512]{2,1,0:T(8,128)} %bitcast.10, f32[1,512]{1,0:T(1,128)} %bitcast.13, f32[3]{0:T(128)} %diff.1, f32[3,512]{1,0:T(4,128)} %ang.1, f32[4]{0:T(128)} %rate.1, s32[4,3]{1,0:T(4,128)} %smap.1, s32[3,32]{1,0:T(4,128)} %flags.1), custom_call_target="tpu_custom_call" | custom-call | flops 1 | bytes 1 | tf_op jit(solution)/shard_map/pallas_call | solution.py:24
  9.5 1.6 %collective-permute-start.2 = (f32[3,32,512]{2,1,0:T(8,128)}, f32[3,32,512]{2,1,0:T(8,128)S(1)}, u32[]{:S(2)}, u32[]{:S(2)}) collective-permute-start(f32[3,32,512]{2,1,0:T(8,128)} %get-tuple-element.34), channel_id=1, source_target_pairs={{0,1},{1,0},{2,3},{3,2},{4,5},{5,4},{6,7},{7,6},{8,9},{9,8},{10,11... | collective-permute-start | bytes 589832 | tf_op jit(solution)/shard_map/ppermute | solution.py:505
  11.0 2.3 %collective-permute-done.before = f32[3,16,512]{2,1,0:T(8,128)S(1)} collective-permute-done((f32[3,16,512]{2,1,0:T(8,128)S(1)}, f32[3,16,512]{2,1,0:T(8,128)S(1)}, u32[]{:S(2)}, u32[]{:S(2)}) %collective-permute-start) | collective-permute-done | bytes 98336 | tf_op jit(solution)/shard_map/ppermute | solution.py:537
  13.4 0.9 copy-done.2
  14.3 1.6 %shard_map.85 = (bf16[3,48,512]{2,1,0:T(8,128)(2,1)S(1)}, bf16[3,112,512]{2,1,0:T(8,128)(2,1)S(1)}) custom-call(f32[3,512,512]{2,1,0:T(8,128)S(1)} %bitcast.11, f32[15,8,512]{2,1,0:T(8,128)S(1)} %copy-done.2), custom_call_target="tpu_custom_call" | custom-call | flops 1 | bytes 1 | tf_op jit(solution)/shard_map/pallas_call | solution.py:24
  15.9 3.0 %collective-permute-start.5 = (bf16[3,48,512]{2,1,0:T(8,128)(2,1)S(1)}, bf16[3,48,512]{2,1,0:T(8,128)(2,1)S(1)}, u32[]{:S(2)}, u32[]{:S(2)}) collective-permute-start(bf16[3,48,512]{2,1,0:T(8,128)(2,1)S(1)} %get-tuple-element.42.refs_1_), channel_id=1, source_target_pairs={{0,16},{2,18},{4,20},{6,22},{8,24},{10,26},{12,28},{14,30},{16,0},... | collective-permute-start | bytes 442376 | tf_op jit(solution)/shard_map/ppermute | solution.py:580
  18.9 3.0 %shard_map.83 = (bf16[3,128,512]{2,1,0:T(8,128)(2,1)S(1)}, bf16[3,160,512]{2,1,0:T(8,128)(2,1)S(1)}) custom-call(f32[3,512,512]{2,1,0:T(8,128)S(1)} %bitcast.12, f32[3,16,512]{2,1,0:T(8,128)S(1)} %collective-permute-done.before, f32[3,16,512]{2,1,0:T(8,128)S(1)} %collective-permute-done.1.after, f32[3,32,512]{2,1,0:T(8,128)S(1)} %collective-permute-done.2.low.high, ...), custom_call_target="tpu_custom_call" | custom-call | flops 1 | bytes 1 | tf_op jit(solution)/shard_map/pallas_call | solution.py:24
  21.9 6.5 %collective-permute-done.5.refs_3_ = bf16[3,48,512]{2,1,0:T(8,128)(2,1)S(1)} collective-permute-done((bf16[3,48,512]{2,1,0:T(8,128)(2,1)S(1)}, bf16[3,48,512]{2,1,0:T(8,128)(2,1)S(1)}, u32[]{:S(2)}, u32[]{:S(2)}) %collective-permute-start.5) | collective-permute-done | bytes 147488 | tf_op jit(solution)/shard_map/ppermute | solution.py:580
  28.3 2.9 %collective-permute-start.4 = (bf16[3,160,512]{2,1,0:T(8,128)(2,1)S(1)}, bf16[3,160,512]{2,1,0:T(8,128)(2,1)S(1)}, u32[]{:S(2)}, u32[]{:S(2)}) collective-permute-start(bf16[3,160,512]{2,1,0:T(8,128)(2,1)S(1)} %get-tuple-element.40.refs_0_), channel_id=1, source_target_pairs={{0,16},{2,18},{4,20},{6,22},{8,24},{10,26},{12,28},{14,30},{16,0},... | collective-permute-start | bytes 1474568 | tf_op jit(solution)/shard_map/ppermute | solution.py:591
  31.2 2.4 %shard_map.84 = (bf16[3,512,1024]{2,1,0:T(8,128)(2,1)S(1)}, f32[2,3,32,128]{3,2,1,0:T(8,128)S(1)}) custom-call(bf16[3,1024,1024]{2,1,0:T(8,128)(2,1)S(1)} %copy-done.1, bf16[224,512]{1,0:T(8,128)(2,1)S(1)} %copy-done.4, bf16[224,512]{1,0:T(8,128)(2,1)S(1)} %collective-permute-done.3.theirs.refs_2_), custom_call_target="tpu_custom_call" | custom-call | flops 1 | bytes 1 | tf_op jit(solution)/shard_map/pallas_call | solution.py:24
  33.7 2.1 %shard_map.86.refs_2_ = f32[2,3,112,512]{3,2,1,0:T(8,128)S(1)} custom-call(bf16[3,512,1024]{2,1,0:T(8,128)(2,1)S(1)} %get-tuple-element.38.weights.refs_0_, f32[2,3,32,128]{3,2,1,0:T(8,128)S(1)} %get-tuple-element.39.keep.refs_1_, bf16[224,512]{1,0:T(8,128)(2,1)S(1)} %copy-done.4, bf16[3,48,512]{2,1,0:T(8,128)(2,1)S(1)} %get-tuple-element.42.refs_1_, ...), custom_call_target="tpu_custom_call" | custom-call | flops 1 | bytes 1 | tf_op jit(solution)/shard_map/pallas_call | solution.py:24
  35.8 24.4 %collective-permute-done.6.refs_1_ = bf16[3,128,512]{2,1,0:T(8,128)(2,1)S(1)} collective-permute-done((bf16[3,128,512]{2,1,0:T(8,128)(2,1)S(1)}, bf16[3,128,512]{2,1,0:T(8,128)(2,1)S(1)}, u32[]{:S(2)}, u32[]{:S(2)}) %collective-permute-start.6) | collective-permute-done | bytes 393248 | tf_op jit(solution)/shard_map/ppermute | solution.py:593
  60.2 1.0 %shard_map.87.refs_3_ = f32[2,3,128,512]{3,2,1,0:T(8,128)S(1)} custom-call(bf16[3,512,1024]{2,1,0:T(8,128)(2,1)S(1)} %get-tuple-element.38.weights.refs_0_, f32[2,3,32,128]{3,2,1,0:T(8,128)S(1)} %get-tuple-element.39.keep.refs_1_, bf16[3,128,512]{2,1,0:T(8,128)(2,1)S(1)} %get-tuple-element.43.refs_0_, bf16[3,128,512]{2,1,0:T(8,128)(2,1)S(1)} %collective-permute-done.6.refs_1_), custom_call_target="tpu_custom_call" | custom-call | flops 1 | bytes 1 | tf_op jit(solution)/shard_map/pallas_call | solution.py:24
  61.2 0.0 copy-start.3
  61.3 16.9 %collective-permute-done.4.refs_1_ = bf16[3,160,512]{2,1,0:T(8,128)(2,1)S(1)} collective-permute-done((bf16[3,160,512]{2,1,0:T(8,128)(2,1)S(1)}, bf16[3,160,512]{2,1,0:T(8,128)(2,1)S(1)}, u32[]{:S(2)}, u32[]{:S(2)}) %collective-permute-start.4) | collective-permute-done | bytes 491552 | tf_op jit(solution)/shard_map/ppermute | solution.py:591
  78.1 1.5 %shard_map.88 = (f32[2,3,144,512]{3,2,1,0:T(8,128)S(1)}, f32[2,3,256,512]{3,2,1,0:T(8,128)S(1)}, bf16[2,3,32,512]{3,2,1,0:T(8,128)(2,1)S(1)}, bf16[2,3,16,512]{3...) custom-call(bf16[3,512,1024]{2,1,0:T(8,128)(2,1)S(1)} %get-tuple-element.38.weights.refs_0_, ...), custom_call_target="tpu_custom_call" | custom-call | flops 1 | bytes 1 | tf_op jit(solution)/shard_map/pallas_call | solution.py:24
  79.7 0.6 collective-permute-start.9
  80.3 2.6 %collective-permute-start.8 = (bf16[2,3,16,512]{3,2,1,0:T(8,128)(2,1)S(1)}, bf16[2,3,16,512]{3,2,1,0:T(8,128)(2,1)S(1)}, u32[]{:S(2)}, u32[]{:S(2)}) collective-permute-start(bf16[2,3,16,512]{3,2,1,0:T(8,128)(2,1)S(1)} %get-tuple-element.52), channel_id=1, source_target_pairs={{0,14},{2,0},{4,2},{6,4},{8,6},{10,8},{12,10},{14,12},{16,30},{18,... | collective-permute-start | bytes 294920 | tf_op jit(solution)/shard_map/ppermute | solution.py:656
  82.9 3.8 %collective-permute-done.7.refs_4_ = bf16[2,3,16,512]{3,2,1,0:T(8,128)(2,1)S(1)} collective-permute-done((bf16[2,3,16,512]{3,2,1,0:T(8,128)(2,1)S(1)}, bf16[2,3,16,512]{3,2,1,0:T(8,128)(2,1)S(1)}, u32[]{:S(2)}, u32[]{:S(2)}) %collective-permute-start.7) | collective-permute-done | bytes 98336 | tf_op jit(solution)/shard_map/ppermute | solution.py:655
  86.7 4.8 %shard_map.89.given = f32[3,32,16,512]{3,2,1,0:T(8,128)} custom-call(bf16[3,512,1024]{2,1,0:T(8,128)(2,1)S(1)} %get-tuple-element.38.weights.refs_0_, f32[2,3,32,128]{3,2,1,0:T(8,128)S(1)} %get-tuple-element.39.keep.refs_1_, f32[2,3,144,512]{3,2,1,0:T(8,128)S(1)} %get-tuple-element.49.refs_2_.state, f32[2,3,256,512]{3,2,1,0:T(8,128)S(1)} %get-tuple-element.50.refs_3_.outer, ...), custom_call_target="tpu_custom_call" | custom-call | flops 1 | bytes 1 | tf_op jit(solution)/shard_map/pallas_call | solution.py:24
  91.5 5.4 %shard_map.90 = f32[3,32,16,512]{3,2,1,0:T(8,128)} custom-call(f32[3,32,16,512]{3,2,1,0:T(8,128)} %shard_map.89.given, f32[2,3,144,512]{3,2,1,0:T(8,128)S(1)} %get-tuple-element.49.refs_2_.state, bf16[3,512,1024]{2,1,0:T(8,128)(2,1)S(1)} %get-tuple-element.38.weights.refs_0_, ...), custom_call_target="tpu_custom_call", output_to_operand_aliasing={{}: (0, {})} | custom-call | flops 1 | bytes 1 | tf_op jit(solution)/shard_map/pallas_call | solution.py:24
  (18 shorter events, 0.0 us)
Async XLA Ops:
  0.0 13.4 %copy-start = (f32[3,32,16,512]{3,2,1,0:T(8,128)S(1)}, f32[3,32,16,512]{3,2,1,0:T(8,128)}, u32[]{:S(2)}) copy-start(f32[3,32,16,512]{3,2,1,0:T(8,128)} %param.8) | copy-start | bytes 9437188
  1.1 9.9 %collective-permute-start.1 = (f32[3,16,512]{2,1,0:T(8,128)S(1)}, f32[3,16,512]{2,1,0:T(8,128)S(1)}, u32[]{:S(2)}, u32[]{:S(2)}) collective-permute-start(f32[3,16,512]{2,1,0:T(8,128)S(1)} %get-tuple-element.55), channel_id=1, source_target_pairs={{0,30},{2,0},{4,2},{6,4},{8,6},{10,8},{12,10},{14,12},{16,14},{18,... | collective-permute-start | bytes 294920 | tf_op jit(solution)/shard_map/ppermute | solution.py:540
  6.6 6.7 %collective-permute-start = (f32[3,16,512]{2,1,0:T(8,128)S(1)}, f32[3,16,512]{2,1,0:T(8,128)S(1)}, u32[]{:S(2)}, u32[]{:S(2)}) collective-permute-start(f32[3,16,512]{2,1,0:T(8,128)S(1)} %get-tuple-element.56), channel_id=1, source_target_pairs={{0,2},{2,4},{4,6},{6,8},{8,10},{10,12},{12,14},{14,16},{16,18},{18... | collective-permute-start | bytes 294920 | tf_op jit(solution)/shard_map/ppermute | solution.py:537
  9.5 9.4 %collective-permute-start.2 = (f32[3,32,512]{2,1,0:T(8,128)}, f32[3,32,512]{2,1,0:T(8,128)S(1)}, u32[]{:S(2)}, u32[]{:S(2)}) collective-permute-start(f32[3,32,512]{2,1,0:T(8,128)} %get-tuple-element.34), channel_id=1, source_target_pairs={{0,1},{1,0},{2,3},{3,2},{4,5},{5,4},{6,7},{7,6},{8,9},{9,8},{10,11... | collective-permute-start | bytes 589832 | tf_op jit(solution)/shard_map/ppermute | solution.py:505
  13.3 15.0 %collective-permute-start.3 = (bf16[224,512]{1,0:T(8,128)(2,1)}, bf16[224,512]{1,0:T(8,128)(2,1)S(1)}, u32[]{:S(2)}, u32[]{:S(2)}) collective-permute-start(bf16[224,512]{1,0:T(8,128)(2,1)} %get-tuple-element.31.mine.refs_0_), channel_id=1, source_target_pairs={{0,16},{2,18},{4,20},{6,22},{8,24},{10,26},{12,28},{14,30},{16,0},... | collective-permute-start | bytes 688136 | tf_op jit(solution)/shard_map/ppermute | solution.py:564
  13.4 0.9 copy-start.2
  14.3 16.9 %copy-start.1 = (bf16[3,1024,1024]{2,1,0:T(8,128)(2,1)S(1)}, bf16[3,1024,1024]{2,1,0:T(8,128)(2,1)}, u32[]{:S(2)}) copy-start(bf16[3,1024,1024]{2,1,0:T(8,128)(2,1)} %matrix.1) | copy-start | bytes 18874372
  14.3 16.9 %copy-start.4 = (bf16[224,512]{1,0:T(8,128)(2,1)S(1)}, bf16[224,512]{1,0:T(8,128)(2,1)}, u32[]{:S(2)}) copy-start(bf16[224,512]{1,0:T(8,128)(2,1)} %get-tuple-element.31.mine.refs_0_) | copy-start | bytes 688132
  15.9 12.4 %collective-permute-start.5 = (bf16[3,48,512]{2,1,0:T(8,128)(2,1)S(1)}, bf16[3,48,512]{2,1,0:T(8,128)(2,1)S(1)}, u32[]{:S(2)}, u32[]{:S(2)}) collective-permute-start(bf16[3,48,512]{2,1,0:T(8,128)(2,1)S(1)} %get-tuple-element.42.refs_1_), channel_id=1, source_target_pairs={{0,16},{2,18},{4,20},{6,22},{8,24},{10,26},{12,28},{14,30},{16,0},... | collective-permute-start | bytes 442376 | tf_op jit(solution)/shard_map/ppermute | solution.py:580
  28.3 31.9 %collective-permute-start.6 = (bf16[3,128,512]{2,1,0:T(8,128)(2,1)S(1)}, bf16[3,128,512]{2,1,0:T(8,128)(2,1)S(1)}, u32[]{:S(2)}, u32[]{:S(2)}) collective-permute-start(bf16[3,128,512]{2,1,0:T(8,128)(2,1)S(1)} %get-tuple-element.43.refs_0_), channel_id=1, source_target_pairs={{0,16},{2,18},{4,20},{6,22},{8,24},{10,26},{12,28},{14,30},{16,0},... | collective-permute-start | bytes 1179656 | tf_op jit(solution)/shard_map/ppermute | solution.py:593
  28.3 49.8 %collective-permute-start.4 = (bf16[3,160,512]{2,1,0:T(8,128)(2,1)S(1)}, bf16[3,160,512]{2,1,0:T(8,128)(2,1)S(1)}, u32[]{:S(2)}, u32[]{:S(2)}) collective-permute-start(bf16[3,160,512]{2,1,0:T(8,128)(2,1)S(1)} %get-tuple-element.40.refs_0_), channel_id=1, source_target_pairs={{0,16},{2,18},{4,20},{6,22},{8,24},{10,26},{12,28},{14,30},{16,0},... | collective-permute-start | bytes 1474568 | tf_op jit(solution)/shard_map/ppermute | solution.py:591
  60.2 31.3 %collective-permute-start.10 = (bf16[3,112,512]{2,1,0:T(8,128)(2,1)S(1)}, bf16[3,112,512]{2,1,0:T(8,128)(2,1)S(1)}, u32[]{:S(2)}, u32[]{:S(2)}) collective-permute-start(bf16[3,112,512]{2,1,0:T(8,128)(2,1)S(1)} %get-tuple-element.54.mine), channel_id=1, source_target_pairs={{0,16},{2,18},{4,20},{6,22},{8,24},{10,26},{12,28},{14,30},{16,0},... | collective-permute-start | bytes 1032200 | tf_op jit(solution)/shard_map/ppermute | solution.py:625
  61.2 25.5 %copy-start.3 = (f32[15,8,512]{2,1,0:T(8,128)S(1)}, f32[15,8,512]{2,1,0:T(8,128)}, u32[]{:S(2)}) copy-start(f32[15,8,512]{2,1,0:T(8,128)} %get-tuple-element.35.coef_in.coef.refs_8_) | copy-start | bytes 737284
  79.7 7.0 %collective-permute-start.9 = (bf16[2,3,32,512]{3,2,1,0:T(8,128)(2,1)S(1)}, bf16[2,3,32,512]{3,2,1,0:T(8,128)(2,1)S(1)}, u32[]{:S(2)}, u32[]{:S(2)}) collective-permute-start(bf16[2,3,32,512]{3,2,1,0:T(8,128)(2,1)S(1)} %get-tuple-element.53), channel_id=1, source_target_pairs={{0,1},{1,0},{2,3},{3,2},{4,5},{5,4},{6,7},{7,6},{8,9},{9,8},{10,11... | collective-permute-start | bytes 589832 | tf_op jit(solution)/shard_map/ppermute | solution.py:505
  80.3 6.4 %collective-permute-start.7 = (bf16[2,3,16,512]{3,2,1,0:T(8,128)(2,1)S(1)}, bf16[2,3,16,512]{3,2,1,0:T(8,128)(2,1)S(1)}, u32[]{:S(2)}, u32[]{:S(2)}) collective-permute-start(bf16[2,3,16,512]{3,2,1,0:T(8,128)(2,1)S(1)} %get-tuple-element.51), channel_id=1, source_target_pairs={{0,2},{2,4},{4,6},{6,8},{8,10},{10,12},{12,14},{14,0},{16,18},{18,... | collective-permute-start | bytes 294920 | tf_op jit(solution)/shard_map/ppermute | solution.py:655
  80.3 6.4 %collective-permute-start.8 = (bf16[2,3,16,512]{3,2,1,0:T(8,128)(2,1)S(1)}, bf16[2,3,16,512]{3,2,1,0:T(8,128)(2,1)S(1)}, u32[]{:S(2)}, u32[]{:S(2)}) collective-permute-start(bf16[2,3,16,512]{3,2,1,0:T(8,128)(2,1)S(1)} %get-tuple-element.52), channel_id=1, source_target_pairs={{0,14},{2,0},{4,2},{6,4},{8,6},{10,8},{12,10},{14,12},{16,30},{18,... | collective-permute-start | bytes 294920 | tf_op jit(solution)/shard_map/ppermute | solution.py:656

commit v9 on v8

--- a/solution.py
+++ b/solution.py
@@ -525,7 +525,7 @@
     quarter = na // 4
     ends = 2
     side = na // 2
-    a_lo, a_cut, a_hi, x_hi = ends, ends + na // 4, side, na - ends
+    a_lo, a_cut, a_hi, x_hi = ends, ends + na // 4, side + ends, na - ends
     opposite = [(i, (i + count // 2) % count) for i in range(count)]
 
     def dma(*dims):
@@ -621,7 +621,7 @@
         8,
     )
     opp_1, mid_first = after(opp_1, mid_first)
-    mid_x, opp_1 = after(mid_x, opp_1)
+    mid_x, (opp_1, opp_2) = after(mid_x, (opp_1, opp_2))
     opp_x = lax.ppermute(mid_x, "ang", opposite)
     (outer_first,) = call(
         functools.partial(radial_kernel, (((0, 0, 0, side),),), (), half),

time: 97.1 us -> 93.9 us (0.967)
  the two profiles are of different devices: /device:TPU:0 before, /device:TPU:7 now
where the time goes in v9:
time: 93.9 us; the launch traced here: 93.7 us
  waiting for transfers between devices  57.9 us (62%)
  Pallas kernels  25 us (27%)
  starting transfers between devices  8.71 us (9%)
  local copies, waits for them, and re-layouts  2.07 us (2%)
    pallas_call x9, Pallas kernels, call(): pl.pallas_call(body, out_shape=out_shape, in_specs=in_specs, out_specs=ou...  25 us
    ppermute x1, waiting for transfers between devices, per_device(): opp_1 = lax.ppermute(out1, 'ang', opposite)  22.7 us
    ppermute x1, waiting for transfers between devices, per_device(): opp_b = lax.ppermute(mid_b, 'ang', opposite)  14.7 us
    ppermute x1, waiting for transfers between devices, per_device(): angle_after = lax.ppermute(first, 'ang', ring(count, -1))  8.05 us
    ppermute x1, waiting for transfers between devices, per_device(): opp_a = lax.ppermute(mid_a, 'ang', opposite)  6.99 us
    ppermute x2, waiting for transfers between devices, plane_halos(): got = lax.ppermute(edges[0], 'ax', [(0, 1), (1, 0)])  3.24 us
    ppermute x1, starting transfers between devices, per_device(): angle_before = lax.ppermute(last, 'ang', ring(count, 1))  2.91 us
    ppermute x1, starting transfers between devices, per_device(): opp_a = lax.ppermute(mid_a, 'ang', opposite)  2.37 us
  transfers between devices with their start and end apart: 11, of which 6 were waited for; matrix products, arithmetic and copies ran while one was open for 0% of the time, Pallas kernels for 21%

profile of v9, /device:TPU:7, one launch (start us, length us, event | category | flops | bytes accessed | tf_op | source)
XLA Modules:
  0.0 93.7 jit_solution(1240499250749033087)
XLA Ops:
  0.0 1.1 %slice_bitcast_fusion = (f32[3,16,512]{2,1,0:T(8,128)S(1)}, f32[3,16,512]{2,1,0:T(8,128)S(1)}) fusion(f32[3,32,16,512]{3,2,1,0:T(8,128)} %param.8), kind=kLoop, calls=%fused_computation | loop fusion | bytes 393216 | tf_op jit(solution)/shard_map/squeeze | solution.py:541
  1.1 0.7 collective-permute-start.1
  1.8 2.0 %collective-permute-start = (f32[3,16,512]{2,1,0:T(8,128)S(1)}, f32[3,16,512]{2,1,0:T(8,128)S(1)}, u32[]{:S(2)}, u32[]{:S(2)}) collective-permute-start(f32[3,16,512]{2,1,0:T(8,128)S(1)} %get-tuple-element.58), channel_id=1, source_target_pairs={{0,2},{2,4},{4,6},{6,8},{8,10},{10,12},{12,14},{14,16},{16,18},{18... | collective-permute-start | bytes 294920 | tf_op jit(solution)/shard_map/ppermute | solution.py:537
  3.8 2.9 %shard_map.82 = (f32[3,32,512]{2,1,0:T(8,128)}, bf16[224,512]{1,0:T(8,128)(2,1)}, f32[15,8,512]{2,1,0:T(8,128)}) custom-call(f32[3,512,512]{2,1,0:T(8,128)} %bitcast.10, f32[1,512]{1,0:T(1,128)} %bitcast.13, f32[3]{0:T(128)} %diff.1, f32[3,512]{1,0:T(4,128)} %ang.1, f32[4]{0:T(128)} %rate.1, s32[4,3]{1,0:T(4,128)} %smap.1, s32[3,32]{1,0:T(4,128)} %flags.1), custom_call_target="tpu_custom_call" | custom-call | flops 1 | bytes 1 | tf_op jit(solution)/shard_map/pallas_call | solution.py:24
  6.7 2.4 %collective-permute-start.3 = (bf16[224,512]{1,0:T(8,128)(2,1)}, bf16[224,512]{1,0:T(8,128)(2,1)S(1)}, u32[]{:S(2)}, u32[]{:S(2)}) collective-permute-start(bf16[224,512]{1,0:T(8,128)(2,1)} %get-tuple-element.32.mine.refs_0_), channel_id=1, source_target_pairs={{0,16},{2,18},{4,20},{6,22},{8,24},{10,26},{12,28},{14,30},{16,0},... | collective-permute-start | bytes 688136 | tf_op jit(solution)/shard_map/ppermute | solution.py:564
  9.1 0.3 collective-permute-start.2
  9.3 0.9 %copy-done.2 = f32[15,8,512]{2,1,0:T(8,128)S(1)} copy-done((f32[15,8,512]{2,1,0:T(8,128)S(1)}, f32[15,8,512]{2,1,0:T(8,128)}, u32[]{:S(2)}) %copy-start.2) | copy-done | bytes 245784
  10.3 1.6 %shard_map.85 = (bf16[3,64,512]{2,1,0:T(8,128)(2,1)S(1)}, bf16[3,96,512]{2,1,0:T(8,128)(2,1)S(1)}) custom-call(f32[3,512,512]{2,1,0:T(8,128)S(1)} %bitcast.11, f32[15,8,512]{2,1,0:T(8,128)S(1)} %copy-done.2), custom_call_target="tpu_custom_call" | custom-call | flops 1 | bytes 1 | tf_op jit(solution)/shard_map/pallas_call | solution.py:24
  11.8 0.1 collective-permute-start.4
  12.0 3.2 %collective-permute-done.2.low.high = f32[3,32,512]{2,1,0:T(8,128)S(1)} collective-permute-done((f32[3,32,512]{2,1,0:T(8,128)}, f32[3,32,512]{2,1,0:T(8,128)S(1)}, u32[]{:S(2)}, u32[]{:S(2)}) %collective-permute-start.2) | collective-permute-done | bytes 196640 | tf_op jit(solution)/shard_map/ppermute | solution.py:505
  15.2 3.0 %shard_map.83 = (bf16[3,128,512]{2,1,0:T(8,128)(2,1)S(1)}, bf16[3,160,512]{2,1,0:T(8,128)(2,1)S(1)}) custom-call(f32[3,512,512]{2,1,0:T(8,128)S(1)} %bitcast.12, f32[3,16,512]{2,1,0:T(8,128)S(1)} %collective-permute-done.before, f32[3,16,512]{2,1,0:T(8,128)S(1)} %collective-permute-done.1.after, f32[3,32,512]{2,1,0:T(8,128)S(1)} %collective-permute-done.2.low.high, ...), custom_call_target="tpu_custom_call" | custom-call | flops 1 | bytes 1 | tf_op jit(solution)/shard_map/pallas_call | solution.py:24
  18.2 7.0 %collective-permute-done.3.theirs.refs_2_ = bf16[224,512]{1,0:T(8,128)(2,1)S(1)} collective-permute-done((bf16[224,512]{1,0:T(8,128)(2,1)}, bf16[224,512]{1,0:T(8,128)(2,1)S(1)}, u32[]{:S(2)}, u32[]{:S(2)}) %collective-permute-start.3) | collective-permute-done | bytes 229408 | tf_op jit(solution)/shard_map/ppermute | solution.py:564
  25.2 14.7 %collective-permute-done.4.refs_3_ = bf16[3,64,512]{2,1,0:T(8,128)(2,1)S(1)} collective-permute-done((bf16[3,64,512]{2,1,0:T(8,128)(2,1)S(1)}, bf16[3,64,512]{2,1,0:T(8,128)(2,1)S(1)}, u32[]{:S(2)}, u32[]{:S(2)}) %collective-permute-start.4) | collective-permute-done | bytes 196640 | tf_op jit(solution)/shard_map/ppermute | solution.py:580
  40.0 2.4 %shard_map.84 = (bf16[3,512,1024]{2,1,0:T(8,128)(2,1)S(1)}, f32[2,3,32,128]{3,2,1,0:T(8,128)S(1)}) custom-call(bf16[3,1024,1024]{2,1,0:T(8,128)(2,1)S(1)} %copy-done.1, bf16[224,512]{1,0:T(8,128)(2,1)S(1)} %copy-done.4, bf16[224,512]{1,0:T(8,128)(2,1)S(1)} %collective-permute-done.3.theirs.refs_2_), custom_call_target="tpu_custom_call" | custom-call | flops 1 | bytes 1 | tf_op jit(solution)/shard_map/pallas_call | solution.py:24
  42.4 2.2 %shard_map.86.refs_2_ = f32[2,3,128,512]{3,2,1,0:T(8,128)S(1)} custom-call(bf16[3,512,1024]{2,1,0:T(8,128)(2,1)S(1)} %get-tuple-element.39.weights.refs_0_, f32[2,3,32,128]{3,2,1,0:T(8,128)S(1)} %get-tuple-element.40.keep.refs_1_, bf16[224,512]{1,0:T(8,128)(2,1)S(1)} %copy-done.4, bf16[3,64,512]{2,1,0:T(8,128)(2,1)S(1)} %get-tuple-element.44.refs_1_, ...), custom_call_target="tpu_custom_call" | custom-call | flops 1 | bytes 1 | tf_op jit(solution)/shard_map/pallas_call | solution.py:24
  44.6 22.7 %collective-permute-done.5.refs_1_ = bf16[3,128,512]{2,1,0:T(8,128)(2,1)S(1)} collective-permute-done((bf16[3,128,512]{2,1,0:T(8,128)(2,1)S(1)}, bf16[3,128,512]{2,1,0:T(8,128)(2,1)S(1)}, u32[]{:S(2)}, u32[]{:S(2)}) %collective-permute-start.5) | collective-permute-done | bytes 393248 | tf_op jit(solution)/shard_map/ppermute | solution.py:593
  67.3 1.0 %shard_map.87.refs_3_ = f32[2,3,128,512]{3,2,1,0:T(8,128)S(1)} custom-call(bf16[3,512,1024]{2,1,0:T(8,128)(2,1)S(1)} %get-tuple-element.39.weights.refs_0_, f32[2,3,32,128]{3,2,1,0:T(8,128)S(1)} %get-tuple-element.40.keep.refs_1_, bf16[3,128,512]{2,1,0:T(8,128)(2,1)S(1)} %get-tuple-element.45.refs_0_, bf16[3,128,512]{2,1,0:T(8,128)(2,1)S(1)} %collective-permute-done.5.refs_1_), custom_call_target="tpu_custom_call" | custom-call | flops 1 | bytes 1 | tf_op jit(solution)/shard_map/pallas_call | solution.py:24
  68.4 1.6 %shard_map.88 = (f32[2,3,160,512]{3,2,1,0:T(8,128)S(1)}, f32[2,3,256,512]{3,2,1,0:T(8,128)S(1)}, bf16[2,3,32,512]{3,2,1,0:T(8,128)(2,1)S(1)}, bf16[2,3,16,512]{3...) custom-call(bf16[3,512,1024]{2,1,0:T(8,128)(2,1)S(1)} %get-tuple-element.39.weights.refs_0_, ...), custom_call_target="tpu_custom_call" | custom-call | flops 1 | bytes 1 | tf_op jit(solution)/shard_map/pallas_call | solution.py:24
  69.9 0.3 collective-permute-start.9
  70.3 2.9 %collective-permute-start.7 = (bf16[2,3,16,512]{3,2,1,0:T(8,128)(2,1)S(1)}, bf16[2,3,16,512]{3,2,1,0:T(8,128)(2,1)S(1)}, u32[]{:S(2)}, u32[]{:S(2)}) collective-permute-start(bf16[2,3,16,512]{3,2,1,0:T(8,128)(2,1)S(1)} %get-tuple-element.53), channel_id=1, source_target_pairs={{0,2},{2,4},{4,6},{6,8},{8,10},{10,12},{12,14},{14,0},{16,18},{18,... | collective-permute-start | bytes 294920 | tf_op jit(solution)/shard_map/ppermute | solution.py:655
  73.2 2.1 %collective-permute-done.7.refs_4_ = bf16[2,3,16,512]{3,2,1,0:T(8,128)(2,1)S(1)} collective-permute-done((bf16[2,3,16,512]{3,2,1,0:T(8,128)(2,1)S(1)}, bf16[2,3,16,512]{3,2,1,0:T(8,128)(2,1)S(1)}, u32[]{:S(2)}, u32[]{:S(2)}) %collective-permute-start.7) | collective-permute-done | bytes 98336 | tf_op jit(solution)/shard_map/ppermute | solution.py:655
  75.3 8.1 %collective-permute-done.8.refs_5_ = bf16[2,3,16,512]{3,2,1,0:T(8,128)(2,1)S(1)} collective-permute-done((bf16[2,3,16,512]{3,2,1,0:T(8,128)(2,1)S(1)}, bf16[2,3,16,512]{3,2,1,0:T(8,128)(2,1)S(1)}, u32[]{:S(2)}, u32[]{:S(2)}) %collective-permute-start.8) | collective-permute-done | bytes 98336 | tf_op jit(solution)/shard_map/ppermute | solution.py:656
  83.3 5.2 %shard_map.89.given = f32[3,32,16,512]{3,2,1,0:T(8,128)} custom-call(bf16[3,512,1024]{2,1,0:T(8,128)(2,1)S(1)} %get-tuple-element.39.weights.refs_0_, f32[2,3,32,128]{3,2,1,0:T(8,128)S(1)} %get-tuple-element.40.keep.refs_1_, f32[2,3,160,512]{3,2,1,0:T(8,128)S(1)} %get-tuple-element.51.refs_2_.state, f32[2,3,256,512]{3,2,1,0:T(8,128)S(1)} %get-tuple-element.52.refs_3_.outer, ...), custom_call_target="tpu_custom_call" | custom-call | flops 1 | bytes 1 | tf_op jit(solution)/shard_map/pallas_call | solution.py:24
  88.5 5.2 %shard_map.90 = f32[3,32,16,512]{3,2,1,0:T(8,128)} custom-call(f32[3,32,16,512]{3,2,1,0:T(8,128)} %shard_map.89.given, f32[2,3,160,512]{3,2,1,0:T(8,128)S(1)} %get-tuple-element.51.refs_2_.state, bf16[3,512,1024]{2,1,0:T(8,128)(2,1)S(1)} %get-tuple-element.39.weights.refs_0_, ...), custom_call_target="tpu_custom_call", output_to_operand_aliasing={{}: (0, {})} | custom-call | flops 1 | bytes 1 | tf_op jit(solution)/shard_map/pallas_call | solution.py:24
  (18 shorter events, 0.0 us)
Async XLA Ops:
  0.0 9.3 %copy-start = (f32[3,32,16,512]{3,2,1,0:T(8,128)S(1)}, f32[3,32,16,512]{3,2,1,0:T(8,128)}, u32[]{:S(2)}) copy-start(f32[3,32,16,512]{3,2,1,0:T(8,128)} %param.8) | copy-start | bytes 9437188
  1.1 5.6 %collective-permute-start.1 = (f32[3,16,512]{2,1,0:T(8,128)S(1)}, f32[3,16,512]{2,1,0:T(8,128)S(1)}, u32[]{:S(2)}, u32[]{:S(2)}) collective-permute-start(f32[3,16,512]{2,1,0:T(8,128)S(1)} %get-tuple-element.57), channel_id=1, source_target_pairs={{0,30},{2,0},{4,2},{6,4},{8,6},{10,8},{12,10},{14,12},{16,14},{18,... | collective-permute-start | bytes 294920 | tf_op jit(solution)/shard_map/ppermute | solution.py:540
  1.8 4.8 %collective-permute-start = (f32[3,16,512]{2,1,0:T(8,128)S(1)}, f32[3,16,512]{2,1,0:T(8,128)S(1)}, u32[]{:S(2)}, u32[]{:S(2)}) collective-permute-start(f32[3,16,512]{2,1,0:T(8,128)S(1)} %get-tuple-element.58), channel_id=1, source_target_pairs={{0,2},{2,4},{4,6},{6,8},{8,10},{10,12},{12,14},{14,16},{16,18},{18... | collective-permute-start | bytes 294920 | tf_op jit(solution)/shard_map/ppermute | solution.py:537
  6.7 18.5 %collective-permute-start.3 = (bf16[224,512]{1,0:T(8,128)(2,1)}, bf16[224,512]{1,0:T(8,128)(2,1)S(1)}, u32[]{:S(2)}, u32[]{:S(2)}) collective-permute-start(bf16[224,512]{1,0:T(8,128)(2,1)} %get-tuple-element.32.mine.refs_0_), channel_id=1, source_target_pairs={{0,16},{2,18},{4,20},{6,22},{8,24},{10,26},{12,28},{14,30},{16,0},... | collective-permute-start | bytes 688136 | tf_op jit(solution)/shard_map/ppermute | solution.py:564
  9.1 6.2 %collective-permute-start.2 = (f32[3,32,512]{2,1,0:T(8,128)}, f32[3,32,512]{2,1,0:T(8,128)S(1)}, u32[]{:S(2)}, u32[]{:S(2)}) collective-permute-start(f32[3,32,512]{2,1,0:T(8,128)} %get-tuple-element.35), channel_id=1, source_target_pairs={{0,1},{1,0},{2,3},{3,2},{4,5},{5,4},{6,7},{7,6},{8,9},{9,8},{10,11... | collective-permute-start | bytes 589832 | tf_op jit(solution)/shard_map/ppermute | solution.py:505
  9.3 0.9 %copy-start.2 = (f32[15,8,512]{2,1,0:T(8,128)S(1)}, f32[15,8,512]{2,1,0:T(8,128)}, u32[]{:S(2)}) copy-start(f32[15,8,512]{2,1,0:T(8,128)} %get-tuple-element.36.coef_in.coef.refs_8_) | copy-start | bytes 737284
  10.3 29.7 %copy-start.1 = (bf16[3,1024,1024]{2,1,0:T(8,128)(2,1)S(1)}, bf16[3,1024,1024]{2,1,0:T(8,128)(2,1)}, u32[]{:S(2)}) copy-start(bf16[3,1024,1024]{2,1,0:T(8,128)(2,1)} %matrix.1) | copy-start | bytes 18874372
  10.3 29.7 %copy-start.4 = (bf16[224,512]{1,0:T(8,128)(2,1)S(1)}, bf16[224,512]{1,0:T(8,128)(2,1)}, u32[]{:S(2)}) copy-start(bf16[224,512]{1,0:T(8,128)(2,1)} %get-tuple-element.32.mine.refs_0_) | copy-start | bytes 688132
  11.8 28.1 %collective-permute-start.4 = (bf16[3,64,512]{2,1,0:T(8,128)(2,1)S(1)}, bf16[3,64,512]{2,1,0:T(8,128)(2,1)S(1)}, u32[]{:S(2)}, u32[]{:S(2)}) collective-permute-start(bf16[3,64,512]{2,1,0:T(8,128)(2,1)S(1)} %get-tuple-element.44.refs_1_), channel_id=1, source_target_pairs={{0,16},{2,18},{4,20},{6,22},{8,24},{10,26},{12,28},{14,30},{16,0},... | collective-permute-start | bytes 589832 | tf_op jit(solution)/shard_map/ppermute | solution.py:580
  25.2 42.1 %collective-permute-start.6 = (bf16[3,160,512]{2,1,0:T(8,128)(2,1)S(1)}, bf16[3,160,512]{2,1,0:T(8,128)(2,1)S(1)}, u32[]{:S(2)}, u32[]{:S(2)}) collective-permute-start(bf16[3,160,512]{2,1,0:T(8,128)(2,1)S(1)} %get-tuple-element.41.refs_0_), channel_id=1, source_target_pairs={{0,16},{2,18},{4,20},{6,22},{8,24},{10,26},{12,28},{14,30},{16,0},... | collective-permute-start | bytes 1474568 | tf_op jit(solution)/shard_map/ppermute | solution.py:591
  39.9 27.4 %collective-permute-start.5 = (bf16[3,128,512]{2,1,0:T(8,128)(2,1)S(1)}, bf16[3,128,512]{2,1,0:T(8,128)(2,1)S(1)}, u32[]{:S(2)}, u32[]{:S(2)}) collective-permute-start(bf16[3,128,512]{2,1,0:T(8,128)(2,1)S(1)} %get-tuple-element.45.refs_0_), channel_id=1, source_target_pairs={{0,16},{2,18},{4,20},{6,22},{8,24},{10,26},{12,28},{14,30},{16,0},... | collective-permute-start | bytes 1179656 | tf_op jit(solution)/shard_map/ppermute | solution.py:593
  67.3 21.2 %collective-permute-start.10 = (bf16[3,96,512]{2,1,0:T(8,128)(2,1)S(1)}, bf16[3,96,512]{2,1,0:T(8,128)(2,1)S(1)}, u32[]{:S(2)}, u32[]{:S(2)}) collective-permute-start(bf16[3,96,512]{2,1,0:T(8,128)(2,1)S(1)} %get-tuple-element.56.mine), channel_id=1, source_target_pairs={{0,16},{2,18},{4,20},{6,22},{8,24},{10,26},{12,28},{14,30},{16,0},... | collective-permute-start | bytes 884744 | tf_op jit(solution)/shard_map/ppermute | solution.py:625
  68.4 15.0 %copy-start.3 = (f32[15,8,512]{2,1,0:T(8,128)S(1)}, f32[15,8,512]{2,1,0:T(8,128)}, u32[]{:S(2)}) copy-start(f32[15,8,512]{2,1,0:T(8,128)} %get-tuple-element.36.coef_in.coef.refs_8_) | copy-start | bytes 737284
  69.9 13.4 %collective-permute-start.9 = (bf16[2,3,32,512]{3,2,1,0:T(8,128)(2,1)S(1)}, bf16[2,3,32,512]{3,2,1,0:T(8,128)(2,1)S(1)}, u32[]{:S(2)}, u32[]{:S(2)}) collective-permute-start(bf16[2,3,32,512]{3,2,1,0:T(8,128)(2,1)S(1)} %get-tuple-element.55), channel_id=1, source_target_pairs={{0,1},{1,0},{2,3},{3,2},{4,5},{5,4},{6,7},{7,6},{8,9},{9,8},{10,11... | collective-permute-start | bytes 589832 | tf_op jit(solution)/shard_map/ppermute | solution.py:505
  70.3 5.0 %collective-permute-start.7 = (bf16[2,3,16,512]{3,2,1,0:T(8,128)(2,1)S(1)}, bf16[2,3,16,512]{3,2,1,0:T(8,128)(2,1)S(1)}, u32[]{:S(2)}, u32[]{:S(2)}) collective-permute-start(bf16[2,3,16,512]{3,2,1,0:T(8,128)(2,1)S(1)} %get-tuple-element.53), channel_id=1, source_target_pairs={{0,2},{2,4},{4,6},{6,8},{8,10},{10,12},{12,14},{14,0},{16,18},{18,... | collective-permute-start | bytes 294920 | tf_op jit(solution)/shard_map/ppermute | solution.py:655
  73.2 10.1 %collective-permute-start.8 = (bf16[2,3,16,512]{3,2,1,0:T(8,128)(2,1)S(1)}, bf16[2,3,16,512]{3,2,1,0:T(8,128)(2,1)S(1)}, u32[]{:S(2)}, u32[]{:S(2)}) collective-permute-start(bf16[2,3,16,512]{3,2,1,0:T(8,128)(2,1)S(1)} %get-tuple-element.54), channel_id=1, source_target_pairs={{0,14},{2,0},{4,2},{6,4},{8,6},{10,8},{12,10},{14,12},{16,30},{18,... | collective-permute-start | bytes 294920 | tf_op jit(solution)/shard_map/ppermute | solution.py:656

commit v10 on v9

--- a/solution.py
+++ b/solution.py
@@ -525,7 +525,7 @@
     quarter = na // 4
     ends = 2
     side = na // 2
-    a_lo, a_cut, a_hi, x_hi = ends, ends + na // 4, side + ends, na - ends
+    a_lo, a_cut, a_hi, x_hi = ends, na // 4, 7 * na // 16, na - ends
     opposite = [(i, (i + count // 2) % count) for i in range(count)]
 
     def dma(*dims):

time: 93.9 us -> 94.3 us (level)
  the two profiles are of different devices: /device:TPU:7 before, /device:TPU:24 now
where the time goes in v10:
time: 94.3 us; the launch traced here: 94.2 us
  waiting for transfers between devices  58.9 us (62%)
  Pallas kernels  24.9 us (26%)
  starting transfers between devices  8.22 us (9%)
  local copies, waits for them, and re-layouts  2.07 us (2%)
    pallas_call x9, Pallas kernels, call(): pl.pallas_call(body, out_shape=out_shape, in_specs=in_specs, out_specs=ou...  24.9 us
    ppermute x1, waiting for transfers between devices, per_device(): opp_a = lax.ppermute(mid_a, 'ang', opposite)  24.7 us
    ppermute x1, waiting for transfers between devices, per_device(): opp_1 = lax.ppermute(out1, 'ang', opposite)  14.4 us
    ppermute x1, waiting for transfers between devices, per_device(): opp_b = lax.ppermute(mid_b, 'ang', opposite)  11.6 us
    ppermute x1, waiting for transfers between devices, per_device(): angle_before = lax.ppermute(last, 'ang', ring(count, 1))  7.46 us
    ppermute x1, starting transfers between devices, per_device(): opp_b = lax.ppermute(mid_b, 'ang', opposite)  2.65 us
    ppermute x1, starting transfers between devices, per_device(): angle_after = lax.ppermute(first, 'ang', ring(count, -1))  2.62 us
  transfers between devices with their start and end apart: 11, of which 6 were waited for; matrix products, arithmetic and copies ran while one was open for 0% of the time, Pallas kernels for 20%

profile of v10, /device:TPU:24, one launch (start us, length us, event | category | flops | bytes accessed | tf_op | source)
XLA Modules:
  0.0 94.2 jit_solution(8026878909339567035)
XLA Ops:
  0.0 1.1 %slice_bitcast_fusion = (f32[3,16,512]{2,1,0:T(8,128)S(1)}, f32[3,16,512]{2,1,0:T(8,128)S(1)}) fusion(f32[3,32,16,512]{3,2,1,0:T(8,128)} %param.8), kind=kLoop, calls=%fused_computation | loop fusion | bytes 393216 | tf_op jit(solution)/shard_map/squeeze | solution.py:541
  1.1 0.9 collective-permute-start.1
  2.0 2.8 %shard_map.82 = (f32[3,32,512]{2,1,0:T(8,128)}, bf16[176,512]{1,0:T(8,128)(2,1)}, f32[15,8,512]{2,1,0:T(8,128)}) custom-call(f32[3,512,512]{2,1,0:T(8,128)} %bitcast.10, f32[1,512]{1,0:T(1,128)} %bitcast.13, f32[3]{0:T(128)} %diff.1, f32[3,512]{1,0:T(4,128)} %ang.1, f32[4]{0:T(128)} %rate.1, s32[4,3]{1,0:T(4,128)} %smap.1, s32[3,32]{1,0:T(4,128)} %flags.1), custom_call_target="tpu_custom_call" | custom-call | flops 1 | bytes 1 | tf_op jit(solution)/shard_map/pallas_call | solution.py:24
  4.8 1.6 %collective-permute-start.2 = (f32[3,32,512]{2,1,0:T(8,128)}, f32[3,32,512]{2,1,0:T(8,128)S(1)}, u32[]{:S(2)}, u32[]{:S(2)}) collective-permute-start(f32[3,32,512]{2,1,0:T(8,128)} %get-tuple-element.35), channel_id=1, source_target_pairs={{0,1},{1,0},{2,3},{3,2},{4,5},{5,4},{6,7},{7,6},{8,9},{9,8},{10,11... | collective-permute-start | bytes 589832 | tf_op jit(solution)/shard_map/ppermute | solution.py:505
  6.4 0.5 collective-permute-done.before
  6.9 0.3 collective-permute-start.3
  7.3 0.9 %copy-done.2 = f32[15,8,512]{2,1,0:T(8,128)S(1)} copy-done((f32[15,8,512]{2,1,0:T(8,128)S(1)}, f32[15,8,512]{2,1,0:T(8,128)}, u32[]{:S(2)}) %copy-start.2) | copy-done | bytes 245784
  8.2 1.7 %shard_map.85 = (bf16[3,48,512]{2,1,0:T(8,128)(2,1)S(1)}, bf16[3,128,512]{2,1,0:T(8,128)(2,1)S(1)}) custom-call(f32[3,512,512]{2,1,0:T(8,128)S(1)} %bitcast.11, f32[15,8,512]{2,1,0:T(8,128)S(1)} %copy-done.2), custom_call_target="tpu_custom_call" | custom-call | flops 1 | bytes 1 | tf_op jit(solution)/shard_map/pallas_call | solution.py:24
  9.9 2.7 %collective-permute-start.4 = (bf16[3,48,512]{2,1,0:T(8,128)(2,1)S(1)}, bf16[3,48,512]{2,1,0:T(8,128)(2,1)S(1)}, u32[]{:S(2)}, u32[]{:S(2)}) collective-permute-start(bf16[3,48,512]{2,1,0:T(8,128)(2,1)S(1)} %get-tuple-element.44.refs_1_), channel_id=1, source_target_pairs={{0,16},{2,18},{4,20},{6,22},{8,24},{10,26},{12,28},{14,30},{16,0},... | collective-permute-start | bytes 442376 | tf_op jit(solution)/shard_map/ppermute | solution.py:580
  12.6 0.2 collective-permute-done.2.low.high
  12.8 3.0 %shard_map.83 = (bf16[3,128,512]{2,1,0:T(8,128)(2,1)S(1)}, bf16[3,160,512]{2,1,0:T(8,128)(2,1)S(1)}) custom-call(f32[3,512,512]{2,1,0:T(8,128)S(1)} %bitcast.12, f32[3,16,512]{2,1,0:T(8,128)S(1)} %collective-permute-done.before, f32[3,16,512]{2,1,0:T(8,128)S(1)} %collective-permute-done.1.after, f32[3,32,512]{2,1,0:T(8,128)S(1)} %collective-permute-done.2.low.high, ...), custom_call_target="tpu_custom_call" | custom-call | flops 1 | bytes 1 | tf_op jit(solution)/shard_map/pallas_call | solution.py:24
  15.8 24.7 %collective-permute-done.3.theirs.refs_2_ = bf16[176,512]{1,0:T(8,128)(2,1)S(1)} collective-permute-done((bf16[176,512]{1,0:T(8,128)(2,1)}, bf16[176,512]{1,0:T(8,128)(2,1)S(1)}, u32[]{:S(2)}, u32[]{:S(2)}) %collective-permute-start.3) | collective-permute-done | bytes 180256 | tf_op jit(solution)/shard_map/ppermute | solution.py:564
  40.5 11.6 %collective-permute-done.4.refs_3_ = bf16[3,48,512]{2,1,0:T(8,128)(2,1)S(1)} collective-permute-done((bf16[3,48,512]{2,1,0:T(8,128)(2,1)S(1)}, bf16[3,48,512]{2,1,0:T(8,128)(2,1)S(1)}, u32[]{:S(2)}, u32[]{:S(2)}) %collective-permute-start.4) | collective-permute-done | bytes 147488 | tf_op jit(solution)/shard_map/ppermute | solution.py:580
  52.1 2.4 %shard_map.84 = (bf16[3,512,1024]{2,1,0:T(8,128)(2,1)S(1)}, f32[2,3,32,128]{3,2,1,0:T(8,128)S(1)}) custom-call(bf16[3,1024,1024]{2,1,0:T(8,128)(2,1)S(1)} %copy-done.1, bf16[176,512]{1,0:T(8,128)(2,1)S(1)} %copy-done.4, bf16[176,512]{1,0:T(8,128)(2,1)S(1)} %collective-permute-done.3.theirs.refs_2_), custom_call_target="tpu_custom_call" | custom-call | flops 1 | bytes 1 | tf_op jit(solution)/shard_map/pallas_call | solution.py:24
  54.5 2.0 %shard_map.86.refs_2_ = f32[2,3,96,512]{3,2,1,0:T(8,128)S(1)} custom-call(bf16[3,512,1024]{2,1,0:T(8,128)(2,1)S(1)} %get-tuple-element.39.weights.refs_0_, f32[2,3,32,128]{3,2,1,0:T(8,128)S(1)} %get-tuple-element.40.keep.refs_1_, bf16[176,512]{1,0:T(8,128)(2,1)S(1)} %copy-done.4, bf16[3,48,512]{2,1,0:T(8,128)(2,1)S(1)} %get-tuple-element.44.refs_1_, ...), custom_call_target="tpu_custom_call" | custom-call | flops 1 | bytes 1 | tf_op jit(solution)/shard_map/pallas_call | solution.py:24
  56.6 14.4 %collective-permute-done.5.refs_1_ = bf16[3,128,512]{2,1,0:T(8,128)(2,1)S(1)} collective-permute-done((bf16[3,128,512]{2,1,0:T(8,128)(2,1)S(1)}, bf16[3,128,512]{2,1,0:T(8,128)(2,1)S(1)}, u32[]{:S(2)}, u32[]{:S(2)}) %collective-permute-start.5) | collective-permute-done | bytes 393248 | tf_op jit(solution)/shard_map/ppermute | solution.py:593
  71.0 1.0 %shard_map.87.refs_3_ = f32[2,3,128,512]{3,2,1,0:T(8,128)S(1)} custom-call(bf16[3,512,1024]{2,1,0:T(8,128)(2,1)S(1)} %get-tuple-element.39.weights.refs_0_, f32[2,3,32,128]{3,2,1,0:T(8,128)S(1)} %get-tuple-element.40.keep.refs_1_, bf16[3,128,512]{2,1,0:T(8,128)(2,1)S(1)} %get-tuple-element.45.refs_0_, bf16[3,128,512]{2,1,0:T(8,128)(2,1)S(1)} %collective-permute-done.5.refs_1_), custom_call_target="tpu_custom_call" | custom-call | flops 1 | bytes 1 | tf_op jit(solution)/shard_map/pallas_call | solution.py:24
  72.0 1.5 %shard_map.88 = (f32[2,3,128,512]{3,2,1,0:T(8,128)S(1)}, f32[2,3,256,512]{3,2,1,0:T(8,128)S(1)}, bf16[2,3,32,512]{3,2,1,0:T(8,128)(2,1)S(1)}, bf16[2,3,16,512]{3...) custom-call(bf16[3,512,1024]{2,1,0:T(8,128)(2,1)S(1)} %get-tuple-element.39.weights.refs_0_, ...), custom_call_target="tpu_custom_call" | custom-call | flops 1 | bytes 1 | tf_op jit(solution)/shard_map/pallas_call | solution.py:24
  73.5 0.1 collective-permute-start.9
  73.6 0.1 collective-permute-start.7
  73.7 2.6 %collective-permute-start.8 = (bf16[2,3,16,512]{3,2,1,0:T(8,128)(2,1)S(1)}, bf16[2,3,16,512]{3,2,1,0:T(8,128)(2,1)S(1)}, u32[]{:S(2)}, u32[]{:S(2)}) collective-permute-start(bf16[2,3,16,512]{3,2,1,0:T(8,128)(2,1)S(1)} %get-tuple-element.54), channel_id=1, source_target_pairs={{0,14},{2,0},{4,2},{6,4},{8,6},{10,8},{12,10},{14,12},{16,30},{18,... | collective-permute-start | bytes 294920 | tf_op jit(solution)/shard_map/ppermute | solution.py:656
  76.3 7.5 %collective-permute-done.7.refs_4_ = bf16[2,3,16,512]{3,2,1,0:T(8,128)(2,1)S(1)} collective-permute-done((bf16[2,3,16,512]{3,2,1,0:T(8,128)(2,1)S(1)}, bf16[2,3,16,512]{3,2,1,0:T(8,128)(2,1)S(1)}, u32[]{:S(2)}, u32[]{:S(2)}) %collective-permute-start.7) | collective-permute-done | bytes 98336 | tf_op jit(solution)/shard_map/ppermute | solution.py:655
  83.8 4.6 %shard_map.89.given = f32[3,32,16,512]{3,2,1,0:T(8,128)} custom-call(bf16[3,512,1024]{2,1,0:T(8,128)(2,1)S(1)} %get-tuple-element.39.weights.refs_0_, f32[2,3,32,128]{3,2,1,0:T(8,128)S(1)} %get-tuple-element.40.keep.refs_1_, f32[2,3,128,512]{3,2,1,0:T(8,128)S(1)} %get-tuple-element.51.refs_2_.state, f32[2,3,256,512]{3,2,1,0:T(8,128)S(1)} %get-tuple-element.52.refs_3_.outer, ...), custom_call_target="tpu_custom_call" | custom-call | flops 1 | bytes 1 | tf_op jit(solution)/shard_map/pallas_call | solution.py:24
  88.5 5.7 %shard_map.90 = f32[3,32,16,512]{3,2,1,0:T(8,128)} custom-call(f32[3,32,16,512]{3,2,1,0:T(8,128)} %shard_map.89.given, f32[2,3,128,512]{3,2,1,0:T(8,128)S(1)} %get-tuple-element.51.refs_2_.state, bf16[3,512,1024]{2,1,0:T(8,128)(2,1)S(1)} %get-tuple-element.39.weights.refs_0_, ...), custom_call_target="tpu_custom_call", output_to_operand_aliasing={{}: (0, {})} | custom-call | flops 1 | bytes 1 | tf_op jit(solution)/shard_map/pallas_call | solution.py:24
  (18 shorter events, 0.0 us)
Async XLA Ops:
  0.0 7.3 %copy-start = (f32[3,32,16,512]{3,2,1,0:T(8,128)S(1)}, f32[3,32,16,512]{3,2,1,0:T(8,128)}, u32[]{:S(2)}) copy-start(f32[3,32,16,512]{3,2,1,0:T(8,128)} %param.8) | copy-start | bytes 9437188
  1.1 5.3 %collective-permute-start.1 = (f32[3,16,512]{2,1,0:T(8,128)S(1)}, f32[3,16,512]{2,1,0:T(8,128)S(1)}, u32[]{:S(2)}, u32[]{:S(2)}) collective-permute-start(f32[3,16,512]{2,1,0:T(8,128)S(1)} %get-tuple-element.57), channel_id=1, source_target_pairs={{0,30},{2,0},{4,2},{6,4},{8,6},{10,8},{12,10},{14,12},{16,14},{18,... | collective-permute-start | bytes 294920 | tf_op jit(solution)/shard_map/ppermute | solution.py:540
  2.0 4.9 %collective-permute-start = (f32[3,16,512]{2,1,0:T(8,128)S(1)}, f32[3,16,512]{2,1,0:T(8,128)S(1)}, u32[]{:S(2)}, u32[]{:S(2)}) collective-permute-start(f32[3,16,512]{2,1,0:T(8,128)S(1)} %get-tuple-element.58), channel_id=1, source_target_pairs={{0,2},{2,4},{4,6},{6,8},{8,10},{10,12},{12,14},{14,16},{16,18},{18... | collective-permute-start | bytes 294920 | tf_op jit(solution)/shard_map/ppermute | solution.py:537
  4.8 7.9 %collective-permute-start.2 = (f32[3,32,512]{2,1,0:T(8,128)}, f32[3,32,512]{2,1,0:T(8,128)S(1)}, u32[]{:S(2)}, u32[]{:S(2)}) collective-permute-start(f32[3,32,512]{2,1,0:T(8,128)} %get-tuple-element.35), channel_id=1, source_target_pairs={{0,1},{1,0},{2,3},{3,2},{4,5},{5,4},{6,7},{7,6},{8,9},{9,8},{10,11... | collective-permute-start | bytes 589832 | tf_op jit(solution)/shard_map/ppermute | solution.py:505
  6.9 33.6 %collective-permute-start.3 = (bf16[176,512]{1,0:T(8,128)(2,1)}, bf16[176,512]{1,0:T(8,128)(2,1)S(1)}, u32[]{:S(2)}, u32[]{:S(2)}) collective-permute-start(bf16[176,512]{1,0:T(8,128)(2,1)} %get-tuple-element.32.mine.refs_0_), channel_id=1, source_target_pairs={{0,16},{2,18},{4,20},{6,22},{8,24},{10,26},{12,28},{14,30},{16,0},... | collective-permute-start | bytes 540680 | tf_op jit(solution)/shard_map/ppermute | solution.py:564
  7.3 0.9 %copy-start.2 = (f32[15,8,512]{2,1,0:T(8,128)S(1)}, f32[15,8,512]{2,1,0:T(8,128)}, u32[]{:S(2)}) copy-start(f32[15,8,512]{2,1,0:T(8,128)} %get-tuple-element.36.coef_in.coef.refs_8_) | copy-start | bytes 737284
  8.2 43.9 %copy-start.1 = (bf16[3,1024,1024]{2,1,0:T(8,128)(2,1)S(1)}, bf16[3,1024,1024]{2,1,0:T(8,128)(2,1)}, u32[]{:S(2)}) copy-start(bf16[3,1024,1024]{2,1,0:T(8,128)(2,1)} %matrix.1) | copy-start | bytes 18874372
  8.2 43.9 %copy-start.4 = (bf16[176,512]{1,0:T(8,128)(2,1)S(1)}, bf16[176,512]{1,0:T(8,128)(2,1)}, u32[]{:S(2)}) copy-start(bf16[176,512]{1,0:T(8,128)(2,1)} %get-tuple-element.32.mine.refs_0_) | copy-start | bytes 540676
  9.9 42.2 %collective-permute-start.4 = (bf16[3,48,512]{2,1,0:T(8,128)(2,1)S(1)}, bf16[3,48,512]{2,1,0:T(8,128)(2,1)S(1)}, u32[]{:S(2)}, u32[]{:S(2)}) collective-permute-start(bf16[3,48,512]{2,1,0:T(8,128)(2,1)S(1)} %get-tuple-element.44.refs_1_), channel_id=1, source_target_pairs={{0,16},{2,18},{4,20},{6,22},{8,24},{10,26},{12,28},{14,30},{16,0},... | collective-permute-start | bytes 442376 | tf_op jit(solution)/shard_map/ppermute | solution.py:580
  40.5 30.5 %collective-permute-start.6 = (bf16[3,160,512]{2,1,0:T(8,128)(2,1)S(1)}, bf16[3,160,512]{2,1,0:T(8,128)(2,1)S(1)}, u32[]{:S(2)}, u32[]{:S(2)}) collective-permute-start(bf16[3,160,512]{2,1,0:T(8,128)(2,1)S(1)} %get-tuple-element.41.refs_0_), channel_id=1, source_target_pairs={{0,16},{2,18},{4,20},{6,22},{8,24},{10,26},{12,28},{14,30},{16,0},... | collective-permute-start | bytes 1474568 | tf_op jit(solution)/shard_map/ppermute | solution.py:591
  52.1 18.9 %collective-permute-start.5 = (bf16[3,128,512]{2,1,0:T(8,128)(2,1)S(1)}, bf16[3,128,512]{2,1,0:T(8,128)(2,1)S(1)}, u32[]{:S(2)}, u32[]{:S(2)}) collective-permute-start(bf16[3,128,512]{2,1,0:T(8,128)(2,1)S(1)} %get-tuple-element.45.refs_0_), channel_id=1, source_target_pairs={{0,16},{2,18},{4,20},{6,22},{8,24},{10,26},{12,28},{14,30},{16,0},... | collective-permute-start | bytes 1179656 | tf_op jit(solution)/shard_map/ppermute | solution.py:593
  71.0 17.5 %collective-permute-start.10 = (bf16[3,128,512]{2,1,0:T(8,128)(2,1)S(1)}, bf16[3,128,512]{2,1,0:T(8,128)(2,1)S(1)}, u32[]{:S(2)}, u32[]{:S(2)}) collective-permute-start(bf16[3,128,512]{2,1,0:T(8,128)(2,1)S(1)} %get-tuple-element.56.mine), channel_id=1, source_target_pairs={{0,16},{2,18},{4,20},{6,22},{8,24},{10,26},{12,28},{14,30},{16,0},... | collective-permute-start | bytes 1179656 | tf_op jit(solution)/shard_map/ppermute | solution.py:625
  72.0 11.8 %copy-start.3 = (f32[15,8,512]{2,1,0:T(8,128)S(1)}, f32[15,8,512]{2,1,0:T(8,128)}, u32[]{:S(2)}) copy-start(f32[15,8,512]{2,1,0:T(8,128)} %get-tuple-element.36.coef_in.coef.refs_8_) | copy-start | bytes 737284
  73.5 10.2 %collective-permute-start.9 = (bf16[2,3,32,512]{3,2,1,0:T(8,128)(2,1)S(1)}, bf16[2,3,32,512]{3,2,1,0:T(8,128)(2,1)S(1)}, u32[]{:S(2)}, u32[]{:S(2)}) collective-permute-start(bf16[2,3,32,512]{3,2,1,0:T(8,128)(2,1)S(1)} %get-tuple-element.55), channel_id=1, source_target_pairs={{0,1},{1,0},{2,3},{3,2},{4,5},{5,4},{6,7},{7,6},{8,9},{9,8},{10,11... | collective-permute-start | bytes 589832 | tf_op jit(solution)/shard_map/ppermute | solution.py:505
  73.6 10.2 %collective-permute-start.7 = (bf16[2,3,16,512]{3,2,1,0:T(8,128)(2,1)S(1)}, bf16[2,3,16,512]{3,2,1,0:T(8,128)(2,1)S(1)}, u32[]{:S(2)}, u32[]{:S(2)}) collective-permute-start(bf16[2,3,16,512]{3,2,1,0:T(8,128)(2,1)S(1)} %get-tuple-element.53), channel_id=1, source_target_pairs={{0,2},{2,4},{4,6},{6,8},{8,10},{10,12},{12,14},{14,0},{16,18},{18,... | collective-permute-start | bytes 294920 | tf_op jit(solution)/shard_map/ppermute | solution.py:655
  73.7 10.1 %collective-permute-start.8 = (bf16[2,3,16,512]{3,2,1,0:T(8,128)(2,1)S(1)}, bf16[2,3,16,512]{3,2,1,0:T(8,128)(2,1)S(1)}, u32[]{:S(2)}, u32[]{:S(2)}) collective-permute-start(bf16[2,3,16,512]{3,2,1,0:T(8,128)(2,1)S(1)} %get-tuple-element.54), channel_id=1, source_target_pairs={{0,14},{2,0},{4,2},{6,4},{8,6},{10,8},{12,10},{14,12},{16,30},{18,... | collective-permute-start | bytes 294920 | tf_op jit(solution)/shard_map/ppermute | solution.py:656

commit v11 on v10

--- a/solution.py
+++ b/solution.py
@@ -525,7 +525,7 @@
     quarter = na // 4
     ends = 2
     side = na // 2
-    a_lo, a_cut, a_hi, x_hi = ends, na // 4, 7 * na // 16, na - ends
+    a_lo, a_hi, x_hi = ends, side, na - ends
     opposite = [(i, (i + count // 2) % count) for i in range(count)]
 
     def dma(*dims):
@@ -543,10 +543,10 @@
     conc = concentration.reshape(ns, na * nz, nr)
     field = pltpu.VMEM((ns, na * nz, nr), F32)
     *edges, mid_a, coef = call(
-        functools.partial(head_kernel, (na, nz, a_lo, a_cut, planes)),
+        functools.partial(head_kernel, (na, nz, a_lo, a_hi, planes)),
         [shape(ns, na, nr)] * n_edges
         + [
-            shape(ns * (a_cut - a_lo) * half + na, nr, dtype=BF16),
+            shape(ns * (a_hi - a_lo) * half + na, nr, dtype=BF16),
             shape(RATE + 3, half, nr),
         ],
         [HBM] * 7,
@@ -563,21 +563,19 @@
     mid_a, (angle_before, angle_after) = after(mid_a, (angle_before, angle_after))
     opp_a = lax.ppermute(mid_a, "ang", opposite)
     low, high = plane_halos(edges, planes)
-    bounds = (a_cut, a_hi, x_hi)
-    mid_b, mid_x = call(
+    (mid_x,) = call(
         functools.partial(
             inner_kernel,
             (na, nz),
-            tuple((k, ((bounds[k], bounds[k + 1] - bounds[k]),)) for k in range(2)),
+            ((0, ((a_hi, x_hi - a_hi),)),),
         ),
-        [message(bounds[k + 1] - bounds[k]) for k in range(2)],
+        [message(x_hi - a_hi)],
         [ANY, VM],
-        [VM] * 2,
+        [VM],
         [field, pltpu.SemaphoreType.DMA],
         (conc, coef),
         8,
     )
-    opp_b = lax.ppermute(mid_b, "ang", opposite)
     out1, out2 = call(
         functools.partial(frame_kernel, (na, nz, ends, planes)),
         [message(na // 2), message(na // 2 + 2 * ends)],
@@ -587,9 +585,8 @@
         (conc, angle_before, angle_after, low, high, coef),
         8,
     )
-    out2, opp_a = after(out2, opp_a)
+    (out1, out2), opp_a = after((out1, out2), opp_a)
     opp_2 = lax.ppermute(out2, "ang", opposite)
-    out1, opp_b = after(out1, opp_b)
     opp_1 = lax.ppermute(out1, "ang", opposite)
 
     weights, keep = call(
@@ -605,19 +602,14 @@
     def state(angles):
         return shape(2, ns, angles * half, nr)
 
-    count_a, count_b = a_cut - a_lo, a_hi - a_cut
+    count_a = a_hi - a_lo
     (mid_first,) = call(
-        functools.partial(
-            radial_kernel,
-            (((0, a_lo, 0, count_a),), ((0, a_cut, count_a, count_b),)),
-            (),
-            half,
-        ),
-        [state(count_a + count_b)],
-        [VM] * 6,
+        functools.partial(radial_kernel, (((0, a_lo, 0, count_a),),), (), half),
+        [state(count_a)],
+        [VM] * 4,
         [VM],
         [],
-        (weights, keep, mid_a, mid_b, opp_a, opp_b),
+        (weights, keep, mid_a, opp_a),
         8,
     )
     opp_1, mid_first = after(opp_1, mid_first)
@@ -638,7 +630,7 @@
             radial_edges_kernel,
             (na, nz, planes),
             plan,
-            ((0, 0, 0, ends, count_a + count_b), (1, 0, 1, 0, side)),
+            ((0, 0, 0, ends, count_a), (1, 0, 1, 0, side)),
             half,
         ),
         [state(a_hi + ends), state(na)]

time: 94.3 us -> 95.1 us (level)
  the two profiles are of different devices: /device:TPU:24 before, /device:TPU:5 now
where the time goes in v11:
time: 95.1 us; the launch traced here: 94.9 us
  waiting for transfers between devices  58.3 us (61%)
  Pallas kernels  23.7 us (25%)
  starting transfers between devices  10.7 us (11%)
  local copies, waits for them, and re-layouts  2.06 us (2%)
    ppermute x1, waiting for transfers between devices, per_device(): opp_1 = lax.ppermute(out1, 'ang', opposite)  34.1 us
    pallas_call x9, Pallas kernels, call(): pl.pallas_call(body, out_shape=out_shape, in_specs=in_specs, out_specs=ou...  23.7 us
    ppermute x1, waiting for transfers between devices, per_device(): angle_after = lax.ppermute(first, 'ang', ring(count, -1))  7.26 us
    ppermute x1, waiting for transfers between devices, per_device(): opp_a = lax.ppermute(mid_a, 'ang', opposite)  7.11 us
    ppermute x2, waiting for transfers between devices, plane_halos(): got = lax.ppermute(edges[0], 'ax', [(0, 1), (1, 0)])  5.5 us
    ppermute x1, waiting for transfers between devices, per_device(): angle_before = lax.ppermute(last, 'ang', ring(count, 1))  4.36 us
    ppermute x2, starting transfers between devices, plane_halos(): got = lax.ppermute(edges[0], 'ax', [(0, 1), (1, 0)])  2.49 us
    ppermute x1, starting transfers between devices, per_device(): opp_a = lax.ppermute(mid_a, 'ang', opposite)  2.37 us
  transfers between devices with their start and end apart: 10, of which 5 were waited for; matrix products, arithmetic and copies ran while one was open for 0% of the time, Pallas kernels for 19%

profile of v11, /device:TPU:5, one launch (start us, length us, event | category | flops | bytes accessed | tf_op | source)
XLA Modules:
  0.0 94.9 jit_solution(5525209461493354199)
XLA Ops:
  0.0 1.1 %slice_bitcast_fusion = (f32[3,16,512]{2,1,0:T(8,128)S(1)}, f32[3,16,512]{2,1,0:T(8,128)S(1)}) fusion(f32[3,32,16,512]{3,2,1,0:T(8,128)} %param.8), kind=kLoop, calls=%fused_computation | loop fusion | bytes 393216 | tf_op jit(solution)/shard_map/squeeze | solution.py:541
  1.1 0.7 collective-permute-start.1
  1.8 2.0 %collective-permute-start = (f32[3,16,512]{2,1,0:T(8,128)S(1)}, f32[3,16,512]{2,1,0:T(8,128)S(1)}, u32[]{:S(2)}, u32[]{:S(2)}) collective-permute-start(f32[3,16,512]{2,1,0:T(8,128)S(1)} %get-tuple-element.52), channel_id=1, source_target_pairs={{0,2},{2,4},{4,6},{6,8},{8,10},{10,12},{12,14},{14,16},{16,18},{18... | collective-permute-start | bytes 294920 | tf_op jit(solution)/shard_map/ppermute | solution.py:537
  3.8 3.3 %shard_map.82 = (f32[3,32,512]{2,1,0:T(8,128)}, bf16[368,512]{1,0:T(8,128)(2,1)}, f32[15,8,512]{2,1,0:T(8,128)}) custom-call(f32[3,512,512]{2,1,0:T(8,128)} %bitcast.10, f32[1,512]{1,0:T(1,128)} %bitcast.13, f32[3]{0:T(128)} %diff.1, f32[3,512]{1,0:T(4,128)} %ang.1, f32[4]{0:T(128)} %rate.1, s32[4,3]{1,0:T(4,128)} %smap.1, s32[3,32]{1,0:T(4,128)} %flags.1), custom_call_target="tpu_custom_call" | custom-call | flops 1 | bytes 1 | tf_op jit(solution)/shard_map/pallas_call | solution.py:24
  7.2 2.4 %collective-permute-start.3 = (bf16[368,512]{1,0:T(8,128)(2,1)}, bf16[368,512]{1,0:T(8,128)(2,1)S(1)}, u32[]{:S(2)}, u32[]{:S(2)}) collective-permute-start(bf16[368,512]{1,0:T(8,128)(2,1)} %get-tuple-element.29.mine.refs_0_), channel_id=1, source_target_pairs={{0,16},{2,18},{4,20},{6,22},{8,24},{10,26},{12,28},{14,30},{16,0},... | collective-permute-start | bytes 1130504 | tf_op jit(solution)/shard_map/ppermute | solution.py:564
  9.6 1.2 %collective-permute-start.2 = (f32[3,32,512]{2,1,0:T(8,128)}, f32[3,32,512]{2,1,0:T(8,128)S(1)}, u32[]{:S(2)}, u32[]{:S(2)}) collective-permute-start(f32[3,32,512]{2,1,0:T(8,128)} %get-tuple-element.32), channel_id=1, source_target_pairs={{0,1},{1,0},{2,3},{3,2},{4,5},{5,4},{6,7},{7,6},{8,9},{9,8},{10,11... | collective-permute-start | bytes 589832 | tf_op jit(solution)/shard_map/ppermute | solution.py:505
  10.8 5.5 %collective-permute-done.2.low.high = f32[3,32,512]{2,1,0:T(8,128)S(1)} collective-permute-done((f32[3,32,512]{2,1,0:T(8,128)}, f32[3,32,512]{2,1,0:T(8,128)S(1)}, u32[]{:S(2)}, u32[]{:S(2)}) %collective-permute-start.2) | collective-permute-done | bytes 196640 | tf_op jit(solution)/shard_map/ppermute | solution.py:505
  16.3 0.9 copy-done.2
  17.2 3.0 %shard_map.83 = (bf16[3,128,512]{2,1,0:T(8,128)(2,1)S(1)}, bf16[3,160,512]{2,1,0:T(8,128)(2,1)S(1)}) custom-call(f32[3,512,512]{2,1,0:T(8,128)S(1)} %bitcast.11, f32[3,16,512]{2,1,0:T(8,128)S(1)} %collective-permute-done.before, f32[3,16,512]{2,1,0:T(8,128)S(1)} %collective-permute-done.1.after, f32[3,32,512]{2,1,0:T(8,128)S(1)} %collective-permute-done.2.low.high, ...), custom_call_target="tpu_custom_call" | custom-call | flops 1 | bytes 1 | tf_op jit(solution)/shard_map/pallas_call | solution.py:24
  20.2 7.1 %collective-permute-done.3.theirs.refs_1_ = bf16[368,512]{1,0:T(8,128)(2,1)S(1)} collective-permute-done((bf16[368,512]{1,0:T(8,128)(2,1)}, bf16[368,512]{1,0:T(8,128)(2,1)S(1)}, u32[]{:S(2)}, u32[]{:S(2)}) %collective-permute-start.3) | collective-permute-done | bytes 376864 | tf_op jit(solution)/shard_map/ppermute | solution.py:564
  27.3 2.4 %collective-permute-start.4 = (bf16[3,128,512]{2,1,0:T(8,128)(2,1)S(1)}, bf16[3,128,512]{2,1,0:T(8,128)(2,1)S(1)}, u32[]{:S(2)}, u32[]{:S(2)}) collective-permute-start(bf16[3,128,512]{2,1,0:T(8,128)(2,1)S(1)} %get-tuple-element.40.refs_0_), channel_id=1, source_target_pairs={{0,16},{2,18},{4,20},{6,22},{8,24},{10,26},{12,28},{14,30},{16,0},... | collective-permute-start | bytes 1179656 | tf_op jit(solution)/shard_map/ppermute | solution.py:590
  29.7 1.2 %shard_map.85.mine = bf16[3,112,512]{2,1,0:T(8,128)(2,1)S(1)} custom-call(f32[3,512,512]{2,1,0:T(8,128)S(1)} %bitcast.12, f32[15,8,512]{2,1,0:T(8,128)S(1)} %copy-done.2), custom_call_target="tpu_custom_call" | custom-call | flops 1 | bytes 1 | tf_op jit(solution)/shard_map/pallas_call | solution.py:24
  30.9 2.4 %shard_map.84 = (bf16[3,512,1024]{2,1,0:T(8,128)(2,1)S(1)}, f32[2,3,32,128]{3,2,1,0:T(8,128)S(1)}) custom-call(bf16[3,1024,1024]{2,1,0:T(8,128)(2,1)S(1)} %copy-done.1, bf16[368,512]{1,0:T(8,128)(2,1)S(1)} %copy-done.4, bf16[368,512]{1,0:T(8,128)(2,1)S(1)} %collective-permute-done.3.theirs.refs_1_), custom_call_target="tpu_custom_call" | custom-call | flops 1 | bytes 1 | tf_op jit(solution)/shard_map/pallas_call | solution.py:24
  33.3 1.1 %shard_map.86.refs_2_ = f32[2,3,112,512]{3,2,1,0:T(8,128)S(1)} custom-call(bf16[3,512,1024]{2,1,0:T(8,128)(2,1)S(1)} %get-tuple-element.37.weights.refs_0_, f32[2,3,32,128]{3,2,1,0:T(8,128)S(1)} %get-tuple-element.38.keep.refs_1_, bf16[368,512]{1,0:T(8,128)(2,1)S(1)} %copy-done.4, bf16[368,512]{1,0:T(8,128)(2,1)S(1)} %collective-permute-done.3.theirs.refs_1_), custom_call_target="tpu_custom_call" | custom-call | flops 1 | bytes 1 | tf_op jit(solution)/shard_map/pallas_call | solution.py:24
  34.4 34.1 %collective-permute-done.4.refs_1_ = bf16[3,128,512]{2,1,0:T(8,128)(2,1)S(1)} collective-permute-done((bf16[3,128,512]{2,1,0:T(8,128)(2,1)S(1)}, bf16[3,128,512]{2,1,0:T(8,128)(2,1)S(1)}, u32[]{:S(2)}, u32[]{:S(2)}) %collective-permute-start.4) | collective-permute-done | bytes 393248 | tf_op jit(solution)/shard_map/ppermute | solution.py:590
  68.5 1.0 %shard_map.87.refs_3_ = f32[2,3,128,512]{3,2,1,0:T(8,128)S(1)} custom-call(bf16[3,512,1024]{2,1,0:T(8,128)(2,1)S(1)} %get-tuple-element.37.weights.refs_0_, f32[2,3,32,128]{3,2,1,0:T(8,128)S(1)} %get-tuple-element.38.keep.refs_1_, bf16[3,128,512]{2,1,0:T(8,128)(2,1)S(1)} %get-tuple-element.40.refs_0_, bf16[3,128,512]{2,1,0:T(8,128)(2,1)S(1)} %collective-permute-done.4.refs_1_), custom_call_target="tpu_custom_call" | custom-call | flops 1 | bytes 1 | tf_op jit(solution)/shard_map/pallas_call | solution.py:24
  69.5 1.5 %shard_map.88 = (f32[2,3,144,512]{3,2,1,0:T(8,128)S(1)}, f32[2,3,256,512]{3,2,1,0:T(8,128)S(1)}, bf16[2,3,32,512]{3,2,1,0:T(8,128)(2,1)S(1)}, bf16[2,3,16,512]{3...) custom-call(bf16[3,512,1024]{2,1,0:T(8,128)(2,1)S(1)} %get-tuple-element.37.weights.refs_0_, ...), custom_call_target="tpu_custom_call" | custom-call | flops 1 | bytes 1 | tf_op jit(solution)/shard_map/pallas_call | solution.py:24
  71.0 1.3 %collective-permute-start.8 = (bf16[2,3,32,512]{3,2,1,0:T(8,128)(2,1)S(1)}, bf16[2,3,32,512]{3,2,1,0:T(8,128)(2,1)S(1)}, u32[]{:S(2)}, u32[]{:S(2)}) collective-permute-start(bf16[2,3,32,512]{3,2,1,0:T(8,128)(2,1)S(1)} %get-tuple-element.49), channel_id=1, source_target_pairs={{0,1},{1,0},{2,3},{3,2},{4,5},{5,4},{6,7},{7,6},{8,9},{9,8},{10,11... | collective-permute-start | bytes 589832 | tf_op jit(solution)/shard_map/ppermute | solution.py:505
  72.3 0.6 collective-permute-start.6
  72.9 0.1 collective-permute-start.7
  73.1 4.4 %collective-permute-done.6.refs_4_ = bf16[2,3,16,512]{3,2,1,0:T(8,128)(2,1)S(1)} collective-permute-done((bf16[2,3,16,512]{3,2,1,0:T(8,128)(2,1)S(1)}, bf16[2,3,16,512]{3,2,1,0:T(8,128)(2,1)S(1)}, u32[]{:S(2)}, u32[]{:S(2)}) %collective-permute-start.6) | collective-permute-done | bytes 98336 | tf_op jit(solution)/shard_map/ppermute | solution.py:647
  77.4 7.3 %collective-permute-done.7.refs_5_ = bf16[2,3,16,512]{3,2,1,0:T(8,128)(2,1)S(1)} collective-permute-done((bf16[2,3,16,512]{3,2,1,0:T(8,128)(2,1)S(1)}, bf16[2,3,16,512]{3,2,1,0:T(8,128)(2,1)S(1)}, u32[]{:S(2)}, u32[]{:S(2)}) %collective-permute-start.7) | collective-permute-done | bytes 98336 | tf_op jit(solution)/shard_map/ppermute | solution.py:648
  84.7 4.8 %shard_map.89.given = f32[3,32,16,512]{3,2,1,0:T(8,128)} custom-call(bf16[3,512,1024]{2,1,0:T(8,128)(2,1)S(1)} %get-tuple-element.37.weights.refs_0_, f32[2,3,32,128]{3,2,1,0:T(8,128)S(1)} %get-tuple-element.38.keep.refs_1_, f32[2,3,144,512]{3,2,1,0:T(8,128)S(1)} %get-tuple-element.45.refs_2_.state, f32[2,3,256,512]{3,2,1,0:T(8,128)S(1)} %get-tuple-element.46.refs_3_.outer, ...), custom_call_target="tpu_custom_call" | custom-call | flops 1 | bytes 1 | tf_op jit(solution)/shard_map/pallas_call | solution.py:24
  89.5 5.4 %shard_map.90 = f32[3,32,16,512]{3,2,1,0:T(8,128)} custom-call(f32[3,32,16,512]{3,2,1,0:T(8,128)} %shard_map.89.given, f32[2,3,144,512]{3,2,1,0:T(8,128)S(1)} %get-tuple-element.45.refs_2_.state, bf16[3,512,1024]{2,1,0:T(8,128)(2,1)S(1)} %get-tuple-element.37.weights.refs_0_, ...), custom_call_target="tpu_custom_call", output_to_operand_aliasing={{}: (0, {})} | custom-call | flops 1 | bytes 1 | tf_op jit(solution)/shard_map/pallas_call | solution.py:24
  (16 shorter events, 0.0 us)
Async XLA Ops:
  0.0 16.3 %copy-start = (f32[3,32,16,512]{3,2,1,0:T(8,128)S(1)}, f32[3,32,16,512]{3,2,1,0:T(8,128)}, u32[]{:S(2)}) copy-start(f32[3,32,16,512]{3,2,1,0:T(8,128)} %param.8) | copy-start | bytes 9437188
  1.1 6.1 %collective-permute-start.1 = (f32[3,16,512]{2,1,0:T(8,128)S(1)}, f32[3,16,512]{2,1,0:T(8,128)S(1)}, u32[]{:S(2)}, u32[]{:S(2)}) collective-permute-start(f32[3,16,512]{2,1,0:T(8,128)S(1)} %get-tuple-element.51), channel_id=1, source_target_pairs={{0,30},{2,0},{4,2},{6,4},{8,6},{10,8},{12,10},{14,12},{16,14},{18,... | collective-permute-start | bytes 294920 | tf_op jit(solution)/shard_map/ppermute | solution.py:540
  1.8 5.3 %collective-permute-start = (f32[3,16,512]{2,1,0:T(8,128)S(1)}, f32[3,16,512]{2,1,0:T(8,128)S(1)}, u32[]{:S(2)}, u32[]{:S(2)}) collective-permute-start(f32[3,16,512]{2,1,0:T(8,128)S(1)} %get-tuple-element.52), channel_id=1, source_target_pairs={{0,2},{2,4},{4,6},{6,8},{8,10},{10,12},{12,14},{14,16},{16,18},{18... | collective-permute-start | bytes 294920 | tf_op jit(solution)/shard_map/ppermute | solution.py:537
  7.2 20.1 %collective-permute-start.3 = (bf16[368,512]{1,0:T(8,128)(2,1)}, bf16[368,512]{1,0:T(8,128)(2,1)S(1)}, u32[]{:S(2)}, u32[]{:S(2)}) collective-permute-start(bf16[368,512]{1,0:T(8,128)(2,1)} %get-tuple-element.29.mine.refs_0_), channel_id=1, source_target_pairs={{0,16},{2,18},{4,20},{6,22},{8,24},{10,26},{12,28},{14,30},{16,0},... | collective-permute-start | bytes 1130504 | tf_op jit(solution)/shard_map/ppermute | solution.py:564
  9.6 6.7 %collective-permute-start.2 = (f32[3,32,512]{2,1,0:T(8,128)}, f32[3,32,512]{2,1,0:T(8,128)S(1)}, u32[]{:S(2)}, u32[]{:S(2)}) collective-permute-start(f32[3,32,512]{2,1,0:T(8,128)} %get-tuple-element.32), channel_id=1, source_target_pairs={{0,1},{1,0},{2,3},{3,2},{4,5},{5,4},{6,7},{7,6},{8,9},{9,8},{10,11... | collective-permute-start | bytes 589832 | tf_op jit(solution)/shard_map/ppermute | solution.py:505
  16.3 0.9 copy-start.2
  17.2 13.6 %copy-start.1 = (bf16[3,1024,1024]{2,1,0:T(8,128)(2,1)S(1)}, bf16[3,1024,1024]{2,1,0:T(8,128)(2,1)}, u32[]{:S(2)}) copy-start(bf16[3,1024,1024]{2,1,0:T(8,128)(2,1)} %matrix.1) | copy-start | bytes 18874372
  17.2 13.7 %copy-start.4 = (bf16[368,512]{1,0:T(8,128)(2,1)S(1)}, bf16[368,512]{1,0:T(8,128)(2,1)}, u32[]{:S(2)}) copy-start(bf16[368,512]{1,0:T(8,128)(2,1)} %get-tuple-element.29.mine.refs_0_) | copy-start | bytes 1130500
  27.3 41.1 %collective-permute-start.5 = (bf16[3,160,512]{2,1,0:T(8,128)(2,1)S(1)}, bf16[3,160,512]{2,1,0:T(8,128)(2,1)S(1)}, u32[]{:S(2)}, u32[]{:S(2)}) collective-permute-start(bf16[3,160,512]{2,1,0:T(8,128)(2,1)S(1)} %get-tuple-element.39.refs_0_), channel_id=1, source_target_pairs={{0,16},{2,18},{4,20},{6,22},{8,24},{10,26},{12,28},{14,30},{16,0},... | collective-permute-start | bytes 1474568 | tf_op jit(solution)/shard_map/ppermute | solution.py:589
  27.3 41.1 %collective-permute-start.4 = (bf16[3,128,512]{2,1,0:T(8,128)(2,1)S(1)}, bf16[3,128,512]{2,1,0:T(8,128)(2,1)S(1)}, u32[]{:S(2)}, u32[]{:S(2)}) collective-permute-start(bf16[3,128,512]{2,1,0:T(8,128)(2,1)S(1)} %get-tuple-element.40.refs_0_), channel_id=1, source_target_pairs={{0,16},{2,18},{4,20},{6,22},{8,24},{10,26},{12,28},{14,30},{16,0},... | collective-permute-start | bytes 1179656 | tf_op jit(solution)/shard_map/ppermute | solution.py:590
  68.5 21.1 %collective-permute-start.9 = (bf16[3,112,512]{2,1,0:T(8,128)(2,1)S(1)}, bf16[3,112,512]{2,1,0:T(8,128)(2,1)S(1)}, u32[]{:S(2)}, u32[]{:S(2)}) collective-permute-start(bf16[3,112,512]{2,1,0:T(8,128)(2,1)S(1)} %shard_map.85.mine), channel_id=1, source_target_pairs={{0,16},{2,18},{4,20},{6,22},{8,24},{10,26},{12,28},{14,30},{16,0},... | collective-permute-start | bytes 1032200 | tf_op jit(solution)/shard_map/ppermute | solution.py:617
  69.5 15.2 %copy-start.3 = (f32[15,8,512]{2,1,0:T(8,128)S(1)}, f32[15,8,512]{2,1,0:T(8,128)}, u32[]{:S(2)}) copy-start(f32[15,8,512]{2,1,0:T(8,128)} %get-tuple-element.33.coef_in.coef.refs_8_) | copy-start | bytes 737284
  71.0 13.7 %collective-permute-start.8 = (bf16[2,3,32,512]{3,2,1,0:T(8,128)(2,1)S(1)}, bf16[2,3,32,512]{3,2,1,0:T(8,128)(2,1)S(1)}, u32[]{:S(2)}, u32[]{:S(2)}) collective-permute-start(bf16[2,3,32,512]{3,2,1,0:T(8,128)(2,1)S(1)} %get-tuple-element.49), channel_id=1, source_target_pairs={{0,1},{1,0},{2,3},{3,2},{4,5},{5,4},{6,7},{7,6},{8,9},{9,8},{10,11... | collective-permute-start | bytes 589832 | tf_op jit(solution)/shard_map/ppermute | solution.py:505
  72.3 5.1 %collective-permute-start.6 = (bf16[2,3,16,512]{3,2,1,0:T(8,128)(2,1)S(1)}, bf16[2,3,16,512]{3,2,1,0:T(8,128)(2,1)S(1)}, u32[]{:S(2)}, u32[]{:S(2)}) collective-permute-start(bf16[2,3,16,512]{3,2,1,0:T(8,128)(2,1)S(1)} %get-tuple-element.47), channel_id=1, source_target_pairs={{0,2},{2,4},{4,6},{6,8},{8,10},{10,12},{12,14},{14,0},{16,18},{18,... | collective-permute-start | bytes 294920 | tf_op jit(solution)/shard_map/ppermute | solution.py:647
  72.9 11.8 %collective-permute-start.7 = (bf16[2,3,16,512]{3,2,1,0:T(8,128)(2,1)S(1)}, bf16[2,3,16,512]{3,2,1,0:T(8,128)(2,1)S(1)}, u32[]{:S(2)}, u32[]{:S(2)}) collective-permute-start(bf16[2,3,16,512]{3,2,1,0:T(8,128)(2,1)S(1)} %get-tuple-element.48), channel_id=1, source_target_pairs={{0,14},{2,0},{4,2},{6,4},{8,6},{10,8},{12,10},{14,12},{16,30},{18,... | collective-permute-start | bytes 294920 | tf_op jit(solution)/shard_map/ppermute | solution.py:648
